TPU v7x, 256 devices: a whole 4x4x8 slice. The times are simulated.
256 devices in a mesh: dp: 4 (over x_lo, core), eig: 64 (over z, x_hi, y).
Axes of the slice: x: 4 (x_hi: 2, x_lo: 2; x = x_hi * 2 + x_lo), y: 4, z: 8, core: 2. Of those that a mesh axis runs over, the one named last changes fastest.
Arguments:
- activations: bfloat16 [8192, 5120], P(('dp', 'eig')), may hold values from -6 to 6
- out_grads: bfloat16 [13824, 8192], P('eig', 'dp'), may hold values from -6 to 6
- basis_in: bfloat16 [5120, 5120], P('eig'), may hold values from -0.078125 to 0.078125
- basis_out: bfloat16 [13824, 13824], P('eig'), may hold values from -0.0546875 to 0.0546875
- block_ids: int32 [8], replicated, may hold values from 0 to 107, as said below
- seq_lens: int32 [8], P('dp'), may hold values from 128 to 1024, as said below
- query_grads: bfloat16 [32, 5120, 1024], P('dp', 'eig'), may hold values from -7.6293945e-05 to 7.6293945e-05
Outputs:
- scores: float32 [8, 32], P(None, 'dp')
Inputs may be any that keep to these rules, and one draw needn't show every extreme that they name: `block_ids`: distinct block numbers; blocks of 128 columns of basis_out. `seq_lens`: slots of a sequence from its count on are padding.
All inputs are finite; a program needn't handle non-finite values.
Results may differ from a plain program's by a relative error of at most 0.0052.
Values may be sent and summed in bfloat16 or wider, within the bound.
No kernel may reach another device: no remote copies, remote signals or barrier semaphores. Data moves between devices by JAX's collectives and lax.ppermute only.
A program may use at most 128 MiB of HBM per device.

v0:
```python
import jax
import jax.numpy as jnp
from jax import lax
from jax.sharding import PartitionSpec as P

BLOCK = 128
NSEL = 8
LEN = 1024


def per_device(activations, out_grads, basis_in, basis_out, block_ids, seq_lens, query_grads):
    rotated_act = lax.dot_general(
        basis_in,
        lax.all_gather(activations, "eig", axis=0, tiled=True),
        (((1,), (1,)), ((), ())),
        preferred_element_type=jnp.float32,
    ).astype(jnp.bfloat16)
    chosen_basis = jnp.concatenate(
        [
            lax.dynamic_slice_in_dim(basis_out, block_ids[number] * BLOCK, BLOCK, 1)
            for number in range(NSEL)
        ],
        axis=1,
    )
    width = chosen_basis.shape[1]
    summed_grad = lax.psum(
        lax.dot_general(
            chosen_basis, out_grads, (((0,), (0,)), ((), ())), preferred_element_type=jnp.float32
        ),
        "eig",
    ).astype(jnp.bfloat16)
    seq_count = seq_lens.shape[0]
    live_slots = lax.broadcasted_iota(jnp.int32, (seq_count, LEN), 1) < seq_lens[:, None]
    rotated_grad = jnp.where(
        live_slots.reshape(1, seq_count * LEN), summed_grad, jnp.zeros((), jnp.bfloat16)
    )
    grad_blocks = rotated_grad.reshape(width, seq_count, LEN)
    act_blocks = rotated_act.reshape(rotated_act.shape[0], seq_count, LEN)
    seq_grads = jnp.einsum(
        "ksl,isl->sik", grad_blocks, act_blocks, preferred_element_type=jnp.float32
    ).astype(jnp.bfloat16)
    every_seq = lax.all_gather(seq_grads, "dp", axis=0, tiled=True)
    partial_scores = jnp.einsum(
        "sik,qik->sq", every_seq, query_grads, preferred_element_type=jnp.float32
    )
    return lax.psum(partial_scores, "eig")


def solution(mesh):
    in_specs = (
        P(("dp", "eig"), None),
        P("eig", "dp"),
        P("eig", None),
        P("eig", None),
        P(),
        P("dp"),
        P("dp", "eig", None),
    )
    out_specs = P(None, "dp")
    return jax.shard_map(
        per_device, mesh=mesh, in_specs=in_specs, out_specs=out_specs, check_vma=False
    )
```

profile of v0, /device:TPU:24, one launch (start us, length us, event | category | flops | bytes accessed | tf_op | source)
XLA Modules:
  0.0 710.6 jit_solution(18155666218534469740)
XLA Ops:
  6.5 0.0 copy-start
  6.5 0.0 all-gather.3.cloned.1.call-start
  6.5 0.7 all-gather.3.cloned.1.call-update
  7.3 0.0 all-gather.5.cloned.1.call-start
  7.3 1.6 fusion.10
  14.0 0.7 iota_compare_fusion
  14.7 0.8 dynamic-slice_dynamic-update-slice_fusion.7
  15.6 0.8 dynamic-slice_dynamic-update-slice_fusion.6
  16.4 0.8 dynamic-slice_dynamic-update-slice_fusion.5
  17.3 0.8 dynamic-slice_dynamic-update-slice_fusion.4
  18.1 0.8 dynamic-slice_dynamic-update-slice_fusion.3
  18.9 0.8 dynamic-slice_dynamic-update-slice_fusion.2
  19.8 0.8 dynamic-slice_dynamic-update-slice_fusion.1
  20.6 0.8 dynamic-slice_dynamic-update-slice_fusion
  21.5 5.8 fusion.11
  27.2 443.5 %all-reduce.1 = bf16[1024,2048]{1,0:T(8,128)(2,1)} all-reduce(f32[1024,2048]{1,0:T(8,128)} %fusion.11), channel_id=1, replica_groups=mesh['dp'=4,'eig'=64] {'eig'}, use_global_device_ids=true, to_apply=%region_0.0 | all-reduce | flops 2097152 | bytes 12582912 | tf_op jit(solution)/shard_map/psum | solution.py:26
  470.7 4.4 convert_select_fusion
  475.1 6.5 copy.13
  481.6 10.7 %convolution_convert_fusion = bf16[80,2048]{1,0:T(8,128)(2,1)S(1)} fusion(bf16[80,5120]{1,0:T(8,128)(2,1)S(1)} %copy-done.2, bf16[2048,5120]{1,0:T(8,128)(2,1)} %all-gather.3.cloned.1.call-done), kind=kOutput, calls=%fused_computation.1 | convolution fusion | flops 1677885440 | bytes 22118400 | tf_op jit(solution)/shard_map/dot_general | solution.py:12
  492.3 1.6 convolution_convert_fusion.1
  493.9 0.0 all-gather.5.cloned.1.call-update
  493.9 33.8 %all-gather.5.cloned.1.call-done = bf16[8,80,1024]{2,1,0:T(8,128)(2,1)} async-done(((bf16[2,80,1024]{2,1,0:T(8,128)(2,1)}), bf16[8,80,1024]{2,1,0:T(8,128)(2,1)}) %all-gather.5.cloned.1.call-update) | async-done | bytes 1310736 | tf_op jit(solution)/shard_map/all_gather | solution.py:42
  527.8 4.1 fusion.3
  531.9 171.9 %psum.15 = f32[8,8]{1,0:T(8,128)} all-reduce(f32[8,8]{1,0:T(8,128)S(1)} %fusion.3), channel_id=1, replica_groups=mesh['dp'=4,'eig'=64] {'eig'}, use_global_device_ids=true, to_apply=%region_1.2 | all-reduce | flops 64 | bytes 512 | tf_op jit(solution)/shard_map/psum | solution.py:46
  (7 shorter events, 0.0 us)
Async XLA Ops:
  6.5 521.2 %copy-start = (bf16[8,80,1024]{2,1,0:T(8,128)(2,1)S(1)}, bf16[8,80,1024]{2,1,0:T(8,128)(2,1)}, u32[]{:S(2)}) copy-start(bf16[8,80,1024]{2,1,0:T(8,128)(2,1)} %param.13) | copy-start | bytes 3932164
  6.5 475.1 %all-gather.3.cloned.1.call-start = ((), (), s32[]{:S(2)}) async-start(), calls=%async_computation | async-start | bytes 21299200 | tf_op jit(solution)/shard_map/all_gather | solution.py:14
  7.3 520.5 %all-gather.5.cloned.1.call-start = ((), (), s32[]{:S(2)}) async-start(), calls=%async_computation.1 | async-start | bytes 1638400 | tf_op jit(solution)/shard_map/all_gather | solution.py:42
  475.1 6.5 copy-start.2
  481.6 10.7 %copy-start.1 = (bf16[1024,2048]{0,1:T(8,128)(2,1)S(1)}, bf16[1024,2048]{0,1:T(8,128)(2,1)}, u32[]{:S(2)}) copy-start(bf16[1024,2048]{0,1:T(8,128)(2,1)} %copy.13) | copy-start | bytes 12582916
Sparse Core Ops, SparseCore 0:
  11.0 329.2 all-gather.2
  494.1 33.6 all-gather.4
where the time goes:
time: 723 us; the launch traced here: 711 us
  blocking collectives  615 us (85%)
  waiting for transfers between devices  34.5 us (5%)
  matrix products  22.2 us (3%)
  between operations  18.5 us (3%)
  local copies, waits for them, and re-layouts  14.8 us (2%)
    psum x1, blocking collectives, per_device(): lax.psum(lax.dot_general(chosen_basis, out_grads, (((0,), (0,)), ((), ())...  443 us
    psum x1, blocking collectives, per_device(): return lax.psum(partial_scores, 'eig')  172 us
    all_gather x1, waiting for transfers between devices, per_device(): every_seq = lax.all_gather(seq_grads, 'dp', axis=0, tiled=True)  33.8 us
  transfers between devices with their start and end apart: 2, of which 1 were waited for; matrix products, arithmetic and copies ran while one was open for 4% of the time, Pallas kernels for 0%

commit v1 on v0

v1 whole, which is shorter than its diff:
```python
import jax
import jax.numpy as jnp
import numpy as np
from jax import lax
from jax.sharding import Mesh, PartitionSpec as P

BLOCK = 128
NSEL = 8
LEN = 1024
BF = jnp.bfloat16
F32 = jnp.float32


def spread(x, axes, count):
    return lax.all_to_all(
        jnp.broadcast_to(x[None], (count,) + x.shape), axes, split_axis=0, concat_axis=0, tiled=True
    )


def dot(a, b, ca, cb):
    return lax.dot_general(a, b, (((ca,), (cb,)), ((), ())), preferred_element_type=F32)


def per_device(activations, out_grads, basis_in, basis_out, block_ids, seq_lens, query_grads):
    chosen = jnp.concatenate(
        [
            lax.dynamic_slice_in_dim(basis_out, block_ids[number] * BLOCK, BLOCK, 1)
            for number in range(NSEL)
        ],
        axis=1,
    )
    y = lax.axis_index("y")
    rows = out_grads.shape[0]
    grads_out = out_grads.reshape(rows, 16, 4, 32).transpose(2, 0, 1, 3).reshape(4, rows, 512)
    grads = lax.all_to_all(grads_out, "y", split_axis=0, concat_axis=0, tiled=True)
    chosen_all = spread(chosen, "y", 4)
    partial = dot(chosen_all.reshape(4 * rows, 1024), grads.reshape(4 * rows, 512), 0, 0).astype(BF)
    parts = lax.all_to_all(partial.reshape(16, 64, 512), ("xh", "z"), split_axis=0, concat_axis=0, tiled=True)
    summed = jnp.sum(parts.astype(F32), axis=0).astype(BF)
    col = lax.broadcasted_iota(jnp.int32, (1, 512), 1)
    pos = (col // 32 % 8) * 128 + y * 32 + col % 32
    limit = jnp.where(col < 256, seq_lens[0], seq_lens[1])
    rotated = jnp.where(pos < limit, summed, jnp.zeros((), BF))
    rotated_all = spread(rotated, "z", 8).reshape(512, 512)

    acts = lax.all_gather(activations, "xh", axis=0, tiled=True)
    acts = lax.all_gather(acts, "z", axis=0, tiled=True)
    basis = spread(basis_in, "y", 4).reshape(320, -1)
    rotated_act = dot(basis, acts, 1, 1).astype(BF)
    act_all = lax.all_gather(rotated_act, "xh", axis=0, tiled=True)

    seq_parts = jnp.stack(
        [dot(act_all[:, s * 256 : s * 256 + 256], rotated_all[:, s * 256 : s * 256 + 256], 1, 1) for s in range(2)]
    ).astype(BF)
    sent = seq_parts.reshape(2, 8, 80, 512).transpose(1, 0, 2, 3)
    got = lax.all_to_all(sent, ("xh", "y"), split_axis=0, concat_axis=0, tiled=True)
    seq_grads = jnp.sum(got.reshape(2, 4, 2, 80, 512).astype(F32), axis=1).astype(BF)
    every = lax.all_gather(seq_grads, ("xl", "core"), axis=1, tiled=True)
    queries = query_grads.reshape(8, 80, 2, 512)
    scores = sum(
        jnp.einsum("sik,qik->sq", every[h], queries[:, :, h], preferred_element_type=F32) for h in range(2)
    )
    scores = jnp.sum(spread(scores, ("xh", "y"), 8), axis=0)
    return jnp.sum(spread(scores, "z", 8), axis=0)


def solution(mesh):
    fine = Mesh(mesh.devices.reshape(2, 2, 8, 2, 4), ("xl", "core", "z", "xh", "y"))
    dp, eig = ("xl", "core"), ("z", "xh", "y")
    in_specs = (
        P(dp + eig, None),
        P(eig, dp),
        P(eig, None),
        P(eig, None),
        P(),
        P(dp),
        P(dp, eig, None),
    )
    return jax.shard_map(
        per_device, mesh=fine, in_specs=in_specs, out_specs=P(None, dp), check_vma=False
    )
```

time: 723 us -> 259 us (0.36); the launches traced: 711 us -> 257 us
  blocking collectives: 615 us -> 140 us
  waiting for transfers between devices: 34.5 us -> 52.3 us
  starting transfers between devices: 0.04 us -> 13.7 us
  matrix products: 22.2 us -> 9.7 us
    psum x2 -> x0, blocking collectives: 615 us -> none  [the longest x1 443 us: per_device(): lax.psum(lax.dot_general(chosen_basis, out_grads, (((0,), (0,)), ((), ())...]
    all_to_all x0 -> x5, blocking collectives: none -> 117 us  [the longest x3 51.5 us: spread(): lax.all_to_all(jnp.broadcast_to(x[None], (count,) + x.shape), axes, split...]
    all_to_all x0 -> x3, waiting for transfers between devices: none -> 33.5 us  [the longest x2 33.5 us: spread(): lax.all_to_all(jnp.broadcast_to(x[None], (count,) + x.shape), axes, split...]
    all_gather x0 -> x2, blocking collectives: none -> 22.7 us  [the longest x1 13.5 us: per_device(): acts = lax.all_gather(activations, 'xh', axis=0, tiled=True)]
    all_gather x2, waiting for transfers between devices: 33.8 us -> 18.8 us  [the longest x1 18.7 us: per_device(): every = lax.all_gather(seq_grads, ('xl', 'core'), axis=1, tiled=True)]
    all_to_all x0 -> x3, starting transfers between devices: none -> 13.7 us  [the longest x2 8.98 us: spread(): lax.all_to_all(jnp.broadcast_to(x[None], (count,) + x.shape), axes, split...]
    dot_general x4 -> x6, matrix products: 22.2 us -> 9.7 us  [the longest x4 7.4 us: dot(): lax.dot_general(a, b, (((ca,), (cb,)), ((), ())), preferred_element_type=...]
  transfers between devices with their start and end apart: 2 -> 5, of which waited for: 1 -> 3; matrix products, arithmetic and copies ran while one was open for 4% -> 10% of each run, Pallas kernels for 0% -> 0%
where the time goes in v1:
time: 259 us; the launch traced here: 257 us
  blocking collectives  140 us (54%)
  waiting for transfers between devices  52.3 us (20%)
  local copies, waits for them, and re-layouts  20.3 us (8%)
  between operations  18.6 us (7%)
  starting transfers between devices  13.7 us (5%)
  matrix products  9.7 us (4%)
    all_to_all x3, blocking collectives, spread(): lax.all_to_all(jnp.broadcast_to(x[None], (count,) + x.shape), axes, split...  51.5 us
    all_to_all x1, blocking collectives, per_device(): lax.all_to_all(partial.reshape(16, 64, 512), ('xh', 'z'), split_axis=0, c...  45.7 us
    all_to_all x2, waiting for transfers between devices, spread(): lax.all_to_all(jnp.broadcast_to(x[None], (count,) + x.shape), axes, split...  33.5 us
    all_to_all x1, blocking collectives, per_device(): lax.all_to_all(sent, ('xh', 'y'), split_axis=0, concat_axis=0, tiled=True)  19.9 us
    all_gather x1, waiting for transfers between devices, per_device(): every = lax.all_gather(seq_grads, ('xl', 'core'), axis=1, tiled=True)  18.7 us
    all_gather x1, blocking collectives, per_device(): acts = lax.all_gather(activations, 'xh', axis=0, tiled=True)  13.5 us
    all_gather x1, blocking collectives, per_device(): act_all = lax.all_gather(rotated_act, 'xh', axis=0, tiled=True)  9.26 us
    all_to_all x2, starting transfers between devices, spread(): lax.all_to_all(jnp.broadcast_to(x[None], (count,) + x.shape), axes, split...  8.98 us
  transfers between devices with their start and end apart: 5, of which 3 were waited for; matrix products, arithmetic and copies ran while one was open for 10% of the time, Pallas kernels for 0%

profile of v1, /device:TPU:24, one launch (start us, length us, event | category | flops | bytes accessed | tf_op | source)
XLA Modules:
  0.0 256.8 jit_solution(14438870961192848578)
XLA Ops:
  6.5 13.5 %all_gather.12 = bf16[64,5120]{1,0:T(8,128)(2,1)} all-gather(bf16[32,5120]{1,0:T(8,128)(2,1)} %param.7), channel_id=1, replica_groups=mesh['xl'=2,'core'=2,'z'=8,'xh'=2,'y'=4] {'xh'}, dimensions={0}, use_global_device_ids=true | all-gather | bytes 983040 | tf_op jit(solution)/shard_map/all_gather | solution.py:46
  20.7 1.3 copy.26
  22.0 4.7 %all-to-all-start.2 = ((bf16[4,216,512]{2,1,0:T(8,128)(2,1)}), bf16[4,216,512]{2,1,0:T(8,128)(2,1)S(1)}, u32[]{:S(2)}, u32[]{:S(2)}) async-start(bf16[4,216,512]{2,1,0:T(8,128)(2,1)} %copy.26), calls=%async_computation.2 | async-start | bytes 1769472 | tf_op jit(solution)/shard_map/all_to_all | solution.py:35
  32.4 0.8 dynamic-slice_dynamic-update-slice_fusion.7
  39.3 24.2 %all_to_all.40 = bf16[4,216,1024]{2,1,0:T(8,128)(2,1)S(1)} all-to-all(bf16[4,216,1024]{2,1,0:T(8,128)(2,1)S(1)} %broadcast_in_dim.54), channel_id=1, replica_groups=mesh['xl'=2,'core'=2,'z'=8,'xh'=2,'y'=4] {'y'}, dimensions={0} | all-to-all | bytes 3538944 | tf_op jit(solution)/shard_map/all_to_all | solution.py:15
  63.6 1.3 bitcast_convert_fusion
  64.9 45.7 %all_to_all.41 = bf16[16,64,512]{2,1,0:T(8,128)(2,1)S(1)} all-to-all(bf16[16,64,512]{2,1,0:T(8,128)(2,1)S(1)} %bitcast.57), channel_id=1, replica_groups=mesh['xl'=2,'core'=2,'z'=8,'xh'=2,'y'=4] {'xh','z'}, dimensions={0} | all-to-all | bytes 2097152 | tf_op jit(solution)/shard_map/all_to_all | solution.py:38
  110.6 2.1 broadcast_in_dim.30
  112.7 5.0 %all-to-all-start = ((bf16[4,80,5120]{2,1,0:T(8,128)(2,1)}), bf16[4,80,5120]{2,1,0:T(8,128)(2,1)}, u32[]{:S(2)}, u32[]{:S(2)}) async-start(bf16[4,80,5120]{2,1,0:T(8,128)(2,1)} %broadcast_in_dim.30), calls=%async_computation | async-start | bytes 6553600 | tf_op jit(solution)/shard_map/all_to_all | solution.py:15
  118.3 1.3 fusion.13
  119.9 33.1 %all-to-all-done = bf16[4,80,5120]{2,1,0:T(8,128)(2,1)} async-done(((bf16[4,80,5120]{2,1,0:T(8,128)(2,1)}), bf16[4,80,5120]{2,1,0:T(8,128)(2,1)}, u32[]{:S(2)}, u32[]{:S(2)}) %all-to-all-start) | async-done | bytes 3276832 | tf_op jit(solution)/shard_map/all_to_all | solution.py:15
  153.0 0.9 broadcast_in_dim.56
  153.8 4.0 %all-to-all-start.4 = ((bf16[8,64,512]{2,1,0:T(8,128)(2,1)}), bf16[8,64,512]{2,1,0:T(8,128)(2,1)S(1)}, u32[]{:S(2)}, u32[]{:S(2)}) async-start(bf16[8,64,512]{2,1,0:T(8,128)(2,1)} %broadcast_in_dim.56), calls=%async_computation.4 | async-start | bytes 1048576 | tf_op jit(solution)/shard_map/all_to_all | solution.py:15
  158.0 5.4 %convolution_convert_fusion.2 = bf16[320,512]{1,0:T(8,128)(2,1)S(1)} fusion(bf16[320,5120]{1,0:T(8,128)(2,1)} %bitcast, bf16[512,5120]{1,0:T(8,128)(2,1)} %all-gather.3.cloned.1.call-done), kind=kOutput, calls=%fused_computation.5 | convolution fusion | flops 1677885440 | bytes 8847360 | tf_op jit(solution)/shard_map/dot_general | solution.py:21
  163.3 9.3 %all_gather.14 = bf16[640,512]{1,0:T(8,128)(2,1)S(1)} all-gather(bf16[320,512]{1,0:T(8,128)(2,1)S(1)} %convolution_convert_fusion.2), channel_id=1, replica_groups=mesh['xl'=2,'core'=2,'z'=8,'xh'=2,'y'=4] {'xh'}, dimensions={0}, use_global_device_ids=true | all-gather | bytes 983040 | tf_op jit(solution)/shard_map/all_gather | solution.py:50
  173.9 19.9 %all_to_all.42 = bf16[8,2,80,512]{3,2,1,0:T(8,128)(2,1)S(1)} all-to-all(bf16[8,2,80,512]{3,2,1,0:T(8,128)(2,1)S(1)} %maximum_bitcast_fusion), channel_id=1, replica_groups=mesh['xl'=2,'core'=2,'z'=8,'xh'=2,'y'=4] {'xh','y'}, dimensions={0} | all-to-all | bytes 2621440 | tf_op jit(solution)/shard_map/all_to_all | solution.py:56
  195.2 1.0 reshape.155
  196.2 3.5 %fusion.18 = (bf16[8,80,1,512]{3,2,1,0:T(2,128)(2,1)S(1)}, bf16[8,80,1,512]{3,2,1,0:T(2,128)(2,1)}) fusion(bf16[8,80,2,512]{3,2,1,0:T(2,128)(2,1)S(1)} %reshape.155), kind=kLoop, calls=%fused_computation.47 | loop fusion | bytes 2621440 | tf_op jit(solution)/shard_map/slice | solution.py:61
  199.7 18.7 %all-gather.5.cloned.1.call-done = bf16[2,8,80,512]{3,2,0,1:T(8,128)(2,1)} async-done(((bf16[2,2,80,512]{3,2,0,1:T(8,128)(2,1)}), bf16[2,8,80,512]{3,2,0,1:T(8,128)(2,1)}) %all-gather.5.cloned.1.call-update) | async-done | bytes 1310736 | tf_op jit(solution)/shard_map/all_gather | solution.py:58
  218.4 1.4 fusion.17
  219.8 1.1 convolution_bitcast_fusion
  220.9 1.2 fusion
  222.1 12.4 %all_to_all.43 = f32[8,8,8]{2,1,0:T(8,128)S(1)} all-to-all(f32[8,8,8]{2,1,0:T(8,128)S(1)} %broadcast_in_dim.57), channel_id=1, replica_groups=mesh['xl'=2,'core'=2,'z'=8,'xh'=2,'y'=4] {'xh','y'}, dimensions={0} | all-to-all | bytes 4096 | tf_op jit(solution)/shard_map/all_to_all | solution.py:15
  234.5 14.8 %all_to_all.44 = f32[8,8,8]{2,1,0:T(8,128)S(1)} all-to-all(f32[8,8,8]{2,1,0:T(8,128)S(1)} %broadcast_in_dim.58), channel_id=1, replica_groups=mesh['xl'=2,'core'=2,'z'=8,'xh'=2,'y'=4] {'z'}, dimensions={0} | all-to-all | bytes 4096 | tf_op jit(solution)/shard_map/all_to_all | solution.py:15
  (42 shorter events, 11.6 us)
Async XLA Ops:
  6.5 13.5 %copy-start.2 = (bf16[216,2048]{1,0:T(8,128)(2,1)S(1)}, bf16[216,2048]{1,0:T(8,128)(2,1)}, u32[]{:S(2)}) copy-start(bf16[216,2048]{1,0:T(8,128)(2,1)} %param.8) | copy-start | bytes 2654212
  6.5 151.4 %all-gather.3.cloned.1.call-start = ((), (), s32[]{:S(2)}) async-start(), calls=%async_computation.8 | async-start | bytes 5898240 | tf_op jit(solution)/shard_map/all_gather | solution.py:47
  20.7 6.0 %copy-start.4 = (s32[8]{0:T(128)S(1)}, s32[8]{0:T(128)}, u32[]{:S(2)}) copy-start(s32[8]{0:T(128)} %param.11) | copy-start | bytes 100
  22.0 17.1 %all-to-all-start.2 = ((bf16[4,216,512]{2,1,0:T(8,128)(2,1)}), bf16[4,216,512]{2,1,0:T(8,128)(2,1)S(1)}, u32[]{:S(2)}, u32[]{:S(2)}) async-start(bf16[4,216,512]{2,1,0:T(8,128)(2,1)} %copy.26), calls=%async_computation.2 | async-start | bytes 1769472 | tf_op jit(solution)/shard_map/all_to_all | solution.py:35
  64.9 45.7 %copy-start.3 = (bf16[80,5120]{1,0:T(8,128)(2,1)S(1)}, bf16[80,5120]{1,0:T(8,128)(2,1)}, u32[]{:S(2)}) copy-start(bf16[80,5120]{1,0:T(8,128)(2,1)} %param.9) | copy-start | bytes 2457604
  112.7 5.0 %copy-start.5 = (s32[2]{0:T(128)S(1)}, s32[2]{0:T(128)}, u32[]{:S(2)}) copy-start(s32[2]{0:T(128)} %param.12) | copy-start | bytes 28
  112.7 40.2 %all-to-all-start = ((bf16[4,80,5120]{2,1,0:T(8,128)(2,1)}), bf16[4,80,5120]{2,1,0:T(8,128)(2,1)}, u32[]{:S(2)}, u32[]{:S(2)}) async-start(bf16[4,80,5120]{2,1,0:T(8,128)(2,1)} %broadcast_in_dim.30), calls=%async_computation | async-start | bytes 6553600 | tf_op jit(solution)/shard_map/all_to_all | solution.py:15
  153.8 19.1 %all-to-all-start.4 = ((bf16[8,64,512]{2,1,0:T(8,128)(2,1)}), bf16[8,64,512]{2,1,0:T(8,128)(2,1)S(1)}, u32[]{:S(2)}, u32[]{:S(2)}) async-start(bf16[8,64,512]{2,1,0:T(8,128)(2,1)} %broadcast_in_dim.56), calls=%async_computation.4 | async-start | bytes 1048576 | tf_op jit(solution)/shard_map/all_to_all | solution.py:15
  157.9 60.5 %all-gather.5.cloned.1.call-start = ((), (), s32[]{:S(2)}) async-start(), calls=%async_computation.9 | async-start | bytes 1638400 | tf_op jit(solution)/shard_map/all_gather | solution.py:58
  193.7 1.4 copy-start.1
  199.7 20.1 %copy-start = (bf16[8,80,1,512]{3,2,1,0:T(2,128)(2,1)S(1)}, bf16[8,80,1,512]{3,2,1,0:T(2,128)(2,1)}, u32[]{:S(2)}) copy-start(bf16[8,80,1,512]{3,2,1,0:T(2,128)(2,1)} %get-tuple-element.8) | copy-start | bytes 1966084
Sparse Core Ops, SparseCore 0:
  20.2 87.9 all-gather.2
  194.8 23.5 all-gather.4

commit v2 on v1

v2 whole, which is shorter than its diff:
```python
import jax
import jax.numpy as jnp
from jax import lax
from jax.experimental import pallas as pl
from jax.experimental.pallas import tpu as pltpu
from jax.sharding import Mesh, PartitionSpec as P

BLOCK = 128
LEN = 1024
BF = jnp.bfloat16
F32 = jnp.float32
SIZES = {"xl": 2, "core": 2, "z": 8, "xh": 2, "y": 4}
DY = (0, 1, -1, 2)
VMEM = pl.BlockSpec(memory_space=pltpu.VMEM)
SMEM = pl.BlockSpec(memory_space=pltpu.SMEM)
ROOM = pltpu.CompilerParams(vmem_limit_bytes=48 * 1024 * 1024)


def shift(x, **by):
    axes = tuple(by)
    count = 1
    for a in axes:
        count *= SIZES[a]
    pairs = []
    for source in range(count):
        rest, target, scale = source, 0, 1
        for a in reversed(axes):
            target += (rest % SIZES[a] + by[a]) % SIZES[a] * scale
            rest //= SIZES[a]
            scale *= SIZES[a]
        pairs.append((source, target))
    return lax.ppermute(x, axes, pairs)


def spread(x, axes, count):
    return lax.all_to_all(
        jnp.broadcast_to(x[None], (count,) + x.shape), axes, split_axis=0, concat_axis=0, tiled=True
    )


def dot(a, b, ca, cb):
    return lax.dot_general(a, b, (((ca,), (cb,)), ((), ())), preferred_element_type=F32)


def pick_kernel(s_ref, b0, b1, g_ref, c_ref, *o_refs):
    c_ref[:, :128] = b0[...]
    c_ref[:, 128:] = b1[...]
    y = s_ref[8]
    xh = pl.program_id(0) // 2
    lane = lax.broadcasted_iota(jnp.int32, (1, 128), 1) // 32
    cols = [g_ref[:, pl.ds(pl.multiple_of((2 * j + xh) * 128, 128), 128)].astype(F32) for j in range(4)]
    for n, dy in enumerate(DY):
        total = None
        for j in range(4):
            moved = pltpu.roll(cols[j], ((j - dy - y + 8) % 4) * 32, 1)
            total = moved if total is None else jnp.where(lane == j, moved, total)
        o_refs[n][...] = total.astype(BF)


def pick(block_ids, y, basis_out, out_grads):
    rows, tokens = out_grads.shape
    scalars = jnp.concatenate([block_ids, y[None].astype(jnp.int32)])
    spec = pltpu.PrefetchScalarGridSpec(
        num_scalar_prefetch=1,
        grid=(4,),
        in_specs=[
            pl.BlockSpec((rows, BLOCK), lambda g, s: (0, s[2 * g])),
            pl.BlockSpec((rows, BLOCK), lambda g, s: (0, s[2 * g + 1])),
            pl.BlockSpec((rows, 1024), lambda g, s: (0, g % 2)),
        ],
        out_specs=[pl.BlockSpec((rows, 256), lambda g, s: (0, g))]
        + [pl.BlockSpec((rows, 128), lambda g, s: (0, g))] * 4,
    )
    return pl.pallas_call(
        pick_kernel,
        grid_spec=spec,
        out_shape=[jax.ShapeDtypeStruct((rows, 1024), BF)] + [jax.ShapeDtypeStruct((rows, 512), BF)] * 4,
        compiler_params=ROOM,
        name="pick",
    )(scalars, basis_out, basis_out, out_grads)


def grads_kernel(c0, c1, c2, c3a, c3b, g0, g1, g2, g3, o_ref):
    for part in range(4):
        ks = slice(part * 256, part * 256 + 256)
        last = c3a[:, ks] if part < 2 else c3b[:, part * 256 - 512 : part * 256 - 256]
        total = dot(c0[:, ks], g0[...], 0, 0) + dot(c1[:, ks], g1[...], 0, 0)
        total += dot(c2[:, ks], g2[...], 0, 0) + dot(last, g3[...], 0, 0)
        o_ref[ks, :] = total.astype(BF)


def acts_kernel(s_ref, a_ref, *refs):
    o_ref = refs[-1]
    core = s_ref[0]
    half = a_ref.shape[1] // 2
    mine = a_ref[:, pl.ds(pl.multiple_of(core * half, 128), half)]
    other = a_ref[:, pl.ds(pl.multiple_of((1 - core) * half, 128), half)]
    row = 0
    for own, sent in zip(refs[:5], refs[5:10]):
        n = own.shape[0]
        total = dot(own[...], mine, 1, 1) + dot(sent[...], other, 1, 1)
        o_ref[row : row + n, :] = total.astype(BF)
        row += n


def seq_kernel(s_ref, ra, rb, rg, *o_refs):
    xh = s_ref[0]
    for s in range(2):
        near = rg[:, pl.ds(pl.multiple_of(xh * 256 + s * 128, 128), 128)]
        far = rg[:, pl.ds(pl.multiple_of((1 - xh) * 256 + s * 128, 128), 128)]
        cols = slice(s * 128, s * 128 + 128)
        right = jnp.concatenate([near, far], axis=1)
        for n in range(4):
            for dx in range(2):
                mine = ra[n * 160 + dx * 80 : n * 160 + dx * 80 + 80, cols]
                other = rb[n * 160 + 80 - dx * 80 : n * 160 + 160 - dx * 80, cols]
                left = jnp.concatenate([mine, other], axis=1)
                o_refs[n * 2 + dx][s] = dot(left, right, 1, 1).astype(BF)


def sum_kernel(s_ref, *refs):
    o_ref = refs[-1]
    xh = s_ref[0]
    for dx in range(2):
        total = sum(refs[n * 2 + dx][...].astype(F32) for n in range(4))
        place = jnp.where(dx == 0, xh, 1 - xh) * 512
        o_ref[:, :, pl.ds(pl.multiple_of(place, 128), 512)] = total.astype(BF)


def call(kernel, out, name, n_in, scalars=None):
    specs = [VMEM] * n_in
    if scalars is not None:
        specs = [SMEM] + specs
    many = isinstance(out, list)
    f = pl.pallas_call(
        kernel,
        out_shape=out,
        in_specs=specs,
        out_specs=[VMEM] * len(out) if many else VMEM,
        compiler_params=ROOM,
        name=name,
    )
    return f if scalars is None else lambda *a: f(scalars, *a)


def per_device(activations, out_grads, basis_in, basis_out, block_ids, seq_lens, query_grads):
    xl, core, xh, y = (lax.axis_index(a).astype(jnp.int32) for a in ("xl", "core", "xh", "y"))
    acts = lax.all_gather(activations, "z", axis=0, tiled=True)

    chosen, g0, g1, g2, g3 = pick(block_ids, y, basis_out, out_grads)
    g1, g2, g3 = shift(g1, y=1), shift(g2, y=-1), shift(g3, y=2)
    c1, c2 = shift(chosen, y=1), shift(chosen, y=-1)
    c3a, c3b = shift(c1[:, :512], y=1), shift(c2[:, 512:], y=-1)

    features = basis_in.shape[1]
    half = lax.dynamic_slice_in_dim(basis_in, core * (features // 2), features // 2, 1)
    own = jnp.concatenate([half, shift(half, xh=1)], axis=0)
    b1, b2 = shift(own, y=1), shift(own, y=-1)
    b3a, b3b = shift(b1[:80], y=1), shift(b2[80:], y=-1)
    bases = [own, b1, b2, b3a, b3b]
    bases += [shift(b, core=1) for b in bases]

    partial = call(grads_kernel, jax.ShapeDtypeStruct((1024, 512), BF), "grads", 9)(
        chosen, c1, c2, c3a, c3b, g0, g1, g2, g3
    )
    parts = lax.all_to_all(partial.reshape(16, 64, 512), ("xh", "z"), split_axis=0, concat_axis=0, tiled=True)
    summed = jnp.sum(parts.astype(F32), axis=0).astype(BF)
    col = lax.broadcasted_iota(jnp.int32, (1, 512), 1)
    pos = (col // 32 % 4) * 256 + col // 256 * 128 + y * 32 + col % 32
    limit = jnp.where(col % 256 < 128, seq_lens[0], seq_lens[1])
    rotated = jnp.where(pos < limit, summed, jnp.zeros((), BF))
    rotated_all = spread(rotated, "z", 8).reshape(512, 512)

    ra = call(acts_kernel, jax.ShapeDtypeStruct((640, 256), BF), "acts", 11, core[None])(acts, *bases)
    rb = shift(ra, xh=1)
    tiles = call(seq_kernel, [jax.ShapeDtypeStruct((2, 80, 512), BF)] * 8, "seq", 3, xh[None])(ra, rb, rotated_all)
    got = []
    for n, dy in enumerate((0, -1, 1, 2)):
        for dx in range(2):
            tile = tiles[n * 2 + dx]
            got.append(shift(tile, xh=dx, y=dy) if dx or dy else tile)
    seq_grads = call(sum_kernel, jax.ShapeDtypeStruct((2, 80, 1024), BF), "sums", 8, xh[None])(*got)

    sibling = shift(seq_grads, core=1)
    across = shift(seq_grads, xl=1)
    diagonal = shift(across, core=1)

    def score(grads):
        return jnp.einsum("sik,qik->sq", grads, query_grads, preferred_element_type=F32)

    pieces = jnp.stack([score(seq_grads), score(sibling), score(across), score(diagonal)])
    here = xl * 2 + core
    scores = jnp.concatenate(
        [lax.dynamic_index_in_dim(pieces, here ^ d, 0, keepdims=False) for d in range(4)], axis=0
    )
    scores = jnp.sum(spread(scores, ("xh", "y"), 8), axis=0)
    return jnp.sum(spread(scores, "z", 8), axis=0)


def solution(mesh):
    fine = Mesh(mesh.devices.reshape(2, 2, 8, 2, 4), ("xl", "core", "z", "xh", "y"))
    dp, eig = ("xl", "core"), ("z", "xh", "y")
    in_specs = (
        P(dp + eig, None),
        P(eig, dp),
        P(eig, None),
        P(eig, None),
        P(),
        P(dp),
        P(dp, eig, None),
    )
    return jax.shard_map(
        per_device, mesh=fine, in_specs=in_specs, out_specs=P(None, dp), check_vma=False
    )
```

time: 259 us -> 209 us (0.81)
  blocking collectives: 140 us -> 28.5 us
  starting transfers between devices: 13.7 us -> 55.7 us
  waiting for transfers between devices: 52.3 us -> 71.6 us
  Pallas kernels: 0 us -> 18.1 us
  local copies, waits for them, and re-layouts: 20.3 us -> 10.2 us
  between operations: 18.6 us -> 13.6 us
  matrix products: 9.7 us -> 5.87 us
    ppermute x0 -> x28, waiting for transfers between devices: none -> 67.5 us  [shift(): return lax.ppermute(x, axes, pairs)]
    all_to_all x2 -> x0, blocking collectives: 65.6 us -> none  [the longest x1 45.7 us: per_device(): lax.all_to_all(partial.reshape(16, 64, 512), ('xh', 'z'), split_axis=0, c...]
    ppermute x0 -> x28, starting transfers between devices: none -> 33.6 us  [shift(): return lax.ppermute(x, axes, pairs)]
    all_to_all x2 -> x1, waiting for transfers between devices: 33.5 us -> 3.37 us  [spread(): lax.all_to_all(jnp.broadcast_to(x[None], (count,) + x.shape), axes, split...]
    all_to_all x3 -> x2, blocking collectives: 51.5 us -> 28.5 us  [spread(): lax.all_to_all(jnp.broadcast_to(x[None], (count,) + x.shape), axes, split...]
    all_gather x2 -> x0, blocking collectives: 22.7 us -> none  [the longest x1 13.5 us: per_device(): acts = lax.all_gather(activations, 'xh', axis=0, tiled=True)]
    all_gather x2 -> x1, waiting for transfers between devices: 18.8 us -> 0.01 us  [per_device(): acts = lax.all_gather(activations, 'z', axis=0, tiled=True)]
    pallas_call x0 -> x5, Pallas kernels: none -> 18.1 us  [the longest x3 10.4 us: call(): return f if scalars is None else lambda *a: f(scalars, *a)]
  transfers between devices with their start and end apart: 5 -> 31, of which waited for: 3 -> 15; matrix products, arithmetic and copies ran while one was open for 10% -> 6% of each run, Pallas kernels for 0% -> 7%
where the time goes in v2:
time: 209 us; the launch traced here: 207 us
  waiting for transfers between devices  71.6 us (34%)
  starting transfers between devices  55.7 us (27%)
  blocking collectives  28.5 us (14%)
  Pallas kernels  18.1 us (9%)
  between operations  13.6 us (7%)
  local copies, waits for them, and re-layouts  10.2 us (5%)
  matrix products  5.87 us (3%)
  other arithmetic  4.02 us (2%)
    ppermute x28, waiting for transfers between devices, shift(): return lax.ppermute(x, axes, pairs)  67.5 us
    ppermute x28, starting transfers between devices, shift(): return lax.ppermute(x, axes, pairs)  33.6 us
    all_to_all x2, blocking collectives, spread(): lax.all_to_all(jnp.broadcast_to(x[None], (count,) + x.shape), axes, split...  28.5 us
    all_to_all x1, starting transfers between devices, per_device(): lax.all_to_all(partial.reshape(16, 64, 512), ('xh', 'z'), split_axis=0, c...  11.2 us
    all_to_all x1, starting transfers between devices, spread(): lax.all_to_all(jnp.broadcast_to(x[None], (count,) + x.shape), axes, split...  10.9 us
    pallas_call x3, Pallas kernels, call(): return f if scalars is None else lambda *a: f(scalars, *a)  10.4 us
    dot_general x4, matrix products, score(): jnp.einsum('sik,qik->sq', grads, query_grads, preferred_element_type=F32)  5.87 us
    unnamed x16, local copies, waits for them, and re-layouts  4.71 us
  transfers between devices with their start and end apart: 31, of which 15 were waited for; matrix products, arithmetic and copies ran while one was open for 6% of the time, Pallas kernels for 7%

profile of v2, /device:TPU:24, one launch (start us, length us, event | category | flops | bytes accessed | tf_op | source)
XLA Modules:
  0.0 207.5 jit_solution(17018723433316353281)
XLA Ops:
  9.2 4.3 %pick.1 = (bf16[216,1024]{1,0:T(8,128)(2,1)S(1)}, bf16[216,512]{1,0:T(8,128)(2,1)S(1)}, bf16[216,512]{1,0:T(8,128)(2,1)}, bf16[216,512]{1,0:T(8,128)(2,1)}, bf16[216,512]{1,0:T(8,128)(2,1)}) custom-call(s32[9]{0:T(128)S(1)} %pad_add_fusion.s_ref, bf16[216,13824]{1,0:T(8,128)(2,1)} %b1.1, bf16[216,13824]{1,0:T(8,128)(2,1)} %b1.1, bf16[216,2048]{1,0:T(8,128)(2,1)S(1)} %copy-done.1), custom_call_target="tpu_custom_call" | custom-call | tf_op jit(solution)/shard_map/pick/pallas_call | solution.py:74
  15.5 3.2 %collective-permute-start.15 = (bf16[216,512]{1,0:T(8,128)(2,1)}, bf16[216,512]{1,0:T(8,128)(2,1)S(1)}, u32[]{:S(2)}, u32[]{:S(2)}) collective-permute-start(bf16[216,512]{1,0:T(8,128)(2,1)} %get-tuple-element.20), channel_id=1, source_target_pairs={{0,1},{1,2},{2,3},{3,0},{4,5},{5,6},{6,7},{7,4},{8,9},{9,10},{10,1... | collective-permute-start | bytes 663560 | tf_op jit(solution)/shard_map/ppermute | solution.py:32
  20.1 6.4 %collective-permute-done.11.c1 = bf16[216,1024]{1,0:T(8,128)(2,1)S(1)} collective-permute-done((bf16[216,1024]{1,0:T(8,128)(2,1)S(1)}, bf16[216,1024]{1,0:T(8,128)(2,1)S(1)}, u32[]{:S(2)}, u32[]{:S(2)}) %collective-permute-start.11) | collective-permute-done | bytes 442400 | tf_op jit(solution)/shard_map/ppermute | solution.py:32
  27.2 2.7 %collective-permute-start.13 = (bf16[216,512]{1,0:T(8,128)(2,1)}, bf16[216,512]{1,0:T(8,128)(2,1)}, u32[]{:S(2)}, u32[]{:S(2)}) collective-permute-start(bf16[216,512]{1,0:T(8,128)(2,1)} %slice.26), channel_id=1, source_target_pairs={{0,1},{1,2},{2,3},{3,0},{4,5},{5,6},{6,7},{7,4},{8,9},{9,10},{10,1... | collective-permute-start | bytes 663560 | tf_op jit(solution)/shard_map/ppermute | solution.py:32
  30.6 3.6 %collective-permute-done.15.g1 = bf16[216,512]{1,0:T(8,128)(2,1)S(1)} collective-permute-done((bf16[216,512]{1,0:T(8,128)(2,1)}, bf16[216,512]{1,0:T(8,128)(2,1)S(1)}, u32[]{:S(2)}, u32[]{:S(2)}) %collective-permute-start.15) | collective-permute-done | bytes 221216 | tf_op jit(solution)/shard_map/ppermute | solution.py:32
  34.3 3.6 %collective-permute-done.16.g2 = bf16[216,512]{1,0:T(8,128)(2,1)S(1)} collective-permute-done((bf16[216,512]{1,0:T(8,128)(2,1)}, bf16[216,512]{1,0:T(8,128)(2,1)S(1)}, u32[]{:S(2)}, u32[]{:S(2)}) %collective-permute-start.16) | collective-permute-done | bytes 221216 | tf_op jit(solution)/shard_map/ppermute | solution.py:32
  41.0 3.4 %grads.1 = bf16[1024,512]{1,0:T(8,128)(2,1)} custom-call(bf16[216,1024]{1,0:T(8,128)(2,1)S(1)} %get-tuple-element.18.c0, bf16[216,1024]{1,0:T(8,128)(2,1)S(1)} %collective-permute-done.11.c1, bf16[216,1024]{1,0:T(8,128)(2,1)S(1)} %collective-permute-done.12.c2, bf16[216,512]{1,0:T(8,128)(2,1)} %collective-permute-done.13.c3a, ...), custom_call_target="tpu_custom_call" | custom-call | tf_op jit(solution)/shard_map/grads/pallas_call | solution.py:163
  44.3 11.2 %all-to-all-start = ((bf16[16,64,512]{2,1,0:T(8,128)(2,1)}), bf16[16,64,512]{2,1,0:T(8,128)(2,1)}, u32[]{:S(2)}, u32[]{:S(2)}) async-start(bf16[16,64,512]{2,1,0:T(8,128)(2,1)} %bitcast.5), calls=%async_computation | async-start | bytes 2097152 | tf_op jit(solution)/shard_map/all_to_all | solution.py:166
  55.6 3.5 %collective-permute-start = (bf16[80,2560]{1,0:T(8,128)(2,1)S(1)}, bf16[80,2560]{1,0:T(8,128)(2,1)S(1)}, u32[]{:S(2)}, u32[]{:S(2)}) collective-permute-start(bf16[80,2560]{1,0:T(8,128)(2,1)S(1)} %constant_dynamic-slice_fusion.4), channel_id=1, source_target_pairs={{0,4},{4,0},{1,5},{5,1},{2,6},{6,2},{3,7},{7,3},{8,12},{12,8},{9,1... | collective-permute-start | bytes 1228808 | tf_op jit(solution)/shard_map/ppermute | solution.py:32
  59.1 16.5 %collective-permute-done = bf16[80,2560]{1,0:T(8,128)(2,1)S(1)} collective-permute-done((bf16[80,2560]{1,0:T(8,128)(2,1)S(1)}, bf16[80,2560]{1,0:T(8,128)(2,1)S(1)}, u32[]{:S(2)}, u32[]{:S(2)}) %collective-permute-start) | collective-permute-done | bytes 409632 | tf_op jit(solution)/shard_map/ppermute | solution.py:32
  78.3 14.7 %collective-permute-done.1.refs_1_ = bf16[160,2560]{1,0:T(8,128)(2,1)S(1)} collective-permute-done((bf16[160,2560]{1,0:T(8,128)(2,1)S(1)}, bf16[160,2560]{1,0:T(8,128)(2,1)S(1)}, u32[]{:S(2)}, u32[]{:S(2)}) %collective-permute-start.1) | collective-permute-done | bytes 819232 | tf_op jit(solution)/shard_map/ppermute | solution.py:32
  101.6 10.9 %all-to-all-start.1 = ((bf16[8,64,512]{2,1,0:T(8,128)(2,1)}), bf16[8,64,512]{2,1,0:T(8,128)(2,1)S(1)}, u32[]{:S(2)}, u32[]{:S(2)}) async-start(bf16[8,64,512]{2,1,0:T(8,128)(2,1)} %broadcast_in_dim.55), calls=%async_computation.1 | async-start | bytes 1048576 | tf_op jit(solution)/shard_map/all_to_all | solution.py:36
  118.1 7.9 %acts.1.ra = bf16[640,256]{1,0:T(8,128)(2,1)} custom-call(s32[1]{0:T(128)} %bitcast.1.s_ref, bf16[256,5120]{1,0:T(8,128)(2,1)} %all-gather.2.cloned.1.call-done.a_ref, bf16[160,2560]{1,0:T(8,128)(2,1)S(1)} %pad_maximum_fusion.refs_0_, bf16[160,2560]{1,0:T(8,128)(2,1)S(1)} %collective-permute-done.1.refs_1_, ...), custom_call_target="tpu_custom_call" | custom-call | tf_op jit(solution)/shard_map/acts/pallas_call | solution.py:143
  126.8 3.4 %all-to-all-done.1 = bf16[8,64,512]{2,1,0:T(8,128)(2,1)S(1)} async-done(((bf16[8,64,512]{2,1,0:T(8,128)(2,1)}), bf16[8,64,512]{2,1,0:T(8,128)(2,1)S(1)}, u32[]{:S(2)}, u32[]{:S(2)}) %all-to-all-start.1) | async-done | bytes 524320 | tf_op jit(solution)/shard_map/all_to_all | solution.py:36
  130.1 7.3 %collective-permute-done.10.rb = bf16[640,256]{1,0:T(8,128)(2,1)S(1)} collective-permute-done((bf16[640,256]{1,0:T(8,128)(2,1)}, bf16[640,256]{1,0:T(8,128)(2,1)S(1)}, u32[]{:S(2)}, u32[]{:S(2)}) %collective-permute-start.10) | collective-permute-done | bytes 327712 | tf_op jit(solution)/shard_map/ppermute | solution.py:32
  137.4 2.4 %seq.1 = (bf16[2,80,512]{2,1,0:T(8,128)(2,1)S(1)}, bf16[2,80,512]{2,1,0:T(8,128)(2,1)S(1)}, bf16[2,80,512]{2,1,0:T(8,128)(2,1)S(1)}, bf16[2,80,512]{2,1,0:T(8,12...) custom-call(s32[1]{0:T(128)} %bitcast.s_ref, ...), custom_call_target="tpu_custom_call" | custom-call | tf_op jit(solution)/shard_map/seq/pallas_call | solution.py:143
  140.7 3.1 %collective-permute-start.20 = (bf16[2,80,512]{2,1,0:T(8,128)(2,1)S(1)}, bf16[2,80,512]{2,1,0:T(8,128)(2,1)S(1)}, u32[]{:S(2)}, u32[]{:S(2)}) collective-permute-start(bf16[2,80,512]{2,1,0:T(8,128)(2,1)S(1)} %get-tuple-element.26), channel_id=1, source_target_pairs={{0,7},{1,4},{2,5},{3,6},{4,3},{5,0},{6,1},{7,2},{8,15},{9,12},{10,... | collective-permute-start | bytes 491528 | tf_op jit(solution)/shard_map/ppermute | solution.py:32
  143.7 2.3 %collective-permute-start.21 = (bf16[2,80,512]{2,1,0:T(8,128)(2,1)S(1)}, bf16[2,80,512]{2,1,0:T(8,128)(2,1)S(1)}, u32[]{:S(2)}, u32[]{:S(2)}) collective-permute-start(bf16[2,80,512]{2,1,0:T(8,128)(2,1)S(1)} %get-tuple-element.27), channel_id=1, source_target_pairs={{0,1},{1,2},{2,3},{3,0},{4,5},{5,6},{6,7},{7,4},{8,9},{9,10},{10,1... | collective-permute-start | bytes 491528 | tf_op jit(solution)/shard_map/ppermute | solution.py:32
  146.1 2.2 %collective-permute-start.22 = (bf16[2,80,512]{2,1,0:T(8,128)(2,1)S(1)}, bf16[2,80,512]{2,1,0:T(8,128)(2,1)S(1)}, u32[]{:S(2)}, u32[]{:S(2)}) collective-permute-start(bf16[2,80,512]{2,1,0:T(8,128)(2,1)S(1)} %get-tuple-element.28), channel_id=1, source_target_pairs={{0,5},{1,6},{2,7},{3,4},{4,1},{5,2},{6,3},{7,0},{8,13},{9,14},{10,... | collective-permute-start | bytes 491528 | tf_op jit(solution)/shard_map/ppermute | solution.py:32
  149.3 4.8 %collective-permute-start.24 = (bf16[2,80,512]{2,1,0:T(8,128)(2,1)S(1)}, bf16[2,80,512]{2,1,0:T(8,128)(2,1)S(1)}, u32[]{:S(2)}, u32[]{:S(2)}) collective-permute-start(bf16[2,80,512]{2,1,0:T(8,128)(2,1)S(1)} %get-tuple-element.30), channel_id=1, source_target_pairs={{0,6},{1,7},{2,4},{3,5},{4,2},{5,3},{6,0},{7,1},{8,14},{9,15},{10,... | collective-permute-start | bytes 491528 | tf_op jit(solution)/shard_map/ppermute | solution.py:32
  156.5 3.1 %collective-permute-done.23.refs_6_ = bf16[2,80,512]{2,1,0:T(8,128)(2,1)S(1)} collective-permute-done((bf16[2,80,512]{2,1,0:T(8,128)(2,1)S(1)}, bf16[2,80,512]{2,1,0:T(8,128)(2,1)S(1)}, u32[]{:S(2)}, u32[]{:S(2)}) %collective-permute-start.23) | collective-permute-done | bytes 163872 | tf_op jit(solution)/shard_map/ppermute | solution.py:32
  162.0 5.0 %collective-permute-done.26 = bf16[2,80,1024]{2,1,0:T(8,128)(2,1)S(1)} collective-permute-done((bf16[2,80,1024]{2,1,0:T(8,128)(2,1)S(1)}, bf16[2,80,1024]{2,1,0:T(8,128)(2,1)S(1)}, u32[]{:S(2)}, u32[]{:S(2)}) %collective-permute-start.26) | collective-permute-done | bytes 327712 | tf_op jit(solution)/shard_map/ppermute | solution.py:32
  171.5 13.5 %all_to_all.20 = f32[8,8,8]{2,1,0:T(8,128)S(1)} all-to-all(f32[8,8,8]{2,1,0:T(8,128)S(1)} %broadcast_in_dim.56), channel_id=1, replica_groups=mesh['xl'=2,'core'=2,'z'=8,'xh'=2,'y'=4] {'xh','y'}, dimensions={0} | all-to-all | bytes 4096 | tf_op jit(solution)/shard_map/all_to_all | solution.py:36
  185.0 15.0 %all_to_all.21 = f32[8,8,8]{2,1,0:T(8,128)S(1)} all-to-all(f32[8,8,8]{2,1,0:T(8,128)S(1)} %broadcast_in_dim.57), channel_id=1, replica_groups=mesh['xl'=2,'core'=2,'z'=8,'xh'=2,'y'=4] {'z'}, dimensions={0} | all-to-all | bytes 4096 | tf_op jit(solution)/shard_map/all_to_all | solution.py:36
  (85 shorter events, 40.0 us)
Async XLA Ops:
  6.5 109.5 %all-gather.2.cloned.1.call-start = ((), (), s32[]{:S(2)}) async-start(), calls=%async_computation.4 | async-start | bytes 2949120 | tf_op jit(solution)/shard_map/all_gather | solution.py:148
  13.5 13.1 %collective-permute-start.11 = (bf16[216,1024]{1,0:T(8,128)(2,1)S(1)}, bf16[216,1024]{1,0:T(8,128)(2,1)S(1)}, u32[]{:S(2)}, u32[]{:S(2)}) collective-permute-start(bf16[216,1024]{1,0:T(8,128)(2,1)S(1)} %get-tuple-element.18.c0), channel_id=1, source_target_pairs={{0,1},{1,2},{2,3},{3,0},{4,5},{5,6},{6,7},{7,4},{8,9},{9,10},{10,1... | collective-permute-start | bytes 1327112 | tf_op jit(solution)/shard_map/ppermute | solution.py:32
  15.4 14.5 %collective-permute-start.12 = (bf16[216,1024]{1,0:T(8,128)(2,1)S(1)}, bf16[216,1024]{1,0:T(8,128)(2,1)S(1)}, u32[]{:S(2)}, u32[]{:S(2)}) collective-permute-start(bf16[216,1024]{1,0:T(8,128)(2,1)S(1)} %get-tuple-element.18.c0), channel_id=1, source_target_pairs={{0,3},{1,0},{2,1},{3,2},{4,7},{5,4},{6,5},{7,6},{8,11},{9,8},{10,9... | collective-permute-start | bytes 1327112 | tf_op jit(solution)/shard_map/ppermute | solution.py:32
  15.5 18.8 %collective-permute-start.15 = (bf16[216,512]{1,0:T(8,128)(2,1)}, bf16[216,512]{1,0:T(8,128)(2,1)S(1)}, u32[]{:S(2)}, u32[]{:S(2)}) collective-permute-start(bf16[216,512]{1,0:T(8,128)(2,1)} %get-tuple-element.20), channel_id=1, source_target_pairs={{0,1},{1,2},{2,3},{3,0},{4,5},{5,6},{6,7},{7,4},{8,9},{9,10},{10,1... | collective-permute-start | bytes 663560 | tf_op jit(solution)/shard_map/ppermute | solution.py:32
  18.7 19.3 %collective-permute-start.16 = (bf16[216,512]{1,0:T(8,128)(2,1)}, bf16[216,512]{1,0:T(8,128)(2,1)S(1)}, u32[]{:S(2)}, u32[]{:S(2)}) collective-permute-start(bf16[216,512]{1,0:T(8,128)(2,1)} %get-tuple-element.21), channel_id=1, source_target_pairs={{0,3},{1,0},{2,1},{3,2},{4,7},{5,4},{6,5},{7,6},{8,11},{9,8},{10,9... | collective-permute-start | bytes 663560 | tf_op jit(solution)/shard_map/ppermute | solution.py:32
  18.7 19.3 %collective-permute-start.17 = (bf16[216,512]{1,0:T(8,128)(2,1)}, bf16[216,512]{1,0:T(8,128)(2,1)S(1)}, u32[]{:S(2)}, u32[]{:S(2)}) collective-permute-start(bf16[216,512]{1,0:T(8,128)(2,1)} %get-tuple-element.22), channel_id=1, source_target_pairs={{0,2},{1,3},{2,0},{3,1},{4,6},{5,7},{6,4},{7,5},{8,10},{9,11},{10,... | collective-permute-start | bytes 663560 | tf_op jit(solution)/shard_map/ppermute | solution.py:32
  27.2 12.5 %collective-permute-start.13 = (bf16[216,512]{1,0:T(8,128)(2,1)}, bf16[216,512]{1,0:T(8,128)(2,1)}, u32[]{:S(2)}, u32[]{:S(2)}) collective-permute-start(bf16[216,512]{1,0:T(8,128)(2,1)} %slice.26), channel_id=1, source_target_pairs={{0,1},{1,2},{2,3},{3,0},{4,5},{5,6},{6,7},{7,4},{8,9},{9,10},{10,1... | collective-permute-start | bytes 663560 | tf_op jit(solution)/shard_map/ppermute | solution.py:32
  30.6 10.3 %collective-permute-start.14 = (bf16[216,512]{1,0:T(8,128)(2,1)}, bf16[216,512]{1,0:T(8,128)(2,1)}, u32[]{:S(2)}, u32[]{:S(2)}) collective-permute-start(bf16[216,512]{1,0:T(8,128)(2,1)} %slice.27), channel_id=1, source_target_pairs={{0,3},{1,0},{2,1},{3,2},{4,7},{5,4},{6,5},{7,6},{8,11},{9,8},{10,9... | collective-permute-start | bytes 663560 | tf_op jit(solution)/shard_map/ppermute | solution.py:32
  44.3 55.0 %all-to-all-start = ((bf16[16,64,512]{2,1,0:T(8,128)(2,1)}), bf16[16,64,512]{2,1,0:T(8,128)(2,1)}, u32[]{:S(2)}, u32[]{:S(2)}) async-start(bf16[16,64,512]{2,1,0:T(8,128)(2,1)} %bitcast.5), calls=%async_computation | async-start | bytes 2097152 | tf_op jit(solution)/shard_map/all_to_all | solution.py:166
  55.6 20.0 %collective-permute-start = (bf16[80,2560]{1,0:T(8,128)(2,1)S(1)}, bf16[80,2560]{1,0:T(8,128)(2,1)S(1)}, u32[]{:S(2)}, u32[]{:S(2)}) collective-permute-start(bf16[80,2560]{1,0:T(8,128)(2,1)S(1)} %constant_dynamic-slice_fusion.4), channel_id=1, source_target_pairs={{0,4},{4,0},{1,5},{5,1},{2,6},{6,2},{3,7},{7,3},{8,12},{12,8},{9,1... | collective-permute-start | bytes 1228808 | tf_op jit(solution)/shard_map/ppermute | solution.py:32
  75.6 17.4 %collective-permute-start.1 = (bf16[160,2560]{1,0:T(8,128)(2,1)S(1)}, bf16[160,2560]{1,0:T(8,128)(2,1)S(1)}, u32[]{:S(2)}, u32[]{:S(2)}) collective-permute-start(bf16[160,2560]{1,0:T(8,128)(2,1)S(1)} %pad_maximum_fusion.refs_0_), channel_id=1, source_target_pairs={{0,1},{1,2},{2,3},{3,0},{4,5},{5,6},{6,7},{7,4},{8,9},{9,10},{10,1... | collective-permute-start | bytes 2457608 | tf_op jit(solution)/shard_map/ppermute | solution.py:32
  75.7 19.1 %collective-permute-start.2 = (bf16[160,2560]{1,0:T(8,128)(2,1)S(1)}, bf16[160,2560]{1,0:T(8,128)(2,1)}, u32[]{:S(2)}, u32[]{:S(2)}) collective-permute-start(bf16[160,2560]{1,0:T(8,128)(2,1)S(1)} %pad_maximum_fusion.refs_0_), channel_id=1, source_target_pairs={{0,3},{1,0},{2,1},{3,2},{4,7},{5,4},{6,5},{7,6},{8,11},{9,8},{10,9... | collective-permute-start | bytes 2457608 | tf_op jit(solution)/shard_map/ppermute | solution.py:32
  78.3 34.8 %collective-permute-start.5 = (bf16[160,2560]{1,0:T(8,128)(2,1)S(1)}, bf16[160,2560]{1,0:T(8,128)(2,1)}, u32[]{:S(2)}, u32[]{:S(2)}) collective-permute-start(bf16[160,2560]{1,0:T(8,128)(2,1)S(1)} %pad_maximum_fusion.refs_0_), channel_id=1, source_target_pairs={{0,64},{64,0},{1,65},{65,1},{2,66},{66,2},{3,67},{67,3},{4,68},{68... | collective-permute-start | bytes 2457608 | tf_op jit(solution)/shard_map/ppermute | solution.py:32
  93.8 18.7 %collective-permute-start.3 = (bf16[80,2560]{1,0:T(8,128)(2,1)}, bf16[80,2560]{1,0:T(8,128)(2,1)}, u32[]{:S(2)}, u32[]{:S(2)}) collective-permute-start(bf16[80,2560]{1,0:T(8,128)(2,1)} %slice.24), channel_id=1, source_target_pairs={{0,1},{1,2},{2,3},{3,0},{4,5},{5,6},{6,7},{7,4},{8,9},{9,10},{10,1... | collective-permute-start | bytes 1228808 | tf_op jit(solution)/shard_map/ppermute | solution.py:32
  96.7 15.9 %collective-permute-start.4 = (bf16[80,2560]{1,0:T(8,128)(2,1)}, bf16[80,2560]{1,0:T(8,128)(2,1)}, u32[]{:S(2)}, u32[]{:S(2)}) collective-permute-start(bf16[80,2560]{1,0:T(8,128)(2,1)} %slice.25), channel_id=1, source_target_pairs={{0,3},{1,0},{2,1},{3,2},{4,7},{5,4},{6,5},{7,6},{8,11},{9,8},{10,9... | collective-permute-start | bytes 1228808 | tf_op jit(solution)/shard_map/ppermute | solution.py:32
  97.6 18.4 %collective-permute-start.6 = (bf16[160,2560]{1,0:T(8,128)(2,1)S(1)}, bf16[160,2560]{1,0:T(8,128)(2,1)}, u32[]{:S(2)}, u32[]{:S(2)}) collective-permute-start(bf16[160,2560]{1,0:T(8,128)(2,1)S(1)} %collective-permute-done.1.refs_1_), channel_id=1, source_target_pairs={{0,64},{64,0},{1,65},{65,1},{2,66},{66,2},{3,67},{67,3},{4,68},{68... | collective-permute-start | bytes 2457608 | tf_op jit(solution)/shard_map/ppermute | solution.py:32
  97.6 18.4 %collective-permute-start.7 = (bf16[160,2560]{1,0:T(8,128)(2,1)}, bf16[160,2560]{1,0:T(8,128)(2,1)}, u32[]{:S(2)}, u32[]{:S(2)}) collective-permute-start(bf16[160,2560]{1,0:T(8,128)(2,1)} %collective-permute-done.2.refs_2_), channel_id=1, source_target_pairs={{0,64},{64,0},{1,65},{65,1},{2,66},{66,2},{3,67},{67,3},{4,68},{68... | collective-permute-start | bytes 2457608 | tf_op jit(solution)/shard_map/ppermute | solution.py:32
  101.6 28.5 %all-to-all-start.1 = ((bf16[8,64,512]{2,1,0:T(8,128)(2,1)}), bf16[8,64,512]{2,1,0:T(8,128)(2,1)S(1)}, u32[]{:S(2)}, u32[]{:S(2)}) async-start(bf16[8,64,512]{2,1,0:T(8,128)(2,1)} %broadcast_in_dim.55), calls=%async_computation.1 | async-start | bytes 1048576 | tf_op jit(solution)/shard_map/all_to_all | solution.py:36
  126.0 11.5 %collective-permute-start.10 = (bf16[640,256]{1,0:T(8,128)(2,1)}, bf16[640,256]{1,0:T(8,128)(2,1)S(1)}, u32[]{:S(2)}, u32[]{:S(2)}) collective-permute-start(bf16[640,256]{1,0:T(8,128)(2,1)} %acts.1.ra), channel_id=1, source_target_pairs={{0,4},{4,0},{1,5},{5,1},{2,6},{6,2},{3,7},{7,3},{8,12},{12,8},{9,1... | collective-permute-start | bytes 983048 | tf_op jit(solution)/shard_map/ppermute | solution.py:32
  140.7 14.1 %collective-permute-start.20 = (bf16[2,80,512]{2,1,0:T(8,128)(2,1)S(1)}, bf16[2,80,512]{2,1,0:T(8,128)(2,1)S(1)}, u32[]{:S(2)}, u32[]{:S(2)}) collective-permute-start(bf16[2,80,512]{2,1,0:T(8,128)(2,1)S(1)} %get-tuple-element.26), channel_id=1, source_target_pairs={{0,7},{1,4},{2,5},{3,6},{4,3},{5,0},{6,1},{7,2},{8,15},{9,12},{10,... | collective-permute-start | bytes 491528 | tf_op jit(solution)/shard_map/ppermute | solution.py:32
  143.7 12.8 %collective-permute-start.21 = (bf16[2,80,512]{2,1,0:T(8,128)(2,1)S(1)}, bf16[2,80,512]{2,1,0:T(8,128)(2,1)S(1)}, u32[]{:S(2)}, u32[]{:S(2)}) collective-permute-start(bf16[2,80,512]{2,1,0:T(8,128)(2,1)S(1)} %get-tuple-element.27), channel_id=1, source_target_pairs={{0,1},{1,2},{2,3},{3,0},{4,5},{5,6},{6,7},{7,4},{8,9},{9,10},{10,1... | collective-permute-start | bytes 491528 | tf_op jit(solution)/shard_map/ppermute | solution.py:32
  146.1 10.5 %collective-permute-start.22 = (bf16[2,80,512]{2,1,0:T(8,128)(2,1)S(1)}, bf16[2,80,512]{2,1,0:T(8,128)(2,1)S(1)}, u32[]{:S(2)}, u32[]{:S(2)}) collective-permute-start(bf16[2,80,512]{2,1,0:T(8,128)(2,1)S(1)} %get-tuple-element.28), channel_id=1, source_target_pairs={{0,5},{1,6},{2,7},{3,4},{4,1},{5,2},{6,3},{7,0},{8,13},{9,14},{10,... | collective-permute-start | bytes 491528 | tf_op jit(solution)/shard_map/ppermute | solution.py:32
  148.5 11.1 %collective-permute-start.23 = (bf16[2,80,512]{2,1,0:T(8,128)(2,1)S(1)}, bf16[2,80,512]{2,1,0:T(8,128)(2,1)S(1)}, u32[]{:S(2)}, u32[]{:S(2)}) collective-permute-start(bf16[2,80,512]{2,1,0:T(8,128)(2,1)S(1)} %get-tuple-element.29), channel_id=1, source_target_pairs={{0,2},{1,3},{2,0},{3,1},{4,6},{5,7},{6,4},{7,5},{8,10},{9,11},{10,... | collective-permute-start | bytes 491528 | tf_op jit(solution)/shard_map/ppermute | solution.py:32
  149.3 10.4 %collective-permute-start.24 = (bf16[2,80,512]{2,1,0:T(8,128)(2,1)S(1)}, bf16[2,80,512]{2,1,0:T(8,128)(2,1)S(1)}, u32[]{:S(2)}, u32[]{:S(2)}) collective-permute-start(bf16[2,80,512]{2,1,0:T(8,128)(2,1)S(1)} %get-tuple-element.30), channel_id=1, source_target_pairs={{0,6},{1,7},{2,4},{3,5},{4,2},{5,3},{6,0},{7,1},{8,14},{9,15},{10,... | collective-permute-start | bytes 491528 | tf_op jit(solution)/shard_map/ppermute | solution.py:32
  (15 other events, 232.2 us)
Sparse Core Ops, SparseCore 0:
  9.1 44.9 all-gather.1

commit v3 on v2

v3 whole, which is shorter than its diff:
```python
import jax
import jax.numpy as jnp
from jax import lax
from jax.experimental import pallas as pl
from jax.experimental.pallas import tpu as pltpu
from jax.sharding import Mesh, PartitionSpec as P

BLOCK = 128
LEN = 1024
BF = jnp.bfloat16
F32 = jnp.float32
SIZES = {"xl": 2, "core": 2, "z": 8, "xh": 2, "y": 4}
ROWS = (0, -1, 1, 2)
VMEM = pl.BlockSpec(memory_space=pltpu.VMEM)
SMEM = pl.BlockSpec(memory_space=pltpu.SMEM)
ROOM = pltpu.CompilerParams(vmem_limit_bytes=20 * 1024 * 1024)


def shift(x, **by):
    axes = tuple(by)
    count = 1
    for a in axes:
        count *= SIZES[a]
    pairs = []
    for source in range(count):
        rest, target, scale = source, 0, 1
        for a in reversed(axes):
            target += (rest % SIZES[a] + by[a]) % SIZES[a] * scale
            rest //= SIZES[a]
            scale *= SIZES[a]
        pairs.append((source, target))
    return lax.ppermute(x, axes, pairs)


def spread(x, axes, count):
    return lax.all_to_all(
        jnp.broadcast_to(x[None], (count,) + x.shape), axes, split_axis=0, concat_axis=0, tiled=True
    )


def dot(a, b, ca, cb):
    return lax.dot_general(a, b, (((ca,), (cb,)), ((), ())), preferred_element_type=F32)


def reorder(y, g_ref, outs):
    lane = lax.broadcasted_iota(jnp.int32, (1, 128), 1) // 32
    for xh in range(2):
        for part in range(2):
            start = part * 1024 + xh * 128
            cols = [g_ref[:, start + j * 256 : start + j * 256 + 128].astype(F32) for j in range(4)]
            place = xh * 256 + part * 128
            for o_ref, off, dy in outs:
                total = None
                for j in range(4):
                    moved = pltpu.roll(cols[j], ((j - dy - y + 8) % 4) * 32, 1)
                    total = moved if total is None else jnp.where(lane == j, moved, total)
                o_ref[:, off + place : off + place + 128] = total.astype(BF)


def pick_kernel(s_ref, *refs):
    picked, g_ref, up, down = refs[:8], *refs[8:]
    for n, p in enumerate(picked):
        cols = slice(n * 128, n * 128 + 128)
        up[:, cols] = p[...]
        down[:, cols] = p[...]
    reorder(s_ref[8], g_ref, ((up, 1024, 1), (down, 1024, -1)))


def pick(block_ids, y, basis_out, out_grads):
    rows, tokens = out_grads.shape
    whole = lambda width: pl.BlockSpec((rows, width), lambda g, s: (0, 0))
    spec = pltpu.PrefetchScalarGridSpec(
        num_scalar_prefetch=1,
        grid=(1,),
        in_specs=[pl.BlockSpec((rows, BLOCK), lambda g, s, n=n: (0, s[n])) for n in range(8)] + [whole(tokens)],
        out_specs=[whole(1536), whole(1536)],
    )
    return pl.pallas_call(
        pick_kernel,
        grid_spec=spec,
        out_shape=[arr(rows, 1536), arr(rows, 1536)],
        compiler_params=pltpu.CompilerParams(vmem_limit_bytes=52 * 1024 * 1024),
        name="pick",
    )(jnp.concatenate([block_ids, y[None]]), *[basis_out] * 8, out_grads)


def rest_kernel(y_ref, g_ref, aside, g0, g3):
    reorder(y_ref[0], g_ref, ((g3, 0, 2), (g0, 0, 0)))


def join_kernel(b0, b1, b2, aside, o_ref):
    o_ref[:80, :] = b0[...]
    o_ref[80:160, :] = b1[...]
    o_ref[160:, :] = b2[...]


def grads_kernel(here, up, down, c3, g0, g3, *refs):
    o_ref = refs[-1]
    for part in range(4):
        ks = slice(part * 256, part * 256 + 256)
        total = dot(here[:, ks], g0[...], 0, 0) + dot(c3[:, ks], g3[...], 0, 0)
        total += dot(up[:, ks], up[:, 1024:], 0, 0) + dot(down[:, ks], down[:, 1024:], 0, 0)
        o_ref[ks, :] = total.astype(BF)


def live_kernel(y_ref, lens, parts, *refs):
    o_ref = refs[-1]
    total = parts[0].astype(F32)
    for n in range(1, 16):
        total += parts[n].astype(F32)
    col = lax.broadcasted_iota(jnp.int32, (1, 512), 1)
    pos = (col // 32 % 4) * 256 + col // 256 * 128 + y_ref[0] * 32 + col % 32
    limit = jnp.where(col % 256 < 128, lens[0], lens[1])
    total = jnp.where(pos < limit, total, 0.0).astype(BF)
    for n in range(8):
        o_ref[n] = total


def acts_kernel(s_ref, a_ref, *refs):
    o_ref = refs[-1]
    core = s_ref[0]
    half = a_ref.shape[1] // 2
    mine = a_ref[:, pl.ds(pl.multiple_of(core * half, 128), half)]
    other = a_ref[:, pl.ds(pl.multiple_of((1 - core) * half, 128), half)]
    for n, (own, sent) in enumerate(zip(refs[:4], refs[4:8])):
        total = (dot(own[...], mine, 1, 1) + dot(sent[...], other, 1, 1)).astype(BF)
        for row in range(total.shape[0] // 80):
            place = (row + n // 2 * 3) * 160 + n % 2 * 80
            o_ref[place : place + 80, :] = total[row * 80 : row * 80 + 80]


def seq_kernel(xh_ref, y_ref, ra, rb, rg, o_ref):
    xh = xh_ref[0]
    for s in range(2):
        near = rg[:, pl.ds(pl.multiple_of(xh * 256 + s * 128, 128), 128)]
        far = rg[:, pl.ds(pl.multiple_of((1 - xh) * 256 + s * 128, 128), 128)]
        cols = slice(s * 128, s * 128 + 128)
        right = jnp.concatenate([near, far], axis=1)
        for n, dy in enumerate(ROWS):
            for dx in range(2):
                mine = ra[n * 160 + dx * 80 : n * 160 + dx * 80 + 80, cols]
                other = rb[n * 160 + 80 - dx * 80 : n * 160 + 160 - dx * 80, cols]
                left = jnp.concatenate([mine, other], axis=1)
                target = (xh + dx) % 2 * 4 + (y_ref[0] + dy + 4) % 4
                o_ref[target, s] = dot(left, right, 1, 1).astype(BF)


def sum_kernel(parts, o_ref):
    for xh in range(2):
        total = parts[xh * 4].astype(F32)
        for y in range(1, 4):
            total += parts[xh * 4 + y].astype(F32)
        o_ref[:, :, xh * 512 : xh * 512 + 512] = total.astype(BF)


def call(kernel, out, name, args, scalars=(), aside=()):
    specs = [SMEM] * len(scalars) + [VMEM] * len(args) + [pl.BlockSpec(memory_space=pltpu.HBM)] * len(aside)
    return pl.pallas_call(
        kernel,
        out_shape=out,
        in_specs=specs,
        out_specs=jax.tree.map(lambda _: VMEM, out),
        compiler_params=ROOM,
        name=name,
    )(*scalars, *args, *aside)


def arr(*shape):
    return jax.ShapeDtypeStruct(shape, BF)


def per_device(activations, out_grads, basis_in, basis_out, block_ids, seq_lens, query_grads):
    xl, core, xh, y = (lax.axis_index(a).astype(jnp.int32) for a in ("xl", "core", "xh", "y"))
    acts = lax.all_gather(activations, "z", axis=0, tiled=True)

    features = basis_in.shape[1]
    b0 = lax.dynamic_slice_in_dim(basis_in, core * (features // 2), features // 2, 1)
    b1, b2 = shift(b0, y=1), shift(b0, y=-1)
    up, down = pick(block_ids, y, basis_out, out_grads)
    g0, g3 = call(rest_kernel, [arr(216, 512)] * 2, "rest", [out_grads], [y[None]], [up])
    up_got, down_got, g3_got = shift(up, y=1), shift(down, y=-1), shift(g3, y=2)
    c3 = shift(down_got[:, :1024], y=-1)

    near = call(join_kernel, arr(240, features // 2), "join", [b0, b1, b2], (), [g0])
    far = shift(near, xh=1)
    near3 = shift(b1, y=1)
    far3 = shift(near3, xh=1)

    grads_in = [up, up_got, down_got, c3, g0, g3_got]
    partial = call(grads_kernel, arr(1024, 512), "grads", grads_in, (), [far, near3])
    parts = lax.all_to_all(partial.reshape(16, 64, 512), ("xh", "z"), split_axis=0, concat_axis=0, tiled=True)
    pieces = [near, far, near3, far3]
    others = [shift(b, core=1) for b in pieces]
    ra = call(acts_kernel, arr(640, 256), "acts", [acts] + pieces + others, [core[None]])
    copies = call(live_kernel, arr(8, 64, 512), "live", [parts], [y[None], seq_lens], [ra])
    rotated = lax.all_to_all(copies, "z", split_axis=0, concat_axis=0, tiled=True).reshape(512, 512)

    rb = shift(ra, xh=1)
    tiles = call(seq_kernel, arr(8, 2, 80, 512), "seq", [ra, rb, rotated], [xh[None], y[None]])
    got = lax.all_to_all(tiles, ("xh", "y"), split_axis=0, concat_axis=0, tiled=True)
    seq_grads = call(sum_kernel, arr(2, 80, 1024), "sums", [got])

    sibling = shift(seq_grads, core=1)
    across = shift(seq_grads, xl=1)
    diagonal = shift(across, core=1)

    def score(grads):
        return jnp.einsum("sik,qik->sq", grads, query_grads, preferred_element_type=F32)

    scored = jnp.stack([score(seq_grads), score(sibling), score(across), score(diagonal)])
    here = xl * 2 + core
    scores = jnp.concatenate(
        [lax.dynamic_index_in_dim(scored, here ^ d, 0, keepdims=False) for d in range(4)], axis=0
    )
    return jnp.sum(spread(scores, ("z", "xh", "y"), 64), axis=0)


def solution(mesh):
    fine = Mesh(mesh.devices.reshape(2, 2, 8, 2, 4), ("xl", "core", "z", "xh", "y"))
    dp, eig = ("xl", "core"), ("z", "xh", "y")
    in_specs = (
        P(dp + eig, None),
        P(eig, dp),
        P(eig, None),
        P(eig, None),
        P(),
        P(dp),
        P(dp, eig, None),
    )
    return jax.shard_map(
        per_device, mesh=fine, in_specs=in_specs, out_specs=P(None, dp), check_vma=False
    )
```

time: 209 us -> 202 us (0.967)
  starting transfers between devices: 55.7 us -> 33.7 us
  blocking collectives: 28.5 us -> 44.8 us
  Pallas kernels: 18.1 us -> 11.4 us
  local copies, waits for them, and re-layouts: 10.2 us -> 16.9 us
  other arithmetic: 4.02 us -> 1.41 us
    all_to_all x0 -> x1, blocking collectives: none -> 24 us  [per_device(): lax.all_to_all(tiles, ('xh', 'y'), split_axis=0, concat_axis=0, tiled=True)]
    ppermute x28 -> x17, starting transfers between devices: 33.6 us -> 18.2 us  [shift(): return lax.ppermute(x, axes, pairs)]
    unnamed x16 -> x38, local copies, waits for them, and re-layouts: 4.71 us -> 15.8 us
    all_to_all x2 -> x1, blocking collectives: 28.5 us -> 20.9 us  [spread(): lax.all_to_all(jnp.broadcast_to(x[None], (count,) + x.shape), axes, split...]
    pallas_call x5 -> x8, Pallas kernels: 18.1 us -> 11.4 us  [the longest x7 8.74 us: call(): pl.pallas_call(kernel, out_shape=out, in_specs=specs, out_specs=jax.tree....]
    slice x5 -> x1, local copies, waits for them, and re-layouts: 4.55 us -> 0.04 us  [per_device(): c3 = shift(down_got[:, :1024], y=-1)]
    all_to_all x1, starting transfers between devices: 10.9 us -> 6.75 us  [per_device(): lax.all_to_all(copies, 'z', split_axis=0, concat_axis=0, tiled=True)]
    all_to_all x1, waiting for transfers between devices: 3.37 us -> 6.86 us  [per_device(): lax.all_to_all(copies, 'z', split_axis=0, concat_axis=0, tiled=True)]
  transfers between devices with their start and end apart: 31 -> 20, of which waited for: 15 -> 10; matrix products, arithmetic and copies ran while one was open for 6% -> 3% of each run, Pallas kernels for 7% -> 4%
where the time goes in v3:
time: 202 us; the launch traced here: 201 us
  waiting for transfers between devices  73.3 us (36%)
  blocking collectives  44.8 us (22%)
  starting transfers between devices  33.7 us (17%)
  local copies, waits for them, and re-layouts  16.9 us (8%)
  between operations  13.6 us (7%)
  Pallas kernels  11.4 us (6%)
  matrix products  5.87 us (3%)
    ppermute x17, waiting for transfers between devices, shift(): return lax.ppermute(x, axes, pairs)  65.7 us
    all_to_all x1, blocking collectives, per_device(): lax.all_to_all(tiles, ('xh', 'y'), split_axis=0, concat_axis=0, tiled=True)  24 us
    all_to_all x1, blocking collectives, spread(): lax.all_to_all(jnp.broadcast_to(x[None], (count,) + x.shape), axes, split...  20.9 us
    ppermute x17, starting transfers between devices, shift(): return lax.ppermute(x, axes, pairs)  18.2 us
    unnamed x38, local copies, waits for them, and re-layouts  15.8 us
    pallas_call x7, Pallas kernels, call(): pl.pallas_call(kernel, out_shape=out, in_specs=specs, out_specs=jax.tree....  8.74 us
    all_to_all x1, starting transfers between devices, per_device(): lax.all_to_all(partial.reshape(16, 64, 512), ('xh', 'z'), split_axis=0, c...  8.71 us
    all_to_all x1, waiting for transfers between devices, per_device(): lax.all_to_all(copies, 'z', split_axis=0, concat_axis=0, tiled=True)  6.86 us
  transfers between devices with their start and end apart: 20, of which 10 were waited for; matrix products, arithmetic and copies ran while one was open for 3% of the time, Pallas kernels for 4%

profile of v3, /device:TPU:24, one launch (start us, length us, event | category | flops | bytes accessed | tf_op | source)
XLA Modules:
  0.0 201.0 jit_solution(9463794296786815667)
XLA Ops:
  8.3 2.0 %collective-permute-start = (bf16[80,2560]{1,0:T(8,128)(2,1)S(1)}, bf16[80,2560]{1,0:T(8,128)(2,1)S(1)}, u32[]{:S(2)}, u32[]{:S(2)}) collective-permute-start(bf16[80,2560]{1,0:T(8,128)(2,1)S(1)} %constant_dynamic-slice_fusion.4.b0), channel_id=1, source_target_pairs={{0,1},{1,2},{2,3},{3,0},{4,5},{5,6},{6,7},{7,4},{8,9},{9,10},{10,1... | collective-permute-start | bytes 1228808 | tf_op jit(solution)/shard_map/ppermute | solution.py:32
  11.1 2.6 %pick.1 = (bf16[216,1536]{1,0:T(8,128)(2,1)S(1)}, bf16[216,1536]{1,0:T(8,128)(2,1)S(1)}) custom-call(s32[9]{0:T(128)S(1)} %pad_add_fusion.s_ref, bf16[216,13824]{1,0:T(8,128)(2,1)} %refs_7_.1, bf16[216,13824]{1,0:T(8,128)(2,1)} %refs_7_.1, bf16[216,13824]{1,0:T(8,128)(2,1)} %refs_7_.1, bf16[216,13824]{1,0:T(8,128)(2,1)} %refs_7_.1, ...), custom_call_target="tpu_custom_call" | custom-call | tf_op jit(solution)/shard_map/pick/pallas_call | solution.py:78
  14.3 5.2 %collective-permute-done.b1 = bf16[80,2560]{1,0:T(8,128)(2,1)S(1)} collective-permute-done((bf16[80,2560]{1,0:T(8,128)(2,1)S(1)}, bf16[80,2560]{1,0:T(8,128)(2,1)S(1)}, u32[]{:S(2)}, u32[]{:S(2)}) %collective-permute-start) | collective-permute-done | bytes 409632 | tf_op jit(solution)/shard_map/ppermute | solution.py:32
  22.7 3.1 %collective-permute-start.2 = (bf16[240,2560]{1,0:T(8,128)(2,1)S(1)}, bf16[240,2560]{1,0:T(8,128)(2,1)S(1)}, u32[]{:S(2)}, u32[]{:S(2)}) collective-permute-start(bf16[240,2560]{1,0:T(8,128)(2,1)S(1)} %join.1.refs_0_), channel_id=1, source_target_pairs={{0,4},{4,0},{1,5},{5,1},{2,6},{6,2},{3,7},{7,3},{8,12},{12,8},{9,1... | collective-permute-start | bytes 3686408 | tf_op jit(solution)/shard_map/ppermute | solution.py:32
  26.3 2.8 %collective-permute-start.10 = (bf16[216,1536]{1,0:T(8,128)(2,1)S(1)}, bf16[216,1536]{1,0:T(8,128)(2,1)S(1)}, u32[]{:S(2)}, u32[]{:S(2)}) collective-permute-start(bf16[216,1536]{1,0:T(8,128)(2,1)S(1)} %get-tuple-element.9.aside.here), channel_id=1, source_target_pairs={{0,1},{1,2},{2,3},{3,0},{4,5},{5,6},{6,7},{7,4},{8,9},{9,10},{10,1... | collective-permute-start | bytes 1990664 | tf_op jit(solution)/shard_map/ppermute | solution.py:32
  29.1 13.3 %collective-permute-done.11.down = bf16[216,1536]{1,0:T(8,128)(2,1)S(1)} collective-permute-done((bf16[216,1536]{1,0:T(8,128)(2,1)S(1)}, bf16[216,1536]{1,0:T(8,128)(2,1)S(1)}, u32[]{:S(2)}, u32[]{:S(2)}) %collective-permute-start.11) | collective-permute-done | bytes 663584 | tf_op jit(solution)/shard_map/ppermute | solution.py:32
  42.5 3.2 %collective-permute-start.3 = (bf16[80,2560]{1,0:T(8,128)(2,1)S(1)}, bf16[80,2560]{1,0:T(8,128)(2,1)S(1)}, u32[]{:S(2)}, u32[]{:S(2)}) collective-permute-start(bf16[80,2560]{1,0:T(8,128)(2,1)S(1)} %collective-permute-done.b1), channel_id=1, source_target_pairs={{0,1},{1,2},{2,3},{3,0},{4,5},{5,6},{6,7},{7,4},{8,9},{9,10},{10,1... | collective-permute-start | bytes 1228808 | tf_op jit(solution)/shard_map/ppermute | solution.py:32
  45.8 10.3 %collective-permute-done.13.g3 = bf16[216,512]{1,0:T(8,128)(2,1)S(1)} collective-permute-done((bf16[216,512]{1,0:T(8,128)(2,1)S(1)}, bf16[216,512]{1,0:T(8,128)(2,1)S(1)}, u32[]{:S(2)}, u32[]{:S(2)}) %collective-permute-start.13) | collective-permute-done | bytes 221216 | tf_op jit(solution)/shard_map/ppermute | solution.py:32
  60.6 8.7 %all-to-all-start = ((bf16[16,64,512]{2,1,0:T(8,128)(2,1)}), bf16[16,64,512]{2,1,0:T(8,128)(2,1)}, u32[]{:S(2)}, u32[]{:S(2)}) async-start(bf16[16,64,512]{2,1,0:T(8,128)(2,1)} %bitcast.25), calls=%async_computation | async-start | bytes 2097152 | tf_op jit(solution)/shard_map/all_to_all | solution.py:191
  69.9 3.3 %collective-permute-start.4 = (bf16[80,2560]{1,0:T(8,128)(2,1)S(1)}, bf16[80,2560]{1,0:T(8,128)(2,1)S(1)}, u32[]{:S(2)}, u32[]{:S(2)}) collective-permute-start(bf16[80,2560]{1,0:T(8,128)(2,1)S(1)} %collective-permute-done.3.refs_2_.refs_1_), channel_id=1, source_target_pairs={{0,4},{4,0},{1,5},{5,1},{2,6},{6,2},{3,7},{7,3},{8,12},{12,8},{9,1... | collective-permute-start | bytes 1228808 | tf_op jit(solution)/shard_map/ppermute | solution.py:32
  73.2 17.7 %collective-permute-done.4.refs_3_ = bf16[80,2560]{1,0:T(8,128)(2,1)S(1)} collective-permute-done((bf16[80,2560]{1,0:T(8,128)(2,1)S(1)}, bf16[80,2560]{1,0:T(8,128)(2,1)S(1)}, u32[]{:S(2)}, u32[]{:S(2)}) %collective-permute-start.4) | collective-permute-done | bytes 409632 | tf_op jit(solution)/shard_map/ppermute | solution.py:32
  96.6 1.7 copy-done.5
  103.9 3.1 %acts.1.refs_0_.ra = bf16[640,256]{1,0:T(8,128)(2,1)S(1)} custom-call(s32[1]{0:T(128)} %bitcast.2.s_ref, bf16[256,5120]{1,0:T(8,128)(2,1)S(1)} %copy-done.5, bf16[240,2560]{1,0:T(8,128)(2,1)S(1)} %join.1.refs_0_, bf16[240,2560]{1,0:T(8,128)(2,1)S(1)} %copy-done.2, bf16[80,2560]{1,0:T(8,128)(2,1)S(1)} %collective-permute-done.3.refs_2_.refs_1_, ...), custom_call_target="tpu_custom_call" | custom-call | tf_op jit(solution)/shard_map/acts/pallas_call | solution.py:158
  107.0 2.2 %live.1 = bf16[8,64,512]{2,1,0:T(8,128)(2,1)} custom-call(s32[1]{0:T(128)} %bitcast.1.y_ref, s32[2]{0:T(128)S(1)} %copy-done.18, bf16[16,64,512]{2,1,0:T(8,128)(2,1)} %all-to-all-done.parts, bf16[640,256]{1,0:T(8,128)(2,1)S(1)} %acts.1.refs_0_.ra), custom_call_target="tpu_custom_call" | custom-call | tf_op jit(solution)/shard_map/live/pallas_call | solution.py:158
  109.2 6.7 %all-to-all-start.1 = ((bf16[8,64,512]{2,1,0:T(8,128)(2,1)}), bf16[8,64,512]{2,1,0:T(8,128)(2,1)S(1)}, u32[]{:S(2)}, u32[]{:S(2)}) async-start(bf16[8,64,512]{2,1,0:T(8,128)(2,1)} %live.1), calls=%async_computation.1 | async-start | bytes 1048576 | tf_op jit(solution)/shard_map/all_to_all | solution.py:196
  116.9 10.4 %collective-permute-done.9.rb = bf16[640,256]{1,0:T(8,128)(2,1)S(1)} collective-permute-done((bf16[640,256]{1,0:T(8,128)(2,1)S(1)}, bf16[640,256]{1,0:T(8,128)(2,1)S(1)}, u32[]{:S(2)}, u32[]{:S(2)}) %collective-permute-start.9) | collective-permute-done | bytes 327712 | tf_op jit(solution)/shard_map/ppermute | solution.py:32
  127.3 6.9 %all-to-all-done.1 = bf16[8,64,512]{2,1,0:T(8,128)(2,1)S(1)} async-done(((bf16[8,64,512]{2,1,0:T(8,128)(2,1)}), bf16[8,64,512]{2,1,0:T(8,128)(2,1)S(1)}, u32[]{:S(2)}, u32[]{:S(2)}) %all-to-all-start.1) | async-done | bytes 524320 | tf_op jit(solution)/shard_map/all_to_all | solution.py:196
  135.6 24.0 %all_to_all.20.parts = bf16[8,2,80,512]{3,2,1,0:T(8,128)(2,1)S(1)} all-to-all(bf16[8,2,80,512]{3,2,1,0:T(8,128)(2,1)S(1)} %seq.1), channel_id=1, replica_groups=mesh['xl'=2,'core'=2,'z'=8,'xh'=2,'y'=4] {'xh','y'}, dimensions={0} | all-to-all | bytes 2621440 | tf_op jit(solution)/shard_map/all_to_all | solution.py:200
  159.7 1.6 collective-permute-start.15
  161.3 1.5 convolution_bitcast_fusion.3
  162.7 5.3 %collective-permute-done.15 = bf16[2,80,1024]{2,1,0:T(8,128)(2,1)S(1)} collective-permute-done((bf16[2,80,1024]{2,1,0:T(8,128)(2,1)S(1)}, bf16[2,80,1024]{2,1,0:T(8,128)(2,1)S(1)}, u32[]{:S(2)}, u32[]{:S(2)}) %collective-permute-start.15) | collective-permute-done | bytes 327712 | tf_op jit(solution)/shard_map/ppermute | solution.py:32
  169.5 1.5 convolution_bitcast_fusion.2
  171.0 1.5 convolution_bitcast_fusion
  172.6 20.9 %all_to_all.21 = f32[64,8,8]{2,1,0:T(8,128)S(1)} all-to-all(f32[64,8,8]{2,1,0:T(8,128)S(1)} %broadcast_in_dim.21), channel_id=1, replica_groups=mesh['xl'=2,'core'=2,'z'=8,'xh'=2,'y'=4] {'z','xh','y'}, dimensions={0} | all-to-all | bytes 32768 | tf_op jit(solution)/shard_map/all_to_all | solution.py:36
  (77 shorter events, 27.9 us)
Async XLA Ops:
  6.5 154.7 %copy-start = (bf16[8,80,1024]{2,1,0:T(8,128)(2,1)S(1)}, bf16[8,80,1024]{2,1,0:T(8,128)(2,1)}, u32[]{:S(2)}) copy-start(bf16[8,80,1024]{2,1,0:T(8,128)(2,1)} %param.13) | copy-start | bytes 3932164
  6.5 88.8 %all-gather.2.cloned.1.call-start = ((), (), s32[]{:S(2)}) async-start(), calls=%async_computation.4 | async-start | bytes 2949120 | tf_op jit(solution)/shard_map/all_gather | solution.py:174
  8.3 11.3 %collective-permute-start = (bf16[80,2560]{1,0:T(8,128)(2,1)S(1)}, bf16[80,2560]{1,0:T(8,128)(2,1)S(1)}, u32[]{:S(2)}, u32[]{:S(2)}) collective-permute-start(bf16[80,2560]{1,0:T(8,128)(2,1)S(1)} %constant_dynamic-slice_fusion.4.b0), channel_id=1, source_target_pairs={{0,1},{1,2},{2,3},{3,0},{4,5},{5,6},{6,7},{7,4},{8,9},{9,10},{10,1... | collective-permute-start | bytes 1228808 | tf_op jit(solution)/shard_map/ppermute | solution.py:32
  10.3 10.5 %collective-permute-start.1 = (bf16[80,2560]{1,0:T(8,128)(2,1)S(1)}, bf16[80,2560]{1,0:T(8,128)(2,1)S(1)}, u32[]{:S(2)}, u32[]{:S(2)}) collective-permute-start(bf16[80,2560]{1,0:T(8,128)(2,1)S(1)} %constant_dynamic-slice_fusion.4.b0), channel_id=1, source_target_pairs={{0,3},{1,0},{2,1},{3,2},{4,7},{5,4},{6,5},{7,6},{8,11},{9,8},{10,9... | collective-permute-start | bytes 1228808 | tf_op jit(solution)/shard_map/ppermute | solution.py:32
  11.1 2.7 %copy-start.4 = (bf16[216,2048]{1,0:T(8,128)(2,1)S(1)}, bf16[216,2048]{1,0:T(8,128)(2,1)}, u32[]{:S(2)}) copy-start(bf16[216,2048]{1,0:T(8,128)(2,1)} %g_ref.1) | copy-start | bytes 2654212
  22.7 35.4 %collective-permute-start.2 = (bf16[240,2560]{1,0:T(8,128)(2,1)S(1)}, bf16[240,2560]{1,0:T(8,128)(2,1)S(1)}, u32[]{:S(2)}, u32[]{:S(2)}) collective-permute-start(bf16[240,2560]{1,0:T(8,128)(2,1)S(1)} %join.1.refs_0_), channel_id=1, source_target_pairs={{0,4},{4,0},{1,5},{5,1},{2,6},{6,2},{3,7},{7,3},{8,12},{12,8},{9,1... | collective-permute-start | bytes 3686408 | tf_op jit(solution)/shard_map/ppermute | solution.py:32
  25.8 16.6 %collective-permute-start.11 = (bf16[216,1536]{1,0:T(8,128)(2,1)S(1)}, bf16[216,1536]{1,0:T(8,128)(2,1)S(1)}, u32[]{:S(2)}, u32[]{:S(2)}) collective-permute-start(bf16[216,1536]{1,0:T(8,128)(2,1)S(1)} %get-tuple-element.11), channel_id=1, source_target_pairs={{0,3},{1,0},{2,1},{3,2},{4,7},{5,4},{6,5},{7,6},{8,11},{9,8},{10,9... | collective-permute-start | bytes 1990664 | tf_op jit(solution)/shard_map/ppermute | solution.py:32
  26.3 29.8 %collective-permute-start.10 = (bf16[216,1536]{1,0:T(8,128)(2,1)S(1)}, bf16[216,1536]{1,0:T(8,128)(2,1)S(1)}, u32[]{:S(2)}, u32[]{:S(2)}) collective-permute-start(bf16[216,1536]{1,0:T(8,128)(2,1)S(1)} %get-tuple-element.9.aside.here), channel_id=1, source_target_pairs={{0,1},{1,2},{2,3},{3,0},{4,5},{5,6},{6,7},{7,4},{8,9},{9,10},{10,1... | collective-permute-start | bytes 1990664 | tf_op jit(solution)/shard_map/ppermute | solution.py:32
  42.4 15.7 %collective-permute-start.12 = (bf16[216,1024]{1,0:T(8,128)(2,1)S(1)}, bf16[216,1024]{1,0:T(8,128)(2,1)S(1)}, u32[]{:S(2)}, u32[]{:S(2)}) collective-permute-start(bf16[216,1024]{1,0:T(8,128)(2,1)S(1)} %slice.4), channel_id=1, source_target_pairs={{0,3},{1,0},{2,1},{3,2},{4,7},{5,4},{6,5},{7,6},{8,11},{9,8},{10,9... | collective-permute-start | bytes 1327112 | tf_op jit(solution)/shard_map/ppermute | solution.py:32
  42.5 14.2 %collective-permute-start.3 = (bf16[80,2560]{1,0:T(8,128)(2,1)S(1)}, bf16[80,2560]{1,0:T(8,128)(2,1)S(1)}, u32[]{:S(2)}, u32[]{:S(2)}) collective-permute-start(bf16[80,2560]{1,0:T(8,128)(2,1)S(1)} %collective-permute-done.b1), channel_id=1, source_target_pairs={{0,1},{1,2},{2,3},{3,0},{4,5},{5,6},{6,7},{7,4},{8,9},{9,10},{10,1... | collective-permute-start | bytes 1228808 | tf_op jit(solution)/shard_map/ppermute | solution.py:32
  45.8 10.3 %collective-permute-start.13 = (bf16[216,512]{1,0:T(8,128)(2,1)S(1)}, bf16[216,512]{1,0:T(8,128)(2,1)S(1)}, u32[]{:S(2)}, u32[]{:S(2)}) collective-permute-start(bf16[216,512]{1,0:T(8,128)(2,1)S(1)} %get-tuple-element.12), channel_id=1, source_target_pairs={{0,2},{1,3},{2,0},{3,1},{4,6},{5,7},{6,4},{7,5},{8,10},{9,11},{10,... | collective-permute-start | bytes 663560 | tf_op jit(solution)/shard_map/ppermute | solution.py:32
  60.6 46.4 %all-to-all-start = ((bf16[16,64,512]{2,1,0:T(8,128)(2,1)}), bf16[16,64,512]{2,1,0:T(8,128)(2,1)}, u32[]{:S(2)}, u32[]{:S(2)}) async-start(bf16[16,64,512]{2,1,0:T(8,128)(2,1)} %bitcast.25), calls=%async_computation | async-start | bytes 2097152 | tf_op jit(solution)/shard_map/all_to_all | solution.py:191
  69.3 23.1 %collective-permute-start.5 = (bf16[240,2560]{1,0:T(8,128)(2,1)S(1)}, bf16[240,2560]{1,0:T(8,128)(2,1)S(1)}, u32[]{:S(2)}, u32[]{:S(2)}) collective-permute-start(bf16[240,2560]{1,0:T(8,128)(2,1)S(1)} %join.1.refs_0_), channel_id=1, source_target_pairs={{0,64},{64,0},{1,65},{65,1},{2,66},{66,2},{3,67},{67,3},{4,68},{68... | collective-permute-start | bytes 3686408 | tf_op jit(solution)/shard_map/ppermute | solution.py:32
  69.4 24.9 %collective-permute-start.6 = (bf16[240,2560]{1,0:T(8,128)(2,1)}, bf16[240,2560]{1,0:T(8,128)(2,1)S(1)}, u32[]{:S(2)}, u32[]{:S(2)}) collective-permute-start(bf16[240,2560]{1,0:T(8,128)(2,1)} %copy-done.1), channel_id=1, source_target_pairs={{0,64},{64,0},{1,65},{65,1},{2,66},{66,2},{3,67},{67,3},{4,68},{68... | collective-permute-start | bytes 3686408 | tf_op jit(solution)/shard_map/ppermute | solution.py:32
  69.9 21.0 %collective-permute-start.4 = (bf16[80,2560]{1,0:T(8,128)(2,1)S(1)}, bf16[80,2560]{1,0:T(8,128)(2,1)S(1)}, u32[]{:S(2)}, u32[]{:S(2)}) collective-permute-start(bf16[80,2560]{1,0:T(8,128)(2,1)S(1)} %collective-permute-done.3.refs_2_.refs_1_), channel_id=1, source_target_pairs={{0,4},{4,0},{1,5},{5,1},{2,6},{6,2},{3,7},{7,3},{8,12},{12,8},{9,1... | collective-permute-start | bytes 1228808 | tf_op jit(solution)/shard_map/ppermute | solution.py:32
  73.2 18.5 %collective-permute-start.7 = (bf16[80,2560]{1,0:T(8,128)(2,1)S(1)}, bf16[80,2560]{1,0:T(8,128)(2,1)S(1)}, u32[]{:S(2)}, u32[]{:S(2)}) collective-permute-start(bf16[80,2560]{1,0:T(8,128)(2,1)S(1)} %collective-permute-done.3.refs_2_.refs_1_), channel_id=1, source_target_pairs={{0,64},{64,0},{1,65},{65,1},{2,66},{66,2},{3,67},{67,3},{4,68},{68... | collective-permute-start | bytes 1228808 | tf_op jit(solution)/shard_map/ppermute | solution.py:32
  90.9 2.6 %collective-permute-start.8 = (bf16[80,2560]{1,0:T(8,128)(2,1)S(1)}, bf16[80,2560]{1,0:T(8,128)(2,1)S(1)}, u32[]{:S(2)}, u32[]{:S(2)}) collective-permute-start(bf16[80,2560]{1,0:T(8,128)(2,1)S(1)} %collective-permute-done.4.refs_3_), channel_id=1, source_target_pairs={{0,64},{64,0},{1,65},{65,1},{2,66},{66,2},{3,67},{67,3},{4,68},{68... | collective-permute-start | bytes 1228808 | tf_op jit(solution)/shard_map/ppermute | solution.py:32
  96.6 1.7 copy-start.5
  103.9 3.1 %copy-start.18 = (s32[2]{0:T(128)S(1)}, s32[2]{0:T(128)}, u32[]{:S(2)}) copy-start(s32[2]{0:T(128)} %lens.1) | copy-start | bytes 28
  109.2 25.0 %all-to-all-start.1 = ((bf16[8,64,512]{2,1,0:T(8,128)(2,1)}), bf16[8,64,512]{2,1,0:T(8,128)(2,1)S(1)}, u32[]{:S(2)}, u32[]{:S(2)}) async-start(bf16[8,64,512]{2,1,0:T(8,128)(2,1)} %live.1), calls=%async_computation.1 | async-start | bytes 1048576 | tf_op jit(solution)/shard_map/all_to_all | solution.py:196
  115.9 11.4 %collective-permute-start.9 = (bf16[640,256]{1,0:T(8,128)(2,1)S(1)}, bf16[640,256]{1,0:T(8,128)(2,1)S(1)}, u32[]{:S(2)}, u32[]{:S(2)}) collective-permute-start(bf16[640,256]{1,0:T(8,128)(2,1)S(1)} %acts.1.refs_0_.ra), channel_id=1, source_target_pairs={{0,4},{4,0},{1,5},{5,1},{2,6},{6,2},{3,7},{7,3},{8,12},{12,8},{9,1... | collective-permute-start | bytes 983048 | tf_op jit(solution)/shard_map/ppermute | solution.py:32
  159.7 8.4 %collective-permute-start.15 = (bf16[2,80,1024]{2,1,0:T(8,128)(2,1)S(1)}, bf16[2,80,1024]{2,1,0:T(8,128)(2,1)S(1)}, u32[]{:S(2)}, u32[]{:S(2)}) collective-permute-start(bf16[2,80,1024]{2,1,0:T(8,128)(2,1)S(1)} %sums.1), channel_id=1, source_target_pairs={{0,128},{128,0},{1,129},{129,1},{2,130},{130,2},{3,131},{131,3},{4... | collective-permute-start | bytes 983048 | tf_op jit(solution)/shard_map/ppermute | solution.py:32
  161.3 8.2 %collective-permute-start.14 = (bf16[2,80,1024]{2,1,0:T(8,128)(2,1)S(1)}, bf16[2,80,1024]{2,1,0:T(8,128)(2,1)S(1)}, u32[]{:S(2)}, u32[]{:S(2)}) collective-permute-start(bf16[2,80,1024]{2,1,0:T(8,128)(2,1)S(1)} %sums.1), channel_id=1, source_target_pairs={{0,64},{64,0},{1,65},{65,1},{2,66},{66,2},{3,67},{67,3},{4,68},{68... | collective-permute-start | bytes 983048 | tf_op jit(solution)/shard_map/ppermute | solution.py:32
  168.1 2.9 %collective-permute-start.16 = (bf16[2,80,1024]{2,1,0:T(8,128)(2,1)S(1)}, bf16[2,80,1024]{2,1,0:T(8,128)(2,1)S(1)}, u32[]{:S(2)}, u32[]{:S(2)}) collective-permute-start(bf16[2,80,1024]{2,1,0:T(8,128)(2,1)S(1)} %collective-permute-done.15), channel_id=1, source_target_pairs={{0,64},{64,0},{1,65},{65,1},{2,66},{66,2},{3,67},{67,3},{4,68},{68... | collective-permute-start | bytes 983048 | tf_op jit(solution)/shard_map/ppermute | solution.py:32
  (15 other events, 15.4 us)
Sparse Core Ops, SparseCore 0:
  9.1 44.9 all-gather.1

commit v4 on v3

--- a/solution.py
+++ b/solution.py
@@ -13,7 +13,8 @@
 ROWS = (0, -1, 1, 2)
 VMEM = pl.BlockSpec(memory_space=pltpu.VMEM)
 SMEM = pl.BlockSpec(memory_space=pltpu.SMEM)
-ROOM = pltpu.CompilerParams(vmem_limit_bytes=20 * 1024 * 1024)
+WIDE = pltpu.CompilerParams(vmem_limit_bytes=52 * 1024 * 1024)
+ROOM = pltpu.CompilerParams(vmem_limit_bytes=10 * 1024 * 1024)
 
 
 def shift(x, **by):
@@ -79,19 +80,13 @@
         pick_kernel,
         grid_spec=spec,
         out_shape=[arr(rows, 1536), arr(rows, 1536)],
-        compiler_params=pltpu.CompilerParams(vmem_limit_bytes=52 * 1024 * 1024),
+        compiler_params=WIDE,
         name="pick",
     )(jnp.concatenate([block_ids, y[None]]), *[basis_out] * 8, out_grads)
 
 
 def rest_kernel(y_ref, g_ref, aside, g0, g3):
     reorder(y_ref[0], g_ref, ((g3, 0, 2), (g0, 0, 0)))
-
-
-def join_kernel(b0, b1, b2, aside, o_ref):
-    o_ref[:80, :] = b0[...]
-    o_ref[80:160, :] = b1[...]
-    o_ref[160:, :] = b2[...]
 
 
 def grads_kernel(here, up, down, c3, g0, g3, *refs):
@@ -116,31 +111,34 @@
         o_ref[n] = total
 
 
-def acts_kernel(s_ref, a_ref, *refs):
-    o_ref = refs[-1]
-    core = s_ref[0]
-    half = a_ref.shape[1] // 2
-    mine = a_ref[:, pl.ds(pl.multiple_of(core * half, 128), half)]
-    other = a_ref[:, pl.ds(pl.multiple_of((1 - core) * half, 128), half)]
-    for n, (own, sent) in enumerate(zip(refs[:4], refs[4:8])):
-        total = (dot(own[...], mine, 1, 1) + dot(sent[...], other, 1, 1)).astype(BF)
-        for row in range(total.shape[0] // 80):
-            place = (row + n // 2 * 3) * 160 + n % 2 * 80
-            o_ref[place : place + 80, :] = total[row * 80 : row * 80 + 80]
+def acts_kernel(core_ref, a_ref, *refs):
+    keep, send = refs[-2:]
+    core = core_ref[0]
+    for xh in range(2):
+        cols = slice(xh * 256, xh * 256 + 256)
+        for out, which in ((keep, core), (send, 1 - core)):
+            tokens = a_ref[:, xh * 2 + which].reshape(256, a_ref.shape[3])
+            for n in range(4):
+                out[n * 160 : n * 160 + 160, cols] = dot(refs[n][...], tokens, 1, 1).astype(out.dtype)
+
+
+def add_kernel(a, b, keep, send):
+    total = a[...] + b[...].astype(F32)
+    keep[...] = total
+    send[...] = total.astype(BF)
 
 
 def seq_kernel(xh_ref, y_ref, ra, rb, rg, o_ref):
     xh = xh_ref[0]
     for s in range(2):
-        near = rg[:, pl.ds(pl.multiple_of(xh * 256 + s * 128, 128), 128)]
-        far = rg[:, pl.ds(pl.multiple_of((1 - xh) * 256 + s * 128, 128), 128)]
-        cols = slice(s * 128, s * 128 + 128)
-        right = jnp.concatenate([near, far], axis=1)
+        near, far = slice(s * 128, s * 128 + 128), slice(s * 128 + 256, s * 128 + 384)
+        right = jnp.concatenate([rg[:, near], rg[:, far]], axis=1)
         for n, dy in enumerate(ROWS):
             for dx in range(2):
-                mine = ra[n * 160 + dx * 80 : n * 160 + dx * 80 + 80, cols]
-                other = rb[n * 160 + 80 - dx * 80 : n * 160 + 160 - dx * 80, cols]
-                left = jnp.concatenate([mine, other], axis=1)
+                mine = slice(n * 160 + dx * 80, n * 160 + dx * 80 + 80)
+                other = slice(n * 160 + 80 - dx * 80, n * 160 + 160 - dx * 80)
+                left = [ra[mine, cols] + rb[other, cols].astype(F32) for cols in (near, far)]
+                left = jnp.concatenate(left, axis=1).astype(BF)
                 target = (xh + dx) % 2 * 4 + (y_ref[0] + dy + 4) % 4
                 o_ref[target, s] = dot(left, right, 1, 1).astype(BF)
 
@@ -154,7 +152,7 @@
 
 
 def call(kernel, out, name, args, scalars=(), aside=()):
-    specs = [SMEM] * len(scalars) + [VMEM] * len(args) + [pl.BlockSpec(memory_space=pltpu.HBM)] * len(aside)
+    specs = [SMEM] * len(scalars) + [VMEM] * len(args) + [pl.BlockSpec(memory_space=pl.ANY)] * len(aside)
     return pl.pallas_call(
         kernel,
         out_shape=out,
@@ -171,32 +169,35 @@
 
 def per_device(activations, out_grads, basis_in, basis_out, block_ids, seq_lens, query_grads):
     xl, core, xh, y = (lax.axis_index(a).astype(jnp.int32) for a in ("xl", "core", "xh", "y"))
-    acts = lax.all_gather(activations, "z", axis=0, tiled=True)
-
-    features = basis_in.shape[1]
-    b0 = lax.dynamic_slice_in_dim(basis_in, core * (features // 2), features // 2, 1)
+    slots, features = activations.shape
+    part = features // 4
+    acts = activations.reshape(slots, 4, part).transpose(1, 0, 2)
+    acts = lax.all_to_all(acts, ("xh", "core"), split_axis=0, concat_axis=0, tiled=True)
+    acts = lax.all_gather(acts, "z", axis=0, tiled=False)
+
+    def quarter(x):
+        return lax.dynamic_slice_in_dim(basis_in, (x * 2 + core) * part, part, 1)
+
+    b0 = jnp.concatenate([quarter(xh), shift(quarter(1 - xh), xh=1)])
     b1, b2 = shift(b0, y=1), shift(b0, y=-1)
+    b3 = shift(b1, y=1)
+
     up, down = pick(block_ids, y, basis_out, out_grads)
     g0, g3 = call(rest_kernel, [arr(216, 512)] * 2, "rest", [out_grads], [y[None]], [up])
     up_got, down_got, g3_got = shift(up, y=1), shift(down, y=-1), shift(g3, y=2)
     c3 = shift(down_got[:, :1024], y=-1)
 
-    near = call(join_kernel, arr(240, features // 2), "join", [b0, b1, b2], (), [g0])
-    far = shift(near, xh=1)
-    near3 = shift(b1, y=1)
-    far3 = shift(near3, xh=1)
-
     grads_in = [up, up_got, down_got, c3, g0, g3_got]
-    partial = call(grads_kernel, arr(1024, 512), "grads", grads_in, (), [far, near3])
+    partial = call(grads_kernel, arr(1024, 512), "grads", grads_in, (), [b2, b3])
     parts = lax.all_to_all(partial.reshape(16, 64, 512), ("xh", "z"), split_axis=0, concat_axis=0, tiled=True)
-    pieces = [near, far, near3, far3]
-    others = [shift(b, core=1) for b in pieces]
-    ra = call(acts_kernel, arr(640, 256), "acts", [acts] + pieces + others, [core[None]])
-    copies = call(live_kernel, arr(8, 64, 512), "live", [parts], [y[None], seq_lens], [ra])
+    sums = [jax.ShapeDtypeStruct((640, 512), F32), arr(640, 512)]
+    keep, send = call(acts_kernel, sums, "acts", [acts, b0, b1, b2, b3], [core[None]])
+    keep, send = call(add_kernel, sums, "add", [keep, shift(send, core=1)])
+    rb = shift(send, xh=1)
+    copies = call(live_kernel, arr(8, 64, 512), "live", [parts], [y[None], seq_lens], [send])
     rotated = lax.all_to_all(copies, "z", split_axis=0, concat_axis=0, tiled=True).reshape(512, 512)
 
-    rb = shift(ra, xh=1)
-    tiles = call(seq_kernel, arr(8, 2, 80, 512), "seq", [ra, rb, rotated], [xh[None], y[None]])
+    tiles = call(seq_kernel, arr(8, 2, 80, 512), "seq", [keep, rb, rotated], [xh[None], y[None]])
     got = lax.all_to_all(tiles, ("xh", "y"), split_axis=0, concat_axis=0, tiled=True)
     seq_grads = call(sum_kernel, arr(2, 80, 1024), "sums", [got])
 

time: 202 us -> 196 us (0.970)
  blocking collectives: 44.8 us -> 59.8 us
  starting transfers between devices: 33.7 us -> 25.6 us
  local copies, waits for them, and re-layouts: 16.9 us -> 9.59 us
  waiting for transfers between devices: 73.3 us -> 67.6 us
    all_to_all x1, waiting for transfers between devices: 0.01 us -> 12.8 us  [per_device(): lax.all_to_all(partial.reshape(16, 64, 512), ('xh', 'z'), split_axis=0, c...]
    all_to_all x0 -> x1, blocking collectives: none -> 12.4 us  [per_device(): lax.all_to_all(acts, ('xh', 'core'), split_axis=0, concat_axis=0, tiled=T...]
    ppermute x17 -> x13, waiting for transfers between devices: 65.7 us -> 54.7 us  [shift(): return lax.ppermute(x, axes, pairs)]
    unnamed x38 -> x28, local copies, waits for them, and re-layouts: 15.8 us -> 8.08 us
    ppermute x17 -> x13, starting transfers between devices: 18.2 us -> 10.7 us  [shift(): return lax.ppermute(x, axes, pairs)]
    all_to_all x1, waiting for transfers between devices: 6.86 us -> 0.01 us  [per_device(): lax.all_to_all(copies, 'z', split_axis=0, concat_axis=0, tiled=True)]
    all_to_all x1, blocking collectives: 20.9 us -> 24.7 us  [spread(): lax.all_to_all(jnp.broadcast_to(x[None], (count,) + x.shape), axes, split...]
    all_to_all x1, starting transfers between devices: 6.75 us -> 3.58 us  [per_device(): lax.all_to_all(copies, 'z', split_axis=0, concat_axis=0, tiled=True)]
  transfers between devices with their start and end apart: 20 -> 16, of which waited for: 10 -> 8; matrix products, arithmetic and copies ran while one was open for 3% -> 2% of each run, Pallas kernels for 4% -> 5%
where the time goes in v4:
time: 196 us; the launch traced here: 195 us
  waiting for transfers between devices  67.6 us (34%)
  blocking collectives  59.8 us (31%)
  starting transfers between devices  25.6 us (13%)
  between operations  13.6 us (7%)
  Pallas kernels  12.2 us (6%)
  local copies, waits for them, and re-layouts  9.59 us (5%)
  matrix products  5.87 us (3%)
    ppermute x13, waiting for transfers between devices, shift(): return lax.ppermute(x, axes, pairs)  54.7 us
    all_to_all x1, blocking collectives, spread(): lax.all_to_all(jnp.broadcast_to(x[None], (count,) + x.shape), axes, split...  24.7 us
    all_to_all x1, blocking collectives, per_device(): lax.all_to_all(tiles, ('xh', 'y'), split_axis=0, concat_axis=0, tiled=True)  22.6 us
    all_to_all x1, waiting for transfers between devices, per_device(): lax.all_to_all(partial.reshape(16, 64, 512), ('xh', 'z'), split_axis=0, c...  12.8 us
    all_to_all x1, blocking collectives, per_device(): lax.all_to_all(acts, ('xh', 'core'), split_axis=0, concat_axis=0, tiled=T...  12.4 us
    all_to_all x1, starting transfers between devices, per_device(): lax.all_to_all(partial.reshape(16, 64, 512), ('xh', 'z'), split_axis=0, c...  11.3 us
    ppermute x13, starting transfers between devices, shift(): return lax.ppermute(x, axes, pairs)  10.7 us
    pallas_call x7, Pallas kernels, call(): pl.pallas_call(kernel, out_shape=out, in_specs=specs, out_specs=jax.tree....  9.63 us
  transfers between devices with their start and end apart: 16, of which 8 were waited for; matrix products, arithmetic and copies ran while one was open for 2% of the time, Pallas kernels for 5%

profile of v4, /device:TPU:24, one launch (start us, length us, event | category | flops | bytes accessed | tf_op | source)
XLA Modules:
  0.0 195.1 jit_solution(14429362631196729515)
XLA Ops:
  8.0 12.4 %all_to_all.25 = bf16[4,32,1280]{2,1,0:T(8,128)(2,1)} all-to-all(bf16[4,32,1280]{2,1,0:T(8,128)(2,1)S(1)} %copy.52), channel_id=1, replica_groups=mesh['xl'=2,'core'=2,'z'=8,'xh'=2,'y'=4] {'xh','core'}, dimensions={0} | all-to-all | bytes 655360 | tf_op jit(solution)/shard_map/all_to_all | solution.py:175
  21.0 2.6 %pick.1 = (bf16[216,1536]{1,0:T(8,128)(2,1)S(1)}, bf16[216,1536]{1,0:T(8,128)(2,1)S(1)}) custom-call(s32[9]{0:T(128)S(1)} %pad_add_fusion.s_ref, bf16[216,13824]{1,0:T(8,128)(2,1)} %refs_7_.1, bf16[216,13824]{1,0:T(8,128)(2,1)} %refs_7_.1, bf16[216,13824]{1,0:T(8,128)(2,1)} %refs_7_.1, bf16[216,13824]{1,0:T(8,128)(2,1)} %refs_7_.1, ...), custom_call_target="tpu_custom_call" | custom-call | tf_op jit(solution)/shard_map/pick/pallas_call | solution.py:79
  24.5 4.4 %collective-permute-done = bf16[80,1280]{1,0:T(8,128)(2,1)S(1)} collective-permute-done((bf16[80,1280]{1,0:T(8,128)(2,1)S(1)}, bf16[80,1280]{1,0:T(8,128)(2,1)S(1)}, u32[]{:S(2)}, u32[]{:S(2)}) %collective-permute-start) | collective-permute-done | bytes 204832 | tf_op jit(solution)/shard_map/ppermute | solution.py:33
  30.8 10.4 %collective-permute-done.7.down = bf16[216,1536]{1,0:T(8,128)(2,1)S(1)} collective-permute-done((bf16[216,1536]{1,0:T(8,128)(2,1)S(1)}, bf16[216,1536]{1,0:T(8,128)(2,1)S(1)}, u32[]{:S(2)}, u32[]{:S(2)}) %collective-permute-start.7) | collective-permute-done | bytes 663584 | tf_op jit(solution)/shard_map/ppermute | solution.py:33
  41.4 3.2 %collective-permute-start.3 = (bf16[160,1280]{1,0:T(8,128)(2,1)S(1)}, bf16[160,1280]{1,0:T(8,128)(2,1)S(1)}, u32[]{:S(2)}, u32[]{:S(2)}) collective-permute-start(bf16[160,1280]{1,0:T(8,128)(2,1)S(1)} %collective-permute-done.1.refs_1_), channel_id=1, source_target_pairs={{0,1},{1,2},{2,3},{3,0},{4,5},{5,6},{6,7},{7,4},{8,9},{9,10},{10,1... | collective-permute-start | bytes 1228808 | tf_op jit(solution)/shard_map/ppermute | solution.py:33
  45.2 1.5 collective-permute-start.9
  46.7 18.0 %collective-permute-done.9.g3 = bf16[216,512]{1,0:T(8,128)(2,1)S(1)} collective-permute-done((bf16[216,512]{1,0:T(8,128)(2,1)S(1)}, bf16[216,512]{1,0:T(8,128)(2,1)S(1)}, u32[]{:S(2)}, u32[]{:S(2)}) %collective-permute-start.9) | collective-permute-done | bytes 221216 | tf_op jit(solution)/shard_map/ppermute | solution.py:33
  64.7 2.0 %collective-permute-done.2.refs_2_.refs_0_ = bf16[160,1280]{1,0:T(8,128)(2,1)S(1)} collective-permute-done((bf16[160,1280]{1,0:T(8,128)(2,1)S(1)}, bf16[160,1280]{1,0:T(8,128)(2,1)S(1)}, u32[]{:S(2)}, u32[]{:S(2)}) %collective-permute-start.2) | collective-permute-done | bytes 409632 | tf_op jit(solution)/shard_map/ppermute | solution.py:33
  66.7 2.3 %grads.1 = bf16[1024,512]{1,0:T(8,128)(2,1)} custom-call(bf16[216,1536]{1,0:T(8,128)(2,1)S(1)} %get-tuple-element.17.aside.here, bf16[216,1536]{1,0:T(8,128)(2,1)S(1)} %collective-permute-done.6.up, bf16[216,1536]{1,0:T(8,128)(2,1)S(1)} %collective-permute-done.7.down, bf16[216,1024]{1,0:T(8,128)(2,1)S(1)} %collective-permute-done.8.c3, ...), custom_call_target="tpu_custom_call" | custom-call | tf_op jit(solution)/shard_map/grads/pallas_call | solution.py:156
  69.0 11.3 %all-to-all-start.1 = ((bf16[16,64,512]{2,1,0:T(8,128)(2,1)}), bf16[16,64,512]{2,1,0:T(8,128)(2,1)S(1)}, u32[]{:S(2)}, u32[]{:S(2)}) async-start(bf16[16,64,512]{2,1,0:T(8,128)(2,1)} %bitcast.5), calls=%async_computation.1 | async-start | bytes 2097152 | tf_op jit(solution)/shard_map/all_to_all | solution.py:192
  80.3 1.7 copy-done.2
  84.1 3.6 %acts.1 = (f32[640,512]{1,0:T(8,128)S(1)}, bf16[640,512]{1,0:T(8,128)(2,1)S(1)}) custom-call(s32[1]{0:T(128)} %bitcast.2.core_ref, bf16[8,4,32,1280]{3,2,1,0:T(8,128)(2,1)S(1)} %bitcast.27, bf16[160,1280]{1,0:T(8,128)(2,1)S(1)} %copy-done.4, bf16[160,1280]{1,0:T(8,128)(2,1)S(1)} %copy-done.10, bf16[160,1280]{1,0:T(8,128)(2,1)S(1)} %collective-permute-done.2.refs_2_.refs_0_, ...), custom_call_target="tpu_custom_call" | custom-call | tf_op jit(solution)/shard_map/acts/pallas_call | solution.py:156
  87.8 2.1 %collective-permute-done.4.b = bf16[640,512]{1,0:T(8,128)(2,1)S(1)} collective-permute-done((bf16[640,512]{1,0:T(8,128)(2,1)S(1)}, bf16[640,512]{1,0:T(8,128)(2,1)S(1)}, u32[]{:S(2)}, u32[]{:S(2)}) %collective-permute-start.4) | collective-permute-done | bytes 655392 | tf_op jit(solution)/shard_map/ppermute | solution.py:33
  91.1 12.8 %all-to-all-done.1.parts = bf16[16,64,512]{2,1,0:T(8,128)(2,1)S(1)} async-done(((bf16[16,64,512]{2,1,0:T(8,128)(2,1)}), bf16[16,64,512]{2,1,0:T(8,128)(2,1)S(1)}, u32[]{:S(2)}, u32[]{:S(2)}) %all-to-all-start.1) | async-done | bytes 1048608 | tf_op jit(solution)/shard_map/all_to_all | solution.py:192
  103.9 1.5 live.1
  105.4 3.6 %all-to-all-start.2 = ((bf16[8,64,512]{2,1,0:T(8,128)(2,1)}), bf16[8,64,512]{2,1,0:T(8,128)(2,1)S(1)}, u32[]{:S(2)}, u32[]{:S(2)}) async-start(bf16[8,64,512]{2,1,0:T(8,128)(2,1)} %live.1), calls=%async_computation.2 | async-start | bytes 1048576 | tf_op jit(solution)/shard_map/all_to_all | solution.py:198
  109.0 1.7 collective-permute-start.5
  110.7 13.1 %collective-permute-done.5.rb = bf16[640,512]{1,0:T(8,128)(2,1)S(1)} collective-permute-done((bf16[640,512]{1,0:T(8,128)(2,1)S(1)}, bf16[640,512]{1,0:T(8,128)(2,1)S(1)}, u32[]{:S(2)}, u32[]{:S(2)}) %collective-permute-start.5) | collective-permute-done | bytes 655392 | tf_op jit(solution)/shard_map/ppermute | solution.py:33
  128.4 22.6 %all_to_all.26.parts = bf16[8,2,80,512]{3,2,1,0:T(8,128)(2,1)S(1)} all-to-all(bf16[8,2,80,512]{3,2,1,0:T(8,128)(2,1)S(1)} %seq.1), channel_id=1, replica_groups=mesh['xl'=2,'core'=2,'z'=8,'xh'=2,'y'=4] {'xh','y'}, dimensions={0} | all-to-all | bytes 2621440 | tf_op jit(solution)/shard_map/all_to_all | solution.py:201
  152.1 1.5 convolution_bitcast_fusion.3
  153.6 4.8 %collective-permute-done.11 = bf16[2,80,1024]{2,1,0:T(8,128)(2,1)S(1)} collective-permute-done((bf16[2,80,1024]{2,1,0:T(8,128)(2,1)S(1)}, bf16[2,80,1024]{2,1,0:T(8,128)(2,1)S(1)}, u32[]{:S(2)}, u32[]{:S(2)}) %collective-permute-start.11) | collective-permute-done | bytes 327712 | tf_op jit(solution)/shard_map/ppermute | solution.py:33
  159.8 1.5 convolution_bitcast_fusion.2
  161.3 1.5 convolution_bitcast_fusion
  162.9 24.7 %all_to_all.27 = f32[64,8,8]{2,1,0:T(8,128)S(1)} all-to-all(f32[64,8,8]{2,1,0:T(8,128)S(1)} %broadcast_in_dim.21), channel_id=1, replica_groups=mesh['xl'=2,'core'=2,'z'=8,'xh'=2,'y'=4] {'z','xh','y'}, dimensions={0} | all-to-all | bytes 32768 | tf_op jit(solution)/shard_map/all_to_all | solution.py:37
  (63 shorter events, 16.7 us)
Async XLA Ops:
  6.5 145.6 %copy-start = (bf16[8,80,1024]{2,1,0:T(8,128)(2,1)S(1)}, bf16[8,80,1024]{2,1,0:T(8,128)(2,1)}, u32[]{:S(2)}) copy-start(bf16[8,80,1024]{2,1,0:T(8,128)(2,1)} %param.13) | copy-start | bytes 3932164
  6.5 13.9 %copy-start.12 = (bf16[80,5120]{1,0:T(8,128)(2,1)S(1)}, bf16[80,5120]{1,0:T(8,128)(2,1)}, u32[]{:S(2)}) copy-start(bf16[80,5120]{1,0:T(8,128)(2,1)} %param.9) | copy-start | bytes 2457604
  6.5 73.8 %all-gather.3.cloned.1.call-start = ((), (), s32[]{:S(2)}) async-start(), calls=%async_computation.5 | async-start | bytes 2949120 | tf_op jit(solution)/shard_map/all_gather | solution.py:176
  7.9 13.0 %copy-start.13 = (s32[8]{0:T(128)S(1)}, s32[8]{0:T(128)}, u32[]{:S(2)}) copy-start(s32[8]{0:T(128)} %param.11) | copy-start | bytes 100
  20.5 8.3 %collective-permute-start = (bf16[80,1280]{1,0:T(8,128)(2,1)S(1)}, bf16[80,1280]{1,0:T(8,128)(2,1)S(1)}, u32[]{:S(2)}, u32[]{:S(2)}) collective-permute-start(bf16[80,1280]{1,0:T(8,128)(2,1)S(1)} %get-tuple-element.22), channel_id=1, source_target_pairs={{0,4},{4,0},{1,5},{5,1},{2,6},{6,2},{3,7},{7,3},{8,12},{12,8},{9,1... | collective-permute-start | bytes 614408 | tf_op jit(solution)/shard_map/ppermute | solution.py:33
  23.6 21.0 %copy-start.1 = (bf16[216,2048]{1,0:T(8,128)(2,1)S(1)}, bf16[216,2048]{1,0:T(8,128)(2,1)}, u32[]{:S(2)}) copy-start(bf16[216,2048]{1,0:T(8,128)(2,1)} %g_ref.1) | copy-start | bytes 2654212
  23.7 17.5 %collective-permute-start.7 = (bf16[216,1536]{1,0:T(8,128)(2,1)S(1)}, bf16[216,1536]{1,0:T(8,128)(2,1)S(1)}, u32[]{:S(2)}, u32[]{:S(2)}) collective-permute-start(bf16[216,1536]{1,0:T(8,128)(2,1)S(1)} %get-tuple-element.18), channel_id=1, source_target_pairs={{0,3},{1,0},{2,1},{3,2},{4,7},{5,4},{6,5},{7,6},{8,11},{9,8},{10,9... | collective-permute-start | bytes 1990664 | tf_op jit(solution)/shard_map/ppermute | solution.py:33
  28.9 40.1 %copy-start.3 = (bf16[160,1280]{1,0:T(8,128)(2,1)}, bf16[160,1280]{1,0:T(8,128)(2,1)S(1)}, u32[]{:S(2)}) copy-start(bf16[160,1280]{1,0:T(8,128)(2,1)S(1)} %pad_maximum_fusion.refs_0_) | copy-start | bytes 1228804
  28.9 12.5 %collective-permute-start.1 = (bf16[160,1280]{1,0:T(8,128)(2,1)S(1)}, bf16[160,1280]{1,0:T(8,128)(2,1)S(1)}, u32[]{:S(2)}, u32[]{:S(2)}) collective-permute-start(bf16[160,1280]{1,0:T(8,128)(2,1)S(1)} %pad_maximum_fusion.refs_0_), channel_id=1, source_target_pairs={{0,1},{1,2},{2,3},{3,0},{4,5},{5,6},{6,7},{7,4},{8,9},{9,10},{10,1... | collective-permute-start | bytes 1228808 | tf_op jit(solution)/shard_map/ppermute | solution.py:33
  29.8 36.9 %collective-permute-start.6 = (bf16[216,1536]{1,0:T(8,128)(2,1)S(1)}, bf16[216,1536]{1,0:T(8,128)(2,1)S(1)}, u32[]{:S(2)}, u32[]{:S(2)}) collective-permute-start(bf16[216,1536]{1,0:T(8,128)(2,1)S(1)} %get-tuple-element.17.aside.here), channel_id=1, source_target_pairs={{0,1},{1,2},{2,3},{3,0},{4,5},{5,6},{6,7},{7,4},{8,9},{9,10},{10,1... | collective-permute-start | bytes 1990664 | tf_op jit(solution)/shard_map/ppermute | solution.py:33
  41.2 25.5 %collective-permute-start.8 = (bf16[216,1024]{1,0:T(8,128)(2,1)S(1)}, bf16[216,1024]{1,0:T(8,128)(2,1)S(1)}, u32[]{:S(2)}, u32[]{:S(2)}) collective-permute-start(bf16[216,1024]{1,0:T(8,128)(2,1)S(1)} %slice.4), channel_id=1, source_target_pairs={{0,3},{1,0},{2,1},{3,2},{4,7},{5,4},{6,5},{7,6},{8,11},{9,8},{10,9... | collective-permute-start | bytes 1327112 | tf_op jit(solution)/shard_map/ppermute | solution.py:33
  41.3 25.4 %collective-permute-start.2 = (bf16[160,1280]{1,0:T(8,128)(2,1)S(1)}, bf16[160,1280]{1,0:T(8,128)(2,1)S(1)}, u32[]{:S(2)}, u32[]{:S(2)}) collective-permute-start(bf16[160,1280]{1,0:T(8,128)(2,1)S(1)} %pad_maximum_fusion.refs_0_), channel_id=1, source_target_pairs={{0,3},{1,0},{2,1},{3,2},{4,7},{5,4},{6,5},{7,6},{8,11},{9,8},{10,9... | collective-permute-start | bytes 1228808 | tf_op jit(solution)/shard_map/ppermute | solution.py:33
  41.4 27.6 %copy-start.9 = (bf16[160,1280]{1,0:T(8,128)(2,1)}, bf16[160,1280]{1,0:T(8,128)(2,1)S(1)}, u32[]{:S(2)}) copy-start(bf16[160,1280]{1,0:T(8,128)(2,1)S(1)} %collective-permute-done.1.refs_1_) | copy-start | bytes 1228804
  41.4 25.3 %collective-permute-start.3 = (bf16[160,1280]{1,0:T(8,128)(2,1)S(1)}, bf16[160,1280]{1,0:T(8,128)(2,1)S(1)}, u32[]{:S(2)}, u32[]{:S(2)}) collective-permute-start(bf16[160,1280]{1,0:T(8,128)(2,1)S(1)} %collective-permute-done.1.refs_1_), channel_id=1, source_target_pairs={{0,1},{1,2},{2,3},{3,0},{4,5},{5,6},{6,7},{7,4},{8,9},{9,10},{10,1... | collective-permute-start | bytes 1228808 | tf_op jit(solution)/shard_map/ppermute | solution.py:33
  45.2 19.5 %collective-permute-start.9 = (bf16[216,512]{1,0:T(8,128)(2,1)S(1)}, bf16[216,512]{1,0:T(8,128)(2,1)S(1)}, u32[]{:S(2)}, u32[]{:S(2)}) collective-permute-start(bf16[216,512]{1,0:T(8,128)(2,1)S(1)} %get-tuple-element.20), channel_id=1, source_target_pairs={{0,2},{1,3},{2,0},{3,1},{4,6},{5,7},{6,4},{7,5},{8,10},{9,11},{10,... | collective-permute-start | bytes 663560 | tf_op jit(solution)/shard_map/ppermute | solution.py:33
  69.0 34.9 %all-to-all-start.1 = ((bf16[16,64,512]{2,1,0:T(8,128)(2,1)}), bf16[16,64,512]{2,1,0:T(8,128)(2,1)S(1)}, u32[]{:S(2)}, u32[]{:S(2)}) async-start(bf16[16,64,512]{2,1,0:T(8,128)(2,1)} %bitcast.5), calls=%async_computation.1 | async-start | bytes 2097152 | tf_op jit(solution)/shard_map/all_to_all | solution.py:192
  80.3 1.7 copy-start.2
  87.6 16.3 %copy-start.11 = (s32[2]{0:T(128)S(1)}, s32[2]{0:T(128)}, u32[]{:S(2)}) copy-start(s32[2]{0:T(128)} %lens.1) | copy-start | bytes 28
  87.7 2.2 %collective-permute-start.4 = (bf16[640,512]{1,0:T(8,128)(2,1)S(1)}, bf16[640,512]{1,0:T(8,128)(2,1)S(1)}, u32[]{:S(2)}, u32[]{:S(2)}) collective-permute-start(bf16[640,512]{1,0:T(8,128)(2,1)S(1)} %get-tuple-element.14), channel_id=1, source_target_pairs={{0,64},{64,0},{1,65},{65,1},{2,66},{66,2},{3,67},{67,3},{4,68},{68... | collective-permute-start | bytes 1966088 | tf_op jit(solution)/shard_map/ppermute | solution.py:33
  105.4 19.2 %all-to-all-start.2 = ((bf16[8,64,512]{2,1,0:T(8,128)(2,1)}), bf16[8,64,512]{2,1,0:T(8,128)(2,1)S(1)}, u32[]{:S(2)}, u32[]{:S(2)}) async-start(bf16[8,64,512]{2,1,0:T(8,128)(2,1)} %live.1), calls=%async_computation.2 | async-start | bytes 1048576 | tf_op jit(solution)/shard_map/all_to_all | solution.py:198
  109.0 14.8 %collective-permute-start.5 = (bf16[640,512]{1,0:T(8,128)(2,1)S(1)}, bf16[640,512]{1,0:T(8,128)(2,1)S(1)}, u32[]{:S(2)}, u32[]{:S(2)}) collective-permute-start(bf16[640,512]{1,0:T(8,128)(2,1)S(1)} %get-tuple-element.16.refs_0_), channel_id=1, source_target_pairs={{0,4},{4,0},{1,5},{5,1},{2,6},{6,2},{3,7},{7,3},{8,12},{12,8},{9,1... | collective-permute-start | bytes 1966088 | tf_op jit(solution)/shard_map/ppermute | solution.py:33
  151.2 7.2 %collective-permute-start.11 = (bf16[2,80,1024]{2,1,0:T(8,128)(2,1)S(1)}, bf16[2,80,1024]{2,1,0:T(8,128)(2,1)S(1)}, u32[]{:S(2)}, u32[]{:S(2)}) collective-permute-start(bf16[2,80,1024]{2,1,0:T(8,128)(2,1)S(1)} %sums.1), channel_id=1, source_target_pairs={{0,128},{128,0},{1,129},{129,1},{2,130},{130,2},{3,131},{131,3},{4... | collective-permute-start | bytes 983048 | tf_op jit(solution)/shard_map/ppermute | solution.py:33
  152.1 7.7 %collective-permute-start.10 = (bf16[2,80,1024]{2,1,0:T(8,128)(2,1)S(1)}, bf16[2,80,1024]{2,1,0:T(8,128)(2,1)S(1)}, u32[]{:S(2)}, u32[]{:S(2)}) collective-permute-start(bf16[2,80,1024]{2,1,0:T(8,128)(2,1)S(1)} %sums.1), channel_id=1, source_target_pairs={{0,64},{64,0},{1,65},{65,1},{2,66},{66,2},{3,67},{67,3},{4,68},{68... | collective-permute-start | bytes 983048 | tf_op jit(solution)/shard_map/ppermute | solution.py:33
  158.4 2.9 %collective-permute-start.12 = (bf16[2,80,1024]{2,1,0:T(8,128)(2,1)S(1)}, bf16[2,80,1024]{2,1,0:T(8,128)(2,1)S(1)}, u32[]{:S(2)}, u32[]{:S(2)}) collective-permute-start(bf16[2,80,1024]{2,1,0:T(8,128)(2,1)S(1)} %collective-permute-done.11), channel_id=1, source_target_pairs={{0,64},{64,0},{1,65},{65,1},{2,66},{66,2},{3,67},{67,3},{4,68},{68... | collective-permute-start | bytes 983048 | tf_op jit(solution)/shard_map/ppermute | solution.py:33
  (6 other events, 6.3 us)
Sparse Core Ops, SparseCore 0:
  20.5 42.5 all-gather.2

commit v5 on v4

--- a/solution.py
+++ b/solution.py
@@ -59,12 +59,12 @@
 
 
 def pick_kernel(s_ref, *refs):
-    picked, g_ref, up, down = refs[:8], *refs[8:]
+    picked, g_ref, up, down, g0, g3 = refs[:8], *refs[8:]
     for n, p in enumerate(picked):
         cols = slice(n * 128, n * 128 + 128)
         up[:, cols] = p[...]
         down[:, cols] = p[...]
-    reorder(s_ref[8], g_ref, ((up, 1024, 1), (down, 1024, -1)))
+    reorder(s_ref[8], g_ref, ((up, 1024, 1), (down, 1024, -1), (g3, 0, 2), (g0, 0, 0)))
 
 
 def pick(block_ids, y, basis_out, out_grads):
@@ -74,19 +74,46 @@
         num_scalar_prefetch=1,
         grid=(1,),
         in_specs=[pl.BlockSpec((rows, BLOCK), lambda g, s, n=n: (0, s[n])) for n in range(8)] + [whole(tokens)],
-        out_specs=[whole(1536), whole(1536)],
+        out_specs=[whole(1536), whole(1536), whole(512), whole(512)],
     )
     return pl.pallas_call(
         pick_kernel,
         grid_spec=spec,
-        out_shape=[arr(rows, 1536), arr(rows, 1536)],
+        out_shape=[arr(rows, 1536), arr(rows, 1536), arr(rows, 512), arr(rows, 512)],
         compiler_params=WIDE,
         name="pick",
     )(jnp.concatenate([block_ids, y[None]]), *[basis_out] * 8, out_grads)
 
 
-def rest_kernel(y_ref, g_ref, aside, g0, g3):
-    reorder(y_ref[0], g_ref, ((g3, 0, 2), (g0, 0, 0)))
+def cut_kernel(xh_ref, core_ref, a_ref, b_ref, a_own, a_sib, b_own):
+    part = a_ref.shape[1] // 4
+    for near in range(2):
+        x = (xh_ref[0] + near) % 2
+        mine = pl.ds(pl.multiple_of((x * 2 + core_ref[0]) * part, 128), part)
+        other = pl.ds(pl.multiple_of((x * 2 + 1 - core_ref[0]) * part, 128), part)
+        cols = slice(near * part, near * part + part)
+        a_own[:, cols] = a_ref[:, mine]
+        a_sib[:, cols] = a_ref[:, other]
+        b_own[:, cols] = b_ref[:, mine]
+
+
+def pair_kernel(own, sib, aside, near, far):
+    part = near.shape[2]
+    for n, a in enumerate((own, sib)):
+        near[n] = a[:, :part]
+        far[n] = a[:, part:]
+
+
+def stack_kernel(near, far, *refs):
+    o_ref = refs[-1]
+    o_ref[:2] = near[...]
+    o_ref[2:] = far[...]
+
+
+def join_kernel(b0, b1, b2, aside, o_ref):
+    part = b0.shape[1] // 2
+    for n, b in enumerate((b0, b1, b2)):
+        o_ref[n * 80 : n * 80 + 80, :] = b[:, part:]
 
 
 def grads_kernel(here, up, down, c3, g0, g3, *refs):
@@ -111,19 +138,21 @@
         o_ref[n] = total
 
 
-def acts_kernel(core_ref, a_ref, *refs):
-    keep, send = refs[-2:]
-    core = core_ref[0]
+def acts_kernel(xh_ref, a_ref, b0, b1, b2, b3, far, far3, keep, send):
+    part = a_ref.shape[3]
+    rows = [(n * 160, b, slice(0, 80), slice(0, part)) for n, b in enumerate((b0, b1, b2, b3))]
+    rows += [(n * 160 + 80, far, slice(n * 80, n * 80 + 80), slice(0, part)) for n in range(3)]
+    rows += [(560, far3, slice(0, 80), slice(0, part))]
     for xh in range(2):
         cols = slice(xh * 256, xh * 256 + 256)
-        for out, which in ((keep, core), (send, 1 - core)):
-            tokens = a_ref[:, xh * 2 + which].reshape(256, a_ref.shape[3])
-            for n in range(4):
-                out[n * 160 : n * 160 + 160, cols] = dot(refs[n][...], tokens, 1, 1).astype(out.dtype)
+        for core, out in enumerate((keep, send)):
+            tokens = a_ref[:, (xh_ref[0] + xh) % 2 * 2 + core].reshape(256, part)
+            for place, b, r, c in rows:
+                out[place : place + 80, cols] = dot(b[r, c], tokens, 1, 1)
 
 
 def add_kernel(a, b, keep, send):
-    total = a[...] + b[...].astype(F32)
+    total = a[...] + b[...]
     keep[...] = total
     send[...] = total.astype(BF)
 
@@ -158,7 +187,7 @@
         out_shape=out,
         in_specs=specs,
         out_specs=jax.tree.map(lambda _: VMEM, out),
-        compiler_params=ROOM,
+        compiler_params=WIDE if name in ("acts", "seq") else ROOM,
         name=name,
     )(*scalars, *args, *aside)
 
@@ -171,28 +200,28 @@
     xl, core, xh, y = (lax.axis_index(a).astype(jnp.int32) for a in ("xl", "core", "xh", "y"))
     slots, features = activations.shape
     part = features // 4
-    acts = activations.reshape(slots, 4, part).transpose(1, 0, 2)
-    acts = lax.all_to_all(acts, ("xh", "core"), split_axis=0, concat_axis=0, tiled=True)
+    place = [xh[None], core[None]]
+    cuts = [arr(slots, 2 * part), arr(slots, 2 * part), arr(80, 2 * part)]
+    a_own, a_sib, b0 = call(cut_kernel, cuts, "cut", [activations, basis_in], place)
+    b1, b2 = shift(b0, y=1), shift(b0, y=-1)
+    a_sib = shift(a_sib, core=1)
+    up, down, g0, g3 = pick(block_ids, y, basis_out, out_grads)
+    near, a_far = call(pair_kernel, [arr(2, slots, part)] * 2, "pair", [a_own, a_sib], (), [g0])
+    a_far = shift(a_far, xh=1)
+    up_got, down_got, g3_got = shift(up, y=1), shift(down, y=-1), shift(g3, y=2)
+    acts = call(stack_kernel, arr(4, slots, part), "stack", [near, a_far], (), [down_got, up_got, b1, b2])
     acts = lax.all_gather(acts, "z", axis=0, tiled=False)
-
-    def quarter(x):
-        return lax.dynamic_slice_in_dim(basis_in, (x * 2 + core) * part, part, 1)
-
-    b0 = jnp.concatenate([quarter(xh), shift(quarter(1 - xh), xh=1)])
-    b1, b2 = shift(b0, y=1), shift(b0, y=-1)
+    c3 = shift(down_got[:, :1024], y=-1)
     b3 = shift(b1, y=1)
-
-    up, down = pick(block_ids, y, basis_out, out_grads)
-    g0, g3 = call(rest_kernel, [arr(216, 512)] * 2, "rest", [out_grads], [y[None]], [up])
-    up_got, down_got, g3_got = shift(up, y=1), shift(down, y=-1), shift(g3, y=2)
-    c3 = shift(down_got[:, :1024], y=-1)
+    far = shift(call(join_kernel, arr(240, part), "join", [b0, b1, b2], (), [g0]), xh=1)
+    far3 = shift(b3[:, part:], xh=1)
 
     grads_in = [up, up_got, down_got, c3, g0, g3_got]
-    partial = call(grads_kernel, arr(1024, 512), "grads", grads_in, (), [b2, b3])
+    partial = call(grads_kernel, arr(1024, 512), "grads", grads_in, (), [far, b3])
     parts = lax.all_to_all(partial.reshape(16, 64, 512), ("xh", "z"), split_axis=0, concat_axis=0, tiled=True)
-    sums = [jax.ShapeDtypeStruct((640, 512), F32), arr(640, 512)]
-    keep, send = call(acts_kernel, sums, "acts", [acts, b0, b1, b2, b3], [core[None]])
-    keep, send = call(add_kernel, sums, "add", [keep, shift(send, core=1)])
+    wide = jax.ShapeDtypeStruct((640, 512), F32)
+    keep, send = call(acts_kernel, [wide, wide], "acts", [acts, b0, b1, b2, b3, far, far3], [xh[None]])
+    keep, send = call(add_kernel, [wide, arr(640, 512)], "add", [keep, shift(send, core=1)])
     rb = shift(send, xh=1)
     copies = call(live_kernel, arr(8, 64, 512), "live", [parts], [y[None], seq_lens], [send])
     rotated = lax.all_to_all(copies, "z", split_axis=0, concat_axis=0, tiled=True).reshape(512, 512)

time: 196 us -> 221 us (1.13)
  starting transfers between devices: 25.6 us -> 38.4 us
  Pallas kernels: 12.2 us -> 24 us
  waiting for transfers between devices: 67.6 us -> 78.7 us
  blocking collectives: 59.8 us -> 48.7 us
    all_gather x1, waiting for transfers between devices: 0.02 us -> 19.6 us  [per_device(): acts = lax.all_gather(acts, 'z', axis=0, tiled=False)]
    ppermute x13 -> x16, starting transfers between devices: 10.7 us -> 24.5 us  [shift(): return lax.ppermute(x, axes, pairs)]
    all_to_all x1, waiting for transfers between devices: 12.8 us -> 0.01 us  [per_device(): lax.all_to_all(partial.reshape(16, 64, 512), ('xh', 'z'), split_axis=0, c...]
    all_to_all x1 -> x0, blocking collectives: 12.4 us -> none  [per_device(): lax.all_to_all(acts, ('xh', 'core'), split_axis=0, concat_axis=0, tiled=T...]
    pallas_call x7 -> x10, Pallas kernels: 9.63 us -> 19.9 us  [call(): pl.pallas_call(kernel, out_shape=out, in_specs=specs, out_specs=jax.tree....]
    ppermute x13 -> x16, waiting for transfers between devices: 54.7 us -> 59.1 us  [shift(): return lax.ppermute(x, axes, pairs)]
    all_to_all x1, starting transfers between devices: 11.3 us -> 8.59 us  [per_device(): lax.all_to_all(partial.reshape(16, 64, 512), ('xh', 'z'), split_axis=0, c...]
    unnamed x28 -> x32, local copies, waits for them, and re-layouts: 8.08 us -> 8.04 us
  transfers between devices with their start and end apart: 16 -> 19, of which waited for: 8 -> 9; matrix products, arithmetic and copies ran while one was open for 2% -> 2% of each run, Pallas kernels for 5% -> 6%
where the time goes in v5:
time: 221 us; the launch traced here: 220 us
  waiting for transfers between devices  78.7 us (36%)
  blocking collectives  48.7 us (22%)
  starting transfers between devices  38.4 us (17%)
  Pallas kernels  24 us (11%)
  between operations  13.6 us (6%)
  local copies, waits for them, and re-layouts  9.06 us (4%)
  matrix products  5.87 us (3%)
    ppermute x16, waiting for transfers between devices, shift(): return lax.ppermute(x, axes, pairs)  59.1 us
    all_to_all x1, blocking collectives, spread(): lax.all_to_all(jnp.broadcast_to(x[None], (count,) + x.shape), axes, split...  24.7 us
    ppermute x16, starting transfers between devices, shift(): return lax.ppermute(x, axes, pairs)  24.5 us
    all_to_all x1, blocking collectives, per_device(): lax.all_to_all(tiles, ('xh', 'y'), split_axis=0, concat_axis=0, tiled=True)  24 us
    pallas_call x10, Pallas kernels, call(): pl.pallas_call(kernel, out_shape=out, in_specs=specs, out_specs=jax.tree....  19.9 us
    all_gather x1, waiting for transfers between devices, per_device(): acts = lax.all_gather(acts, 'z', axis=0, tiled=False)  19.6 us
    all_to_all x1, starting transfers between devices, per_device(): lax.all_to_all(partial.reshape(16, 64, 512), ('xh', 'z'), split_axis=0, c...  8.59 us
    unnamed x32, local copies, waits for them, and re-layouts  8.04 us
  transfers between devices with their start and end apart: 19, of which 9 were waited for; matrix products, arithmetic and copies ran while one was open for 2% of the time, Pallas kernels for 6%

profile of v5, /device:TPU:24, one launch (start us, length us, event | category | flops | bytes accessed | tf_op | source)
XLA Modules:
  0.0 219.9 jit_solution(9126865424073599671)
XLA Ops:
  7.4 4.1 %pick.1 = (bf16[216,1536]{1,0:T(8,128)(2,1)}, bf16[216,1536]{1,0:T(8,128)(2,1)}, bf16[216,512]{1,0:T(8,128)(2,1)S(1)}, bf16[216,512]{1,0:T(8,128)(2,1)S(1)}) custom-call(s32[9]{0:T(128)S(1)} %pad_add_fusion.s_ref, bf16[216,13824]{1,0:T(8,128)(2,1)} %refs_7_.1, bf16[216,13824]{1,0:T(8,128)(2,1)} %refs_7_.1, bf16[216,13824]{1,0:T(8,128)(2,1)} %refs_7_.1, ...), custom_call_target="tpu_custom_call" | custom-call | tf_op jit(solution)/shard_map/pick/pallas_call | solution.py:79
  12.9 2.5 %collective-permute-start.3 = (bf16[216,1536]{1,0:T(8,128)(2,1)}, bf16[216,1536]{1,0:T(8,128)(2,1)}, u32[]{:S(2)}, u32[]{:S(2)}) collective-permute-start(bf16[216,1536]{1,0:T(8,128)(2,1)} %get-tuple-element.24.here), channel_id=1, source_target_pairs={{0,1},{1,2},{2,3},{3,0},{4,5},{5,6},{6,7},{7,4},{8,9},{9,10},{10,1... | collective-permute-start | bytes 1990664 | tf_op jit(solution)/shard_map/ppermute | solution.py:33
  15.6 3.2 %collective-permute-start.4 = (bf16[80,2560]{1,0:T(8,128)(2,1)S(1)}, bf16[80,2560]{1,0:T(8,128)(2,1)S(1)}, u32[]{:S(2)}, u32[]{:S(2)}) collective-permute-start(bf16[80,2560]{1,0:T(8,128)(2,1)S(1)} %get-tuple-element.25.b0), channel_id=1, source_target_pairs={{0,1},{1,2},{2,3},{3,0},{4,5},{5,6},{6,7},{7,4},{8,9},{9,10},{10,1... | collective-permute-start | bytes 1228808 | tf_op jit(solution)/shard_map/ppermute | solution.py:33
  20.2 3.1 %collective-permute-start.1 = (bf16[2,32,1280]{2,1,0:T(8,128)(2,1)S(1)}, bf16[2,32,1280]{2,1,0:T(8,128)(2,1)S(1)}, u32[]{:S(2)}, u32[]{:S(2)}) collective-permute-start(bf16[2,32,1280]{2,1,0:T(8,128)(2,1)S(1)} %get-tuple-element.22), channel_id=1, source_target_pairs={{0,4},{4,0},{1,5},{5,1},{2,6},{6,2},{3,7},{7,3},{8,12},{12,8},{9,1... | collective-permute-start | bytes 491528 | tf_op jit(solution)/shard_map/ppermute | solution.py:33
  23.3 4.7 %collective-permute-done.1.far = bf16[2,32,1280]{2,1,0:T(8,128)(2,1)S(1)} collective-permute-done((bf16[2,32,1280]{2,1,0:T(8,128)(2,1)S(1)}, bf16[2,32,1280]{2,1,0:T(8,128)(2,1)S(1)}, u32[]{:S(2)}, u32[]{:S(2)}) %collective-permute-start.1) | collective-permute-done | bytes 163872 | tf_op jit(solution)/shard_map/ppermute | solution.py:33
  28.1 11.0 %collective-permute-done.5.refs_3_.b2 = bf16[80,2560]{1,0:T(8,128)(2,1)S(1)} collective-permute-done((bf16[80,2560]{1,0:T(8,128)(2,1)S(1)}, bf16[80,2560]{1,0:T(8,128)(2,1)S(1)}, u32[]{:S(2)}, u32[]{:S(2)}) %collective-permute-start.5) | collective-permute-done | bytes 409632 | tf_op jit(solution)/shard_map/ppermute | solution.py:33
  40.9 3.1 %collective-permute-start.7 = (bf16[240,1280]{1,0:T(8,128)(2,1)S(1)}, bf16[240,1280]{1,0:T(8,128)(2,1)S(1)}, u32[]{:S(2)}, u32[]{:S(2)}) collective-permute-start(bf16[240,1280]{1,0:T(8,128)(2,1)S(1)} %join.1), channel_id=1, source_target_pairs={{0,4},{4,0},{1,5},{5,1},{2,6},{6,2},{3,7},{7,3},{8,12},{12,8},{9,1... | collective-permute-start | bytes 1843208 | tf_op jit(solution)/shard_map/ppermute | solution.py:33
  44.1 3.2 %collective-permute-start.6 = (bf16[80,2560]{1,0:T(8,128)(2,1)S(1)}, bf16[80,2560]{1,0:T(8,128)(2,1)S(1)}, u32[]{:S(2)}, u32[]{:S(2)}) collective-permute-start(bf16[80,2560]{1,0:T(8,128)(2,1)S(1)} %collective-permute-done.4.refs_2_.b1), channel_id=1, source_target_pairs={{0,1},{1,2},{2,3},{3,0},{4,5},{5,6},{6,7},{7,4},{8,9},{9,10},{10,1... | collective-permute-start | bytes 1228808 | tf_op jit(solution)/shard_map/ppermute | solution.py:33
  48.6 13.1 %collective-permute-done.12.g3 = bf16[216,512]{1,0:T(8,128)(2,1)S(1)} collective-permute-done((bf16[216,512]{1,0:T(8,128)(2,1)S(1)}, bf16[216,512]{1,0:T(8,128)(2,1)S(1)}, u32[]{:S(2)}, u32[]{:S(2)}) %collective-permute-start.12) | collective-permute-done | bytes 221216 | tf_op jit(solution)/shard_map/ppermute | solution.py:33
  61.7 4.0 %grads.1 = bf16[1024,512]{1,0:T(8,128)(2,1)} custom-call(bf16[216,1536]{1,0:T(8,128)(2,1)} %get-tuple-element.24.here, bf16[216,1536]{1,0:T(8,128)(2,1)} %collective-permute-done.3.refs_1_.up, bf16[216,1536]{1,0:T(8,128)(2,1)S(1)} %collective-permute-done.2.refs_0_.down, bf16[216,1024]{1,0:T(8,128)(2,1)S(1)} %collective-permute-done.11.c3, ...), custom_call_target="tpu_custom_call" | custom-call | tf_op jit(solution)/shard_map/grads/pallas_call | solution.py:185
  65.7 8.6 %all-to-all-start = ((bf16[16,64,512]{2,1,0:T(8,128)(2,1)}), bf16[16,64,512]{2,1,0:T(8,128)(2,1)S(1)}, u32[]{:S(2)}, u32[]{:S(2)}) async-start(bf16[16,64,512]{2,1,0:T(8,128)(2,1)} %bitcast.4), calls=%async_computation | async-start | bytes 2097152 | tf_op jit(solution)/shard_map/all_to_all | solution.py:221
  75.3 3.7 %collective-permute-start.8 = (bf16[80,1280]{1,0:T(8,128)(2,1)S(1)}, bf16[80,1280]{1,0:T(8,128)(2,1)S(1)}, u32[]{:S(2)}, u32[]{:S(2)}) collective-permute-start(bf16[80,1280]{1,0:T(8,128)(2,1)S(1)} %slice.8), channel_id=1, source_target_pairs={{0,4},{4,0},{1,5},{5,1},{2,6},{6,2},{3,7},{7,3},{8,12},{12,8},{9,1... | collective-permute-start | bytes 614408 | tf_op jit(solution)/shard_map/ppermute | solution.py:33
  79.0 5.3 %collective-permute-done.8.far3 = bf16[80,1280]{1,0:T(8,128)(2,1)S(1)} collective-permute-done((bf16[80,1280]{1,0:T(8,128)(2,1)S(1)}, bf16[80,1280]{1,0:T(8,128)(2,1)S(1)}, u32[]{:S(2)}, u32[]{:S(2)}) %collective-permute-start.8) | collective-permute-done | bytes 204832 | tf_op jit(solution)/shard_map/ppermute | solution.py:33
  84.3 19.6 %all-gather.3.cloned.1.call-done = bf16[32,32,1280]{2,1,0:T(8,128)(2,1)} async-done(((bf16[4,32,1280]{2,1,0:T(8,128)(2,1)}), bf16[32,32,1280]{2,1,0:T(8,128)(2,1)}) %all-gather.3.cloned.1.call-update) | async-done | bytes 2621456 | tf_op jit(solution)/shard_map/all_gather | solution.py:213
  105.9 9.4 %acts.1 = (f32[640,512]{1,0:T(8,128)}, f32[640,512]{1,0:T(8,128)}) custom-call(s32[1]{0:T(128)} %bitcast.xh_ref, bf16[8,4,32,1280]{3,2,1,0:T(8,128)(2,1)} %bitcast.27, bf16[80,2560]{1,0:T(8,128)(2,1)S(1)} %copy-done.6, bf16[80,2560]{1,0:T(8,128)(2,1)S(1)} %collective-permute-done.4.refs_2_.b1, bf16[80,2560]{1,0:T(8,128)(2,1)S(1)} %collective-permute-done.5.refs_3_.b2, ...), custom_call_target="tpu_custom_call" | custom-call | tf_op jit(solution)/shard_map/acts/pallas_call | solution.py:185
  115.3 3.2 %collective-permute-done.9.b = f32[640,512]{1,0:T(8,128)S(1)} collective-permute-done((f32[640,512]{1,0:T(8,128)}, f32[640,512]{1,0:T(8,128)S(1)}, u32[]{:S(2)}, u32[]{:S(2)}) %collective-permute-start.9) | collective-permute-done | bytes 1310752 | tf_op jit(solution)/shard_map/ppermute | solution.py:33
  121.1 1.5 live.1
  122.6 5.4 %all-to-all-start.1 = ((bf16[8,64,512]{2,1,0:T(8,128)(2,1)}), bf16[8,64,512]{2,1,0:T(8,128)(2,1)S(1)}, u32[]{:S(2)}, u32[]{:S(2)}) async-start(bf16[8,64,512]{2,1,0:T(8,128)(2,1)} %live.1), calls=%async_computation.1 | async-start | bytes 1048576 | tf_op jit(solution)/shard_map/all_to_all | solution.py:227
  128.0 3.0 %collective-permute-start.10 = (bf16[640,512]{1,0:T(8,128)(2,1)S(1)}, bf16[640,512]{1,0:T(8,128)(2,1)S(1)}, u32[]{:S(2)}, u32[]{:S(2)}) collective-permute-start(bf16[640,512]{1,0:T(8,128)(2,1)S(1)} %get-tuple-element.29.refs_0_), channel_id=1, source_target_pairs={{0,4},{4,0},{1,5},{5,1},{2,6},{6,2},{3,7},{7,3},{8,12},{12,8},{9,1... | collective-permute-start | bytes 1966088 | tf_op jit(solution)/shard_map/ppermute | solution.py:33
  131.0 15.0 %collective-permute-done.10.rb = bf16[640,512]{1,0:T(8,128)(2,1)S(1)} collective-permute-done((bf16[640,512]{1,0:T(8,128)(2,1)S(1)}, bf16[640,512]{1,0:T(8,128)(2,1)S(1)}, u32[]{:S(2)}, u32[]{:S(2)}) %collective-permute-start.10) | collective-permute-done | bytes 655392 | tf_op jit(solution)/shard_map/ppermute | solution.py:33
  147.9 3.8 %seq.1 = bf16[8,2,80,512]{3,2,1,0:T(8,128)(2,1)} custom-call(s32[1]{0:T(128)} %bitcast.xh_ref, s32[1]{0:T(128)} %bitcast.1.y_ref, f32[640,512]{1,0:T(8,128)} %copy-done.7, bf16[640,512]{1,0:T(8,128)(2,1)S(1)} %copy-done.11, bf16[512,512]{1,0:T(8,128)(2,1)S(1)} %bitcast.26), custom_call_target="tpu_custom_call" | custom-call | tf_op jit(solution)/shard_map/seq/pallas_call | solution.py:185
  151.7 24.0 %all_to_all.20.parts = bf16[8,2,80,512]{3,2,1,0:T(8,128)(2,1)S(1)} all-to-all(bf16[8,2,80,512]{3,2,1,0:T(8,128)(2,1)} %seq.1), channel_id=1, replica_groups=mesh['xl'=2,'core'=2,'z'=8,'xh'=2,'y'=4] {'xh','y'}, dimensions={0} | all-to-all | bytes 2621440 | tf_op jit(solution)/shard_map/all_to_all | solution.py:230
  177.8 5.3 %collective-permute-done.14 = bf16[2,80,1024]{2,1,0:T(8,128)(2,1)S(1)} collective-permute-done((bf16[2,80,1024]{2,1,0:T(8,128)(2,1)S(1)}, bf16[2,80,1024]{2,1,0:T(8,128)(2,1)S(1)}, u32[]{:S(2)}, u32[]{:S(2)}) %collective-permute-start.14) | collective-permute-done | bytes 327712 | tf_op jit(solution)/shard_map/ppermute | solution.py:33
  187.7 24.7 %all_to_all.21 = f32[64,8,8]{2,1,0:T(8,128)S(1)} all-to-all(f32[64,8,8]{2,1,0:T(8,128)S(1)} %broadcast_in_dim.22), channel_id=1, replica_groups=mesh['xl'=2,'core'=2,'z'=8,'xh'=2,'y'=4] {'z','xh','y'}, dimensions={0} | all-to-all | bytes 32768 | tf_op jit(solution)/shard_map/all_to_all | solution.py:37
  (72 shorter events, 21.7 us)
Async XLA Ops:
  6.5 169.8 %copy-start = (bf16[8,80,1024]{2,1,0:T(8,128)(2,1)S(1)}, bf16[8,80,1024]{2,1,0:T(8,128)(2,1)}, u32[]{:S(2)}) copy-start(bf16[8,80,1024]{2,1,0:T(8,128)(2,1)} %param.13) | copy-start | bytes 3932164
  6.5 97.3 %all-gather.3.cloned.1.call-start = ((), (), s32[]{:S(2)}) async-start(), calls=%async_computation.4 | async-start | bytes 2949120 | tf_op jit(solution)/shard_map/all_gather | solution.py:213
  7.4 8.0 %copy-start.9 = (bf16[80,5120]{1,0:T(8,128)(2,1)S(1)}, bf16[80,5120]{1,0:T(8,128)(2,1)}, u32[]{:S(2)}) copy-start(bf16[80,5120]{1,0:T(8,128)(2,1)} %b_ref.1) | copy-start | bytes 2457604
  7.4 8.0 %copy-start.12 = (bf16[32,5120]{1,0:T(8,128)(2,1)S(1)}, bf16[32,5120]{1,0:T(8,128)(2,1)}, u32[]{:S(2)}) copy-start(bf16[32,5120]{1,0:T(8,128)(2,1)} %a_ref.1) | copy-start | bytes 983044
  12.2 26.9 %collective-permute-start.2 = (bf16[216,1536]{1,0:T(8,128)(2,1)}, bf16[216,1536]{1,0:T(8,128)(2,1)S(1)}, u32[]{:S(2)}, u32[]{:S(2)}) collective-permute-start(bf16[216,1536]{1,0:T(8,128)(2,1)} %get-tuple-element.23), channel_id=1, source_target_pairs={{0,3},{1,0},{2,1},{3,2},{4,7},{5,4},{6,5},{7,6},{8,11},{9,8},{10,9... | collective-permute-start | bytes 1990664 | tf_op jit(solution)/shard_map/ppermute | solution.py:33
  12.9 26.1 %collective-permute-start.3 = (bf16[216,1536]{1,0:T(8,128)(2,1)}, bf16[216,1536]{1,0:T(8,128)(2,1)}, u32[]{:S(2)}, u32[]{:S(2)}) collective-permute-start(bf16[216,1536]{1,0:T(8,128)(2,1)} %get-tuple-element.24.here), channel_id=1, source_target_pairs={{0,1},{1,2},{2,3},{3,0},{4,5},{5,6},{6,7},{7,4},{8,9},{9,10},{10,1... | collective-permute-start | bytes 1990664 | tf_op jit(solution)/shard_map/ppermute | solution.py:33
  15.5 23.6 %copy-start.4 = (bf16[80,2560]{1,0:T(8,128)(2,1)}, bf16[80,2560]{1,0:T(8,128)(2,1)S(1)}, u32[]{:S(2)}) copy-start(bf16[80,2560]{1,0:T(8,128)(2,1)S(1)} %get-tuple-element.25.b0) | copy-start | bytes 1228804
  15.5 23.5 %collective-permute-start.5 = (bf16[80,2560]{1,0:T(8,128)(2,1)S(1)}, bf16[80,2560]{1,0:T(8,128)(2,1)S(1)}, u32[]{:S(2)}, u32[]{:S(2)}) collective-permute-start(bf16[80,2560]{1,0:T(8,128)(2,1)S(1)} %get-tuple-element.25.b0), channel_id=1, source_target_pairs={{0,3},{1,0},{2,1},{3,2},{4,7},{5,4},{6,5},{7,6},{8,11},{9,8},{10,9... | collective-permute-start | bytes 1228808 | tf_op jit(solution)/shard_map/ppermute | solution.py:33
  15.6 23.5 %collective-permute-start.4 = (bf16[80,2560]{1,0:T(8,128)(2,1)S(1)}, bf16[80,2560]{1,0:T(8,128)(2,1)S(1)}, u32[]{:S(2)}, u32[]{:S(2)}) collective-permute-start(bf16[80,2560]{1,0:T(8,128)(2,1)S(1)} %get-tuple-element.25.b0), channel_id=1, source_target_pairs={{0,1},{1,2},{2,3},{3,0},{4,5},{5,6},{6,7},{7,4},{8,9},{9,10},{10,1... | collective-permute-start | bytes 1228808 | tf_op jit(solution)/shard_map/ppermute | solution.py:33
  18.8 1.4 collective-permute-start
  20.2 7.8 %collective-permute-start.1 = (bf16[2,32,1280]{2,1,0:T(8,128)(2,1)S(1)}, bf16[2,32,1280]{2,1,0:T(8,128)(2,1)S(1)}, u32[]{:S(2)}, u32[]{:S(2)}) collective-permute-start(bf16[2,32,1280]{2,1,0:T(8,128)(2,1)S(1)} %get-tuple-element.22), channel_id=1, source_target_pairs={{0,4},{4,0},{1,5},{5,1},{2,6},{6,2},{3,7},{7,3},{8,12},{12,8},{9,1... | collective-permute-start | bytes 491528 | tf_op jit(solution)/shard_map/ppermute | solution.py:33
  40.9 6.5 %copy-start.15 = (bf16[216,512]{1,0:T(8,128)(2,1)S(1)}, bf16[216,512]{1,0:T(8,128)(2,1)}, u32[]{:S(2)}) copy-start(bf16[216,512]{1,0:T(8,128)(2,1)} %copy-done.14) | copy-start | bytes 663556
  40.9 20.8 %collective-permute-start.7 = (bf16[240,1280]{1,0:T(8,128)(2,1)S(1)}, bf16[240,1280]{1,0:T(8,128)(2,1)S(1)}, u32[]{:S(2)}, u32[]{:S(2)}) collective-permute-start(bf16[240,1280]{1,0:T(8,128)(2,1)S(1)} %join.1), channel_id=1, source_target_pairs={{0,4},{4,0},{1,5},{5,1},{2,6},{6,2},{3,7},{7,3},{8,12},{12,8},{9,1... | collective-permute-start | bytes 1843208 | tf_op jit(solution)/shard_map/ppermute | solution.py:33
  44.1 17.7 %collective-permute-start.11 = (bf16[216,1024]{1,0:T(8,128)(2,1)S(1)}, bf16[216,1024]{1,0:T(8,128)(2,1)S(1)}, u32[]{:S(2)}, u32[]{:S(2)}) collective-permute-start(bf16[216,1024]{1,0:T(8,128)(2,1)S(1)} %slice.9), channel_id=1, source_target_pairs={{0,3},{1,0},{2,1},{3,2},{4,7},{5,4},{6,5},{7,6},{8,11},{9,8},{10,9... | collective-permute-start | bytes 1327112 | tf_op jit(solution)/shard_map/ppermute | solution.py:33
  44.1 17.6 %collective-permute-start.6 = (bf16[80,2560]{1,0:T(8,128)(2,1)S(1)}, bf16[80,2560]{1,0:T(8,128)(2,1)S(1)}, u32[]{:S(2)}, u32[]{:S(2)}) collective-permute-start(bf16[80,2560]{1,0:T(8,128)(2,1)S(1)} %collective-permute-done.4.refs_2_.b1), channel_id=1, source_target_pairs={{0,1},{1,2},{2,3},{3,0},{4,5},{5,6},{6,7},{7,4},{8,9},{9,10},{10,1... | collective-permute-start | bytes 1228808 | tf_op jit(solution)/shard_map/ppermute | solution.py:33
  47.4 14.3 %collective-permute-start.12 = (bf16[216,512]{1,0:T(8,128)(2,1)S(1)}, bf16[216,512]{1,0:T(8,128)(2,1)S(1)}, u32[]{:S(2)}, u32[]{:S(2)}) collective-permute-start(bf16[216,512]{1,0:T(8,128)(2,1)S(1)} %copy-done.15), channel_id=1, source_target_pairs={{0,2},{1,3},{2,0},{3,1},{4,6},{5,7},{6,4},{7,5},{8,10},{9,11},{10,... | collective-permute-start | bytes 663560 | tf_op jit(solution)/shard_map/ppermute | solution.py:33
  65.7 55.4 %all-to-all-start = ((bf16[16,64,512]{2,1,0:T(8,128)(2,1)}), bf16[16,64,512]{2,1,0:T(8,128)(2,1)S(1)}, u32[]{:S(2)}, u32[]{:S(2)}) async-start(bf16[16,64,512]{2,1,0:T(8,128)(2,1)} %bitcast.4), calls=%async_computation | async-start | bytes 2097152 | tf_op jit(solution)/shard_map/all_to_all | solution.py:221
  75.3 9.0 %collective-permute-start.8 = (bf16[80,1280]{1,0:T(8,128)(2,1)S(1)}, bf16[80,1280]{1,0:T(8,128)(2,1)S(1)}, u32[]{:S(2)}, u32[]{:S(2)}) collective-permute-start(bf16[80,1280]{1,0:T(8,128)(2,1)S(1)} %slice.8), channel_id=1, source_target_pairs={{0,4},{4,0},{1,5},{5,1},{2,6},{6,2},{3,7},{7,3},{8,12},{12,8},{9,1... | collective-permute-start | bytes 614408 | tf_op jit(solution)/shard_map/ppermute | solution.py:33
  115.3 3.2 %collective-permute-start.9 = (f32[640,512]{1,0:T(8,128)}, f32[640,512]{1,0:T(8,128)S(1)}, u32[]{:S(2)}, u32[]{:S(2)}) collective-permute-start(f32[640,512]{1,0:T(8,128)} %get-tuple-element.27), channel_id=1, source_target_pairs={{0,64},{64,0},{1,65},{65,1},{2,66},{66,2},{3,67},{67,3},{4,68},{68... | collective-permute-start | bytes 3932168 | tf_op jit(solution)/shard_map/ppermute | solution.py:33
  122.6 24.2 %all-to-all-start.1 = ((bf16[8,64,512]{2,1,0:T(8,128)(2,1)}), bf16[8,64,512]{2,1,0:T(8,128)(2,1)S(1)}, u32[]{:S(2)}, u32[]{:S(2)}) async-start(bf16[8,64,512]{2,1,0:T(8,128)(2,1)} %live.1), calls=%async_computation.1 | async-start | bytes 1048576 | tf_op jit(solution)/shard_map/all_to_all | solution.py:227
  128.0 18.0 %collective-permute-start.10 = (bf16[640,512]{1,0:T(8,128)(2,1)S(1)}, bf16[640,512]{1,0:T(8,128)(2,1)S(1)}, u32[]{:S(2)}, u32[]{:S(2)}) collective-permute-start(bf16[640,512]{1,0:T(8,128)(2,1)S(1)} %get-tuple-element.29.refs_0_), channel_id=1, source_target_pairs={{0,4},{4,0},{1,5},{5,1},{2,6},{6,2},{3,7},{7,3},{8,12},{12,8},{9,1... | collective-permute-start | bytes 1966088 | tf_op jit(solution)/shard_map/ppermute | solution.py:33
  175.9 7.3 %collective-permute-start.14 = (bf16[2,80,1024]{2,1,0:T(8,128)(2,1)S(1)}, bf16[2,80,1024]{2,1,0:T(8,128)(2,1)S(1)}, u32[]{:S(2)}, u32[]{:S(2)}) collective-permute-start(bf16[2,80,1024]{2,1,0:T(8,128)(2,1)S(1)} %sums.1), channel_id=1, source_target_pairs={{0,128},{128,0},{1,129},{129,1},{2,130},{130,2},{3,131},{131,3},{4... | collective-permute-start | bytes 983048 | tf_op jit(solution)/shard_map/ppermute | solution.py:33
  176.4 8.3 %collective-permute-start.13 = (bf16[2,80,1024]{2,1,0:T(8,128)(2,1)S(1)}, bf16[2,80,1024]{2,1,0:T(8,128)(2,1)S(1)}, u32[]{:S(2)}, u32[]{:S(2)}) collective-permute-start(bf16[2,80,1024]{2,1,0:T(8,128)(2,1)S(1)} %sums.1), channel_id=1, source_target_pairs={{0,64},{64,0},{1,65},{65,1},{2,66},{66,2},{3,67},{67,3},{4,68},{68... | collective-permute-start | bytes 983048 | tf_op jit(solution)/shard_map/ppermute | solution.py:33
  183.2 2.9 %collective-permute-start.15 = (bf16[2,80,1024]{2,1,0:T(8,128)(2,1)S(1)}, bf16[2,80,1024]{2,1,0:T(8,128)(2,1)S(1)}, u32[]{:S(2)}, u32[]{:S(2)}) collective-permute-start(bf16[2,80,1024]{2,1,0:T(8,128)(2,1)S(1)} %collective-permute-done.14), channel_id=1, source_target_pairs={{0,64},{64,0},{1,65},{65,1},{2,66},{66,2},{3,67},{67,3},{4,68},{68... | collective-permute-start | bytes 983048 | tf_op jit(solution)/shard_map/ppermute | solution.py:33
  (11 other events, 17.3 us)
Sparse Core Ops, SparseCore 0:
  40.0 63.8 all-gather.2

commit v6 on v5

--- a/solution.py
+++ b/solution.py
@@ -59,27 +59,29 @@
 
 
 def pick_kernel(s_ref, *refs):
-    picked, g_ref, up, down, g0, g3 = refs[:8], *refs[8:]
-    for n, p in enumerate(picked):
+    picked, g_ref, first, up, down, g0, g3 = refs[:8], *refs[8:]
+    for n in range(4):
         cols = slice(n * 128, n * 128 + 128)
-        up[:, cols] = p[...]
-        down[:, cols] = p[...]
-    reorder(s_ref[8], g_ref, ((up, 1024, 1), (down, 1024, -1), (g3, 0, 2), (g0, 0, 0)))
+        first[:, cols] = picked[n][...]
+        up[:, cols] = picked[n + 4][...]
+        down[:, cols] = picked[n + 4][...]
+    reorder(s_ref[8], g_ref, ((up, 512, 1), (down, 512, -1), (g3, 0, 2), (g0, 0, 0)))
 
 
 def pick(block_ids, y, basis_out, out_grads):
     rows, tokens = out_grads.shape
     whole = lambda width: pl.BlockSpec((rows, width), lambda g, s: (0, 0))
+    widths = (512, 1024, 1024, 512, 512)
     spec = pltpu.PrefetchScalarGridSpec(
         num_scalar_prefetch=1,
         grid=(1,),
         in_specs=[pl.BlockSpec((rows, BLOCK), lambda g, s, n=n: (0, s[n])) for n in range(8)] + [whole(tokens)],
-        out_specs=[whole(1536), whole(1536), whole(512), whole(512)],
+        out_specs=[whole(w) for w in widths],
     )
     return pl.pallas_call(
         pick_kernel,
         grid_spec=spec,
-        out_shape=[arr(rows, 1536), arr(rows, 1536), arr(rows, 512), arr(rows, 512)],
+        out_shape=[arr(rows, w) for w in widths],
         compiler_params=WIDE,
         name="pick",
     )(jnp.concatenate([block_ids, y[None]]), *[basis_out] * 8, out_grads)
@@ -97,32 +99,30 @@
         b_own[:, cols] = b_ref[:, mine]
 
 
-def pair_kernel(own, sib, aside, near, far):
+def pair_kernel(own, sib, b_own, aside, near, far):
     part = near.shape[2]
     for n, a in enumerate((own, sib)):
         near[n] = a[:, :part]
-        far[n] = a[:, part:]
-
-
-def stack_kernel(near, far, *refs):
-    o_ref = refs[-1]
+        far[n * 32 : n * 32 + 32, :] = a[:, part:]
+    far[64:, :] = b_own[:, part:]
+
+
+def stack_kernel(near, far, b_own, *refs):
+    o_ref, b0 = refs[-2:]
     o_ref[:2] = near[...]
-    o_ref[2:] = far[...]
-
-
-def join_kernel(b0, b1, b2, aside, o_ref):
-    part = b0.shape[1] // 2
-    for n, b in enumerate((b0, b1, b2)):
-        o_ref[n * 80 : n * 80 + 80, :] = b[:, part:]
-
-
-def grads_kernel(here, up, down, c3, g0, g3, *refs):
-    o_ref = refs[-1]
-    for part in range(4):
-        ks = slice(part * 256, part * 256 + 256)
-        total = dot(here[:, ks], g0[...], 0, 0) + dot(c3[:, ks], g3[...], 0, 0)
-        total += dot(up[:, ks], up[:, 1024:], 0, 0) + dot(down[:, ks], down[:, 1024:], 0, 0)
-        o_ref[ks, :] = total.astype(BF)
+    o_ref[2] = far[:32, :]
+    o_ref[3] = far[32:64, :]
+    b0[:80, :] = b_own[:, : b0.shape[1]]
+    b0[80:, :] = far[64:, :]
+
+
+def grads_kernel(ca, mine, ca1, up, ca2, down, c3a, c3b, g0, g3, o_ref):
+    for n, (c0, c1, c2, c3) in enumerate(((ca, ca1, ca2, c3a), (mine, up, down, c3b))):
+        for place in (0, 256):
+            ks = slice(place, place + 256)
+            total = dot(c0[:, ks], g0[...], 0, 0) + dot(c3[:, ks], g3[...], 0, 0)
+            total += dot(c1[:, ks], up[:, 512:], 0, 0) + dot(c2[:, ks], down[:, 512:], 0, 0)
+            o_ref[n * 512 + place : n * 512 + place + 256, :] = total.astype(BF)
 
 
 def live_kernel(y_ref, lens, parts, *refs):
@@ -138,17 +138,14 @@
         o_ref[n] = total
 
 
-def acts_kernel(xh_ref, a_ref, b0, b1, b2, b3, far, far3, keep, send):
+def acts_kernel(xh_ref, a_ref, b0, b1, b2, b3, keep, send):
     part = a_ref.shape[3]
-    rows = [(n * 160, b, slice(0, 80), slice(0, part)) for n, b in enumerate((b0, b1, b2, b3))]
-    rows += [(n * 160 + 80, far, slice(n * 80, n * 80 + 80), slice(0, part)) for n in range(3)]
-    rows += [(560, far3, slice(0, 80), slice(0, part))]
     for xh in range(2):
         cols = slice(xh * 256, xh * 256 + 256)
         for core, out in enumerate((keep, send)):
             tokens = a_ref[:, (xh_ref[0] + xh) % 2 * 2 + core].reshape(256, part)
-            for place, b, r, c in rows:
-                out[place : place + 80, cols] = dot(b[r, c], tokens, 1, 1)
+            for n, b in enumerate((b0, b1, b2, b3)):
+                out[n * 160 : n * 160 + 160, cols] = dot(b[...], tokens, 1, 1)
 
 
 def add_kernel(a, b, keep, send):
@@ -187,7 +184,7 @@
         out_shape=out,
         in_specs=specs,
         out_specs=jax.tree.map(lambda _: VMEM, out),
-        compiler_params=WIDE if name in ("acts", "seq") else ROOM,
+        compiler_params=ROOM,
         name=name,
     )(*scalars, *args, *aside)
 
@@ -202,25 +199,28 @@
     part = features // 4
     place = [xh[None], core[None]]
     cuts = [arr(slots, 2 * part), arr(slots, 2 * part), arr(80, 2 * part)]
-    a_own, a_sib, b0 = call(cut_kernel, cuts, "cut", [activations, basis_in], place)
+    a_own, a_sib, b_own = call(cut_kernel, cuts, "cut", [activations, basis_in], place)
+    a_sib = shift(a_sib, core=1)
+
+    first, up, down, g0, g3 = pick(block_ids, y, basis_out, out_grads)
+    first_up, first_down = shift(first, y=1), shift(first, y=-1)
+    near, far = call(pair_kernel, [arr(2, slots, part), arr(144, part)], "pair", [a_own, a_sib, b_own], (), [g0])
+    far = shift(far, xh=1)
+    acts, b0 = call(
+        stack_kernel, [arr(4, slots, part), arr(160, part)], "stack", [near, far, b_own], (), [first_up, first_down]
+    )
+    acts = lax.all_gather(acts, "z", axis=0, tiled=False)
+    up_got, down_got, g3_got = shift(up, y=1), shift(down, y=-1), shift(g3, y=2)
+    c3a = shift(first_down, y=-1)
+    c3b = shift(down_got[:, :512], y=-1)
+
+    grads_in = [first, up, first_up, up_got, first_down, down_got, c3a, c3b, g0, g3_got]
+    partial = call(grads_kernel, arr(1024, 512), "grads", grads_in)
     b1, b2 = shift(b0, y=1), shift(b0, y=-1)
-    a_sib = shift(a_sib, core=1)
-    up, down, g0, g3 = pick(block_ids, y, basis_out, out_grads)
-    near, a_far = call(pair_kernel, [arr(2, slots, part)] * 2, "pair", [a_own, a_sib], (), [g0])
-    a_far = shift(a_far, xh=1)
-    up_got, down_got, g3_got = shift(up, y=1), shift(down, y=-1), shift(g3, y=2)
-    acts = call(stack_kernel, arr(4, slots, part), "stack", [near, a_far], (), [down_got, up_got, b1, b2])
-    acts = lax.all_gather(acts, "z", axis=0, tiled=False)
-    c3 = shift(down_got[:, :1024], y=-1)
     b3 = shift(b1, y=1)
-    far = shift(call(join_kernel, arr(240, part), "join", [b0, b1, b2], (), [g0]), xh=1)
-    far3 = shift(b3[:, part:], xh=1)
-
-    grads_in = [up, up_got, down_got, c3, g0, g3_got]
-    partial = call(grads_kernel, arr(1024, 512), "grads", grads_in, (), [far, b3])
     parts = lax.all_to_all(partial.reshape(16, 64, 512), ("xh", "z"), split_axis=0, concat_axis=0, tiled=True)
     wide = jax.ShapeDtypeStruct((640, 512), F32)
-    keep, send = call(acts_kernel, [wide, wide], "acts", [acts, b0, b1, b2, b3, far, far3], [xh[None]])
+    keep, send = call(acts_kernel, [wide, wide], "acts", [acts, b0, b1, b2, b3], [xh[None]])
     keep, send = call(add_kernel, [wide, arr(640, 512)], "add", [keep, shift(send, core=1)])
     rb = shift(send, xh=1)
     copies = call(live_kernel, arr(8, 64, 512), "live", [parts], [y[None], seq_lens], [send])

time: 221 us -> 191 us (0.86)
  waiting for transfers between devices: 78.7 us -> 61.6 us
  Pallas kernels: 24 us -> 14.1 us
  starting transfers between devices: 38.4 us -> 34.9 us
    all_gather x1, waiting for transfers between devices: 19.6 us -> 0.01 us  [per_device(): acts = lax.all_gather(acts, 'z', axis=0, tiled=False)]
    pallas_call x10 -> x9, Pallas kernels: 19.9 us -> 10.9 us  [call(): pl.pallas_call(kernel, out_shape=out, in_specs=specs, out_specs=jax.tree....]
    all_to_all x1, waiting for transfers between devices: 0.01 us -> 5.32 us  [per_device(): lax.all_to_all(partial.reshape(16, 64, 512), ('xh', 'z'), split_axis=0, c...]
    ppermute x16 -> x17, starting transfers between devices: 24.5 us -> 20.3 us  [shift(): return lax.ppermute(x, axes, pairs)]
    ppermute x16 -> x17, waiting for transfers between devices: 59.1 us -> 56.3 us  [shift(): return lax.ppermute(x, axes, pairs)]
    unnamed x32 -> x28, local copies, waits for them, and re-layouts: 8.04 us -> 10.8 us
    all_to_all x1, starting transfers between devices: 8.59 us -> 11 us  [per_device(): lax.all_to_all(partial.reshape(16, 64, 512), ('xh', 'z'), split_axis=0, c...]
  transfers between devices with their start and end apart: 19 -> 20, of which waited for: 9 -> 10; matrix products, arithmetic and copies ran while one was open for 2% -> 3% of each run, Pallas kernels for 6% -> 5%
where the time goes in v6:
time: 191 us
  waiting for transfers between devices  61.6 us (32%)
  blocking collectives  48.5 us (25%)
  starting transfers between devices  34.9 us (18%)
  Pallas kernels  14.1 us (7%)
  between operations  13.6 us (7%)
  local copies, waits for them, and re-layouts  10.9 us (6%)
  matrix products  5.87 us (3%)
    ppermute x17, waiting for transfers between devices, shift(): return lax.ppermute(x, axes, pairs)  56.3 us
    all_to_all x1, blocking collectives, spread(): lax.all_to_all(jnp.broadcast_to(x[None], (count,) + x.shape), axes, split...  25.2 us
    all_to_all x1, blocking collectives, per_device(): lax.all_to_all(tiles, ('xh', 'y'), split_axis=0, concat_axis=0, tiled=True)  23.3 us
    ppermute x17, starting transfers between devices, shift(): return lax.ppermute(x, axes, pairs)  20.3 us
    all_to_all x1, starting transfers between devices, per_device(): lax.all_to_all(partial.reshape(16, 64, 512), ('xh', 'z'), split_axis=0, c...  11 us
    pallas_call x9, Pallas kernels, call(): pl.pallas_call(kernel, out_shape=out, in_specs=specs, out_specs=jax.tree....  10.9 us
    unnamed x28, local copies, waits for them, and re-layouts  10.8 us
    dot_general x4, matrix products, score(): jnp.einsum('sik,qik->sq', grads, query_grads, preferred_element_type=F32)  5.87 us
  transfers between devices with their start and end apart: 20, of which 10 were waited for; matrix products, arithmetic and copies ran while one was open for 3% of the time, Pallas kernels for 5%

profile of v6, /device:TPU:24, one launch (start us, length us, event | category | flops | bytes accessed | tf_op | source)
XLA Modules:
  0.0 190.8 jit_solution(3165348539238254699)
XLA Ops:
  10.2 3.1 %pick.1 = (bf16[216,512]{1,0:T(8,128)(2,1)S(1)}, bf16[216,1024]{1,0:T(8,128)(2,1)S(1)}, bf16[216,1024]{1,0:T(8,128)(2,1)S(1)}, bf16[216,512]{1,0:T(8,128)(2,1)S(1)}, bf16[216,512]{1,0:T(8,128)(2,1)S(1)}) custom-call(s32[9]{0:T(128)S(1)} %pad_add_fusion.s_ref, bf16[216,13824]{1,0:T(8,128)(2,1)} %refs_7_.1, bf16[216,13824]{1,0:T(8,128)(2,1)} %refs_7_.1, ...), custom_call_target="tpu_custom_call" | custom-call | tf_op jit(solution)/shard_map/pick/pallas_call | solution.py:81
  13.4 3.1 %collective-permute-start.1 = (bf16[144,1280]{1,0:T(8,128)(2,1)S(1)}, bf16[144,1280]{1,0:T(8,128)(2,1)S(1)}, u32[]{:S(2)}, u32[]{:S(2)}) collective-permute-start(bf16[144,1280]{1,0:T(8,128)(2,1)S(1)} %get-tuple-element.26), channel_id=1, source_target_pairs={{0,4},{4,0},{1,5},{5,1},{2,6},{6,2},{3,7},{7,3},{8,12},{12,8},{9,1... | collective-permute-start | bytes 1105928 | tf_op jit(solution)/shard_map/ppermute | solution.py:33
  17.3 2.5 %collective-permute-start.2 = (bf16[216,512]{1,0:T(8,128)(2,1)S(1)}, bf16[216,512]{1,0:T(8,128)(2,1)S(1)}, u32[]{:S(2)}, u32[]{:S(2)}) collective-permute-start(bf16[216,512]{1,0:T(8,128)(2,1)S(1)} %get-tuple-element.27.ca), channel_id=1, source_target_pairs={{0,1},{1,2},{2,3},{3,0},{4,5},{5,6},{6,7},{7,4},{8,9},{9,10},{10,1... | collective-permute-start | bytes 663560 | tf_op jit(solution)/shard_map/ppermute | solution.py:33
  19.8 5.5 %collective-permute-done.3.refs_1_.ca2 = bf16[216,512]{1,0:T(8,128)(2,1)S(1)} collective-permute-done((bf16[216,512]{1,0:T(8,128)(2,1)S(1)}, bf16[216,512]{1,0:T(8,128)(2,1)S(1)}, u32[]{:S(2)}, u32[]{:S(2)}) %collective-permute-start.3) | collective-permute-done | bytes 221216 | tf_op jit(solution)/shard_map/ppermute | solution.py:33
  27.7 2.5 %collective-permute-start.9 = (bf16[216,1024]{1,0:T(8,128)(2,1)S(1)}, bf16[216,1024]{1,0:T(8,128)(2,1)S(1)}, u32[]{:S(2)}, u32[]{:S(2)}) collective-permute-start(bf16[216,1024]{1,0:T(8,128)(2,1)S(1)} %get-tuple-element.34.mine), channel_id=1, source_target_pairs={{0,1},{1,2},{2,3},{3,0},{4,5},{5,6},{6,7},{7,4},{8,9},{9,10},{10,1... | collective-permute-start | bytes 1327112 | tf_op jit(solution)/shard_map/ppermute | solution.py:33
  32.1 13.6 %collective-permute-done.10.down = bf16[216,1024]{1,0:T(8,128)(2,1)S(1)} collective-permute-done((bf16[216,1024]{1,0:T(8,128)(2,1)}, bf16[216,1024]{1,0:T(8,128)(2,1)S(1)}, u32[]{:S(2)}, u32[]{:S(2)}) %collective-permute-start.10) | collective-permute-done | bytes 442400 | tf_op jit(solution)/shard_map/ppermute | solution.py:33
  45.8 3.2 %collective-permute-start.4 = (bf16[160,1280]{1,0:T(8,128)(2,1)S(1)}, bf16[160,1280]{1,0:T(8,128)(2,1)}, u32[]{:S(2)}, u32[]{:S(2)}) collective-permute-start(bf16[160,1280]{1,0:T(8,128)(2,1)S(1)} %get-tuple-element.29.b0), channel_id=1, source_target_pairs={{0,1},{1,2},{2,3},{3,0},{4,5},{5,6},{6,7},{7,4},{8,9},{9,10},{10,1... | collective-permute-start | bytes 1228808 | tf_op jit(solution)/shard_map/ppermute | solution.py:33
  49.0 1.9 %collective-permute-done.11.c3a = bf16[216,512]{1,0:T(8,128)(2,1)S(1)} collective-permute-done((bf16[216,512]{1,0:T(8,128)(2,1)S(1)}, bf16[216,512]{1,0:T(8,128)(2,1)S(1)}, u32[]{:S(2)}, u32[]{:S(2)}) %collective-permute-start.11) | collective-permute-done | bytes 221216 | tf_op jit(solution)/shard_map/ppermute | solution.py:33
  50.9 3.4 %collective-permute-done.12.c3b = bf16[216,512]{1,0:T(8,128)(2,1)S(1)} collective-permute-done((bf16[216,512]{1,0:T(8,128)(2,1)S(1)}, bf16[216,512]{1,0:T(8,128)(2,1)S(1)}, u32[]{:S(2)}, u32[]{:S(2)}) %collective-permute-start.12) | collective-permute-done | bytes 221216 | tf_op jit(solution)/shard_map/ppermute | solution.py:33
  54.4 2.3 %grads.1 = bf16[1024,512]{1,0:T(8,128)(2,1)} custom-call(bf16[216,512]{1,0:T(8,128)(2,1)S(1)} %get-tuple-element.27.ca, bf16[216,1024]{1,0:T(8,128)(2,1)S(1)} %get-tuple-element.34.mine, bf16[216,512]{1,0:T(8,128)(2,1)S(1)} %collective-permute-done.2.refs_0_.ca1, bf16[216,1024]{1,0:T(8,128)(2,1)S(1)} %collective-permute-done.9.up, ...), custom_call_target="tpu_custom_call" | custom-call | tf_op jit(solution)/shard_map/grads/pallas_call | solution.py:182
  56.7 11.0 %all-to-all-start = ((bf16[16,64,512]{2,1,0:T(8,128)(2,1)}), bf16[16,64,512]{2,1,0:T(8,128)(2,1)S(1)}, u32[]{:S(2)}, u32[]{:S(2)}) async-start(bf16[16,64,512]{2,1,0:T(8,128)(2,1)} %bitcast.4), calls=%async_computation | async-start | bytes 2097152 | tf_op jit(solution)/shard_map/all_to_all | solution.py:221
  67.8 3.2 %collective-permute-start.6 = (bf16[160,1280]{1,0:T(8,128)(2,1)}, bf16[160,1280]{1,0:T(8,128)(2,1)S(1)}, u32[]{:S(2)}, u32[]{:S(2)}) collective-permute-start(bf16[160,1280]{1,0:T(8,128)(2,1)} %collective-permute-done.4.b1), channel_id=1, source_target_pairs={{0,1},{1,2},{2,3},{3,0},{4,5},{5,6},{6,7},{7,4},{8,9},{9,10},{10,1... | collective-permute-start | bytes 1228808 | tf_op jit(solution)/shard_map/ppermute | solution.py:33
  71.0 7.8 %collective-permute-done.5.b2 = bf16[160,1280]{1,0:T(8,128)(2,1)S(1)} collective-permute-done((bf16[160,1280]{1,0:T(8,128)(2,1)S(1)}, bf16[160,1280]{1,0:T(8,128)(2,1)S(1)}, u32[]{:S(2)}, u32[]{:S(2)}) %collective-permute-start.5) | collective-permute-done | bytes 409632 | tf_op jit(solution)/shard_map/ppermute | solution.py:33
  79.6 1.7 copy-done.1
  82.4 4.6 %acts.1 = (f32[640,512]{1,0:T(8,128)S(1)}, f32[640,512]{1,0:T(8,128)S(1)}) custom-call(s32[1]{0:T(128)} %bitcast.xh_ref, bf16[8,4,32,1280]{3,2,1,0:T(8,128)(2,1)S(1)} %bitcast.26, bf16[160,1280]{1,0:T(8,128)(2,1)S(1)} %get-tuple-element.29.b0, bf16[160,1280]{1,0:T(8,128)(2,1)} %collective-permute-done.4.b1, bf16[160,1280]{1,0:T(8,128)(2,1)S(1)} %collective-permute-done.5.b2, ...), custom_call_target="tpu_custom_call" | custom-call | tf_op jit(solution)/shard_map/acts/pallas_call | solution.py:182
  87.0 3.0 %collective-permute-done.7.b = f32[640,512]{1,0:T(8,128)S(1)} collective-permute-done((f32[640,512]{1,0:T(8,128)S(1)}, f32[640,512]{1,0:T(8,128)S(1)}, u32[]{:S(2)}, u32[]{:S(2)}) %collective-permute-start.7) | collective-permute-done | bytes 1310752 | tf_op jit(solution)/shard_map/ppermute | solution.py:33
  91.3 5.3 %all-to-all-done.parts = bf16[16,64,512]{2,1,0:T(8,128)(2,1)S(1)} async-done(((bf16[16,64,512]{2,1,0:T(8,128)(2,1)}), bf16[16,64,512]{2,1,0:T(8,128)(2,1)S(1)}, u32[]{:S(2)}, u32[]{:S(2)}) %all-to-all-start) | async-done | bytes 1048608 | tf_op jit(solution)/shard_map/all_to_all | solution.py:221
  96.7 1.5 live.1
  98.2 3.5 %all-to-all-start.1 = ((bf16[8,64,512]{2,1,0:T(8,128)(2,1)}), bf16[8,64,512]{2,1,0:T(8,128)(2,1)S(1)}, u32[]{:S(2)}, u32[]{:S(2)}) async-start(bf16[8,64,512]{2,1,0:T(8,128)(2,1)} %live.1), calls=%async_computation.1 | async-start | bytes 1048576 | tf_op jit(solution)/shard_map/all_to_all | solution.py:227
  102.6 15.6 %collective-permute-done.8.rb = bf16[640,512]{1,0:T(8,128)(2,1)S(1)} collective-permute-done((bf16[640,512]{1,0:T(8,128)(2,1)S(1)}, bf16[640,512]{1,0:T(8,128)(2,1)S(1)}, u32[]{:S(2)}, u32[]{:S(2)}) %collective-permute-start.8) | collective-permute-done | bytes 655392 | tf_op jit(solution)/shard_map/ppermute | solution.py:33
  122.8 23.3 %all_to_all.20.parts = bf16[8,2,80,512]{3,2,1,0:T(8,128)(2,1)S(1)} all-to-all(bf16[8,2,80,512]{3,2,1,0:T(8,128)(2,1)S(1)} %seq.1), channel_id=1, replica_groups=mesh['xl'=2,'core'=2,'z'=8,'xh'=2,'y'=4] {'xh','y'}, dimensions={0} | all-to-all | bytes 2621440 | tf_op jit(solution)/shard_map/all_to_all | solution.py:230
  149.0 4.7 %collective-permute-done.15 = bf16[2,80,1024]{2,1,0:T(8,128)(2,1)S(1)} collective-permute-done((bf16[2,80,1024]{2,1,0:T(8,128)(2,1)S(1)}, bf16[2,80,1024]{2,1,0:T(8,128)(2,1)S(1)}, u32[]{:S(2)}, u32[]{:S(2)}) %collective-permute-start.15) | collective-permute-done | bytes 327712 | tf_op jit(solution)/shard_map/ppermute | solution.py:33
  155.1 1.5 convolution_bitcast_fusion.2
  158.1 25.2 %all_to_all.21 = f32[64,8,8]{2,1,0:T(8,128)S(1)} all-to-all(f32[64,8,8]{2,1,0:T(8,128)S(1)} %broadcast_in_dim.22), channel_id=1, replica_groups=mesh['xl'=2,'core'=2,'z'=8,'xh'=2,'y'=4] {'z','xh','y'}, dimensions={0} | all-to-all | bytes 32768 | tf_op jit(solution)/shard_map/all_to_all | solution.py:37
  (68 shorter events, 24.0 us)
Async XLA Ops:
  6.5 141.0 %copy-start = (bf16[8,80,1024]{2,1,0:T(8,128)(2,1)S(1)}, bf16[8,80,1024]{2,1,0:T(8,128)(2,1)}, u32[]{:S(2)}) copy-start(bf16[8,80,1024]{2,1,0:T(8,128)(2,1)} %param.13) | copy-start | bytes 3932164
  6.5 73.1 %all-gather.3.cloned.1.call-start = ((), (), s32[]{:S(2)}) async-start(), calls=%async_computation.4 | async-start | bytes 2949120 | tf_op jit(solution)/shard_map/all_gather | solution.py:212
  9.5 3.9 %collective-permute-start = (bf16[32,2560]{1,0:T(8,128)(2,1)}, bf16[32,2560]{1,0:T(8,128)(2,1)S(1)}, u32[]{:S(2)}, u32[]{:S(2)}) collective-permute-start(bf16[32,2560]{1,0:T(8,128)(2,1)} %get-tuple-element.22), channel_id=1, source_target_pairs={{0,64},{64,0},{1,65},{65,1},{2,66},{66,2},{3,67},{67,3},{4,68},{68... | collective-permute-start | bytes 491528 | tf_op jit(solution)/shard_map/ppermute | solution.py:33
  13.4 3.2 %copy-start.12 = (bf16[216,1024]{1,0:T(8,128)(2,1)}, bf16[216,1024]{1,0:T(8,128)(2,1)S(1)}, u32[]{:S(2)}) copy-start(bf16[216,1024]{1,0:T(8,128)(2,1)S(1)} %get-tuple-element.35) | copy-start | bytes 1327108
  13.4 12.7 %copy-start.13 = (bf16[216,512]{1,0:T(8,128)(2,1)}, bf16[216,512]{1,0:T(8,128)(2,1)S(1)}, u32[]{:S(2)}) copy-start(bf16[216,512]{1,0:T(8,128)(2,1)S(1)} %get-tuple-element.36) | copy-start | bytes 663556
  13.4 12.6 %collective-permute-start.1 = (bf16[144,1280]{1,0:T(8,128)(2,1)S(1)}, bf16[144,1280]{1,0:T(8,128)(2,1)S(1)}, u32[]{:S(2)}, u32[]{:S(2)}) collective-permute-start(bf16[144,1280]{1,0:T(8,128)(2,1)S(1)} %get-tuple-element.26), channel_id=1, source_target_pairs={{0,4},{4,0},{1,5},{5,1},{2,6},{6,2},{3,7},{7,3},{8,12},{12,8},{9,1... | collective-permute-start | bytes 1105928 | tf_op jit(solution)/shard_map/ppermute | solution.py:33
  16.5 8.8 %collective-permute-start.3 = (bf16[216,512]{1,0:T(8,128)(2,1)S(1)}, bf16[216,512]{1,0:T(8,128)(2,1)S(1)}, u32[]{:S(2)}, u32[]{:S(2)}) collective-permute-start(bf16[216,512]{1,0:T(8,128)(2,1)S(1)} %get-tuple-element.27.ca), channel_id=1, source_target_pairs={{0,3},{1,0},{2,1},{3,2},{4,7},{5,4},{6,5},{7,6},{8,11},{9,8},{10,9... | collective-permute-start | bytes 663560 | tf_op jit(solution)/shard_map/ppermute | solution.py:33
  17.3 8.0 %collective-permute-start.2 = (bf16[216,512]{1,0:T(8,128)(2,1)S(1)}, bf16[216,512]{1,0:T(8,128)(2,1)S(1)}, u32[]{:S(2)}, u32[]{:S(2)}) collective-permute-start(bf16[216,512]{1,0:T(8,128)(2,1)S(1)} %get-tuple-element.27.ca), channel_id=1, source_target_pairs={{0,1},{1,2},{2,3},{3,0},{4,5},{5,6},{6,7},{7,4},{8,9},{9,10},{10,1... | collective-permute-start | bytes 663560 | tf_op jit(solution)/shard_map/ppermute | solution.py:33
  26.9 18.8 %collective-permute-start.10 = (bf16[216,1024]{1,0:T(8,128)(2,1)}, bf16[216,1024]{1,0:T(8,128)(2,1)S(1)}, u32[]{:S(2)}, u32[]{:S(2)}) collective-permute-start(bf16[216,1024]{1,0:T(8,128)(2,1)} %copy-done.12), channel_id=1, source_target_pairs={{0,3},{1,0},{2,1},{3,2},{4,7},{5,4},{6,5},{7,6},{8,11},{9,8},{10,9... | collective-permute-start | bytes 1327112 | tf_op jit(solution)/shard_map/ppermute | solution.py:33
  27.7 23.3 %collective-permute-start.9 = (bf16[216,1024]{1,0:T(8,128)(2,1)S(1)}, bf16[216,1024]{1,0:T(8,128)(2,1)S(1)}, u32[]{:S(2)}, u32[]{:S(2)}) collective-permute-start(bf16[216,1024]{1,0:T(8,128)(2,1)S(1)} %get-tuple-element.34.mine), channel_id=1, source_target_pairs={{0,1},{1,2},{2,3},{3,0},{4,5},{5,6},{6,7},{7,4},{8,9},{9,10},{10,1... | collective-permute-start | bytes 1327112 | tf_op jit(solution)/shard_map/ppermute | solution.py:33
  30.2 18.8 %collective-permute-start.13 = (bf16[216,512]{1,0:T(8,128)(2,1)}, bf16[216,512]{1,0:T(8,128)(2,1)S(1)}, u32[]{:S(2)}, u32[]{:S(2)}) collective-permute-start(bf16[216,512]{1,0:T(8,128)(2,1)} %copy-done.13), channel_id=1, source_target_pairs={{0,2},{1,3},{2,0},{3,1},{4,6},{5,7},{6,4},{7,5},{8,10},{9,11},{10,... | collective-permute-start | bytes 663560 | tf_op jit(solution)/shard_map/ppermute | solution.py:33
  30.6 20.3 %collective-permute-start.11 = (bf16[216,512]{1,0:T(8,128)(2,1)S(1)}, bf16[216,512]{1,0:T(8,128)(2,1)S(1)}, u32[]{:S(2)}, u32[]{:S(2)}) collective-permute-start(bf16[216,512]{1,0:T(8,128)(2,1)S(1)} %collective-permute-done.3.refs_1_.ca2), channel_id=1, source_target_pairs={{0,3},{1,0},{2,1},{3,2},{4,7},{5,4},{6,5},{7,6},{8,11},{9,8},{10,9... | collective-permute-start | bytes 663560 | tf_op jit(solution)/shard_map/ppermute | solution.py:33
  45.7 8.7 %collective-permute-start.12 = (bf16[216,512]{1,0:T(8,128)(2,1)S(1)}, bf16[216,512]{1,0:T(8,128)(2,1)S(1)}, u32[]{:S(2)}, u32[]{:S(2)}) collective-permute-start(bf16[216,512]{1,0:T(8,128)(2,1)S(1)} %slice.4), channel_id=1, source_target_pairs={{0,3},{1,0},{2,1},{3,2},{4,7},{5,4},{6,5},{7,6},{8,11},{9,8},{10,9... | collective-permute-start | bytes 663560 | tf_op jit(solution)/shard_map/ppermute | solution.py:33
  45.8 22.0 %collective-permute-start.4 = (bf16[160,1280]{1,0:T(8,128)(2,1)S(1)}, bf16[160,1280]{1,0:T(8,128)(2,1)}, u32[]{:S(2)}, u32[]{:S(2)}) collective-permute-start(bf16[160,1280]{1,0:T(8,128)(2,1)S(1)} %get-tuple-element.29.b0), channel_id=1, source_target_pairs={{0,1},{1,2},{2,3},{3,0},{4,5},{5,6},{6,7},{7,4},{8,9},{9,10},{10,1... | collective-permute-start | bytes 1228808 | tf_op jit(solution)/shard_map/ppermute | solution.py:33
  56.7 40.0 %all-to-all-start = ((bf16[16,64,512]{2,1,0:T(8,128)(2,1)}), bf16[16,64,512]{2,1,0:T(8,128)(2,1)S(1)}, u32[]{:S(2)}, u32[]{:S(2)}) async-start(bf16[16,64,512]{2,1,0:T(8,128)(2,1)} %bitcast.4), calls=%async_computation | async-start | bytes 2097152 | tf_op jit(solution)/shard_map/all_to_all | solution.py:221
  67.7 11.1 %collective-permute-start.5 = (bf16[160,1280]{1,0:T(8,128)(2,1)S(1)}, bf16[160,1280]{1,0:T(8,128)(2,1)S(1)}, u32[]{:S(2)}, u32[]{:S(2)}) collective-permute-start(bf16[160,1280]{1,0:T(8,128)(2,1)S(1)} %get-tuple-element.29.b0), channel_id=1, source_target_pairs={{0,3},{1,0},{2,1},{3,2},{4,7},{5,4},{6,5},{7,6},{8,11},{9,8},{10,9... | collective-permute-start | bytes 1228808 | tf_op jit(solution)/shard_map/ppermute | solution.py:33
  67.8 11.0 %collective-permute-start.6 = (bf16[160,1280]{1,0:T(8,128)(2,1)}, bf16[160,1280]{1,0:T(8,128)(2,1)S(1)}, u32[]{:S(2)}, u32[]{:S(2)}) collective-permute-start(bf16[160,1280]{1,0:T(8,128)(2,1)} %collective-permute-done.4.b1), channel_id=1, source_target_pairs={{0,1},{1,2},{2,3},{3,0},{4,5},{5,6},{6,7},{7,4},{8,9},{9,10},{10,1... | collective-permute-start | bytes 1228808 | tf_op jit(solution)/shard_map/ppermute | solution.py:33
  86.9 3.1 %collective-permute-start.7 = (f32[640,512]{1,0:T(8,128)S(1)}, f32[640,512]{1,0:T(8,128)S(1)}, u32[]{:S(2)}, u32[]{:S(2)}) collective-permute-start(f32[640,512]{1,0:T(8,128)S(1)} %get-tuple-element.31), channel_id=1, source_target_pairs={{0,64},{64,0},{1,65},{65,1},{2,66},{66,2},{3,67},{67,3},{4,68},{68... | collective-permute-start | bytes 3932168 | tf_op jit(solution)/shard_map/ppermute | solution.py:33
  90.1 6.6 %copy-start.11 = (s32[2]{0:T(128)S(1)}, s32[2]{0:T(128)}, u32[]{:S(2)}) copy-start(s32[2]{0:T(128)} %lens.1) | copy-start | bytes 28
  98.2 20.8 %all-to-all-start.1 = ((bf16[8,64,512]{2,1,0:T(8,128)(2,1)}), bf16[8,64,512]{2,1,0:T(8,128)(2,1)S(1)}, u32[]{:S(2)}, u32[]{:S(2)}) async-start(bf16[8,64,512]{2,1,0:T(8,128)(2,1)} %live.1), calls=%async_computation.1 | async-start | bytes 1048576 | tf_op jit(solution)/shard_map/all_to_all | solution.py:227
  101.7 16.5 %collective-permute-start.8 = (bf16[640,512]{1,0:T(8,128)(2,1)S(1)}, bf16[640,512]{1,0:T(8,128)(2,1)S(1)}, u32[]{:S(2)}, u32[]{:S(2)}) collective-permute-start(bf16[640,512]{1,0:T(8,128)(2,1)S(1)} %get-tuple-element.33.refs_0_), channel_id=1, source_target_pairs={{0,4},{4,0},{1,5},{5,1},{2,6},{6,2},{3,7},{7,3},{8,12},{12,8},{9,1... | collective-permute-start | bytes 1966088 | tf_op jit(solution)/shard_map/ppermute | solution.py:33
  146.3 7.3 %collective-permute-start.15 = (bf16[2,80,1024]{2,1,0:T(8,128)(2,1)S(1)}, bf16[2,80,1024]{2,1,0:T(8,128)(2,1)S(1)}, u32[]{:S(2)}, u32[]{:S(2)}) collective-permute-start(bf16[2,80,1024]{2,1,0:T(8,128)(2,1)S(1)} %sums.1), channel_id=1, source_target_pairs={{0,128},{128,0},{1,129},{129,1},{2,130},{130,2},{3,131},{131,3},{4... | collective-permute-start | bytes 983048 | tf_op jit(solution)/shard_map/ppermute | solution.py:33
  147.5 7.6 %collective-permute-start.14 = (bf16[2,80,1024]{2,1,0:T(8,128)(2,1)S(1)}, bf16[2,80,1024]{2,1,0:T(8,128)(2,1)S(1)}, u32[]{:S(2)}, u32[]{:S(2)}) collective-permute-start(bf16[2,80,1024]{2,1,0:T(8,128)(2,1)S(1)} %sums.1), channel_id=1, source_target_pairs={{0,64},{64,0},{1,65},{65,1},{2,66},{66,2},{3,67},{67,3},{4,68},{68... | collective-permute-start | bytes 983048 | tf_op jit(solution)/shard_map/ppermute | solution.py:33
  153.6 2.9 %collective-permute-start.16 = (bf16[2,80,1024]{2,1,0:T(8,128)(2,1)S(1)}, bf16[2,80,1024]{2,1,0:T(8,128)(2,1)S(1)}, u32[]{:S(2)}, u32[]{:S(2)}) collective-permute-start(bf16[2,80,1024]{2,1,0:T(8,128)(2,1)S(1)} %collective-permute-done.15), channel_id=1, source_target_pairs={{0,64},{64,0},{1,65},{65,1},{2,66},{66,2},{3,67},{67,3},{4,68},{68... | collective-permute-start | bytes 983048 | tf_op jit(solution)/shard_map/ppermute | solution.py:33
  (10 other events, 10.8 us)
Sparse Core Ops, SparseCore 0:
  27.0 50.4 all-gather.2

commit v7 on v5

--- a/solution.py
+++ b/solution.py
@@ -59,33 +59,32 @@
 
 
 def pick_kernel(s_ref, *refs):
-    picked, g_ref, up, down, g0, g3 = refs[:8], *refs[8:]
+    picked, g_ref, chosen, g0, g1, g2, g3 = refs[:8], *refs[8:]
     for n, p in enumerate(picked):
-        cols = slice(n * 128, n * 128 + 128)
-        up[:, cols] = p[...]
-        down[:, cols] = p[...]
-    reorder(s_ref[8], g_ref, ((up, 1024, 1), (down, 1024, -1), (g3, 0, 2), (g0, 0, 0)))
+        chosen[:, n * 128 : n * 128 + 128] = p[...]
+    reorder(s_ref[8], g_ref, ((g1, 0, 1), (g2, 0, -1), (g3, 0, 2), (g0, 0, 0)))
 
 
 def pick(block_ids, y, basis_out, out_grads):
     rows, tokens = out_grads.shape
     whole = lambda width: pl.BlockSpec((rows, width), lambda g, s: (0, 0))
+    widths = (1024, 512, 512, 512, 512)
     spec = pltpu.PrefetchScalarGridSpec(
         num_scalar_prefetch=1,
         grid=(1,),
         in_specs=[pl.BlockSpec((rows, BLOCK), lambda g, s, n=n: (0, s[n])) for n in range(8)] + [whole(tokens)],
-        out_specs=[whole(1536), whole(1536), whole(512), whole(512)],
+        out_specs=[whole(w) for w in widths],
     )
     return pl.pallas_call(
         pick_kernel,
         grid_spec=spec,
-        out_shape=[arr(rows, 1536), arr(rows, 1536), arr(rows, 512), arr(rows, 512)],
+        out_shape=[arr(rows, w) for w in widths],
         compiler_params=WIDE,
         name="pick",
     )(jnp.concatenate([block_ids, y[None]]), *[basis_out] * 8, out_grads)
 
 
-def cut_kernel(xh_ref, core_ref, a_ref, b_ref, a_own, a_sib, b_own):
+def cut_kernel(xh_ref, core_ref, a_ref, b_ref, aside, a_own, a_sib, b_own):
     part = a_ref.shape[1] // 4
     for near in range(2):
         x = (xh_ref[0] + near) % 2
@@ -97,11 +96,12 @@
         b_own[:, cols] = b_ref[:, mine]
 
 
-def pair_kernel(own, sib, aside, near, far):
+def pair_kernel(own, sib, b_own, aside, near, far, b_far):
     part = near.shape[2]
     for n, a in enumerate((own, sib)):
         near[n] = a[:, :part]
         far[n] = a[:, part:]
+    b_far[...] = b_own[:, part:]
 
 
 def stack_kernel(near, far, *refs):
@@ -110,18 +110,11 @@
     o_ref[2:] = far[...]
 
 
-def join_kernel(b0, b1, b2, aside, o_ref):
-    part = b0.shape[1] // 2
-    for n, b in enumerate((b0, b1, b2)):
-        o_ref[n * 80 : n * 80 + 80, :] = b[:, part:]
-
-
-def grads_kernel(here, up, down, c3, g0, g3, *refs):
-    o_ref = refs[-1]
+def grads_kernel(c0, c1, c2, c3, g0, g1, g2, g3, aside, o_ref):
     for part in range(4):
         ks = slice(part * 256, part * 256 + 256)
-        total = dot(here[:, ks], g0[...], 0, 0) + dot(c3[:, ks], g3[...], 0, 0)
-        total += dot(up[:, ks], up[:, 1024:], 0, 0) + dot(down[:, ks], down[:, 1024:], 0, 0)
+        total = dot(c0[:, ks], g0[...], 0, 0) + dot(c1[:, ks], g1[...], 0, 0)
+        total += dot(c2[:, ks], g2[...], 0, 0) + dot(c3[:, ks], g3[...], 0, 0)
         o_ref[ks, :] = total.astype(BF)
 
 
@@ -138,17 +131,18 @@
         o_ref[n] = total
 
 
-def acts_kernel(xh_ref, a_ref, b0, b1, b2, b3, far, far3, keep, send):
+def acts_kernel(xh_ref, a_ref, own, own_far, b1, b2, b3a, b3b, keep, send):
     part = a_ref.shape[3]
-    rows = [(n * 160, b, slice(0, 80), slice(0, part)) for n, b in enumerate((b0, b1, b2, b3))]
-    rows += [(n * 160 + 80, far, slice(n * 80, n * 80 + 80), slice(0, part)) for n in range(3)]
-    rows += [(560, far3, slice(0, 80), slice(0, part))]
+    rows = [(0, own, slice(0, part)), (80, own_far, slice(0, part))]
+    rows += [(160, b1, slice(0, part)), (320, b2, slice(0, part))]
     for xh in range(2):
         cols = slice(xh * 256, xh * 256 + 256)
         for core, out in enumerate((keep, send)):
             tokens = a_ref[:, (xh_ref[0] + xh) % 2 * 2 + core].reshape(256, part)
-            for place, b, r, c in rows:
-                out[place : place + 80, cols] = dot(b[r, c], tokens, 1, 1)
+            for place, b, c in rows:
+                out[place : place + b.shape[0], cols] = dot(b[:, c], tokens, 1, 1)
+            out[480:560, cols] = dot(b3a[...], tokens, 1, 1)
+            out[560:, cols] = dot(b3b[...], tokens, 1, 1)
 
 
 def add_kernel(a, b, keep, send):
@@ -157,19 +151,35 @@
     send[...] = total.astype(BF)
 
 
-def seq_kernel(xh_ref, y_ref, ra, rb, rg, o_ref):
-    xh = xh_ref[0]
+def seq_kernel(s_ref, ra, rb, rg, o_ref):
     for s in range(2):
         near, far = slice(s * 128, s * 128 + 128), slice(s * 128 + 256, s * 128 + 384)
         right = jnp.concatenate([rg[:, near], rg[:, far]], axis=1)
-        for n, dy in enumerate(ROWS):
-            for dx in range(2):
-                mine = slice(n * 160 + dx * 80, n * 160 + dx * 80 + 80)
-                other = slice(n * 160 + 80 - dx * 80, n * 160 + 160 - dx * 80)
-                left = [ra[mine, cols] + rb[other, cols].astype(F32) for cols in (near, far)]
-                left = jnp.concatenate(left, axis=1).astype(BF)
-                target = (xh + dx) % 2 * 4 + (y_ref[0] + dy + 4) % 4
-                o_ref[target, s] = dot(left, right, 1, 1).astype(BF)
+        for dx in range(2):
+            mine, other = slice(dx * 80, dx * 80 + 80), slice(80 - dx * 80, 160 - dx * 80)
+            left = [ra[mine, cols] + rb[other, cols].astype(F32) for cols in (near, far)]
+            left = jnp.concatenate(left, axis=1).astype(BF)
+            o_ref[(s_ref[4] + dx) % 2, 0, s] = dot(left, right, 1, 1).astype(BF)
+
+
+def sequences(xh, y, ra, rb, rg):
+    spec = pltpu.PrefetchScalarGridSpec(
+        num_scalar_prefetch=1,
+        grid=(4,),
+        in_specs=[
+            pl.BlockSpec((160, 512), lambda n, s: (n, 0)),
+            pl.BlockSpec((160, 512), lambda n, s: (n, 0)),
+            pl.BlockSpec((512, 512), lambda n, s: (0, 0)),
+        ],
+        out_specs=pl.BlockSpec((2, 1, 2, 80, 512), lambda n, s: (0, s[n], 0, 0, 0)),
+    )
+    return pl.pallas_call(
+        seq_kernel,
+        grid_spec=spec,
+        out_shape=arr(2, 4, 2, 80, 512),
+        compiler_params=WIDE,
+        name="seq",
+    )(jnp.stack([(y + dy + 4) % 4 for dy in ROWS] + [xh]), ra, rb, rg).reshape(8, 2, 80, 512)
 
 
 def sum_kernel(parts, o_ref):
@@ -187,7 +197,7 @@
         out_shape=out,
         in_specs=specs,
         out_specs=jax.tree.map(lambda _: VMEM, out),
-        compiler_params=WIDE if name in ("acts", "seq") else ROOM,
+        compiler_params=ROOM,
         name=name,
     )(*scalars, *args, *aside)
 
@@ -202,31 +212,30 @@
     part = features // 4
     place = [xh[None], core[None]]
     cuts = [arr(slots, 2 * part), arr(slots, 2 * part), arr(80, 2 * part)]
-    a_own, a_sib, b0 = call(cut_kernel, cuts, "cut", [activations, basis_in], place)
+    chosen, g0, g1, g2, g3 = pick(block_ids, y, basis_out, out_grads)
+    a_own, a_sib, b_own = call(cut_kernel, cuts, "cut", [activations, basis_in], place, [g0])
+    a_sib = shift(a_sib, core=1)
+    c1, c2 = shift(chosen, y=1), shift(chosen, y=-1)
+    near, far, b_far = call(pair_kernel, [arr(2, slots, part)] * 2 + [arr(80, part)], "pair", [a_own, a_sib, b_own], (), [g0])
+    far, b_far = shift(far, xh=1), shift(b_far, xh=1)
+    acts = call(stack_kernel, arr(4, slots, part), "stack", [near, far], (), [c1, c2])
+    acts = lax.all_gather(acts, "z", axis=0, tiled=False)
+    g1, g2, g3 = shift(g1, y=1), shift(g2, y=-1), shift(g3, y=2)
+    c3 = shift(c2, y=-1)
+
+    b0 = jnp.concatenate([b_own[:, :part], b_far])
+    partial = call(grads_kernel, arr(1024, 512), "grads", [chosen, c1, c2, c3, g0, g1, g2, g3], (), [b0])
     b1, b2 = shift(b0, y=1), shift(b0, y=-1)
-    a_sib = shift(a_sib, core=1)
-    up, down, g0, g3 = pick(block_ids, y, basis_out, out_grads)
-    near, a_far = call(pair_kernel, [arr(2, slots, part)] * 2, "pair", [a_own, a_sib], (), [g0])
-    a_far = shift(a_far, xh=1)
-    up_got, down_got, g3_got = shift(up, y=1), shift(down, y=-1), shift(g3, y=2)
-    acts = call(stack_kernel, arr(4, slots, part), "stack", [near, a_far], (), [down_got, up_got, b1, b2])
-    acts = lax.all_gather(acts, "z", axis=0, tiled=False)
-    c3 = shift(down_got[:, :1024], y=-1)
-    b3 = shift(b1, y=1)
-    far = shift(call(join_kernel, arr(240, part), "join", [b0, b1, b2], (), [g0]), xh=1)
-    far3 = shift(b3[:, part:], xh=1)
-
-    grads_in = [up, up_got, down_got, c3, g0, g3_got]
-    partial = call(grads_kernel, arr(1024, 512), "grads", grads_in, (), [far, b3])
+    b3a, b3b = shift(b1[:80], y=1), shift(b2[80:], y=-1)
     parts = lax.all_to_all(partial.reshape(16, 64, 512), ("xh", "z"), split_axis=0, concat_axis=0, tiled=True)
     wide = jax.ShapeDtypeStruct((640, 512), F32)
-    keep, send = call(acts_kernel, [wide, wide], "acts", [acts, b0, b1, b2, b3, far, far3], [xh[None]])
+    keep, send = call(acts_kernel, [wide, wide], "acts", [acts, b_own, b_far, b1, b2, b3a, b3b], [xh[None]])
     keep, send = call(add_kernel, [wide, arr(640, 512)], "add", [keep, shift(send, core=1)])
     rb = shift(send, xh=1)
     copies = call(live_kernel, arr(8, 64, 512), "live", [parts], [y[None], seq_lens], [send])
     rotated = lax.all_to_all(copies, "z", split_axis=0, concat_axis=0, tiled=True).reshape(512, 512)
 
-    tiles = call(seq_kernel, arr(8, 2, 80, 512), "seq", [keep, rb, rotated], [xh[None], y[None]])
+    tiles = sequences(xh, y, keep, rb, rotated)
     got = lax.all_to_all(tiles, ("xh", "y"), split_axis=0, concat_axis=0, tiled=True)
     seq_grads = call(sum_kernel, arr(2, 80, 1024), "sums", [got])
 

time: 221 us -> 206 us (0.932)
  waiting for transfers between devices: 78.7 us -> 65 us
  Pallas kernels: 24 us -> 20.5 us
    all_gather x1, waiting for transfers between devices: 19.6 us -> 6.78 us  [per_device(): acts = lax.all_gather(acts, 'z', axis=0, tiled=False)]
    pallas_call x10 -> x8, Pallas kernels: 19.9 us -> 11.7 us  [call(): pl.pallas_call(kernel, out_shape=out, in_specs=specs, out_specs=jax.tree....]
    pallas_call x1 -> x2, Pallas kernels: 4.12 us -> 8.79 us  [the longest x1 4.98 us: sequences(): pl.pallas_call(seq_kernel, grid_spec=spec, out_shape=arr(2, 4, 2, 80, 512...]
    all_to_all x1, blocking collectives: 24 us -> 27.2 us  [per_device(): lax.all_to_all(tiles, ('xh', 'y'), split_axis=0, concat_axis=0, tiled=True)]
    unnamed x32 -> x34, local copies, waits for them, and re-layouts: 8.04 us -> 10.7 us
    ppermute x16 -> x18, starting transfers between devices: 24.5 us -> 22.5 us  [shift(): return lax.ppermute(x, axes, pairs)]
    ppermute x16 -> x18, waiting for transfers between devices: 59.1 us -> 58.2 us  [shift(): return lax.ppermute(x, axes, pairs)]
  transfers between devices with their start and end apart: 19 -> 21, of which waited for: 9 -> 11; matrix products, arithmetic and copies ran while one was open for 2% -> 2% of each run, Pallas kernels for 6% -> 5%
where the time goes in v7:
time: 206 us; the launch traced here: 205 us
  waiting for transfers between devices  65 us (32%)
  blocking collectives  50.7 us (25%)
  starting transfers between devices  37 us (18%)
  Pallas kernels  20.5 us (10%)
  between operations  13.5 us (7%)
  local copies, waits for them, and re-layouts  10.9 us (5%)
  matrix products  5.87 us (3%)
    ppermute x18, waiting for transfers between devices, shift(): return lax.ppermute(x, axes, pairs)  58.2 us
    all_to_all x1, blocking collectives, per_device(): lax.all_to_all(tiles, ('xh', 'y'), split_axis=0, concat_axis=0, tiled=True)  27.2 us
    all_to_all x1, blocking collectives, spread(): lax.all_to_all(jnp.broadcast_to(x[None], (count,) + x.shape), axes, split...  23.5 us
    ppermute x18, starting transfers between devices, shift(): return lax.ppermute(x, axes, pairs)  22.5 us
    pallas_call x8, Pallas kernels, call(): pl.pallas_call(kernel, out_shape=out, in_specs=specs, out_specs=jax.tree....  11.7 us
    unnamed x34, local copies, waits for them, and re-layouts  10.7 us
    all_to_all x1, starting transfers between devices, per_device(): lax.all_to_all(partial.reshape(16, 64, 512), ('xh', 'z'), split_axis=0, c...  8.7 us
    all_gather x1, waiting for transfers between devices, per_device(): acts = lax.all_gather(acts, 'z', axis=0, tiled=False)  6.78 us
  transfers between devices with their start and end apart: 21, of which 11 were waited for; matrix products, arithmetic and copies ran while one was open for 2% of the time, Pallas kernels for 5%

profile of v7, /device:TPU:24, one launch (start us, length us, event | category | flops | bytes accessed | tf_op | source)
XLA Modules:
  0.0 205.0 jit_solution(4120861452496212039)
XLA Ops:
  7.4 3.8 %pick.1 = (bf16[216,1024]{1,0:T(8,128)(2,1)}, bf16[216,512]{1,0:T(8,128)(2,1)S(1)}, bf16[216,512]{1,0:T(8,128)(2,1)S(1)}, bf16[216,512]{1,0:T(8,128)(2,1)S(1)}, bf16[216,512]{1,0:T(8,128)(2,1)S(1)}) custom-call(s32[9]{0:T(128)S(1)} %pad_add_fusion.s_ref, bf16[216,13824]{1,0:T(8,128)(2,1)} %refs_7_.1, bf16[216,13824]{1,0:T(8,128)(2,1)} %refs_7_.1, ...), custom_call_target="tpu_custom_call" | custom-call | tf_op jit(solution)/shard_map/pick/pallas_call | solution.py:78
  14.0 2.5 %collective-permute-start.2 = (bf16[216,1024]{1,0:T(8,128)(2,1)}, bf16[216,1024]{1,0:T(8,128)(2,1)S(1)}, u32[]{:S(2)}, u32[]{:S(2)}) collective-permute-start(bf16[216,1024]{1,0:T(8,128)(2,1)} %get-tuple-element.26.c0), channel_id=1, source_target_pairs={{0,1},{1,2},{2,3},{3,0},{4,5},{5,6},{6,7},{7,4},{8,9},{9,10},{10,1... | collective-permute-start | bytes 1327112 | tf_op jit(solution)/shard_map/ppermute | solution.py:33
  19.9 3.0 %collective-permute-start.1 = (bf16[2,32,1280]{2,1,0:T(8,128)(2,1)S(1)}, bf16[2,32,1280]{2,1,0:T(8,128)(2,1)S(1)}, u32[]{:S(2)}, u32[]{:S(2)}) collective-permute-start(bf16[2,32,1280]{2,1,0:T(8,128)(2,1)S(1)} %get-tuple-element.25), channel_id=1, source_target_pairs={{0,4},{4,0},{1,5},{5,1},{2,6},{6,2},{3,7},{7,3},{8,12},{12,8},{9,1... | collective-permute-start | bytes 491528 | tf_op jit(solution)/shard_map/ppermute | solution.py:33
  22.9 4.7 %collective-permute-done.1.far = bf16[2,32,1280]{2,1,0:T(8,128)(2,1)S(1)} collective-permute-done((bf16[2,32,1280]{2,1,0:T(8,128)(2,1)S(1)}, bf16[2,32,1280]{2,1,0:T(8,128)(2,1)S(1)}, u32[]{:S(2)}, u32[]{:S(2)}) %collective-permute-start.1) | collective-permute-done | bytes 163872 | tf_op jit(solution)/shard_map/ppermute | solution.py:33
  28.4 3.1 %collective-permute-start.4 = (bf16[80,1280]{1,0:T(8,128)(2,1)}, bf16[80,1280]{1,0:T(8,128)(2,1)S(1)}, u32[]{:S(2)}, u32[]{:S(2)}) collective-permute-start(bf16[80,1280]{1,0:T(8,128)(2,1)} %get-tuple-element.27), channel_id=1, source_target_pairs={{0,4},{4,0},{1,5},{5,1},{2,6},{6,2},{3,7},{7,3},{8,12},{12,8},{9,1... | collective-permute-start | bytes 614408 | tf_op jit(solution)/shard_map/ppermute | solution.py:33
  31.5 3.2 %collective-permute-start.12 = (bf16[216,512]{1,0:T(8,128)(2,1)}, bf16[216,512]{1,0:T(8,128)(2,1)S(1)}, u32[]{:S(2)}, u32[]{:S(2)}) collective-permute-start(bf16[216,512]{1,0:T(8,128)(2,1)} %copy-done.16), channel_id=1, source_target_pairs={{0,1},{1,2},{2,3},{3,0},{4,5},{5,6},{6,7},{7,4},{8,9},{9,10},{10,1... | collective-permute-start | bytes 663560 | tf_op jit(solution)/shard_map/ppermute | solution.py:33
  34.7 2.1 %collective-permute-start.14 = (bf16[216,512]{1,0:T(8,128)(2,1)}, bf16[216,512]{1,0:T(8,128)(2,1)S(1)}, u32[]{:S(2)}, u32[]{:S(2)}) collective-permute-start(bf16[216,512]{1,0:T(8,128)(2,1)} %copy-done.14), channel_id=1, source_target_pairs={{0,2},{1,3},{2,0},{3,1},{4,6},{5,7},{6,4},{7,5},{8,10},{9,11},{10,... | collective-permute-start | bytes 663560 | tf_op jit(solution)/shard_map/ppermute | solution.py:33
  37.0 6.4 %collective-permute-done.12.g1 = bf16[216,512]{1,0:T(8,128)(2,1)S(1)} collective-permute-done((bf16[216,512]{1,0:T(8,128)(2,1)}, bf16[216,512]{1,0:T(8,128)(2,1)S(1)}, u32[]{:S(2)}, u32[]{:S(2)}) %collective-permute-start.12) | collective-permute-done | bytes 221216 | tf_op jit(solution)/shard_map/ppermute | solution.py:33
  43.4 9.9 %collective-permute-done.13.g2 = bf16[216,512]{1,0:T(8,128)(2,1)S(1)} collective-permute-done((bf16[216,512]{1,0:T(8,128)(2,1)}, bf16[216,512]{1,0:T(8,128)(2,1)S(1)}, u32[]{:S(2)}, u32[]{:S(2)}) %collective-permute-start.13) | collective-permute-done | bytes 221216 | tf_op jit(solution)/shard_map/ppermute | solution.py:33
  53.3 3.3 %grads.1 = bf16[1024,512]{1,0:T(8,128)(2,1)} custom-call(bf16[216,1024]{1,0:T(8,128)(2,1)} %get-tuple-element.26.c0, bf16[216,1024]{1,0:T(8,128)(2,1)S(1)} %collective-permute-done.2.refs_0_.c1, bf16[216,1024]{1,0:T(8,128)(2,1)S(1)} %collective-permute-done.3.refs_1_.c2, bf16[216,1024]{1,0:T(8,128)(2,1)S(1)} %collective-permute-done.11.c3, ...), custom_call_target="tpu_custom_call" | custom-call | tf_op jit(solution)/shard_map/grads/pallas_call | solution.py:195
  56.6 8.7 %all-to-all-start = ((bf16[16,64,512]{2,1,0:T(8,128)(2,1)}), bf16[16,64,512]{2,1,0:T(8,128)(2,1)S(1)}, u32[]{:S(2)}, u32[]{:S(2)}) async-start(bf16[16,64,512]{2,1,0:T(8,128)(2,1)} %bitcast.8), calls=%async_computation | async-start | bytes 2097152 | tf_op jit(solution)/shard_map/all_to_all | solution.py:230
  65.4 2.0 collective-permute-start.6
  67.5 6.8 %collective-permute-done.5.b1 = bf16[160,1280]{1,0:T(8,128)(2,1)S(1)} collective-permute-done((bf16[160,1280]{1,0:T(8,128)(2,1)S(1)}, bf16[160,1280]{1,0:T(8,128)(2,1)S(1)}, u32[]{:S(2)}, u32[]{:S(2)}) %collective-permute-start.5) | collective-permute-done | bytes 409632 | tf_op jit(solution)/shard_map/ppermute | solution.py:33
  77.2 2.9 %collective-permute-done.7.b3a = bf16[80,1280]{1,0:T(8,128)(2,1)S(1)} collective-permute-done((bf16[80,1280]{1,0:T(8,128)(2,1)S(1)}, bf16[80,1280]{1,0:T(8,128)(2,1)S(1)}, u32[]{:S(2)}, u32[]{:S(2)}) %collective-permute-start.7) | collective-permute-done | bytes 204832 | tf_op jit(solution)/shard_map/ppermute | solution.py:33
  82.8 6.8 %all-gather.3.cloned.1.call-done = bf16[32,32,1280]{2,1,0:T(8,128)(2,1)} async-done(((bf16[4,32,1280]{2,1,0:T(8,128)(2,1)}), bf16[32,32,1280]{2,1,0:T(8,128)(2,1)}) %all-gather.3.cloned.1.call-update) | async-done | bytes 2621456 | tf_op jit(solution)/shard_map/all_gather | solution.py:222
  94.3 5.0 %acts.1 = (f32[640,512]{1,0:T(8,128)S(1)}, f32[640,512]{1,0:T(8,128)S(1)}) custom-call(s32[1]{0:T(128)} %bitcast.4.xh_ref, bf16[8,4,32,1280]{3,2,1,0:T(8,128)(2,1)S(1)} %bitcast.31, bf16[80,2560]{1,0:T(8,128)(2,1)S(1)} %get-tuple-element.23.b_own.own, bf16[80,1280]{1,0:T(8,128)(2,1)S(1)} %collective-permute-done.4.own_far, bf16[160,1280]{1,0:T(8,128)(2,1)S(1)} %copy-done.6, ...), custom_call_target="tpu_custom_call" | custom-call | tf_op jit(solution)/shard_map/acts/pallas_call | solution.py:195
  99.3 3.0 %collective-permute-done.9.b = f32[640,512]{1,0:T(8,128)S(1)} collective-permute-done((f32[640,512]{1,0:T(8,128)S(1)}, f32[640,512]{1,0:T(8,128)S(1)}, u32[]{:S(2)}, u32[]{:S(2)}) %collective-permute-start.9) | collective-permute-done | bytes 1310752 | tf_op jit(solution)/shard_map/ppermute | solution.py:33
  105.2 5.8 %all-to-all-start.1 = ((bf16[8,64,512]{2,1,0:T(8,128)(2,1)}), bf16[8,64,512]{2,1,0:T(8,128)(2,1)S(1)}, u32[]{:S(2)}, u32[]{:S(2)}) async-start(bf16[8,64,512]{2,1,0:T(8,128)(2,1)} %live.1), calls=%async_computation.1 | async-start | bytes 1048576 | tf_op jit(solution)/shard_map/all_to_all | solution.py:236
  111.0 2.5 %collective-permute-start.10 = (bf16[640,512]{1,0:T(8,128)(2,1)S(1)}, bf16[640,512]{1,0:T(8,128)(2,1)}, u32[]{:S(2)}, u32[]{:S(2)}) collective-permute-start(bf16[640,512]{1,0:T(8,128)(2,1)S(1)} %get-tuple-element.31.refs_0_), channel_id=1, source_target_pairs={{0,4},{4,0},{1,5},{5,1},{2,6},{6,2},{3,7},{7,3},{8,12},{12,8},{9,1... | collective-permute-start | bytes 1966088 | tf_op jit(solution)/shard_map/ppermute | solution.py:33
  113.7 15.5 %collective-permute-done.10.rb = bf16[640,512]{1,0:T(8,128)(2,1)} collective-permute-done((bf16[640,512]{1,0:T(8,128)(2,1)S(1)}, bf16[640,512]{1,0:T(8,128)(2,1)}, u32[]{:S(2)}, u32[]{:S(2)}) %collective-permute-start.10) | collective-permute-done | bytes 655392 | tf_op jit(solution)/shard_map/ppermute | solution.py:33
  129.1 5.0 %seq.1 = bf16[2,4,2,80,512]{4,3,2,1,0:T(8,128)(2,1)} custom-call(s32[5]{0:T(128)S(1)} %stack.39.s_ref, f32[640,512]{1,0:T(8,128)} %copy-done.4, bf16[640,512]{1,0:T(8,128)(2,1)} %collective-permute-done.10.rb, bf16[512,512]{1,0:T(8,128)(2,1)S(1)} %bitcast.32), custom_call_target="tpu_custom_call" | custom-call | tf_op jit(solution)/shard_map/seq/pallas_call | solution.py:176
  134.1 27.2 %all_to_all.20.parts = bf16[8,2,80,512]{3,2,1,0:T(8,128)(2,1)S(1)} all-to-all(bf16[8,2,80,512]{3,2,1,0:T(8,128)(2,1)} %bitcast.33), channel_id=1, replica_groups=mesh['xl'=2,'core'=2,'z'=8,'xh'=2,'y'=4] {'xh','y'}, dimensions={0} | all-to-all | bytes 2621440 | tf_op jit(solution)/shard_map/all_to_all | solution.py:239
  164.1 5.5 %collective-permute-done.16 = bf16[2,80,1024]{2,1,0:T(8,128)(2,1)S(1)} collective-permute-done((bf16[2,80,1024]{2,1,0:T(8,128)(2,1)S(1)}, bf16[2,80,1024]{2,1,0:T(8,128)(2,1)S(1)}, u32[]{:S(2)}, u32[]{:S(2)}) %collective-permute-start.16) | collective-permute-done | bytes 327712 | tf_op jit(solution)/shard_map/ppermute | solution.py:33
  174.0 23.5 %all_to_all.21 = f32[64,8,8]{2,1,0:T(8,128)S(1)} all-to-all(f32[64,8,8]{2,1,0:T(8,128)S(1)} %broadcast_in_dim.8), channel_id=1, replica_groups=mesh['xl'=2,'core'=2,'z'=8,'xh'=2,'y'=4] {'z','xh','y'}, dimensions={0} | all-to-all | bytes 32768 | tf_op jit(solution)/shard_map/all_to_all | solution.py:37
  (80 shorter events, 29.0 us)
Async XLA Ops:
  6.5 156.1 %copy-start = (bf16[8,80,1024]{2,1,0:T(8,128)(2,1)S(1)}, bf16[8,80,1024]{2,1,0:T(8,128)(2,1)}, u32[]{:S(2)}) copy-start(bf16[8,80,1024]{2,1,0:T(8,128)(2,1)} %param.13) | copy-start | bytes 3932164
  6.5 83.0 %all-gather.3.cloned.1.call-start = ((), (), s32[]{:S(2)}) async-start(), calls=%async_computation.4 | async-start | bytes 2949120 | tf_op jit(solution)/shard_map/all_gather | solution.py:222
  7.4 9.1 %copy-start.10 = (bf16[32,5120]{1,0:T(8,128)(2,1)S(1)}, bf16[32,5120]{1,0:T(8,128)(2,1)}, u32[]{:S(2)}) copy-start(bf16[32,5120]{1,0:T(8,128)(2,1)} %a_ref.1) | copy-start | bytes 983044
  13.2 14.4 %collective-permute-start.3 = (bf16[216,1024]{1,0:T(8,128)(2,1)}, bf16[216,1024]{1,0:T(8,128)(2,1)S(1)}, u32[]{:S(2)}, u32[]{:S(2)}) collective-permute-start(bf16[216,1024]{1,0:T(8,128)(2,1)} %get-tuple-element.26.c0), channel_id=1, source_target_pairs={{0,3},{1,0},{2,1},{3,2},{4,7},{5,4},{6,5},{7,6},{8,11},{9,8},{10,9... | collective-permute-start | bytes 1327112 | tf_op jit(solution)/shard_map/ppermute | solution.py:33
  14.0 13.6 %collective-permute-start.2 = (bf16[216,1024]{1,0:T(8,128)(2,1)}, bf16[216,1024]{1,0:T(8,128)(2,1)S(1)}, u32[]{:S(2)}, u32[]{:S(2)}) collective-permute-start(bf16[216,1024]{1,0:T(8,128)(2,1)} %get-tuple-element.26.c0), channel_id=1, source_target_pairs={{0,1},{1,2},{2,3},{3,0},{4,5},{5,6},{6,7},{7,4},{8,9},{9,10},{10,1... | collective-permute-start | bytes 1327112 | tf_op jit(solution)/shard_map/ppermute | solution.py:33
  17.7 1.5 collective-permute-start
  19.9 7.8 %collective-permute-start.1 = (bf16[2,32,1280]{2,1,0:T(8,128)(2,1)S(1)}, bf16[2,32,1280]{2,1,0:T(8,128)(2,1)S(1)}, u32[]{:S(2)}, u32[]{:S(2)}) collective-permute-start(bf16[2,32,1280]{2,1,0:T(8,128)(2,1)S(1)} %get-tuple-element.25), channel_id=1, source_target_pairs={{0,4},{4,0},{1,5},{5,1},{2,6},{6,2},{3,7},{7,3},{8,12},{12,8},{9,1... | collective-permute-start | bytes 491528 | tf_op jit(solution)/shard_map/ppermute | solution.py:33
  28.4 8.5 %collective-permute-start.4 = (bf16[80,1280]{1,0:T(8,128)(2,1)}, bf16[80,1280]{1,0:T(8,128)(2,1)S(1)}, u32[]{:S(2)}, u32[]{:S(2)}) collective-permute-start(bf16[80,1280]{1,0:T(8,128)(2,1)} %get-tuple-element.27), channel_id=1, source_target_pairs={{0,4},{4,0},{1,5},{5,1},{2,6},{6,2},{3,7},{7,3},{8,12},{12,8},{9,1... | collective-permute-start | bytes 614408 | tf_op jit(solution)/shard_map/ppermute | solution.py:33
  31.5 21.8 %collective-permute-start.11 = (bf16[216,1024]{1,0:T(8,128)(2,1)S(1)}, bf16[216,1024]{1,0:T(8,128)(2,1)S(1)}, u32[]{:S(2)}, u32[]{:S(2)}) collective-permute-start(bf16[216,1024]{1,0:T(8,128)(2,1)S(1)} %collective-permute-done.3.refs_1_.c2), channel_id=1, source_target_pairs={{0,3},{1,0},{2,1},{3,2},{4,7},{5,4},{6,5},{7,6},{8,11},{9,8},{10,9... | collective-permute-start | bytes 1327112 | tf_op jit(solution)/shard_map/ppermute | solution.py:33
  31.5 11.9 %collective-permute-start.12 = (bf16[216,512]{1,0:T(8,128)(2,1)}, bf16[216,512]{1,0:T(8,128)(2,1)S(1)}, u32[]{:S(2)}, u32[]{:S(2)}) collective-permute-start(bf16[216,512]{1,0:T(8,128)(2,1)} %copy-done.16), channel_id=1, source_target_pairs={{0,1},{1,2},{2,3},{3,0},{4,5},{5,6},{6,7},{7,4},{8,9},{9,10},{10,1... | collective-permute-start | bytes 663560 | tf_op jit(solution)/shard_map/ppermute | solution.py:33
  34.7 18.6 %collective-permute-start.13 = (bf16[216,512]{1,0:T(8,128)(2,1)}, bf16[216,512]{1,0:T(8,128)(2,1)S(1)}, u32[]{:S(2)}, u32[]{:S(2)}) collective-permute-start(bf16[216,512]{1,0:T(8,128)(2,1)} %copy-done.15), channel_id=1, source_target_pairs={{0,3},{1,0},{2,1},{3,2},{4,7},{5,4},{6,5},{7,6},{8,11},{9,8},{10,9... | collective-permute-start | bytes 663560 | tf_op jit(solution)/shard_map/ppermute | solution.py:33
  34.7 18.6 %collective-permute-start.14 = (bf16[216,512]{1,0:T(8,128)(2,1)}, bf16[216,512]{1,0:T(8,128)(2,1)S(1)}, u32[]{:S(2)}, u32[]{:S(2)}) collective-permute-start(bf16[216,512]{1,0:T(8,128)(2,1)} %copy-done.14), channel_id=1, source_target_pairs={{0,2},{1,3},{2,0},{3,1},{4,6},{5,7},{6,4},{7,5},{8,10},{9,11},{10,... | collective-permute-start | bytes 663560 | tf_op jit(solution)/shard_map/ppermute | solution.py:33
  36.9 19.7 %copy-start.2 = (bf16[160,1280]{1,0:T(8,128)(2,1)}, bf16[160,1280]{1,0:T(8,128)(2,1)S(1)}, u32[]{:S(2)}) copy-start(bf16[160,1280]{1,0:T(8,128)(2,1)S(1)} %pad_maximum_fusion.aside) | copy-start | bytes 1228804
  56.6 47.1 %all-to-all-start = ((bf16[16,64,512]{2,1,0:T(8,128)(2,1)}), bf16[16,64,512]{2,1,0:T(8,128)(2,1)S(1)}, u32[]{:S(2)}, u32[]{:S(2)}) async-start(bf16[16,64,512]{2,1,0:T(8,128)(2,1)} %bitcast.8), calls=%async_computation | async-start | bytes 2097152 | tf_op jit(solution)/shard_map/all_to_all | solution.py:230
  65.4 8.9 %collective-permute-start.5 = (bf16[160,1280]{1,0:T(8,128)(2,1)S(1)}, bf16[160,1280]{1,0:T(8,128)(2,1)S(1)}, u32[]{:S(2)}, u32[]{:S(2)}) collective-permute-start(bf16[160,1280]{1,0:T(8,128)(2,1)S(1)} %copy-done.3), channel_id=1, source_target_pairs={{0,1},{1,2},{2,3},{3,0},{4,5},{5,6},{6,7},{7,4},{8,9},{9,10},{10,1... | collective-permute-start | bytes 1228808 | tf_op jit(solution)/shard_map/ppermute | solution.py:33
  65.4 9.3 %collective-permute-start.6 = (bf16[160,1280]{1,0:T(8,128)(2,1)S(1)}, bf16[160,1280]{1,0:T(8,128)(2,1)S(1)}, u32[]{:S(2)}, u32[]{:S(2)}) collective-permute-start(bf16[160,1280]{1,0:T(8,128)(2,1)S(1)} %copy-done.3), channel_id=1, source_target_pairs={{0,3},{1,0},{2,1},{3,2},{4,7},{5,4},{6,5},{7,6},{8,11},{9,8},{10,9... | collective-permute-start | bytes 1228808 | tf_op jit(solution)/shard_map/ppermute | solution.py:33
  74.3 5.8 %collective-permute-start.7 = (bf16[80,1280]{1,0:T(8,128)(2,1)S(1)}, bf16[80,1280]{1,0:T(8,128)(2,1)S(1)}, u32[]{:S(2)}, u32[]{:S(2)}) collective-permute-start(bf16[80,1280]{1,0:T(8,128)(2,1)S(1)} %slice.12), channel_id=1, source_target_pairs={{0,1},{1,2},{2,3},{3,0},{4,5},{5,6},{6,7},{7,4},{8,9},{9,10},{10,1... | collective-permute-start | bytes 614408 | tf_op jit(solution)/shard_map/ppermute | solution.py:33
  75.8 7.0 %collective-permute-start.8 = (bf16[80,1280]{1,0:T(8,128)(2,1)S(1)}, bf16[80,1280]{1,0:T(8,128)(2,1)S(1)}, u32[]{:S(2)}, u32[]{:S(2)}) collective-permute-start(bf16[80,1280]{1,0:T(8,128)(2,1)S(1)} %slice.13), channel_id=1, source_target_pairs={{0,3},{1,0},{2,1},{3,2},{4,7},{5,4},{6,5},{7,6},{8,11},{9,8},{10,9... | collective-permute-start | bytes 614408 | tf_op jit(solution)/shard_map/ppermute | solution.py:33
  99.2 3.1 %collective-permute-start.9 = (f32[640,512]{1,0:T(8,128)S(1)}, f32[640,512]{1,0:T(8,128)S(1)}, u32[]{:S(2)}, u32[]{:S(2)}) collective-permute-start(f32[640,512]{1,0:T(8,128)S(1)} %get-tuple-element.29), channel_id=1, source_target_pairs={{0,64},{64,0},{1,65},{65,1},{2,66},{66,2},{3,67},{67,3},{4,68},{68... | collective-permute-start | bytes 3932168 | tf_op jit(solution)/shard_map/ppermute | solution.py:33
  105.2 23.9 %all-to-all-start.1 = ((bf16[8,64,512]{2,1,0:T(8,128)(2,1)}), bf16[8,64,512]{2,1,0:T(8,128)(2,1)S(1)}, u32[]{:S(2)}, u32[]{:S(2)}) async-start(bf16[8,64,512]{2,1,0:T(8,128)(2,1)} %live.1), calls=%async_computation.1 | async-start | bytes 1048576 | tf_op jit(solution)/shard_map/all_to_all | solution.py:236
  111.0 18.1 %collective-permute-start.10 = (bf16[640,512]{1,0:T(8,128)(2,1)S(1)}, bf16[640,512]{1,0:T(8,128)(2,1)}, u32[]{:S(2)}, u32[]{:S(2)}) collective-permute-start(bf16[640,512]{1,0:T(8,128)(2,1)S(1)} %get-tuple-element.31.refs_0_), channel_id=1, source_target_pairs={{0,4},{4,0},{1,5},{5,1},{2,6},{6,2},{3,7},{7,3},{8,12},{12,8},{9,1... | collective-permute-start | bytes 1966088 | tf_op jit(solution)/shard_map/ppermute | solution.py:33
  161.5 8.0 %collective-permute-start.16 = (bf16[2,80,1024]{2,1,0:T(8,128)(2,1)S(1)}, bf16[2,80,1024]{2,1,0:T(8,128)(2,1)S(1)}, u32[]{:S(2)}, u32[]{:S(2)}) collective-permute-start(bf16[2,80,1024]{2,1,0:T(8,128)(2,1)S(1)} %sums.1), channel_id=1, source_target_pairs={{0,128},{128,0},{1,129},{129,1},{2,130},{130,2},{3,131},{131,3},{4... | collective-permute-start | bytes 983048 | tf_op jit(solution)/shard_map/ppermute | solution.py:33
  162.6 8.4 %collective-permute-start.15 = (bf16[2,80,1024]{2,1,0:T(8,128)(2,1)S(1)}, bf16[2,80,1024]{2,1,0:T(8,128)(2,1)S(1)}, u32[]{:S(2)}, u32[]{:S(2)}) collective-permute-start(bf16[2,80,1024]{2,1,0:T(8,128)(2,1)S(1)} %sums.1), channel_id=1, source_target_pairs={{0,64},{64,0},{1,65},{65,1},{2,66},{66,2},{3,67},{67,3},{4,68},{68... | collective-permute-start | bytes 983048 | tf_op jit(solution)/shard_map/ppermute | solution.py:33
  169.5 2.9 %collective-permute-start.17 = (bf16[2,80,1024]{2,1,0:T(8,128)(2,1)S(1)}, bf16[2,80,1024]{2,1,0:T(8,128)(2,1)S(1)}, u32[]{:S(2)}, u32[]{:S(2)}) collective-permute-start(bf16[2,80,1024]{2,1,0:T(8,128)(2,1)S(1)} %collective-permute-done.16), channel_id=1, source_target_pairs={{0,64},{64,0},{1,65},{65,1},{2,66},{66,2},{3,67},{67,3},{4,68},{68... | collective-permute-start | bytes 983048 | tf_op jit(solution)/shard_map/ppermute | solution.py:33
  (14 other events, 21.3 us)
Sparse Core Ops, SparseCore 0:
  28.5 61.0 all-gather.2

commit v8 on v3

--- a/solution.py
+++ b/solution.py
@@ -13,7 +13,9 @@
 ROWS = (0, -1, 1, 2)
 VMEM = pl.BlockSpec(memory_space=pltpu.VMEM)
 SMEM = pl.BlockSpec(memory_space=pltpu.SMEM)
-ROOM = pltpu.CompilerParams(vmem_limit_bytes=20 * 1024 * 1024)
+TINY = pl.CostEstimate(flops=1, bytes_accessed=1, transcendentals=0)
+WIDE = pltpu.CompilerParams(vmem_limit_bytes=60 * 1024 * 1024)
+ROOM = pltpu.CompilerParams(vmem_limit_bytes=10 * 1024 * 1024)
 
 
 def shift(x, **by):
@@ -58,48 +60,66 @@
 
 
 def pick_kernel(s_ref, *refs):
-    picked, g_ref, up, down = refs[:8], *refs[8:]
+    picked, g_ref, chosen, g0, g1, g2, g3 = refs[:8], *refs[8:]
     for n, p in enumerate(picked):
-        cols = slice(n * 128, n * 128 + 128)
-        up[:, cols] = p[...]
-        down[:, cols] = p[...]
-    reorder(s_ref[8], g_ref, ((up, 1024, 1), (down, 1024, -1)))
+        chosen[:, n * 128 : n * 128 + 128] = p[...]
+    reorder(s_ref[8], g_ref, ((g1, 0, 1), (g2, 0, -1), (g3, 0, 2), (g0, 0, 0)))
 
 
 def pick(block_ids, y, basis_out, out_grads):
     rows, tokens = out_grads.shape
     whole = lambda width: pl.BlockSpec((rows, width), lambda g, s: (0, 0))
+    widths = (1024, 512, 512, 512, 512)
     spec = pltpu.PrefetchScalarGridSpec(
         num_scalar_prefetch=1,
         grid=(1,),
         in_specs=[pl.BlockSpec((rows, BLOCK), lambda g, s, n=n: (0, s[n])) for n in range(8)] + [whole(tokens)],
-        out_specs=[whole(1536), whole(1536)],
+        out_specs=[whole(w) for w in widths],
     )
     return pl.pallas_call(
         pick_kernel,
         grid_spec=spec,
-        out_shape=[arr(rows, 1536), arr(rows, 1536)],
-        compiler_params=pltpu.CompilerParams(vmem_limit_bytes=52 * 1024 * 1024),
+        out_shape=[arr(rows, w) for w in widths],
+        compiler_params=WIDE,
         name="pick",
     )(jnp.concatenate([block_ids, y[None]]), *[basis_out] * 8, out_grads)
 
 
-def rest_kernel(y_ref, g_ref, aside, g0, g3):
-    reorder(y_ref[0], g_ref, ((g3, 0, 2), (g0, 0, 0)))
-
-
-def join_kernel(b0, b1, b2, aside, o_ref):
-    o_ref[:80, :] = b0[...]
-    o_ref[80:160, :] = b1[...]
-    o_ref[160:, :] = b2[...]
-
-
-def grads_kernel(here, up, down, c3, g0, g3, *refs):
+def halve_kernel(s_ref, b_ref, o_ref):
+    o_ref[...] = b_ref[...]
+
+
+def halve(core, basis_in):
+    rows, half = basis_in.shape[0], basis_in.shape[1] // 2
+    spec = pltpu.PrefetchScalarGridSpec(
+        num_scalar_prefetch=1,
+        grid=(1,),
+        in_specs=[pl.BlockSpec((rows, half), lambda g, s: (0, s[0]))],
+        out_specs=pl.BlockSpec((rows, half), lambda g, s: (0, 0)),
+    )
+    return pl.pallas_call(
+        halve_kernel, grid_spec=spec, out_shape=arr(rows, half), compiler_params=ROOM, name="halve"
+    )(core[None], basis_in)
+
+
+def cut_kernel(core_ref, a_ref, *refs):
+    o_ref = refs[-1]
+    half = o_ref.shape[1]
+    o_ref[...] = a_ref[:, pl.ds(pl.multiple_of((1 - core_ref[0]) * half, 128), half)]
+
+
+def join_kernel(b1, b2, *refs):
+    o_ref = refs[-1]
+    o_ref[:80, :] = b1[...]
+    o_ref[80:, :] = b2[...]
+
+
+def grads_kernel(c0, c1, c2, c3, g0, g1, g2, g3, *refs):
     o_ref = refs[-1]
     for part in range(4):
         ks = slice(part * 256, part * 256 + 256)
-        total = dot(here[:, ks], g0[...], 0, 0) + dot(c3[:, ks], g3[...], 0, 0)
-        total += dot(up[:, ks], up[:, 1024:], 0, 0) + dot(down[:, ks], down[:, 1024:], 0, 0)
+        total = dot(c0[:, ks], g0[...], 0, 0) + dot(c1[:, ks], g1[...], 0, 0)
+        total += dot(c2[:, ks], g2[...], 0, 0) + dot(c3[:, ks], g3[...], 0, 0)
         o_ref[ks, :] = total.astype(BF)
 
 
@@ -116,17 +136,16 @@
         o_ref[n] = total
 
 
-def acts_kernel(s_ref, a_ref, *refs):
-    o_ref = refs[-1]
-    core = s_ref[0]
-    half = a_ref.shape[1] // 2
-    mine = a_ref[:, pl.ds(pl.multiple_of(core * half, 128), half)]
-    other = a_ref[:, pl.ds(pl.multiple_of((1 - core) * half, 128), half)]
-    for n, (own, sent) in enumerate(zip(refs[:4], refs[4:8])):
-        total = (dot(own[...], mine, 1, 1) + dot(sent[...], other, 1, 1)).astype(BF)
-        for row in range(total.shape[0] // 80):
-            place = (row + n // 2 * 3) * 160 + n % 2 * 80
-            o_ref[place : place + 80, :] = total[row * 80 : row * 80 + 80]
+def acts_kernel(core_ref, a_ref, sib, b0, far0, near, far, b3, far3, keep, send):
+    half = sib.shape[1]
+    mine = a_ref[:, pl.ds(pl.multiple_of(core_ref[0] * half, 128), half)]
+    for tokens, out in ((sib[...], send), (mine, keep)):
+        for n, (b, r) in enumerate(((b0, 0), (far0, 0), (near, 0), (far, 0), (near, 80), (far, 80), (b3, 0), (far3, 0))):
+            out[n * 80 : n * 80 + 80, :] = dot(b[r : r + 80, :], tokens, 1, 1)
+
+
+def add_kernel(a, b, o_ref):
+    o_ref[...] = (a[...] + b[...]).astype(BF)
 
 
 def seq_kernel(xh_ref, y_ref, ra, rb, rg, o_ref):
@@ -154,7 +173,7 @@
 
 
 def call(kernel, out, name, args, scalars=(), aside=()):
-    specs = [SMEM] * len(scalars) + [VMEM] * len(args) + [pl.BlockSpec(memory_space=pltpu.HBM)] * len(aside)
+    specs = [SMEM] * len(scalars) + [VMEM] * len(args) + [pl.BlockSpec(memory_space=pl.ANY)] * len(aside)
     return pl.pallas_call(
         kernel,
         out_shape=out,
@@ -162,6 +181,7 @@
         out_specs=jax.tree.map(lambda _: VMEM, out),
         compiler_params=ROOM,
         name=name,
+        cost_estimate=TINY,
     )(*scalars, *args, *aside)
 
 
@@ -172,30 +192,29 @@
 def per_device(activations, out_grads, basis_in, basis_out, block_ids, seq_lens, query_grads):
     xl, core, xh, y = (lax.axis_index(a).astype(jnp.int32) for a in ("xl", "core", "xh", "y"))
     acts = lax.all_gather(activations, "z", axis=0, tiled=True)
-
-    features = basis_in.shape[1]
-    b0 = lax.dynamic_slice_in_dim(basis_in, core * (features // 2), features // 2, 1)
+    half = basis_in.shape[1] // 2
+    b0 = halve(core, basis_in)
     b1, b2 = shift(b0, y=1), shift(b0, y=-1)
-    up, down = pick(block_ids, y, basis_out, out_grads)
-    g0, g3 = call(rest_kernel, [arr(216, 512)] * 2, "rest", [out_grads], [y[None]], [up])
-    up_got, down_got, g3_got = shift(up, y=1), shift(down, y=-1), shift(g3, y=2)
-    c3 = shift(down_got[:, :1024], y=-1)
-
-    near = call(join_kernel, arr(240, features // 2), "join", [b0, b1, b2], (), [g0])
-    far = shift(near, xh=1)
-    near3 = shift(b1, y=1)
-    far3 = shift(near3, xh=1)
-
-    grads_in = [up, up_got, down_got, c3, g0, g3_got]
-    partial = call(grads_kernel, arr(1024, 512), "grads", grads_in, (), [far, near3])
+    far0 = shift(b0, xl=1, xh=1)
+
+    chosen, g0, g1, g2, g3 = pick(block_ids, y, basis_out, out_grads)
+    c1, c2 = shift(chosen, y=1), shift(chosen, y=-1)
+    near = call(join_kernel, arr(160, half), "join", [b1, b2], (), [c1, c2])
+    far = shift(near, xl=1, xh=1)
+    g1, g2, g3 = shift(g1, y=1), shift(g2, y=-1), shift(g3, y=2)
+    c3 = shift(c2, y=-1)
+    partial = call(grads_kernel, arr(1024, 512), "grads", [chosen, c1, c2, c3, g0, g1, g2, g3], (), [far, far0])
+    b3 = shift(b1, y=1)
+    far3 = shift(far[:80], y=1)
     parts = lax.all_to_all(partial.reshape(16, 64, 512), ("xh", "z"), split_axis=0, concat_axis=0, tiled=True)
-    pieces = [near, far, near3, far3]
-    others = [shift(b, core=1) for b in pieces]
-    ra = call(acts_kernel, arr(640, 256), "acts", [acts] + pieces + others, [core[None]])
+    wide = jax.ShapeDtypeStruct((640, 256), F32)
+    sib = shift(call(cut_kernel, arr(256, half), "cut", [acts], [core[None]], [partial]), core=1)
+    keep, send = call(acts_kernel, [wide, wide], "acts", [acts, sib, b0, far0, near, far, b3, far3], [core[None]])
+    ra = call(add_kernel, arr(640, 256), "add", [keep, shift(send, core=1)])
+    rb = shift(ra, xh=1)
     copies = call(live_kernel, arr(8, 64, 512), "live", [parts], [y[None], seq_lens], [ra])
     rotated = lax.all_to_all(copies, "z", split_axis=0, concat_axis=0, tiled=True).reshape(512, 512)
 
-    rb = shift(ra, xh=1)
     tiles = call(seq_kernel, arr(8, 2, 80, 512), "seq", [ra, rb, rotated], [xh[None], y[None]])
     got = lax.all_to_all(tiles, ("xh", "y"), split_axis=0, concat_axis=0, tiled=True)
     seq_grads = call(sum_kernel, arr(2, 80, 1024), "sums", [got])

time: 202 us -> 210 us (1.040)
  local copies, waits for them, and re-layouts: 16.9 us -> 8.02 us
  Pallas kernels: 11.4 us -> 17.9 us
  starting transfers between devices: 33.7 us -> 38.4 us
  waiting for transfers between devices: 73.3 us -> 77.2 us
    unnamed x38 -> x36, local copies, waits for them, and re-layouts: 15.8 us -> 7.95 us
    pallas_call x7 -> x8, Pallas kernels: 8.74 us -> 13.6 us  [call(): pl.pallas_call(kernel, out_shape=out, in_specs=specs, out_specs=jax.tree....]
    ppermute x17 -> x18, waiting for transfers between devices: 65.7 us -> 69.7 us  [shift(): return lax.ppermute(x, axes, pairs)]
    ppermute x17 -> x18, starting transfers between devices: 18.2 us -> 21.8 us  [shift(): return lax.ppermute(x, axes, pairs)]
    pallas_call x1 -> x2, Pallas kernels: 2.64 us -> 4.29 us  [the longest x1 4.26 us: pick(): pl.pallas_call(pick_kernel, grid_spec=spec, out_shape=[arr(rows, w) for w...]
  transfers between devices with their start and end apart: 20 -> 21, of which waited for: 10 -> 11; matrix products, arithmetic and copies ran while one was open for 3% -> 3% of each run, Pallas kernels for 4% -> 7%
where the time goes in v8:
time: 210 us
  waiting for transfers between devices  77.2 us (37%)
  blocking collectives  46.6 us (22%)
  starting transfers between devices  38.4 us (18%)
  Pallas kernels  17.9 us (9%)
  between operations  13.6 us (6%)
  local copies, waits for them, and re-layouts  8.02 us (4%)
  matrix products  5.87 us (3%)
    ppermute x18, waiting for transfers between devices, shift(): return lax.ppermute(x, axes, pairs)  69.7 us
    all_to_all x1, blocking collectives, per_device(): lax.all_to_all(tiles, ('xh', 'y'), split_axis=0, concat_axis=0, tiled=True)  25.5 us
    ppermute x18, starting transfers between devices, shift(): return lax.ppermute(x, axes, pairs)  21.8 us
    all_to_all x1, blocking collectives, spread(): lax.all_to_all(jnp.broadcast_to(x[None], (count,) + x.shape), axes, split...  21.2 us
    pallas_call x8, Pallas kernels, call(): pl.pallas_call(kernel, out_shape=out, in_specs=specs, out_specs=jax.tree....  13.6 us
    all_to_all x1, starting transfers between devices, per_device(): lax.all_to_all(partial.reshape(16, 64, 512), ('xh', 'z'), split_axis=0, c...  9.82 us
    unnamed x36, local copies, waits for them, and re-layouts  7.95 us
    all_to_all x1, starting transfers between devices, per_device(): lax.all_to_all(copies, 'z', split_axis=0, concat_axis=0, tiled=True)  6.83 us
  transfers between devices with their start and end apart: 21, of which 11 were waited for; matrix products, arithmetic and copies ran while one was open for 3% of the time, Pallas kernels for 7%

profile of v8, /device:TPU:24, one launch (start us, length us, event | category | flops | bytes accessed | tf_op | source)
XLA Modules:
  0.0 209.5 jit_solution(6721046192719342059)
XLA Ops:
  8.5 4.3 %pick.1 = (bf16[216,1024]{1,0:T(8,128)(2,1)}, bf16[216,512]{1,0:T(8,128)(2,1)}, bf16[216,512]{1,0:T(8,128)(2,1)}, bf16[216,512]{1,0:T(8,128)(2,1)}, bf16[216,512]{1,0:T(8,128)(2,1)}) custom-call(s32[9]{0:T(128)} %pad_add_fusion.s_ref, bf16[216,13824]{1,0:T(8,128)(2,1)} %refs_7_.1, bf16[216,13824]{1,0:T(8,128)(2,1)} %refs_7_.1, bf16[216,13824]{1,0:T(8,128)(2,1)} %refs_7_.1, ...), custom_call_target="tpu_custom_call" | custom-call | tf_op jit(solution)/shard_map/pick/pallas_call | solution.py:79
  13.5 2.5 %collective-permute-start = (bf16[216,1024]{1,0:T(8,128)(2,1)}, bf16[216,1024]{1,0:T(8,128)(2,1)S(1)}, u32[]{:S(2)}, u32[]{:S(2)}) collective-permute-start(bf16[216,1024]{1,0:T(8,128)(2,1)} %get-tuple-element.12.c0), channel_id=1, source_target_pairs={{0,1},{1,2},{2,3},{3,0},{4,5},{5,6},{6,7},{7,4},{8,9},{9,10},{10,1... | collective-permute-start | bytes 1327112 | tf_op jit(solution)/shard_map/ppermute | solution.py:34
  18.2 15.9 %collective-permute-done.6.b1 = bf16[80,2560]{1,0:T(8,128)(2,1)S(1)} collective-permute-done((bf16[80,2560]{1,0:T(8,128)(2,1)S(1)}, bf16[80,2560]{1,0:T(8,128)(2,1)S(1)}, u32[]{:S(2)}, u32[]{:S(2)}) %collective-permute-start.6) | collective-permute-done | bytes 409632 | tf_op jit(solution)/shard_map/ppermute | solution.py:34
  34.9 2.8 %collective-permute-start.8 = (bf16[160,2560]{1,0:T(8,128)(2,1)S(1)}, bf16[160,2560]{1,0:T(8,128)(2,1)S(1)}, u32[]{:S(2)}, u32[]{:S(2)}) collective-permute-start(bf16[160,2560]{1,0:T(8,128)(2,1)S(1)} %join.1.near), channel_id=1, source_target_pairs={{0,132},{4,128},{128,4},{132,0},{1,133},{5,129},{129,5},{133,1},{2... | collective-permute-start | bytes 2457608 | tf_op jit(solution)/shard_map/ppermute | solution.py:34
  38.7 3.0 %collective-permute-start.3 = (bf16[216,512]{1,0:T(8,128)(2,1)S(1)}, bf16[216,512]{1,0:T(8,128)(2,1)S(1)}, u32[]{:S(2)}, u32[]{:S(2)}) collective-permute-start(bf16[216,512]{1,0:T(8,128)(2,1)S(1)} %copy-done.17), channel_id=1, source_target_pairs={{0,1},{1,2},{2,3},{3,0},{4,5},{5,6},{6,7},{7,4},{8,9},{9,10},{10,1... | collective-permute-start | bytes 663560 | tf_op jit(solution)/shard_map/ppermute | solution.py:34
  42.1 3.0 %collective-permute-done.3.g1 = bf16[216,512]{1,0:T(8,128)(2,1)S(1)} collective-permute-done((bf16[216,512]{1,0:T(8,128)(2,1)S(1)}, bf16[216,512]{1,0:T(8,128)(2,1)S(1)}, u32[]{:S(2)}, u32[]{:S(2)}) %collective-permute-start.3) | collective-permute-done | bytes 221216 | tf_op jit(solution)/shard_map/ppermute | solution.py:34
  45.1 2.0 collective-permute-start.5
  47.1 15.4 %collective-permute-done.4.g2 = bf16[216,512]{1,0:T(8,128)(2,1)S(1)} collective-permute-done((bf16[216,512]{1,0:T(8,128)(2,1)S(1)}, bf16[216,512]{1,0:T(8,128)(2,1)S(1)}, u32[]{:S(2)}, u32[]{:S(2)}) %collective-permute-start.4) | collective-permute-done | bytes 221216 | tf_op jit(solution)/shard_map/ppermute | solution.py:34
  64.3 2.3 %grads.1.refs_0_ = bf16[1024,512]{1,0:T(8,128)(2,1)} custom-call(bf16[216,1024]{1,0:T(8,128)(2,1)S(1)} %copy-done.11, bf16[216,1024]{1,0:T(8,128)(2,1)S(1)} %collective-permute-done.refs_0_.c1, bf16[216,1024]{1,0:T(8,128)(2,1)S(1)} %collective-permute-done.1.refs_1_.c2, bf16[216,1024]{1,0:T(8,128)(2,1)S(1)} %collective-permute-done.2.c3, ...), custom_call_target="tpu_custom_call" | custom-call | flops 1 | bytes 1 | tf_op jit(solution)/shard_map/grads/pallas_call | solution.py:177
  70.3 9.8 %all-to-all-start = ((bf16[16,64,512]{2,1,0:T(8,128)(2,1)}), bf16[16,64,512]{2,1,0:T(8,128)(2,1)S(1)}, u32[]{:S(2)}, u32[]{:S(2)}) async-start(bf16[16,64,512]{2,1,0:T(8,128)(2,1)} %bitcast.3), calls=%async_computation | async-start | bytes 2097152 | tf_op jit(solution)/shard_map/all_to_all | solution.py:209
  80.1 2.7 %collective-permute-start.11 = (bf16[80,2560]{1,0:T(8,128)(2,1)}, bf16[80,2560]{1,0:T(8,128)(2,1)S(1)}, u32[]{:S(2)}, u32[]{:S(2)}) collective-permute-start(bf16[80,2560]{1,0:T(8,128)(2,1)} %copy-done.12), channel_id=1, source_target_pairs={{0,1},{1,2},{2,3},{3,0},{4,5},{5,6},{6,7},{7,4},{8,9},{9,10},{10,1... | collective-permute-start | bytes 1228808 | tf_op jit(solution)/shard_map/ppermute | solution.py:34
  83.1 9.8 %collective-permute-done.11.b3 = bf16[80,2560]{1,0:T(8,128)(2,1)S(1)} collective-permute-done((bf16[80,2560]{1,0:T(8,128)(2,1)}, bf16[80,2560]{1,0:T(8,128)(2,1)S(1)}, u32[]{:S(2)}, u32[]{:S(2)}) %collective-permute-start.11) | collective-permute-done | bytes 409632 | tf_op jit(solution)/shard_map/ppermute | solution.py:34
  93.0 8.0 %collective-permute-done.12.far3 = bf16[80,2560]{1,0:T(8,128)(2,1)S(1)} collective-permute-done((bf16[80,2560]{1,0:T(8,128)(2,1)S(1)}, bf16[80,2560]{1,0:T(8,128)(2,1)S(1)}, u32[]{:S(2)}, u32[]{:S(2)}) %collective-permute-start.12) | collective-permute-done | bytes 409632 | tf_op jit(solution)/shard_map/ppermute | solution.py:34
  101.0 1.7 copy-done.2
  104.7 7.7 %acts.1 = (f32[640,256]{1,0:T(8,128)S(1)}, f32[640,256]{1,0:T(8,128)S(1)}) custom-call(s32[1]{0:T(128)} %bitcast.2.s_ref.core_ref, bf16[256,5120]{1,0:T(8,128)(2,1)S(1)} %copy-done.2, bf16[256,2560]{1,0:T(8,128)(2,1)} %collective-permute-done.10.sib, bf16[80,2560]{1,0:T(8,128)(2,1)S(1)} %copy-done.9, bf16[80,2560]{1,0:T(8,128)(2,1)S(1)} %copy-done.7, ...), custom_call_target="tpu_custom_call" | custom-call | flops 1 | bytes 1 | tf_op jit(solution)/shard_map/acts/pallas_call | solution.py:177
  112.5 2.1 collective-permute-done.13.b
  116.2 6.8 %all-to-all-start.1 = ((bf16[8,64,512]{2,1,0:T(8,128)(2,1)}), bf16[8,64,512]{2,1,0:T(8,128)(2,1)S(1)}, u32[]{:S(2)}, u32[]{:S(2)}) async-start(bf16[8,64,512]{2,1,0:T(8,128)(2,1)} %copy-done.5), calls=%async_computation.1 | async-start | bytes 1048576 | tf_op jit(solution)/shard_map/all_to_all | solution.py:216
  123.0 3.0 %collective-permute-start.14 = (bf16[640,256]{1,0:T(8,128)(2,1)S(1)}, bf16[640,256]{1,0:T(8,128)(2,1)S(1)}, u32[]{:S(2)}, u32[]{:S(2)}) collective-permute-start(bf16[640,256]{1,0:T(8,128)(2,1)S(1)} %add.24.refs_0_.ra), channel_id=1, source_target_pairs={{0,4},{4,0},{1,5},{5,1},{2,6},{6,2},{3,7},{7,3},{8,12},{12,8},{9,1... | collective-permute-start | bytes 983048 | tf_op jit(solution)/shard_map/ppermute | solution.py:34
  126.0 8.0 %collective-permute-done.14.rb = bf16[640,256]{1,0:T(8,128)(2,1)S(1)} collective-permute-done((bf16[640,256]{1,0:T(8,128)(2,1)S(1)}, bf16[640,256]{1,0:T(8,128)(2,1)S(1)}, u32[]{:S(2)}, u32[]{:S(2)}) %collective-permute-start.14) | collective-permute-done | bytes 327712 | tf_op jit(solution)/shard_map/ppermute | solution.py:34
  134.0 6.8 %all-to-all-done.1 = bf16[8,64,512]{2,1,0:T(8,128)(2,1)S(1)} async-done(((bf16[8,64,512]{2,1,0:T(8,128)(2,1)}), bf16[8,64,512]{2,1,0:T(8,128)(2,1)S(1)}, u32[]{:S(2)}, u32[]{:S(2)}) %all-to-all-start.1) | async-done | bytes 524320 | tf_op jit(solution)/shard_map/all_to_all | solution.py:216
  142.2 25.5 %all_to_all.20.parts = bf16[8,2,80,512]{3,2,1,0:T(8,128)(2,1)S(1)} all-to-all(bf16[8,2,80,512]{3,2,1,0:T(8,128)(2,1)S(1)} %seq.1), channel_id=1, replica_groups=mesh['xl'=2,'core'=2,'z'=8,'xh'=2,'y'=4] {'xh','y'}, dimensions={0} | all-to-all | bytes 2621440 | tf_op jit(solution)/shard_map/all_to_all | solution.py:219
  167.8 2.0 collective-permute-start.16
  171.3 5.0 %collective-permute-done.16 = bf16[2,80,1024]{2,1,0:T(8,128)(2,1)S(1)} collective-permute-done((bf16[2,80,1024]{2,1,0:T(8,128)(2,1)S(1)}, bf16[2,80,1024]{2,1,0:T(8,128)(2,1)S(1)}, u32[]{:S(2)}, u32[]{:S(2)}) %collective-permute-start.16) | collective-permute-done | bytes 327712 | tf_op jit(solution)/shard_map/ppermute | solution.py:34
  180.8 21.2 %all_to_all.21 = f32[64,8,8]{2,1,0:T(8,128)S(1)} all-to-all(f32[64,8,8]{2,1,0:T(8,128)S(1)} %broadcast_in_dim.22), channel_id=1, replica_groups=mesh['xl'=2,'core'=2,'z'=8,'xh'=2,'y'=4] {'z','xh','y'}, dimensions={0} | all-to-all | bytes 32768 | tf_op jit(solution)/shard_map/all_to_all | solution.py:38
  (78 shorter events, 24.5 us)
Async XLA Ops:
  6.5 163.3 %copy-start = (bf16[8,80,1024]{2,1,0:T(8,128)(2,1)S(1)}, bf16[8,80,1024]{2,1,0:T(8,128)(2,1)}, u32[]{:S(2)}) copy-start(bf16[8,80,1024]{2,1,0:T(8,128)(2,1)} %param.13) | copy-start | bytes 3932164
  6.5 60.8 %all-gather.2.cloned.1.call-start = ((), (), s32[]{:S(2)}) async-start(), calls=%async_computation.4 | async-start | bytes 2949120 | tf_op jit(solution)/shard_map/all_gather | solution.py:194
  12.8 22.1 %collective-permute-start.1 = (bf16[216,1024]{1,0:T(8,128)(2,1)}, bf16[216,1024]{1,0:T(8,128)(2,1)S(1)}, u32[]{:S(2)}, u32[]{:S(2)}) collective-permute-start(bf16[216,1024]{1,0:T(8,128)(2,1)} %get-tuple-element.12.c0), channel_id=1, source_target_pairs={{0,3},{1,0},{2,1},{3,2},{4,7},{5,4},{6,5},{7,6},{8,11},{9,8},{10,9... | collective-permute-start | bytes 1327112 | tf_op jit(solution)/shard_map/ppermute | solution.py:34
  13.5 21.4 %collective-permute-start = (bf16[216,1024]{1,0:T(8,128)(2,1)}, bf16[216,1024]{1,0:T(8,128)(2,1)S(1)}, u32[]{:S(2)}, u32[]{:S(2)}) collective-permute-start(bf16[216,1024]{1,0:T(8,128)(2,1)} %get-tuple-element.12.c0), channel_id=1, source_target_pairs={{0,1},{1,2},{2,3},{3,0},{4,5},{5,6},{6,7},{7,4},{8,9},{9,10},{10,1... | collective-permute-start | bytes 1327112 | tf_op jit(solution)/shard_map/ppermute | solution.py:34
  16.0 48.2 %copy-start.8 = (bf16[80,2560]{1,0:T(8,128)(2,1)}, bf16[80,2560]{1,0:T(8,128)(2,1)S(1)}, u32[]{:S(2)}) copy-start(bf16[80,2560]{1,0:T(8,128)(2,1)S(1)} %halve.1.b0) | copy-start | bytes 1228804
  16.1 48.2 %copy-start.11 = (bf16[216,1024]{1,0:T(8,128)(2,1)S(1)}, bf16[216,1024]{1,0:T(8,128)(2,1)}, u32[]{:S(2)}) copy-start(bf16[216,1024]{1,0:T(8,128)(2,1)} %get-tuple-element.12.c0) | copy-start | bytes 1327108
  16.1 18.0 %collective-permute-start.6 = (bf16[80,2560]{1,0:T(8,128)(2,1)S(1)}, bf16[80,2560]{1,0:T(8,128)(2,1)S(1)}, u32[]{:S(2)}, u32[]{:S(2)}) collective-permute-start(bf16[80,2560]{1,0:T(8,128)(2,1)S(1)} %halve.1.b0), channel_id=1, source_target_pairs={{0,1},{1,2},{2,3},{3,0},{4,5},{5,6},{6,7},{7,4},{8,9},{9,10},{10,1... | collective-permute-start | bytes 1228808 | tf_op jit(solution)/shard_map/ppermute | solution.py:34
  16.9 18.0 %collective-permute-start.7 = (bf16[80,2560]{1,0:T(8,128)(2,1)S(1)}, bf16[80,2560]{1,0:T(8,128)(2,1)S(1)}, u32[]{:S(2)}, u32[]{:S(2)}) collective-permute-start(bf16[80,2560]{1,0:T(8,128)(2,1)S(1)} %halve.1.b0), channel_id=1, source_target_pairs={{0,3},{1,0},{2,1},{3,2},{4,7},{5,4},{6,5},{7,6},{8,11},{9,8},{10,9... | collective-permute-start | bytes 1228808 | tf_op jit(solution)/shard_map/ppermute | solution.py:34
  34.9 29.3 %collective-permute-start.8 = (bf16[160,2560]{1,0:T(8,128)(2,1)S(1)}, bf16[160,2560]{1,0:T(8,128)(2,1)S(1)}, u32[]{:S(2)}, u32[]{:S(2)}) collective-permute-start(bf16[160,2560]{1,0:T(8,128)(2,1)S(1)} %join.1.near), channel_id=1, source_target_pairs={{0,132},{4,128},{128,4},{132,0},{1,133},{5,129},{129,5},{133,1},{2... | collective-permute-start | bytes 2457608 | tf_op jit(solution)/shard_map/ppermute | solution.py:34
  38.7 6.4 %collective-permute-start.3 = (bf16[216,512]{1,0:T(8,128)(2,1)S(1)}, bf16[216,512]{1,0:T(8,128)(2,1)S(1)}, u32[]{:S(2)}, u32[]{:S(2)}) collective-permute-start(bf16[216,512]{1,0:T(8,128)(2,1)S(1)} %copy-done.17), channel_id=1, source_target_pairs={{0,1},{1,2},{2,3},{3,0},{4,5},{5,6},{6,7},{7,4},{8,9},{9,10},{10,1... | collective-permute-start | bytes 663560 | tf_op jit(solution)/shard_map/ppermute | solution.py:34
  41.7 22.6 %collective-permute-start.2 = (bf16[216,1024]{1,0:T(8,128)(2,1)S(1)}, bf16[216,1024]{1,0:T(8,128)(2,1)S(1)}, u32[]{:S(2)}, u32[]{:S(2)}) collective-permute-start(bf16[216,1024]{1,0:T(8,128)(2,1)S(1)} %collective-permute-done.1.refs_1_.c2), channel_id=1, source_target_pairs={{0,3},{1,0},{2,1},{3,2},{4,7},{5,4},{6,5},{7,6},{8,11},{9,8},{10,9... | collective-permute-start | bytes 1327112 | tf_op jit(solution)/shard_map/ppermute | solution.py:34
  41.7 22.6 %collective-permute-start.9 = (bf16[80,2560]{1,0:T(8,128)(2,1)S(1)}, bf16[80,2560]{1,0:T(8,128)(2,1)S(1)}, u32[]{:S(2)}, u32[]{:S(2)}) collective-permute-start(bf16[80,2560]{1,0:T(8,128)(2,1)S(1)} %halve.1.b0), channel_id=1, source_target_pairs={{0,132},{4,128},{128,4},{132,0},{1,133},{5,129},{129,5},{133,1},{2... | collective-permute-start | bytes 1228808 | tf_op jit(solution)/shard_map/ppermute | solution.py:34
  42.1 20.4 %collective-permute-start.4 = (bf16[216,512]{1,0:T(8,128)(2,1)S(1)}, bf16[216,512]{1,0:T(8,128)(2,1)S(1)}, u32[]{:S(2)}, u32[]{:S(2)}) collective-permute-start(bf16[216,512]{1,0:T(8,128)(2,1)S(1)} %copy-done.16), channel_id=1, source_target_pairs={{0,3},{1,0},{2,1},{3,2},{4,7},{5,4},{6,5},{7,6},{8,11},{9,8},{10,9... | collective-permute-start | bytes 663560 | tf_op jit(solution)/shard_map/ppermute | solution.py:34
  45.1 17.4 %collective-permute-start.5 = (bf16[216,512]{1,0:T(8,128)(2,1)S(1)}, bf16[216,512]{1,0:T(8,128)(2,1)S(1)}, u32[]{:S(2)}, u32[]{:S(2)}) collective-permute-start(bf16[216,512]{1,0:T(8,128)(2,1)S(1)} %copy-done.15), channel_id=1, source_target_pairs={{0,2},{1,3},{2,0},{3,1},{4,6},{5,7},{6,4},{7,5},{8,10},{9,11},{10,... | collective-permute-start | bytes 663560 | tf_op jit(solution)/shard_map/ppermute | solution.py:34
  70.3 30.7 %collective-permute-start.10 = (bf16[256,2560]{1,0:T(8,128)(2,1)}, bf16[256,2560]{1,0:T(8,128)(2,1)}, u32[]{:S(2)}, u32[]{:S(2)}) collective-permute-start(bf16[256,2560]{1,0:T(8,128)(2,1)} %cut.1), channel_id=1, source_target_pairs={{0,64},{64,0},{1,65},{65,1},{2,66},{66,2},{3,67},{67,3},{4,68},{68... | collective-permute-start | bytes 3932168 | tf_op jit(solution)/shard_map/ppermute | solution.py:34
  70.3 44.4 %all-to-all-start = ((bf16[16,64,512]{2,1,0:T(8,128)(2,1)}), bf16[16,64,512]{2,1,0:T(8,128)(2,1)S(1)}, u32[]{:S(2)}, u32[]{:S(2)}) async-start(bf16[16,64,512]{2,1,0:T(8,128)(2,1)} %bitcast.3), calls=%async_computation | async-start | bytes 2097152 | tf_op jit(solution)/shard_map/all_to_all | solution.py:209
  80.1 12.9 %collective-permute-start.11 = (bf16[80,2560]{1,0:T(8,128)(2,1)}, bf16[80,2560]{1,0:T(8,128)(2,1)S(1)}, u32[]{:S(2)}, u32[]{:S(2)}) collective-permute-start(bf16[80,2560]{1,0:T(8,128)(2,1)} %copy-done.12), channel_id=1, source_target_pairs={{0,1},{1,2},{2,3},{3,0},{4,5},{5,6},{6,7},{7,4},{8,9},{9,10},{10,1... | collective-permute-start | bytes 1228808 | tf_op jit(solution)/shard_map/ppermute | solution.py:34
  82.9 18.1 %collective-permute-start.12 = (bf16[80,2560]{1,0:T(8,128)(2,1)S(1)}, bf16[80,2560]{1,0:T(8,128)(2,1)S(1)}, u32[]{:S(2)}, u32[]{:S(2)}) collective-permute-start(bf16[80,2560]{1,0:T(8,128)(2,1)S(1)} %slice.4), channel_id=1, source_target_pairs={{0,1},{1,2},{2,3},{3,0},{4,5},{5,6},{6,7},{7,4},{8,9},{9,10},{10,1... | collective-permute-start | bytes 1228808 | tf_op jit(solution)/shard_map/ppermute | solution.py:34
  112.4 2.2 %collective-permute-start.13 = (f32[640,256]{1,0:T(8,128)S(1)}, f32[640,256]{1,0:T(8,128)S(1)}, u32[]{:S(2)}, u32[]{:S(2)}) collective-permute-start(f32[640,256]{1,0:T(8,128)S(1)} %get-tuple-element.18), channel_id=1, source_target_pairs={{0,64},{64,0},{1,65},{65,1},{2,66},{66,2},{3,67},{67,3},{4,68},{68... | collective-permute-start | bytes 1966088 | tf_op jit(solution)/shard_map/ppermute | solution.py:34
  116.2 24.6 %all-to-all-start.1 = ((bf16[8,64,512]{2,1,0:T(8,128)(2,1)}), bf16[8,64,512]{2,1,0:T(8,128)(2,1)S(1)}, u32[]{:S(2)}, u32[]{:S(2)}) async-start(bf16[8,64,512]{2,1,0:T(8,128)(2,1)} %copy-done.5), calls=%async_computation.1 | async-start | bytes 1048576 | tf_op jit(solution)/shard_map/all_to_all | solution.py:216
  123.0 11.0 %collective-permute-start.14 = (bf16[640,256]{1,0:T(8,128)(2,1)S(1)}, bf16[640,256]{1,0:T(8,128)(2,1)S(1)}, u32[]{:S(2)}, u32[]{:S(2)}) collective-permute-start(bf16[640,256]{1,0:T(8,128)(2,1)S(1)} %add.24.refs_0_.ra), channel_id=1, source_target_pairs={{0,4},{4,0},{1,5},{5,1},{2,6},{6,2},{3,7},{7,3},{8,12},{12,8},{9,1... | collective-permute-start | bytes 983048 | tf_op jit(solution)/shard_map/ppermute | solution.py:34
  167.8 8.5 %collective-permute-start.16 = (bf16[2,80,1024]{2,1,0:T(8,128)(2,1)S(1)}, bf16[2,80,1024]{2,1,0:T(8,128)(2,1)S(1)}, u32[]{:S(2)}, u32[]{:S(2)}) collective-permute-start(bf16[2,80,1024]{2,1,0:T(8,128)(2,1)S(1)} %sums.1), channel_id=1, source_target_pairs={{0,128},{128,0},{1,129},{129,1},{2,130},{130,2},{3,131},{131,3},{4... | collective-permute-start | bytes 983048 | tf_op jit(solution)/shard_map/ppermute | solution.py:34
  169.9 7.9 %collective-permute-start.15 = (bf16[2,80,1024]{2,1,0:T(8,128)(2,1)S(1)}, bf16[2,80,1024]{2,1,0:T(8,128)(2,1)S(1)}, u32[]{:S(2)}, u32[]{:S(2)}) collective-permute-start(bf16[2,80,1024]{2,1,0:T(8,128)(2,1)S(1)} %sums.1), channel_id=1, source_target_pairs={{0,64},{64,0},{1,65},{65,1},{2,66},{66,2},{3,67},{67,3},{4,68},{68... | collective-permute-start | bytes 983048 | tf_op jit(solution)/shard_map/ppermute | solution.py:34
  176.3 2.9 %collective-permute-start.17 = (bf16[2,80,1024]{2,1,0:T(8,128)(2,1)S(1)}, bf16[2,80,1024]{2,1,0:T(8,128)(2,1)S(1)}, u32[]{:S(2)}, u32[]{:S(2)}) collective-permute-start(bf16[2,80,1024]{2,1,0:T(8,128)(2,1)S(1)} %collective-permute-done.16), channel_id=1, source_target_pairs={{0,64},{64,0},{1,65},{65,1},{2,66},{66,2},{3,67},{67,3},{4,68},{68... | collective-permute-start | bytes 983048 | tf_op jit(solution)/shard_map/ppermute | solution.py:34
  (15 other events, 172.0 us)
Sparse Core Ops, SparseCore 0:
  9.1 44.9 all-gather.1

commit v9 on v8

--- a/solution.py
+++ b/solution.py
@@ -108,14 +108,9 @@
     o_ref[...] = a_ref[:, pl.ds(pl.multiple_of((1 - core_ref[0]) * half, 128), half)]
 
 
-def join_kernel(b1, b2, *refs):
-    o_ref = refs[-1]
-    o_ref[:80, :] = b1[...]
-    o_ref[80:, :] = b2[...]
-
-
-def grads_kernel(c0, c1, c2, c3, g0, g1, g2, g3, *refs):
-    o_ref = refs[-1]
+def grads_kernel(c0, c1, c2, c3, g0, g1, g2, g3, b_own, b_far, o_ref, b0):
+    b0[:80, :] = b_own[...]
+    b0[80:, :] = b_far[...]
     for part in range(4):
         ks = slice(part * 256, part * 256 + 256)
         total = dot(c0[:, ks], g0[...], 0, 0) + dot(c1[:, ks], g1[...], 0, 0)
@@ -136,12 +131,13 @@
         o_ref[n] = total
 
 
-def acts_kernel(core_ref, a_ref, sib, b0, far0, near, far, b3, far3, keep, send):
+def acts_kernel(core_ref, a_ref, sib, b0, b1, b2, b3a, b3b, keep, send):
     half = sib.shape[1]
     mine = a_ref[:, pl.ds(pl.multiple_of(core_ref[0] * half, 128), half)]
     for tokens, out in ((sib[...], send), (mine, keep)):
-        for n, (b, r) in enumerate(((b0, 0), (far0, 0), (near, 0), (far, 0), (near, 80), (far, 80), (b3, 0), (far3, 0))):
-            out[n * 80 : n * 80 + 80, :] = dot(b[r : r + 80, :], tokens, 1, 1)
+        for n, b in enumerate((b0, b1, b2)):
+            out[n * 160 : n * 160 + 160, :] = dot(b[...], tokens, 1, 1)
+        out[480:, :] = dot(b3a[...], tokens[:, : half // 2], 1, 1) + dot(b3b[...], tokens[:, half // 2 :], 1, 1)
 
 
 def add_kernel(a, b, o_ref):
@@ -193,26 +189,24 @@
     xl, core, xh, y = (lax.axis_index(a).astype(jnp.int32) for a in ("xl", "core", "xh", "y"))
     acts = lax.all_gather(activations, "z", axis=0, tiled=True)
     half = basis_in.shape[1] // 2
-    b0 = halve(core, basis_in)
-    b1, b2 = shift(b0, y=1), shift(b0, y=-1)
-    far0 = shift(b0, xl=1, xh=1)
-
     chosen, g0, g1, g2, g3 = pick(block_ids, y, basis_out, out_grads)
     c1, c2 = shift(chosen, y=1), shift(chosen, y=-1)
-    near = call(join_kernel, arr(160, half), "join", [b1, b2], (), [c1, c2])
-    far = shift(near, xl=1, xh=1)
     g1, g2, g3 = shift(g1, y=1), shift(g2, y=-1), shift(g3, y=2)
     c3 = shift(c2, y=-1)
-    partial = call(grads_kernel, arr(1024, 512), "grads", [chosen, c1, c2, c3, g0, g1, g2, g3], (), [far, far0])
-    b3 = shift(b1, y=1)
-    far3 = shift(far[:80], y=1)
+    b_own = halve(core, basis_in)
+    b_far = shift(b_own, xl=1, xh=1)
+    partial, b0 = call(
+        grads_kernel, [arr(1024, 512), arr(160, half)], "grads", [chosen, c1, c2, c3, g0, g1, g2, g3, b_own, b_far]
+    )
+    b1, b2 = shift(b0, y=1), shift(b0, y=-1)
+    b3a, b3b = shift(b1[:, : half // 2], y=1), shift(b2[:, half // 2 :], y=-1)
     parts = lax.all_to_all(partial.reshape(16, 64, 512), ("xh", "z"), split_axis=0, concat_axis=0, tiled=True)
     wide = jax.ShapeDtypeStruct((640, 256), F32)
-    sib = shift(call(cut_kernel, arr(256, half), "cut", [acts], [core[None]], [partial]), core=1)
-    keep, send = call(acts_kernel, [wide, wide], "acts", [acts, sib, b0, far0, near, far, b3, far3], [core[None]])
+    sib = shift(call(cut_kernel, arr(256, half), "cut", [acts], [core[None]], [b1, b2]), core=1)
+    keep, send = call(acts_kernel, [wide, wide], "acts", [acts, sib, b0, b1, b2, b3a, b3b], [core[None]])
     ra = call(add_kernel, arr(640, 256), "add", [keep, shift(send, core=1)])
     rb = shift(ra, xh=1)
-    copies = call(live_kernel, arr(8, 64, 512), "live", [parts], [y[None], seq_lens], [ra])
+    copies = call(live_kernel, arr(8, 64, 512), "live", [parts], [y[None], seq_lens], [send])
     rotated = lax.all_to_all(copies, "z", split_axis=0, concat_axis=0, tiled=True).reshape(512, 512)
 
     tiles = call(seq_kernel, arr(8, 2, 80, 512), "seq", [ra, rb, rotated], [xh[None], y[None]])

time: 210 us -> 189 us (0.900)
  waiting for transfers between devices: 77.2 us -> 62.4 us
  local copies, waits for them, and re-layouts: 8.02 us -> 3.7 us
    ppermute x18 -> x17, waiting for transfers between devices: 69.7 us -> 46.8 us  [shift(): return lax.ppermute(x, axes, pairs)]
    all_to_all x1, waiting for transfers between devices: 6.82 us -> 15 us  [per_device(): lax.all_to_all(copies, 'z', split_axis=0, concat_axis=0, tiled=True)]
    unnamed x36 -> x20, local copies, waits for them, and re-layouts: 7.95 us -> 3.61 us
    all_to_all x1, starting transfers between devices: 6.83 us -> 9.15 us  [per_device(): lax.all_to_all(copies, 'z', split_axis=0, concat_axis=0, tiled=True)]
    ppermute x18 -> x17, starting transfers between devices: 21.8 us -> 19.9 us  [shift(): return lax.ppermute(x, axes, pairs)]
    pallas_call x8 -> x7, Pallas kernels: 13.6 us -> 12 us  [call(): pl.pallas_call(kernel, out_shape=out, in_specs=specs, out_specs=jax.tree....]
  transfers between devices with their start and end apart: 21 -> 20, of which waited for: 11 -> 8; matrix products, arithmetic and copies ran while one was open for 3% -> 3% of each run, Pallas kernels for 7% -> 8%
where the time goes in v9:
time: 189 us
  waiting for transfers between devices  62.4 us (33%)
  blocking collectives  44.7 us (24%)
  starting transfers between devices  40.2 us (21%)
  Pallas kernels  16.3 us (9%)
  between operations  13.6 us (7%)
  matrix products  5.86 us (3%)
  local copies, waits for them, and re-layouts  3.7 us (2%)
  other arithmetic  1.92 us (1%)
    ppermute x17, waiting for transfers between devices, shift(): return lax.ppermute(x, axes, pairs)  46.8 us
    all_to_all x1, blocking collectives, per_device(): lax.all_to_all(tiles, ('xh', 'y'), split_axis=0, concat_axis=0, tiled=True)  24.5 us
    all_to_all x1, blocking collectives, spread(): lax.all_to_all(jnp.broadcast_to(x[None], (count,) + x.shape), axes, split...  20.2 us
    ppermute x17, starting transfers between devices, shift(): return lax.ppermute(x, axes, pairs)  19.9 us
    all_to_all x1, waiting for transfers between devices, per_device(): lax.all_to_all(copies, 'z', split_axis=0, concat_axis=0, tiled=True)  15 us
    pallas_call x7, Pallas kernels, call(): pl.pallas_call(kernel, out_shape=out, in_specs=specs, out_specs=jax.tree....  12 us
    all_to_all x1, starting transfers between devices, per_device(): lax.all_to_all(partial.reshape(16, 64, 512), ('xh', 'z'), split_axis=0, c...  11.2 us
    all_to_all x1, starting transfers between devices, per_device(): lax.all_to_all(copies, 'z', split_axis=0, concat_axis=0, tiled=True)  9.15 us
  transfers between devices with their start and end apart: 20, of which 8 were waited for; matrix products, arithmetic and copies ran while one was open for 3% of the time, Pallas kernels for 8%

profile of v9, /device:TPU:24, one launch (start us, length us, event | category | flops | bytes accessed | tf_op | source)
XLA Modules:
  0.0 188.7 jit_solution(15931593817069808090)
XLA Ops:
  8.5 4.3 %pick.1 = (bf16[216,1024]{1,0:T(8,128)(2,1)}, bf16[216,512]{1,0:T(8,128)(2,1)}, bf16[216,512]{1,0:T(8,128)(2,1)}, bf16[216,512]{1,0:T(8,128)(2,1)}, bf16[216,512]{1,0:T(8,128)(2,1)}) custom-call(s32[9]{0:T(128)} %pad_add_fusion.s_ref, bf16[216,13824]{1,0:T(8,128)(2,1)} %refs_7_.1, bf16[216,13824]{1,0:T(8,128)(2,1)} %refs_7_.1, bf16[216,13824]{1,0:T(8,128)(2,1)} %refs_7_.1, ...), custom_call_target="tpu_custom_call" | custom-call | tf_op jit(solution)/shard_map/pick/pallas_call | solution.py:79
  13.5 2.5 %collective-permute-start.3 = (bf16[216,512]{1,0:T(8,128)(2,1)}, bf16[216,512]{1,0:T(8,128)(2,1)}, u32[]{:S(2)}, u32[]{:S(2)}) collective-permute-start(bf16[216,512]{1,0:T(8,128)(2,1)} %get-tuple-element.16), channel_id=1, source_target_pairs={{0,1},{1,2},{2,3},{3,0},{4,5},{5,6},{6,7},{7,4},{8,9},{9,10},{10,1... | collective-permute-start | bytes 663560 | tf_op jit(solution)/shard_map/ppermute | solution.py:34
  16.8 9.3 %collective-permute-done.1.c2 = bf16[216,1024]{1,0:T(8,128)(2,1)S(1)} collective-permute-done((bf16[216,1024]{1,0:T(8,128)(2,1)}, bf16[216,1024]{1,0:T(8,128)(2,1)S(1)}, u32[]{:S(2)}, u32[]{:S(2)}) %collective-permute-start.1) | collective-permute-done | bytes 442400 | tf_op jit(solution)/shard_map/ppermute | solution.py:34
  26.2 2.8 %collective-permute-start.6 = (bf16[80,2560]{1,0:T(8,128)(2,1)S(1)}, bf16[80,2560]{1,0:T(8,128)(2,1)S(1)}, u32[]{:S(2)}, u32[]{:S(2)}) collective-permute-start(bf16[80,2560]{1,0:T(8,128)(2,1)S(1)} %halve.1.b_own), channel_id=1, source_target_pairs={{0,132},{4,128},{128,4},{132,0},{1,133},{5,129},{129,5},{133,1},{2... | collective-permute-start | bytes 1228808 | tf_op jit(solution)/shard_map/ppermute | solution.py:34
  29.0 4.7 %collective-permute-start.5 = (bf16[216,512]{1,0:T(8,128)(2,1)}, bf16[216,512]{1,0:T(8,128)(2,1)S(1)}, u32[]{:S(2)}, u32[]{:S(2)}) collective-permute-start(bf16[216,512]{1,0:T(8,128)(2,1)} %get-tuple-element.18), channel_id=1, source_target_pairs={{0,2},{1,3},{2,0},{3,1},{4,6},{5,7},{6,4},{7,5},{8,10},{9,11},{10,... | collective-permute-start | bytes 663560 | tf_op jit(solution)/shard_map/ppermute | solution.py:34
  33.7 14.1 %collective-permute-done.4.g2 = bf16[216,512]{1,0:T(8,128)(2,1)S(1)} collective-permute-done((bf16[216,512]{1,0:T(8,128)(2,1)}, bf16[216,512]{1,0:T(8,128)(2,1)S(1)}, u32[]{:S(2)}, u32[]{:S(2)}) %collective-permute-start.4) | collective-permute-done | bytes 221216 | tf_op jit(solution)/shard_map/ppermute | solution.py:34
  47.9 3.3 %grads.1 = (bf16[1024,512]{1,0:T(8,128)(2,1)S(1)}, bf16[160,2560]{1,0:T(8,128)(2,1)}) custom-call(bf16[216,1024]{1,0:T(8,128)(2,1)S(1)} %copy-done.7, bf16[216,1024]{1,0:T(8,128)(2,1)S(1)} %collective-permute-done.c1, bf16[216,1024]{1,0:T(8,128)(2,1)S(1)} %collective-permute-done.1.c2, bf16[216,1024]{1,0:T(8,128)(2,1)} %collective-permute-done.2.c3, ...), custom_call_target="tpu_custom_call" | custom-call | flops 1 | bytes 1 | tf_op jit(solution)/shard_map/grads/pallas_call | solution.py:173
  52.2 2.0 %collective-permute-start.8 = (bf16[160,2560]{1,0:T(8,128)(2,1)}, bf16[160,2560]{1,0:T(8,128)(2,1)S(1)}, u32[]{:S(2)}, u32[]{:S(2)}) collective-permute-start(bf16[160,2560]{1,0:T(8,128)(2,1)} %get-tuple-element.19.b0), channel_id=1, source_target_pairs={{0,3},{1,0},{2,1},{3,2},{4,7},{5,4},{6,5},{7,6},{8,11},{9,8},{10,9... | collective-permute-start | bytes 2457608 | tf_op jit(solution)/shard_map/ppermute | solution.py:34
  54.2 11.2 %all-to-all-start = ((bf16[16,64,512]{2,1,0:T(8,128)(2,1)}), bf16[16,64,512]{2,1,0:T(8,128)(2,1)}, u32[]{:S(2)}, u32[]{:S(2)}) async-start(bf16[16,64,512]{2,1,0:T(8,128)(2,1)} %bitcast.26), calls=%async_computation | async-start | bytes 2097152 | tf_op jit(solution)/shard_map/all_to_all | solution.py:203
  65.4 3.1 %collective-permute-done.7.refs_0_.b1 = bf16[160,2560]{1,0:T(8,128)(2,1)S(1)} collective-permute-done((bf16[160,2560]{1,0:T(8,128)(2,1)}, bf16[160,2560]{1,0:T(8,128)(2,1)S(1)}, u32[]{:S(2)}, u32[]{:S(2)}) %collective-permute-start.7) | collective-permute-done | bytes 819232 | tf_op jit(solution)/shard_map/ppermute | solution.py:34
  68.4 1.6 collective-permute-done.8.refs_1_.b2
  70.0 1.7 copy-done.1
  72.0 1.8 collective-permute-start.10
  74.4 9.5 %collective-permute-done.10.b3a = bf16[160,1280]{1,0:T(8,128)(2,1)S(1)} collective-permute-done((bf16[160,1280]{1,0:T(8,128)(2,1)S(1)}, bf16[160,1280]{1,0:T(8,128)(2,1)S(1)}, u32[]{:S(2)}, u32[]{:S(2)}) %collective-permute-start.10) | collective-permute-done | bytes 409632 | tf_op jit(solution)/shard_map/ppermute | solution.py:34
  83.9 2.9 %collective-permute-done.11.b3b = bf16[160,1280]{1,0:T(8,128)(2,1)S(1)} collective-permute-done((bf16[160,1280]{1,0:T(8,128)(2,1)S(1)}, bf16[160,1280]{1,0:T(8,128)(2,1)S(1)}, u32[]{:S(2)}, u32[]{:S(2)}) %collective-permute-start.11) | collective-permute-done | bytes 409632 | tf_op jit(solution)/shard_map/ppermute | solution.py:34
  86.9 4.7 %acts.1 = (f32[640,256]{1,0:T(8,128)S(1)}, f32[640,256]{1,0:T(8,128)}) custom-call(s32[1]{0:T(128)} %bitcast.2.s_ref.core_ref, bf16[256,5120]{1,0:T(8,128)(2,1)S(1)} %copy-done.2, bf16[256,2560]{1,0:T(8,128)(2,1)S(1)} %collective-permute-done.9.sib, bf16[160,2560]{1,0:T(8,128)(2,1)} %get-tuple-element.19.b0, ...), custom_call_target="tpu_custom_call" | custom-call | flops 1 | bytes 1 | tf_op jit(solution)/shard_map/acts/pallas_call | solution.py:173
  92.4 2.3 %live.1 = bf16[8,64,512]{2,1,0:T(8,128)(2,1)} custom-call(s32[1]{0:T(128)} %bitcast.1.y_ref, s32[2]{0:T(128)S(1)} %copy-done.9, bf16[16,64,512]{2,1,0:T(8,128)(2,1)} %all-to-all-done.parts, f32[640,256]{1,0:T(8,128)} %get-tuple-element.21.refs_0_), custom_call_target="tpu_custom_call" | custom-call | flops 1 | bytes 1 | tf_op jit(solution)/shard_map/live/pallas_call | solution.py:173
  94.7 9.2 %all-to-all-start.1 = ((bf16[8,64,512]{2,1,0:T(8,128)(2,1)}), bf16[8,64,512]{2,1,0:T(8,128)(2,1)S(1)}, u32[]{:S(2)}, u32[]{:S(2)}) async-start(bf16[8,64,512]{2,1,0:T(8,128)(2,1)} %live.1), calls=%async_computation.1 | async-start | bytes 1048576 | tf_op jit(solution)/shard_map/all_to_all | solution.py:210
  104.0 3.1 %collective-permute-start.13 = (bf16[640,256]{1,0:T(8,128)(2,1)S(1)}, bf16[640,256]{1,0:T(8,128)(2,1)S(1)}, u32[]{:S(2)}, u32[]{:S(2)}) collective-permute-start(bf16[640,256]{1,0:T(8,128)(2,1)S(1)} %add.24.ra), channel_id=1, source_target_pairs={{0,4},{4,0},{1,5},{5,1},{2,6},{6,2},{3,7},{7,3},{8,12},{12,8},{9,1... | collective-permute-start | bytes 983048 | tf_op jit(solution)/shard_map/ppermute | solution.py:34
  107.1 15.0 %all-to-all-done.1 = bf16[8,64,512]{2,1,0:T(8,128)(2,1)S(1)} async-done(((bf16[8,64,512]{2,1,0:T(8,128)(2,1)}), bf16[8,64,512]{2,1,0:T(8,128)(2,1)S(1)}, u32[]{:S(2)}, u32[]{:S(2)}) %all-to-all-start.1) | async-done | bytes 524320 | tf_op jit(solution)/shard_map/all_to_all | solution.py:210
  123.4 24.5 %all_to_all.20.parts = bf16[8,2,80,512]{3,2,1,0:T(8,128)(2,1)S(1)} all-to-all(bf16[8,2,80,512]{3,2,1,0:T(8,128)(2,1)S(1)} %seq.1), channel_id=1, replica_groups=mesh['xl'=2,'core'=2,'z'=8,'xh'=2,'y'=4] {'xh','y'}, dimensions={0} | all-to-all | bytes 2621440 | tf_op jit(solution)/shard_map/all_to_all | solution.py:213
  150.3 6.1 %collective-permute-done.15 = bf16[2,80,1024]{2,1,0:T(8,128)(2,1)S(1)} collective-permute-done((bf16[2,80,1024]{2,1,0:T(8,128)(2,1)S(1)}, bf16[2,80,1024]{2,1,0:T(8,128)(2,1)S(1)}, u32[]{:S(2)}, u32[]{:S(2)}) %collective-permute-start.15) | collective-permute-done | bytes 327712 | tf_op jit(solution)/shard_map/ppermute | solution.py:34
  157.9 1.5 convolution_bitcast_fusion.2
  161.0 20.2 %all_to_all.21 = f32[64,8,8]{2,1,0:T(8,128)S(1)} all-to-all(f32[64,8,8]{2,1,0:T(8,128)S(1)} %broadcast_in_dim.22), channel_id=1, replica_groups=mesh['xl'=2,'core'=2,'z'=8,'xh'=2,'y'=4] {'z','xh','y'}, dimensions={0} | all-to-all | bytes 32768 | tf_op jit(solution)/shard_map/all_to_all | solution.py:38
  (60 shorter events, 13.7 us)
Async XLA Ops:
  6.5 142.3 %copy-start = (bf16[8,80,1024]{2,1,0:T(8,128)(2,1)S(1)}, bf16[8,80,1024]{2,1,0:T(8,128)(2,1)}, u32[]{:S(2)}) copy-start(bf16[8,80,1024]{2,1,0:T(8,128)(2,1)} %param.13) | copy-start | bytes 3932164
  6.5 63.5 %all-gather.2.cloned.1.call-start = ((), (), s32[]{:S(2)}) async-start(), calls=%async_computation.4 | async-start | bytes 2949120 | tf_op jit(solution)/shard_map/all_gather | solution.py:190
  12.8 35.1 %copy-start.7 = (bf16[216,1024]{1,0:T(8,128)(2,1)S(1)}, bf16[216,1024]{1,0:T(8,128)(2,1)}, u32[]{:S(2)}) copy-start(bf16[216,1024]{1,0:T(8,128)(2,1)} %get-tuple-element.14.c0) | copy-start | bytes 1327108
  12.8 13.3 %collective-permute-start.1 = (bf16[216,1024]{1,0:T(8,128)(2,1)}, bf16[216,1024]{1,0:T(8,128)(2,1)S(1)}, u32[]{:S(2)}, u32[]{:S(2)}) collective-permute-start(bf16[216,1024]{1,0:T(8,128)(2,1)} %get-tuple-element.14.c0), channel_id=1, source_target_pairs={{0,3},{1,0},{2,1},{3,2},{4,7},{5,4},{6,5},{7,6},{8,11},{9,8},{10,9... | collective-permute-start | bytes 1327112 | tf_op jit(solution)/shard_map/ppermute | solution.py:34
  13.5 15.5 %collective-permute-start.3 = (bf16[216,512]{1,0:T(8,128)(2,1)}, bf16[216,512]{1,0:T(8,128)(2,1)}, u32[]{:S(2)}, u32[]{:S(2)}) collective-permute-start(bf16[216,512]{1,0:T(8,128)(2,1)} %get-tuple-element.16), channel_id=1, source_target_pairs={{0,1},{1,2},{2,3},{3,0},{4,5},{5,6},{6,7},{7,4},{8,9},{9,10},{10,1... | collective-permute-start | bytes 663560 | tf_op jit(solution)/shard_map/ppermute | solution.py:34
  16.0 31.8 %collective-permute-start = (bf16[216,1024]{1,0:T(8,128)(2,1)}, bf16[216,1024]{1,0:T(8,128)(2,1)S(1)}, u32[]{:S(2)}, u32[]{:S(2)}) collective-permute-start(bf16[216,1024]{1,0:T(8,128)(2,1)} %get-tuple-element.14.c0), channel_id=1, source_target_pairs={{0,1},{1,2},{2,3},{3,0},{4,5},{5,6},{6,7},{7,4},{8,9},{9,10},{10,1... | collective-permute-start | bytes 1327112 | tf_op jit(solution)/shard_map/ppermute | solution.py:34
  26.1 21.7 %collective-permute-start.2 = (bf16[216,1024]{1,0:T(8,128)(2,1)S(1)}, bf16[216,1024]{1,0:T(8,128)(2,1)}, u32[]{:S(2)}, u32[]{:S(2)}) collective-permute-start(bf16[216,1024]{1,0:T(8,128)(2,1)S(1)} %collective-permute-done.1.c2), channel_id=1, source_target_pairs={{0,3},{1,0},{2,1},{3,2},{4,7},{5,4},{6,5},{7,6},{8,11},{9,8},{10,9... | collective-permute-start | bytes 1327112 | tf_op jit(solution)/shard_map/ppermute | solution.py:34
  26.1 21.8 %copy-start.8 = (bf16[216,512]{1,0:T(8,128)(2,1)S(1)}, bf16[216,512]{1,0:T(8,128)(2,1)}, u32[]{:S(2)}) copy-start(bf16[216,512]{1,0:T(8,128)(2,1)} %get-tuple-element.15.g0) | copy-start | bytes 663556
  26.2 21.7 %collective-permute-start.6 = (bf16[80,2560]{1,0:T(8,128)(2,1)S(1)}, bf16[80,2560]{1,0:T(8,128)(2,1)S(1)}, u32[]{:S(2)}, u32[]{:S(2)}) collective-permute-start(bf16[80,2560]{1,0:T(8,128)(2,1)S(1)} %halve.1.b_own), channel_id=1, source_target_pairs={{0,132},{4,128},{128,4},{132,0},{1,133},{5,129},{129,5},{133,1},{2... | collective-permute-start | bytes 1228808 | tf_op jit(solution)/shard_map/ppermute | solution.py:34
  29.0 18.8 %collective-permute-start.4 = (bf16[216,512]{1,0:T(8,128)(2,1)}, bf16[216,512]{1,0:T(8,128)(2,1)S(1)}, u32[]{:S(2)}, u32[]{:S(2)}) collective-permute-start(bf16[216,512]{1,0:T(8,128)(2,1)} %get-tuple-element.17), channel_id=1, source_target_pairs={{0,3},{1,0},{2,1},{3,2},{4,7},{5,4},{6,5},{7,6},{8,11},{9,8},{10,9... | collective-permute-start | bytes 663560 | tf_op jit(solution)/shard_map/ppermute | solution.py:34
  29.0 18.8 %collective-permute-start.5 = (bf16[216,512]{1,0:T(8,128)(2,1)}, bf16[216,512]{1,0:T(8,128)(2,1)S(1)}, u32[]{:S(2)}, u32[]{:S(2)}) collective-permute-start(bf16[216,512]{1,0:T(8,128)(2,1)} %get-tuple-element.18), channel_id=1, source_target_pairs={{0,2},{1,3},{2,0},{3,1},{4,6},{5,7},{6,4},{7,5},{8,10},{9,11},{10,... | collective-permute-start | bytes 663560 | tf_op jit(solution)/shard_map/ppermute | solution.py:34
  52.2 16.3 %collective-permute-start.7 = (bf16[160,2560]{1,0:T(8,128)(2,1)}, bf16[160,2560]{1,0:T(8,128)(2,1)S(1)}, u32[]{:S(2)}, u32[]{:S(2)}) collective-permute-start(bf16[160,2560]{1,0:T(8,128)(2,1)} %get-tuple-element.19.b0), channel_id=1, source_target_pairs={{0,1},{1,2},{2,3},{3,0},{4,5},{5,6},{6,7},{7,4},{8,9},{9,10},{10,1... | collective-permute-start | bytes 2457608 | tf_op jit(solution)/shard_map/ppermute | solution.py:34
  52.2 17.8 %collective-permute-start.8 = (bf16[160,2560]{1,0:T(8,128)(2,1)}, bf16[160,2560]{1,0:T(8,128)(2,1)S(1)}, u32[]{:S(2)}, u32[]{:S(2)}) collective-permute-start(bf16[160,2560]{1,0:T(8,128)(2,1)} %get-tuple-element.19.b0), channel_id=1, source_target_pairs={{0,3},{1,0},{2,1},{3,2},{4,7},{5,4},{6,5},{7,6},{8,11},{9,8},{10,9... | collective-permute-start | bytes 2457608 | tf_op jit(solution)/shard_map/ppermute | solution.py:34
  54.2 38.2 %all-to-all-start = ((bf16[16,64,512]{2,1,0:T(8,128)(2,1)}), bf16[16,64,512]{2,1,0:T(8,128)(2,1)}, u32[]{:S(2)}, u32[]{:S(2)}) async-start(bf16[16,64,512]{2,1,0:T(8,128)(2,1)} %bitcast.26), calls=%async_computation | async-start | bytes 2097152 | tf_op jit(solution)/shard_map/all_to_all | solution.py:203
  71.8 15.0 %collective-permute-start.9 = (bf16[256,2560]{1,0:T(8,128)(2,1)S(1)}, bf16[256,2560]{1,0:T(8,128)(2,1)S(1)}, u32[]{:S(2)}, u32[]{:S(2)}) collective-permute-start(bf16[256,2560]{1,0:T(8,128)(2,1)S(1)} %cut.1), channel_id=1, source_target_pairs={{0,64},{64,0},{1,65},{65,1},{2,66},{66,2},{3,67},{67,3},{4,68},{68... | collective-permute-start | bytes 3932168 | tf_op jit(solution)/shard_map/ppermute | solution.py:34
  72.0 11.9 %collective-permute-start.10 = (bf16[160,1280]{1,0:T(8,128)(2,1)S(1)}, bf16[160,1280]{1,0:T(8,128)(2,1)S(1)}, u32[]{:S(2)}, u32[]{:S(2)}) collective-permute-start(bf16[160,1280]{1,0:T(8,128)(2,1)S(1)} %slice.8), channel_id=1, source_target_pairs={{0,1},{1,2},{2,3},{3,0},{4,5},{5,6},{6,7},{7,4},{8,9},{9,10},{10,1... | collective-permute-start | bytes 1228808 | tf_op jit(solution)/shard_map/ppermute | solution.py:34
  73.8 18.7 %copy-start.9 = (s32[2]{0:T(128)S(1)}, s32[2]{0:T(128)}, u32[]{:S(2)}) copy-start(s32[2]{0:T(128)} %lens.1) | copy-start | bytes 28
  73.8 13.1 %collective-permute-start.11 = (bf16[160,1280]{1,0:T(8,128)(2,1)S(1)}, bf16[160,1280]{1,0:T(8,128)(2,1)S(1)}, u32[]{:S(2)}, u32[]{:S(2)}) collective-permute-start(bf16[160,1280]{1,0:T(8,128)(2,1)S(1)} %slice.9), channel_id=1, source_target_pairs={{0,3},{1,0},{2,1},{3,2},{4,7},{5,4},{6,5},{7,6},{8,11},{9,8},{10,9... | collective-permute-start | bytes 1228808 | tf_op jit(solution)/shard_map/ppermute | solution.py:34
  92.4 11.5 %collective-permute-start.12 = (f32[640,256]{1,0:T(8,128)}, f32[640,256]{1,0:T(8,128)S(1)}, u32[]{:S(2)}, u32[]{:S(2)}) collective-permute-start(f32[640,256]{1,0:T(8,128)} %get-tuple-element.21.refs_0_), channel_id=1, source_target_pairs={{0,64},{64,0},{1,65},{65,1},{2,66},{66,2},{3,67},{67,3},{4,68},{68... | collective-permute-start | bytes 1966088 | tf_op jit(solution)/shard_map/ppermute | solution.py:34
  94.7 27.3 %all-to-all-start.1 = ((bf16[8,64,512]{2,1,0:T(8,128)(2,1)}), bf16[8,64,512]{2,1,0:T(8,128)(2,1)S(1)}, u32[]{:S(2)}, u32[]{:S(2)}) async-start(bf16[8,64,512]{2,1,0:T(8,128)(2,1)} %live.1), calls=%async_computation.1 | async-start | bytes 1048576 | tf_op jit(solution)/shard_map/all_to_all | solution.py:210
  104.0 18.1 %collective-permute-start.13 = (bf16[640,256]{1,0:T(8,128)(2,1)S(1)}, bf16[640,256]{1,0:T(8,128)(2,1)S(1)}, u32[]{:S(2)}, u32[]{:S(2)}) collective-permute-start(bf16[640,256]{1,0:T(8,128)(2,1)S(1)} %add.24.ra), channel_id=1, source_target_pairs={{0,4},{4,0},{1,5},{5,1},{2,6},{6,2},{3,7},{7,3},{8,12},{12,8},{9,1... | collective-permute-start | bytes 983048 | tf_op jit(solution)/shard_map/ppermute | solution.py:34
  148.1 8.4 %collective-permute-start.15 = (bf16[2,80,1024]{2,1,0:T(8,128)(2,1)S(1)}, bf16[2,80,1024]{2,1,0:T(8,128)(2,1)S(1)}, u32[]{:S(2)}, u32[]{:S(2)}) collective-permute-start(bf16[2,80,1024]{2,1,0:T(8,128)(2,1)S(1)} %sums.1), channel_id=1, source_target_pairs={{0,128},{128,0},{1,129},{129,1},{2,130},{130,2},{3,131},{131,3},{4... | collective-permute-start | bytes 983048 | tf_op jit(solution)/shard_map/ppermute | solution.py:34
  148.9 9.1 %collective-permute-start.14 = (bf16[2,80,1024]{2,1,0:T(8,128)(2,1)S(1)}, bf16[2,80,1024]{2,1,0:T(8,128)(2,1)S(1)}, u32[]{:S(2)}, u32[]{:S(2)}) collective-permute-start(bf16[2,80,1024]{2,1,0:T(8,128)(2,1)S(1)} %sums.1), channel_id=1, source_target_pairs={{0,64},{64,0},{1,65},{65,1},{2,66},{66,2},{3,67},{67,3},{4,68},{68... | collective-permute-start | bytes 983048 | tf_op jit(solution)/shard_map/ppermute | solution.py:34
  156.5 2.9 %collective-permute-start.16 = (bf16[2,80,1024]{2,1,0:T(8,128)(2,1)S(1)}, bf16[2,80,1024]{2,1,0:T(8,128)(2,1)S(1)}, u32[]{:S(2)}, u32[]{:S(2)}) collective-permute-start(bf16[2,80,1024]{2,1,0:T(8,128)(2,1)S(1)} %collective-permute-done.15), channel_id=1, source_target_pairs={{0,64},{64,0},{1,65},{65,1},{2,66},{66,2},{3,67},{67,3},{4,68},{68... | collective-permute-start | bytes 983048 | tf_op jit(solution)/shard_map/ppermute | solution.py:34
  (6 other events, 47.8 us)
Sparse Core Ops, SparseCore 0:
  9.1 44.9 all-gather.1

commit v10 on v9

--- a/solution.py
+++ b/solution.py
@@ -59,21 +59,22 @@
                 o_ref[:, off + place : off + place + 128] = total.astype(BF)
 
 
-def pick_kernel(s_ref, *refs):
-    picked, g_ref, chosen, g0, g1, g2, g3 = refs[:8], *refs[8:]
+def pick_kernel(ids, y_ref, core_ref, *refs):
+    picked, g_ref, chosen, half, g0, g1, g2, g3 = refs[:8], *refs[8:]
     for n, p in enumerate(picked):
         chosen[:, n * 128 : n * 128 + 128] = p[...]
-    reorder(s_ref[8], g_ref, ((g1, 0, 1), (g2, 0, -1), (g3, 0, 2), (g0, 0, 0)))
-
-
-def pick(block_ids, y, basis_out, out_grads):
+    half[...] = chosen[:, pl.ds(pl.multiple_of(core_ref[0] * 512, 128), 512)]
+    reorder(y_ref[0], g_ref, ((g1, 0, 1), (g2, 0, -1), (g3, 0, 2), (g0, 0, 0)))
+
+
+def pick(block_ids, y, core, basis_out, out_grads):
     rows, tokens = out_grads.shape
-    whole = lambda width: pl.BlockSpec((rows, width), lambda g, s: (0, 0))
-    widths = (1024, 512, 512, 512, 512)
+    whole = lambda width: pl.BlockSpec((rows, width), lambda g, *s: (0, 0))
+    widths = (1024, 512, 512, 512, 512, 512)
     spec = pltpu.PrefetchScalarGridSpec(
-        num_scalar_prefetch=1,
+        num_scalar_prefetch=3,
         grid=(1,),
-        in_specs=[pl.BlockSpec((rows, BLOCK), lambda g, s, n=n: (0, s[n])) for n in range(8)] + [whole(tokens)],
+        in_specs=[pl.BlockSpec((rows, BLOCK), lambda g, s, y, c, n=n: (0, s[n])) for n in range(8)] + [whole(tokens)],
         out_specs=[whole(w) for w in widths],
     )
     return pl.pallas_call(
@@ -82,7 +83,7 @@
         out_shape=[arr(rows, w) for w in widths],
         compiler_params=WIDE,
         name="pick",
-    )(jnp.concatenate([block_ids, y[None]]), *[basis_out] * 8, out_grads)
+    )(block_ids, y[None], core[None], *[basis_out] * 8, out_grads)
 
 
 def halve_kernel(s_ref, b_ref, o_ref):
@@ -108,14 +109,16 @@
     o_ref[...] = a_ref[:, pl.ds(pl.multiple_of((1 - core_ref[0]) * half, 128), half)]
 
 
-def grads_kernel(c0, c1, c2, c3, g0, g1, g2, g3, b_own, b_far, o_ref, b0):
+def grads_kernel(core_ref, c0, h1, h2, h3, o1, o2, o3, g0, g1, g2, g3, b_own, b_far, o_ref, b0):
     b0[:80, :] = b_own[...]
     b0[80:, :] = b_far[...]
-    for part in range(4):
-        ks = slice(part * 256, part * 256 + 256)
-        total = dot(c0[:, ks], g0[...], 0, 0) + dot(c1[:, ks], g1[...], 0, 0)
-        total += dot(c2[:, ks], g2[...], 0, 0) + dot(c3[:, ks], g3[...], 0, 0)
-        o_ref[ks, :] = total.astype(BF)
+    for which, (a1, a2, a3) in ((core_ref[0], (h1, h2, h3)), (1 - core_ref[0], (o1, o2, o3))):
+        for off in (0, 256):
+            ks = slice(off, off + 256)
+            place = pl.ds(pl.multiple_of(which * 512 + off, 256), 256)
+            total = dot(c0[:, place], g0[...], 0, 0) + dot(a1[:, ks], g1[...], 0, 0)
+            total += dot(a2[:, ks], g2[...], 0, 0) + dot(a3[:, ks], g3[...], 0, 0)
+            o_ref[place, :] = total.astype(BF)
 
 
 def live_kernel(y_ref, lens, parts, *refs):
@@ -189,14 +192,19 @@
     xl, core, xh, y = (lax.axis_index(a).astype(jnp.int32) for a in ("xl", "core", "xh", "y"))
     acts = lax.all_gather(activations, "z", axis=0, tiled=True)
     half = basis_in.shape[1] // 2
-    chosen, g0, g1, g2, g3 = pick(block_ids, y, basis_out, out_grads)
-    c1, c2 = shift(chosen, y=1), shift(chosen, y=-1)
+    chosen, c0, g0, g1, g2, g3 = pick(block_ids, y, core, basis_out, out_grads)
+    c1, c2 = shift(c0, y=1), shift(c0, y=-1)
     g1, g2, g3 = shift(g1, y=1), shift(g2, y=-1), shift(g3, y=2)
     c3 = shift(c2, y=-1)
+    others = [shift(c, core=1) for c in (c1, c2, c3)]
     b_own = halve(core, basis_in)
     b_far = shift(b_own, xl=1, xh=1)
     partial, b0 = call(
-        grads_kernel, [arr(1024, 512), arr(160, half)], "grads", [chosen, c1, c2, c3, g0, g1, g2, g3, b_own, b_far]
+        grads_kernel,
+        [arr(1024, 512), arr(160, half)],
+        "grads",
+        [chosen, c1, c2, c3, *others, g0, g1, g2, g3, b_own, b_far],
+        [core[None]],
     )
     b1, b2 = shift(b0, y=1), shift(b0, y=-1)
     b3a, b3b = shift(b1[:, : half // 2], y=1), shift(b2[:, half // 2 :], y=-1)

time: 189 us -> 178 us (0.942)
  waiting for transfers between devices: 62.4 us -> 56.5 us
  starting transfers between devices: 40.2 us -> 37.2 us
    ppermute x17 -> x20, waiting for transfers between devices: 46.8 us -> 40.8 us  [shift(): return lax.ppermute(x, axes, pairs)]
    ppermute x17 -> x20, starting transfers between devices: 19.9 us -> 17.7 us  [shift(): return lax.ppermute(x, axes, pairs)]
  transfers between devices with their start and end apart: 20 -> 23, of which waited for: 8 -> 10; matrix products, arithmetic and copies ran while one was open for 3% -> 3% of each run, Pallas kernels for 8% -> 8%
where the time goes in v10:
time: 178 us; the launch traced here: 177 us
  waiting for transfers between devices  56.5 us (32%)
  blocking collectives  44.7 us (25%)
  starting transfers between devices  37.2 us (21%)
  Pallas kernels  15.2 us (9%)
  between operations  13.6 us (8%)
  matrix products  5.87 us (3%)
  local copies, waits for them, and re-layouts  3.69 us (2%)
    ppermute x20, waiting for transfers between devices, shift(): return lax.ppermute(x, axes, pairs)  40.8 us
    all_to_all x1, blocking collectives, per_device(): lax.all_to_all(tiles, ('xh', 'y'), split_axis=0, concat_axis=0, tiled=True)  24.5 us
    all_to_all x1, blocking collectives, spread(): lax.all_to_all(jnp.broadcast_to(x[None], (count,) + x.shape), axes, split...  20.2 us
    ppermute x20, starting transfers between devices, shift(): return lax.ppermute(x, axes, pairs)  17.7 us
    all_to_all x1, waiting for transfers between devices, per_device(): lax.all_to_all(copies, 'z', split_axis=0, concat_axis=0, tiled=True)  15 us
    all_to_all x1, starting transfers between devices, per_device(): lax.all_to_all(partial.reshape(16, 64, 512), ('xh', 'z'), split_axis=0, c...  11.1 us
    pallas_call x7, Pallas kernels, call(): pl.pallas_call(kernel, out_shape=out, in_specs=specs, out_specs=jax.tree....  10.9 us
    all_to_all x1, starting transfers between devices, per_device(): lax.all_to_all(copies, 'z', split_axis=0, concat_axis=0, tiled=True)  8.47 us
  transfers between devices with their start and end apart: 23, of which 10 were waited for; matrix products, arithmetic and copies ran while one was open for 3% of the time, Pallas kernels for 8%

profile of v10, /device:TPU:24, one launch (start us, length us, event | category | flops | bytes accessed | tf_op | source)
XLA Modules:
  0.0 177.5 jit_solution(12328461904226454550)
XLA Ops:
  7.3 4.3 %pick.1 = (bf16[216,1024]{1,0:T(8,128)(2,1)}, bf16[216,512]{1,0:T(8,128)(2,1)}, bf16[216,512]{1,0:T(8,128)(2,1)}, bf16[216,512]{1,0:T(8,128)(2,1)}, bf16[216,512]{1,0:T(8,128)(2,1)}, /*index=5*/bf16[216,512]{1,0:T(8,128)(2,1)}) custom-call(s32[8]{0:T(128)} %ids.1, s32[1]{0:T(128)} %bitcast.1.y_ref, s32[1]{0:T(128)} %bitcast.2.core_ref.s_ref, ...), custom_call_target="tpu_custom_call" | custom-call | tf_op jit(solution)/shard_map/pick/pallas_call | solution.py:80
  12.4 2.5 %collective-permute-start = (bf16[216,512]{1,0:T(8,128)(2,1)}, bf16[216,512]{1,0:T(8,128)(2,1)S(1)}, u32[]{:S(2)}, u32[]{:S(2)}) collective-permute-start(bf16[216,512]{1,0:T(8,128)(2,1)} %get-tuple-element.16), channel_id=1, source_target_pairs={{0,1},{1,2},{2,3},{3,0},{4,5},{5,6},{6,7},{7,4},{8,9},{9,10},{10,1... | collective-permute-start | bytes 663560 | tf_op jit(solution)/shard_map/ppermute | solution.py:34
  16.9 4.5 %collective-permute-done.1.h2 = bf16[216,512]{1,0:T(8,128)(2,1)S(1)} collective-permute-done((bf16[216,512]{1,0:T(8,128)(2,1)}, bf16[216,512]{1,0:T(8,128)(2,1)S(1)}, u32[]{:S(2)}, u32[]{:S(2)}) %collective-permute-start.1) | collective-permute-done | bytes 221216 | tf_op jit(solution)/shard_map/ppermute | solution.py:34
  21.4 2.8 %collective-permute-start.9 = (bf16[80,2560]{1,0:T(8,128)(2,1)S(1)}, bf16[80,2560]{1,0:T(8,128)(2,1)S(1)}, u32[]{:S(2)}, u32[]{:S(2)}) collective-permute-start(bf16[80,2560]{1,0:T(8,128)(2,1)S(1)} %halve.1.b_own), channel_id=1, source_target_pairs={{0,132},{4,128},{128,4},{132,0},{1,133},{5,129},{129,5},{133,1},{2... | collective-permute-start | bytes 1228808 | tf_op jit(solution)/shard_map/ppermute | solution.py:34
  26.1 8.3 %collective-permute-done.2.h3 = bf16[216,512]{1,0:T(8,128)(2,1)S(1)} collective-permute-done((bf16[216,512]{1,0:T(8,128)(2,1)S(1)}, bf16[216,512]{1,0:T(8,128)(2,1)S(1)}, u32[]{:S(2)}, u32[]{:S(2)}) %collective-permute-start.2) | collective-permute-done | bytes 221216 | tf_op jit(solution)/shard_map/ppermute | solution.py:34
  35.9 2.2 %grads.1 = (bf16[1024,512]{1,0:T(8,128)(2,1)S(1)}, bf16[160,2560]{1,0:T(8,128)(2,1)}) custom-call(s32[1]{0:T(128)} %bitcast.2.core_ref.s_ref, bf16[216,1024]{1,0:T(8,128)(2,1)S(1)} %copy-done.7, bf16[216,512]{1,0:T(8,128)(2,1)S(1)} %collective-permute-done.h1, bf16[216,512]{1,0:T(8,128)(2,1)S(1)} %collective-permute-done.1.h2, ...), custom_call_target="tpu_custom_call" | custom-call | flops 1 | bytes 1 | tf_op jit(solution)/shard_map/grads/pallas_call | solution.py:176
  39.1 2.0 %collective-permute-start.11 = (bf16[160,2560]{1,0:T(8,128)(2,1)}, bf16[160,2560]{1,0:T(8,128)(2,1)S(1)}, u32[]{:S(2)}, u32[]{:S(2)}) collective-permute-start(bf16[160,2560]{1,0:T(8,128)(2,1)} %get-tuple-element.21.b0), channel_id=1, source_target_pairs={{0,3},{1,0},{2,1},{3,2},{4,7},{5,4},{6,5},{7,6},{8,11},{9,8},{10,9... | collective-permute-start | bytes 2457608 | tf_op jit(solution)/shard_map/ppermute | solution.py:34
  41.2 11.1 %all-to-all-start = ((bf16[16,64,512]{2,1,0:T(8,128)(2,1)}), bf16[16,64,512]{2,1,0:T(8,128)(2,1)}, u32[]{:S(2)}, u32[]{:S(2)}) async-start(bf16[16,64,512]{2,1,0:T(8,128)(2,1)} %bitcast.26), calls=%async_computation | async-start | bytes 2097152 | tf_op jit(solution)/shard_map/all_to_all | solution.py:211
  52.3 7.4 %collective-permute-done.10.refs_0_.b1 = bf16[160,2560]{1,0:T(8,128)(2,1)S(1)} collective-permute-done((bf16[160,2560]{1,0:T(8,128)(2,1)}, bf16[160,2560]{1,0:T(8,128)(2,1)S(1)}, u32[]{:S(2)}, u32[]{:S(2)}) %collective-permute-start.10) | collective-permute-done | bytes 819232 | tf_op jit(solution)/shard_map/ppermute | solution.py:34
  60.9 1.7 copy-done.1
  63.4 1.8 %collective-permute-start.14 = (bf16[160,1280]{1,0:T(8,128)(2,1)S(1)}, bf16[160,1280]{1,0:T(8,128)(2,1)S(1)}, u32[]{:S(2)}, u32[]{:S(2)}) collective-permute-start(bf16[160,1280]{1,0:T(8,128)(2,1)S(1)} %slice.9), channel_id=1, source_target_pairs={{0,3},{1,0},{2,1},{3,2},{4,7},{5,4},{6,5},{7,6},{8,11},{9,8},{10,9... | collective-permute-start | bytes 1228808 | tf_op jit(solution)/shard_map/ppermute | solution.py:34
  65.2 9.7 %collective-permute-done.13.b3a = bf16[160,1280]{1,0:T(8,128)(2,1)S(1)} collective-permute-done((bf16[160,1280]{1,0:T(8,128)(2,1)S(1)}, bf16[160,1280]{1,0:T(8,128)(2,1)S(1)}, u32[]{:S(2)}, u32[]{:S(2)}) %collective-permute-start.13) | collective-permute-done | bytes 409632 | tf_op jit(solution)/shard_map/ppermute | solution.py:34
  76.3 4.7 %acts.1 = (f32[640,256]{1,0:T(8,128)S(1)}, f32[640,256]{1,0:T(8,128)}) custom-call(s32[1]{0:T(128)} %bitcast.2.core_ref.s_ref, bf16[256,5120]{1,0:T(8,128)(2,1)S(1)} %copy-done.2, bf16[256,2560]{1,0:T(8,128)(2,1)S(1)} %collective-permute-done.12.sib, bf16[160,2560]{1,0:T(8,128)(2,1)} %get-tuple-element.21.b0, ...), custom_call_target="tpu_custom_call" | custom-call | flops 1 | bytes 1 | tf_op jit(solution)/shard_map/acts/pallas_call | solution.py:176
  81.9 2.3 %live.1 = bf16[8,64,512]{2,1,0:T(8,128)(2,1)} custom-call(s32[1]{0:T(128)} %bitcast.1.y_ref, s32[2]{0:T(128)S(1)} %copy-done.9, bf16[16,64,512]{2,1,0:T(8,128)(2,1)} %all-to-all-done.parts, f32[640,256]{1,0:T(8,128)} %get-tuple-element.23.refs_0_), custom_call_target="tpu_custom_call" | custom-call | flops 1 | bytes 1 | tf_op jit(solution)/shard_map/live/pallas_call | solution.py:176
  84.2 8.5 %all-to-all-start.1 = ((bf16[8,64,512]{2,1,0:T(8,128)(2,1)}), bf16[8,64,512]{2,1,0:T(8,128)(2,1)S(1)}, u32[]{:S(2)}, u32[]{:S(2)}) async-start(bf16[8,64,512]{2,1,0:T(8,128)(2,1)} %live.1), calls=%async_computation.1 | async-start | bytes 1048576 | tf_op jit(solution)/shard_map/all_to_all | solution.py:218
  92.7 3.1 %collective-permute-start.16 = (bf16[640,256]{1,0:T(8,128)(2,1)S(1)}, bf16[640,256]{1,0:T(8,128)(2,1)S(1)}, u32[]{:S(2)}, u32[]{:S(2)}) collective-permute-start(bf16[640,256]{1,0:T(8,128)(2,1)S(1)} %add.22.ra), channel_id=1, source_target_pairs={{0,4},{4,0},{1,5},{5,1},{2,6},{6,2},{3,7},{7,3},{8,12},{12,8},{9,1... | collective-permute-start | bytes 983048 | tf_op jit(solution)/shard_map/ppermute | solution.py:34
  95.8 15.0 %all-to-all-done.1 = bf16[8,64,512]{2,1,0:T(8,128)(2,1)S(1)} async-done(((bf16[8,64,512]{2,1,0:T(8,128)(2,1)}), bf16[8,64,512]{2,1,0:T(8,128)(2,1)S(1)}, u32[]{:S(2)}, u32[]{:S(2)}) %all-to-all-start.1) | async-done | bytes 524320 | tf_op jit(solution)/shard_map/all_to_all | solution.py:218
  112.2 24.5 %all_to_all.20.parts = bf16[8,2,80,512]{3,2,1,0:T(8,128)(2,1)S(1)} all-to-all(bf16[8,2,80,512]{3,2,1,0:T(8,128)(2,1)S(1)} %seq.1), channel_id=1, replica_groups=mesh['xl'=2,'core'=2,'z'=8,'xh'=2,'y'=4] {'xh','y'}, dimensions={0} | all-to-all | bytes 2621440 | tf_op jit(solution)/shard_map/all_to_all | solution.py:221
  137.6 1.5 convolution_bitcast_fusion.3
  139.1 6.1 %collective-permute-done.18 = bf16[2,80,1024]{2,1,0:T(8,128)(2,1)S(1)} collective-permute-done((bf16[2,80,1024]{2,1,0:T(8,128)(2,1)S(1)}, bf16[2,80,1024]{2,1,0:T(8,128)(2,1)S(1)}, u32[]{:S(2)}, u32[]{:S(2)}) %collective-permute-start.18) | collective-permute-done | bytes 327712 | tf_op jit(solution)/shard_map/ppermute | solution.py:34
  145.2 1.5 convolution_bitcast_fusion.1
  146.7 1.5 convolution_bitcast_fusion.2
  148.2 1.5 convolution_bitcast_fusion
  149.7 20.2 %all_to_all.21 = f32[64,8,8]{2,1,0:T(8,128)S(1)} all-to-all(f32[64,8,8]{2,1,0:T(8,128)S(1)} %broadcast_in_dim.11), channel_id=1, replica_groups=mesh['xl'=2,'core'=2,'z'=8,'xh'=2,'y'=4] {'z','xh','y'}, dimensions={0} | all-to-all | bytes 32768 | tf_op jit(solution)/shard_map/all_to_all | solution.py:38
  (65 shorter events, 15.2 us)
Async XLA Ops:
  6.5 131.1 %copy-start = (bf16[8,80,1024]{2,1,0:T(8,128)(2,1)S(1)}, bf16[8,80,1024]{2,1,0:T(8,128)(2,1)}, u32[]{:S(2)}) copy-start(bf16[8,80,1024]{2,1,0:T(8,128)(2,1)} %param.13) | copy-start | bytes 3932164
  6.5 54.3 %all-gather.2.cloned.1.call-start = ((), (), s32[]{:S(2)}) async-start(), calls=%async_computation.4 | async-start | bytes 2949120 | tf_op jit(solution)/shard_map/all_gather | solution.py:193
  11.6 9.8 %collective-permute-start.1 = (bf16[216,512]{1,0:T(8,128)(2,1)}, bf16[216,512]{1,0:T(8,128)(2,1)S(1)}, u32[]{:S(2)}, u32[]{:S(2)}) collective-permute-start(bf16[216,512]{1,0:T(8,128)(2,1)} %get-tuple-element.16), channel_id=1, source_target_pairs={{0,3},{1,0},{2,1},{3,2},{4,7},{5,4},{6,5},{7,6},{8,11},{9,8},{10,9... | collective-permute-start | bytes 663560 | tf_op jit(solution)/shard_map/ppermute | solution.py:34
  12.4 11.9 %collective-permute-start = (bf16[216,512]{1,0:T(8,128)(2,1)}, bf16[216,512]{1,0:T(8,128)(2,1)S(1)}, u32[]{:S(2)}, u32[]{:S(2)}) collective-permute-start(bf16[216,512]{1,0:T(8,128)(2,1)} %get-tuple-element.16), channel_id=1, source_target_pairs={{0,1},{1,2},{2,3},{3,0},{4,5},{5,6},{6,7},{7,4},{8,9},{9,10},{10,1... | collective-permute-start | bytes 663560 | tf_op jit(solution)/shard_map/ppermute | solution.py:34
  14.9 10.5 %collective-permute-start.6 = (bf16[216,512]{1,0:T(8,128)(2,1)}, bf16[216,512]{1,0:T(8,128)(2,1)S(1)}, u32[]{:S(2)}, u32[]{:S(2)}) collective-permute-start(bf16[216,512]{1,0:T(8,128)(2,1)} %get-tuple-element.18), channel_id=1, source_target_pairs={{0,1},{1,2},{2,3},{3,0},{4,5},{5,6},{6,7},{7,4},{8,9},{9,10},{10,1... | collective-permute-start | bytes 663560 | tf_op jit(solution)/shard_map/ppermute | solution.py:34
  15.6 10.5 %collective-permute-start.7 = (bf16[216,512]{1,0:T(8,128)(2,1)}, bf16[216,512]{1,0:T(8,128)(2,1)S(1)}, u32[]{:S(2)}, u32[]{:S(2)}) collective-permute-start(bf16[216,512]{1,0:T(8,128)(2,1)} %get-tuple-element.19), channel_id=1, source_target_pairs={{0,3},{1,0},{2,1},{3,2},{4,7},{5,4},{6,5},{7,6},{8,11},{9,8},{10,9... | collective-permute-start | bytes 663560 | tf_op jit(solution)/shard_map/ppermute | solution.py:34
  21.4 13.1 %collective-permute-start.2 = (bf16[216,512]{1,0:T(8,128)(2,1)S(1)}, bf16[216,512]{1,0:T(8,128)(2,1)S(1)}, u32[]{:S(2)}, u32[]{:S(2)}) collective-permute-start(bf16[216,512]{1,0:T(8,128)(2,1)S(1)} %collective-permute-done.1.h2), channel_id=1, source_target_pairs={{0,3},{1,0},{2,1},{3,2},{4,7},{5,4},{6,5},{7,6},{8,11},{9,8},{10,9... | collective-permute-start | bytes 663560 | tf_op jit(solution)/shard_map/ppermute | solution.py:34
  21.4 13.0 %collective-permute-start.9 = (bf16[80,2560]{1,0:T(8,128)(2,1)S(1)}, bf16[80,2560]{1,0:T(8,128)(2,1)S(1)}, u32[]{:S(2)}, u32[]{:S(2)}) collective-permute-start(bf16[80,2560]{1,0:T(8,128)(2,1)S(1)} %halve.1.b_own), channel_id=1, source_target_pairs={{0,132},{4,128},{128,4},{132,0},{1,133},{5,129},{129,5},{133,1},{2... | collective-permute-start | bytes 1228808 | tf_op jit(solution)/shard_map/ppermute | solution.py:34
  24.3 10.2 %collective-permute-start.8 = (bf16[216,512]{1,0:T(8,128)(2,1)}, bf16[216,512]{1,0:T(8,128)(2,1)S(1)}, u32[]{:S(2)}, u32[]{:S(2)}) collective-permute-start(bf16[216,512]{1,0:T(8,128)(2,1)} %get-tuple-element.20), channel_id=1, source_target_pairs={{0,2},{1,3},{2,0},{3,1},{4,6},{5,7},{6,4},{7,5},{8,10},{9,11},{10,... | collective-permute-start | bytes 663560 | tf_op jit(solution)/shard_map/ppermute | solution.py:34
  25.4 9.1 %collective-permute-start.4 = (bf16[216,512]{1,0:T(8,128)(2,1)S(1)}, bf16[216,512]{1,0:T(8,128)(2,1)S(1)}, u32[]{:S(2)}, u32[]{:S(2)}) collective-permute-start(bf16[216,512]{1,0:T(8,128)(2,1)S(1)} %collective-permute-done.1.h2), channel_id=1, source_target_pairs={{0,64},{64,0},{1,65},{65,1},{2,66},{66,2},{3,67},{67,3},{4,68},{68... | collective-permute-start | bytes 663560 | tf_op jit(solution)/shard_map/ppermute | solution.py:34
  26.1 8.4 %collective-permute-start.3 = (bf16[216,512]{1,0:T(8,128)(2,1)S(1)}, bf16[216,512]{1,0:T(8,128)(2,1)S(1)}, u32[]{:S(2)}, u32[]{:S(2)}) collective-permute-start(bf16[216,512]{1,0:T(8,128)(2,1)S(1)} %collective-permute-done.h1), channel_id=1, source_target_pairs={{0,64},{64,0},{1,65},{65,1},{2,66},{66,2},{3,67},{67,3},{4,68},{68... | collective-permute-start | bytes 663560 | tf_op jit(solution)/shard_map/ppermute | solution.py:34
  34.5 1.5 collective-permute-start.5
  39.1 20.5 %collective-permute-start.10 = (bf16[160,2560]{1,0:T(8,128)(2,1)}, bf16[160,2560]{1,0:T(8,128)(2,1)S(1)}, u32[]{:S(2)}, u32[]{:S(2)}) collective-permute-start(bf16[160,2560]{1,0:T(8,128)(2,1)} %get-tuple-element.21.b0), channel_id=1, source_target_pairs={{0,1},{1,2},{2,3},{3,0},{4,5},{5,6},{6,7},{7,4},{8,9},{9,10},{10,1... | collective-permute-start | bytes 2457608 | tf_op jit(solution)/shard_map/ppermute | solution.py:34
  39.1 21.7 %collective-permute-start.11 = (bf16[160,2560]{1,0:T(8,128)(2,1)}, bf16[160,2560]{1,0:T(8,128)(2,1)S(1)}, u32[]{:S(2)}, u32[]{:S(2)}) collective-permute-start(bf16[160,2560]{1,0:T(8,128)(2,1)} %get-tuple-element.21.b0), channel_id=1, source_target_pairs={{0,3},{1,0},{2,1},{3,2},{4,7},{5,4},{6,5},{7,6},{8,11},{9,8},{10,9... | collective-permute-start | bytes 2457608 | tf_op jit(solution)/shard_map/ppermute | solution.py:34
  41.2 40.7 %all-to-all-start = ((bf16[16,64,512]{2,1,0:T(8,128)(2,1)}), bf16[16,64,512]{2,1,0:T(8,128)(2,1)}, u32[]{:S(2)}, u32[]{:S(2)}) async-start(bf16[16,64,512]{2,1,0:T(8,128)(2,1)} %bitcast.26), calls=%async_computation | async-start | bytes 2097152 | tf_op jit(solution)/shard_map/all_to_all | solution.py:211
  62.7 13.6 %collective-permute-start.12 = (bf16[256,2560]{1,0:T(8,128)(2,1)S(1)}, bf16[256,2560]{1,0:T(8,128)(2,1)S(1)}, u32[]{:S(2)}, u32[]{:S(2)}) collective-permute-start(bf16[256,2560]{1,0:T(8,128)(2,1)S(1)} %cut.1), channel_id=1, source_target_pairs={{0,64},{64,0},{1,65},{65,1},{2,66},{66,2},{3,67},{67,3},{4,68},{68... | collective-permute-start | bytes 3932168 | tf_op jit(solution)/shard_map/ppermute | solution.py:34
  62.8 12.1 %collective-permute-start.13 = (bf16[160,1280]{1,0:T(8,128)(2,1)S(1)}, bf16[160,1280]{1,0:T(8,128)(2,1)S(1)}, u32[]{:S(2)}, u32[]{:S(2)}) collective-permute-start(bf16[160,1280]{1,0:T(8,128)(2,1)S(1)} %slice.8), channel_id=1, source_target_pairs={{0,1},{1,2},{2,3},{3,0},{4,5},{5,6},{6,7},{7,4},{8,9},{9,10},{10,1... | collective-permute-start | bytes 1228808 | tf_op jit(solution)/shard_map/ppermute | solution.py:34
  63.4 12.9 %collective-permute-start.14 = (bf16[160,1280]{1,0:T(8,128)(2,1)S(1)}, bf16[160,1280]{1,0:T(8,128)(2,1)S(1)}, u32[]{:S(2)}, u32[]{:S(2)}) collective-permute-start(bf16[160,1280]{1,0:T(8,128)(2,1)S(1)} %slice.9), channel_id=1, source_target_pairs={{0,3},{1,0},{2,1},{3,2},{4,7},{5,4},{6,5},{7,6},{8,11},{9,8},{10,9... | collective-permute-start | bytes 1228808 | tf_op jit(solution)/shard_map/ppermute | solution.py:34
  81.9 10.8 %collective-permute-start.15 = (f32[640,256]{1,0:T(8,128)}, f32[640,256]{1,0:T(8,128)S(1)}, u32[]{:S(2)}, u32[]{:S(2)}) collective-permute-start(f32[640,256]{1,0:T(8,128)} %get-tuple-element.23.refs_0_), channel_id=1, source_target_pairs={{0,64},{64,0},{1,65},{65,1},{2,66},{66,2},{3,67},{67,3},{4,68},{68... | collective-permute-start | bytes 1966088 | tf_op jit(solution)/shard_map/ppermute | solution.py:34
  84.2 26.6 %all-to-all-start.1 = ((bf16[8,64,512]{2,1,0:T(8,128)(2,1)}), bf16[8,64,512]{2,1,0:T(8,128)(2,1)S(1)}, u32[]{:S(2)}, u32[]{:S(2)}) async-start(bf16[8,64,512]{2,1,0:T(8,128)(2,1)} %live.1), calls=%async_computation.1 | async-start | bytes 1048576 | tf_op jit(solution)/shard_map/all_to_all | solution.py:218
  92.7 18.1 %collective-permute-start.16 = (bf16[640,256]{1,0:T(8,128)(2,1)S(1)}, bf16[640,256]{1,0:T(8,128)(2,1)S(1)}, u32[]{:S(2)}, u32[]{:S(2)}) collective-permute-start(bf16[640,256]{1,0:T(8,128)(2,1)S(1)} %add.22.ra), channel_id=1, source_target_pairs={{0,4},{4,0},{1,5},{5,1},{2,6},{6,2},{3,7},{7,3},{8,12},{12,8},{9,1... | collective-permute-start | bytes 983048 | tf_op jit(solution)/shard_map/ppermute | solution.py:34
  136.8 8.4 %collective-permute-start.18 = (bf16[2,80,1024]{2,1,0:T(8,128)(2,1)S(1)}, bf16[2,80,1024]{2,1,0:T(8,128)(2,1)S(1)}, u32[]{:S(2)}, u32[]{:S(2)}) collective-permute-start(bf16[2,80,1024]{2,1,0:T(8,128)(2,1)S(1)} %sums.1), channel_id=1, source_target_pairs={{0,128},{128,0},{1,129},{129,1},{2,130},{130,2},{3,131},{131,3},{4... | collective-permute-start | bytes 983048 | tf_op jit(solution)/shard_map/ppermute | solution.py:34
  137.6 9.1 %collective-permute-start.17 = (bf16[2,80,1024]{2,1,0:T(8,128)(2,1)S(1)}, bf16[2,80,1024]{2,1,0:T(8,128)(2,1)S(1)}, u32[]{:S(2)}, u32[]{:S(2)}) collective-permute-start(bf16[2,80,1024]{2,1,0:T(8,128)(2,1)S(1)} %sums.1), channel_id=1, source_target_pairs={{0,64},{64,0},{1,65},{65,1},{2,66},{66,2},{3,67},{67,3},{4,68},{68... | collective-permute-start | bytes 983048 | tf_op jit(solution)/shard_map/ppermute | solution.py:34
  145.2 2.9 %collective-permute-start.19 = (bf16[2,80,1024]{2,1,0:T(8,128)(2,1)S(1)}, bf16[2,80,1024]{2,1,0:T(8,128)(2,1)S(1)}, u32[]{:S(2)}, u32[]{:S(2)}) collective-permute-start(bf16[2,80,1024]{2,1,0:T(8,128)(2,1)S(1)} %collective-permute-done.18), channel_id=1, source_target_pairs={{0,64},{64,0},{1,65},{65,1},{2,66},{66,2},{3,67},{67,3},{4,68},{68... | collective-permute-start | bytes 983048 | tf_op jit(solution)/shard_map/ppermute | solution.py:34
  (9 other events, 109.4 us)
Sparse Core Ops, SparseCore 0:
  9.1 44.9 all-gather.1

commit v11 on v10

--- a/solution.py
+++ b/solution.py
@@ -59,22 +59,41 @@
                 o_ref[:, off + place : off + place + 128] = total.astype(BF)
 
 
-def pick_kernel(ids, y_ref, core_ref, *refs):
-    picked, g_ref, chosen, half, g0, g1, g2, g3 = refs[:8], *refs[8:]
+def half_kernel(ids, core_ref, *refs):
+    *picked, o_ref = refs
+    for n, p in enumerate(picked):
+        o_ref[:, n * 128 : n * 128 + 128] = p[...]
+
+
+def pick_half(block_ids, core, basis_out):
+    rows = basis_out.shape[0]
+    spec = pltpu.PrefetchScalarGridSpec(
+        num_scalar_prefetch=2,
+        grid=(1,),
+        in_specs=[pl.BlockSpec((rows, BLOCK), lambda g, s, c, n=n: (0, s[c[0] * 4 + n])) for n in range(4)],
+        out_specs=pl.BlockSpec((rows, 512), lambda g, s, c: (0, 0)),
+    )
+    return pl.pallas_call(
+        half_kernel, grid_spec=spec, out_shape=arr(rows, 512), compiler_params=WIDE, name="pick_half"
+    )(block_ids, core[None], *[basis_out] * 4)
+
+
+def pick_kernel(ids, y_ref, *refs):
+    picked, g_ref, aside, chosen, g0, g1, g2, g3 = refs[:8], *refs[8:]
     for n, p in enumerate(picked):
         chosen[:, n * 128 : n * 128 + 128] = p[...]
-    half[...] = chosen[:, pl.ds(pl.multiple_of(core_ref[0] * 512, 128), 512)]
     reorder(y_ref[0], g_ref, ((g1, 0, 1), (g2, 0, -1), (g3, 0, 2), (g0, 0, 0)))
 
 
-def pick(block_ids, y, core, basis_out, out_grads):
+def pick(block_ids, y, basis_out, out_grads, aside):
     rows, tokens = out_grads.shape
     whole = lambda width: pl.BlockSpec((rows, width), lambda g, *s: (0, 0))
-    widths = (1024, 512, 512, 512, 512, 512)
+    widths = (1024, 512, 512, 512, 512)
     spec = pltpu.PrefetchScalarGridSpec(
-        num_scalar_prefetch=3,
+        num_scalar_prefetch=2,
         grid=(1,),
-        in_specs=[pl.BlockSpec((rows, BLOCK), lambda g, s, y, c, n=n: (0, s[n])) for n in range(8)] + [whole(tokens)],
+        in_specs=[pl.BlockSpec((rows, BLOCK), lambda g, s, y, n=n: (0, s[n])) for n in range(8)]
+        + [whole(tokens), pl.BlockSpec(memory_space=pl.ANY)],
         out_specs=[whole(w) for w in widths],
     )
     return pl.pallas_call(
@@ -83,7 +102,7 @@
         out_shape=[arr(rows, w) for w in widths],
         compiler_params=WIDE,
         name="pick",
-    )(block_ids, y[None], core[None], *[basis_out] * 8, out_grads)
+    )(block_ids, y[None], *[basis_out] * 8, out_grads, aside)
 
 
 def halve_kernel(s_ref, b_ref, o_ref):
@@ -103,9 +122,10 @@
     )(core[None], basis_in)
 
 
-def cut_kernel(core_ref, a_ref, *refs):
-    o_ref = refs[-1]
+def cut_kernel(core_ref, a_ref, b1, b2, o_ref, left, right):
     half = o_ref.shape[1]
+    left[...] = b1[:, : half // 2]
+    right[...] = b2[:, half // 2 :]
     o_ref[...] = a_ref[:, pl.ds(pl.multiple_of((1 - core_ref[0]) * half, 128), half)]
 
 
@@ -192,8 +212,9 @@
     xl, core, xh, y = (lax.axis_index(a).astype(jnp.int32) for a in ("xl", "core", "xh", "y"))
     acts = lax.all_gather(activations, "z", axis=0, tiled=True)
     half = basis_in.shape[1] // 2
-    chosen, c0, g0, g1, g2, g3 = pick(block_ids, y, core, basis_out, out_grads)
+    c0 = pick_half(block_ids, core, basis_out)
     c1, c2 = shift(c0, y=1), shift(c0, y=-1)
+    chosen, g0, g1, g2, g3 = pick(block_ids, y, basis_out, out_grads, c0)
     g1, g2, g3 = shift(g1, y=1), shift(g2, y=-1), shift(g3, y=2)
     c3 = shift(c2, y=-1)
     others = [shift(c, core=1) for c in (c1, c2, c3)]
@@ -207,10 +228,11 @@
         [core[None]],
     )
     b1, b2 = shift(b0, y=1), shift(b0, y=-1)
-    b3a, b3b = shift(b1[:, : half // 2], y=1), shift(b2[:, half // 2 :], y=-1)
     parts = lax.all_to_all(partial.reshape(16, 64, 512), ("xh", "z"), split_axis=0, concat_axis=0, tiled=True)
     wide = jax.ShapeDtypeStruct((640, 256), F32)
-    sib = shift(call(cut_kernel, arr(256, half), "cut", [acts], [core[None]], [b1, b2]), core=1)
+    cuts = [arr(256, half), arr(160, half // 2), arr(160, half // 2)]
+    sib, left, right = call(cut_kernel, cuts, "cut", [acts, b1, b2], [core[None]])
+    sib, b3a, b3b = shift(sib, core=1), shift(left, y=1), shift(right, y=-1)
     keep, send = call(acts_kernel, [wide, wide], "acts", [acts, sib, b0, b1, b2, b3a, b3b], [core[None]])
     ra = call(add_kernel, arr(640, 256), "add", [keep, shift(send, core=1)])
     rb = shift(ra, xh=1)

time: 178 us -> 179 us (level)
  waiting for transfers between devices: 56.5 us -> 51 us
  Pallas kernels: 15.2 us -> 19.4 us
  starting transfers between devices: 37.2 us -> 39.9 us
    ppermute x20, waiting for transfers between devices: 40.8 us -> 36.3 us  [shift(): return lax.ppermute(x, axes, pairs)]
    ppermute x20, starting transfers between devices: 17.7 us -> 20.3 us  [shift(): return lax.ppermute(x, axes, pairs)]
    pallas_call x0 -> x1, Pallas kernels: none -> 2.29 us  [pick_half(): pl.pallas_call(half_kernel, grid_spec=spec, out_shape=arr(rows, 512), com...]
    pallas_call x7, Pallas kernels: 10.9 us -> 12.7 us  [call(): pl.pallas_call(kernel, out_shape=out, in_specs=specs, out_specs=jax.tree....]
    unnamed x20 -> x22, local copies, waits for them, and re-layouts: 3.6 us -> 3.61 us
  transfers between devices with their start and end apart: 23 -> 23, of which waited for: 10 -> 10; matrix products, arithmetic and copies ran while one was open for 3% -> 2% of each run, Pallas kernels for 8% -> 10%
where the time goes in v11:
time: 179 us
  waiting for transfers between devices  51 us (28%)
  blocking collectives  44.8 us (25%)
  starting transfers between devices  39.9 us (22%)
  Pallas kernels  19.4 us (11%)
  between operations  13.5 us (8%)
  matrix products  5.87 us (3%)
  local copies, waits for them, and re-layouts  3.65 us (2%)
    ppermute x20, waiting for transfers between devices, shift(): return lax.ppermute(x, axes, pairs)  36.3 us
    all_to_all x1, blocking collectives, per_device(): lax.all_to_all(tiles, ('xh', 'y'), split_axis=0, concat_axis=0, tiled=True)  24.5 us
    ppermute x20, starting transfers between devices, shift(): return lax.ppermute(x, axes, pairs)  20.3 us
    all_to_all x1, blocking collectives, spread(): lax.all_to_all(jnp.broadcast_to(x[None], (count,) + x.shape), axes, split...  20.2 us
    all_to_all x1, waiting for transfers between devices, per_device(): lax.all_to_all(copies, 'z', split_axis=0, concat_axis=0, tiled=True)  13.9 us
    pallas_call x7, Pallas kernels, call(): pl.pallas_call(kernel, out_shape=out, in_specs=specs, out_specs=jax.tree....  12.7 us
    all_to_all x1, starting transfers between devices, per_device(): lax.all_to_all(partial.reshape(16, 64, 512), ('xh', 'z'), split_axis=0, c...  11 us
    all_to_all x1, starting transfers between devices, per_device(): lax.all_to_all(copies, 'z', split_axis=0, concat_axis=0, tiled=True)  8.6 us
  transfers between devices with their start and end apart: 23, of which 10 were waited for; matrix products, arithmetic and copies ran while one was open for 2% of the time, Pallas kernels for 10%

profile of v11, /device:TPU:24, one launch (start us, length us, event | category | flops | bytes accessed | tf_op | source)
XLA Modules:
  0.0 178.7 jit_solution(9211761164509132530)
XLA Ops:
  7.3 2.3 %pick_half.1.refs_9_ = bf16[216,512]{1,0:T(8,128)(2,1)} custom-call(s32[8]{0:T(128)} %ids.3, s32[1]{0:T(128)} %bitcast.2.core_ref.s_ref, bf16[216,13824]{1,0:T(8,128)(2,1)} %refs_7_.1, bf16[216,13824]{1,0:T(8,128)(2,1)} %refs_7_.1, bf16[216,13824]{1,0:T(8,128)(2,1)} %refs_7_.1, bf16[216,13824]{1,0:T(8,128)(2,1)} %refs_7_.1), custom_call_target="tpu_custom_call" | custom-call | tf_op jit(solution)/shard_map/pick_half/pallas_call | solution.py:76
  10.3 4.3 %pick.1 = (bf16[216,1024]{1,0:T(8,128)(2,1)}, bf16[216,512]{1,0:T(8,128)(2,1)}, bf16[216,512]{1,0:T(8,128)(2,1)}, bf16[216,512]{1,0:T(8,128)(2,1)}, bf16[216,512]{1,0:T(8,128)(2,1)}) custom-call(s32[8]{0:T(128)} %ids.3, s32[1]{0:T(128)} %bitcast.1.y_ref, bf16[216,13824]{1,0:T(8,128)(2,1)} %refs_7_.1, bf16[216,13824]{1,0:T(8,128)(2,1)} %refs_7_.1, ...), custom_call_target="tpu_custom_call" | custom-call | tf_op jit(solution)/shard_map/pick/pallas_call | solution.py:99
  14.6 2.6 %collective-permute-start.6 = (bf16[216,512]{1,0:T(8,128)(2,1)}, bf16[216,512]{1,0:T(8,128)(2,1)S(1)}, u32[]{:S(2)}, u32[]{:S(2)}) collective-permute-start(bf16[216,512]{1,0:T(8,128)(2,1)} %get-tuple-element.19), channel_id=1, source_target_pairs={{0,1},{1,2},{2,3},{3,0},{4,5},{5,6},{6,7},{7,4},{8,9},{9,10},{10,1... | collective-permute-start | bytes 663560 | tf_op jit(solution)/shard_map/ppermute | solution.py:34
  17.2 3.2 %collective-permute-start = (bf16[216,512]{1,0:T(8,128)(2,1)S(1)}, bf16[216,512]{1,0:T(8,128)(2,1)S(1)}, u32[]{:S(2)}, u32[]{:S(2)}) collective-permute-start(bf16[216,512]{1,0:T(8,128)(2,1)S(1)} %copy-done.10), channel_id=1, source_target_pairs={{0,1},{1,2},{2,3},{3,0},{4,5},{5,6},{6,7},{7,4},{8,9},{9,10},{10,1... | collective-permute-start | bytes 663560 | tf_op jit(solution)/shard_map/ppermute | solution.py:34
  20.5 2.8 %collective-permute-start.9 = (bf16[80,2560]{1,0:T(8,128)(2,1)S(1)}, bf16[80,2560]{1,0:T(8,128)(2,1)S(1)}, u32[]{:S(2)}, u32[]{:S(2)}) collective-permute-start(bf16[80,2560]{1,0:T(8,128)(2,1)S(1)} %halve.1.b_own), channel_id=1, source_target_pairs={{0,132},{4,128},{128,4},{132,0},{1,133},{5,129},{129,5},{133,1},{2... | collective-permute-start | bytes 1228808 | tf_op jit(solution)/shard_map/ppermute | solution.py:34
  23.4 2.6 %collective-permute-start.8 = (bf16[216,512]{1,0:T(8,128)(2,1)}, bf16[216,512]{1,0:T(8,128)(2,1)S(1)}, u32[]{:S(2)}, u32[]{:S(2)}) collective-permute-start(bf16[216,512]{1,0:T(8,128)(2,1)} %get-tuple-element.21), channel_id=1, source_target_pairs={{0,2},{1,3},{2,0},{3,1},{4,6},{5,7},{6,4},{7,5},{8,10},{9,11},{10,... | collective-permute-start | bytes 663560 | tf_op jit(solution)/shard_map/ppermute | solution.py:34
  25.9 1.6 collective-permute-done.7.g2
  27.5 3.8 %collective-permute-done.h1 = bf16[216,512]{1,0:T(8,128)(2,1)S(1)} collective-permute-done((bf16[216,512]{1,0:T(8,128)(2,1)S(1)}, bf16[216,512]{1,0:T(8,128)(2,1)S(1)}, u32[]{:S(2)}, u32[]{:S(2)}) %collective-permute-start) | collective-permute-done | bytes 221216 | tf_op jit(solution)/shard_map/ppermute | solution.py:34
  31.3 3.4 %collective-permute-done.2.h3 = bf16[216,512]{1,0:T(8,128)(2,1)S(1)} collective-permute-done((bf16[216,512]{1,0:T(8,128)(2,1)S(1)}, bf16[216,512]{1,0:T(8,128)(2,1)S(1)}, u32[]{:S(2)}, u32[]{:S(2)}) %collective-permute-start.2) | collective-permute-done | bytes 221216 | tf_op jit(solution)/shard_map/ppermute | solution.py:34
  36.2 2.2 %grads.1 = (bf16[1024,512]{1,0:T(8,128)(2,1)S(1)}, bf16[160,2560]{1,0:T(8,128)(2,1)}) custom-call(s32[1]{0:T(128)} %bitcast.2.core_ref.s_ref, bf16[216,1024]{1,0:T(8,128)(2,1)S(1)} %copy-done.7, bf16[216,512]{1,0:T(8,128)(2,1)S(1)} %collective-permute-done.h1, bf16[216,512]{1,0:T(8,128)(2,1)S(1)} %collective-permute-done.1.h2, ...), custom_call_target="tpu_custom_call" | custom-call | flops 1 | bytes 1 | tf_op jit(solution)/shard_map/grads/pallas_call | solution.py:196
  41.4 11.0 %all-to-all-start = ((bf16[16,64,512]{2,1,0:T(8,128)(2,1)}), bf16[16,64,512]{2,1,0:T(8,128)(2,1)S(1)}, u32[]{:S(2)}, u32[]{:S(2)}) async-start(bf16[16,64,512]{2,1,0:T(8,128)(2,1)} %bitcast.26), calls=%async_computation | async-start | bytes 2097152 | tf_op jit(solution)/shard_map/all_to_all | solution.py:231
  52.4 7.4 %collective-permute-done.10.b1 = bf16[160,2560]{1,0:T(8,128)(2,1)S(1)} collective-permute-done((bf16[160,2560]{1,0:T(8,128)(2,1)}, bf16[160,2560]{1,0:T(8,128)(2,1)S(1)}, u32[]{:S(2)}, u32[]{:S(2)}) %collective-permute-start.10) | collective-permute-done | bytes 819232 | tf_op jit(solution)/shard_map/ppermute | solution.py:34
  59.8 1.7 collective-permute-done.11.b2
  61.5 1.7 copy-done.1
  65.3 1.8 %collective-permute-start.14 = (bf16[160,1280]{1,0:T(8,128)(2,1)S(1)}, bf16[160,1280]{1,0:T(8,128)(2,1)S(1)}, u32[]{:S(2)}, u32[]{:S(2)}) collective-permute-start(bf16[160,1280]{1,0:T(8,128)(2,1)S(1)} %get-tuple-element.25), channel_id=1, source_target_pairs={{0,3},{1,0},{2,1},{3,2},{4,7},{5,4},{6,5},{7,6},{8,11},{9,8},{10,9... | collective-permute-start | bytes 1228808 | tf_op jit(solution)/shard_map/ppermute | solution.py:34
  67.1 9.6 %collective-permute-done.13.b3a = bf16[160,1280]{1,0:T(8,128)(2,1)S(1)} collective-permute-done((bf16[160,1280]{1,0:T(8,128)(2,1)S(1)}, bf16[160,1280]{1,0:T(8,128)(2,1)S(1)}, u32[]{:S(2)}, u32[]{:S(2)}) %collective-permute-start.13) | collective-permute-done | bytes 409632 | tf_op jit(solution)/shard_map/ppermute | solution.py:34
  77.9 4.9 %acts.1 = (f32[640,256]{1,0:T(8,128)S(1)}, f32[640,256]{1,0:T(8,128)}) custom-call(s32[1]{0:T(128)} %bitcast.2.core_ref.s_ref, bf16[256,5120]{1,0:T(8,128)(2,1)S(1)} %copy-done.2, bf16[256,2560]{1,0:T(8,128)(2,1)S(1)} %collective-permute-done.12.sib, bf16[160,2560]{1,0:T(8,128)(2,1)} %get-tuple-element.22.b0, ...), custom_call_target="tpu_custom_call" | custom-call | flops 1 | bytes 1 | tf_op jit(solution)/shard_map/acts/pallas_call | solution.py:196
  83.7 1.5 live.1
  85.2 8.6 %all-to-all-start.1 = ((bf16[8,64,512]{2,1,0:T(8,128)(2,1)}), bf16[8,64,512]{2,1,0:T(8,128)(2,1)S(1)}, u32[]{:S(2)}, u32[]{:S(2)}) async-start(bf16[8,64,512]{2,1,0:T(8,128)(2,1)} %live.1), calls=%async_computation.1 | async-start | bytes 1048576 | tf_op jit(solution)/shard_map/all_to_all | solution.py:240
  95.0 3.1 %collective-permute-start.16 = (bf16[640,256]{1,0:T(8,128)(2,1)S(1)}, bf16[640,256]{1,0:T(8,128)(2,1)S(1)}, u32[]{:S(2)}, u32[]{:S(2)}) collective-permute-start(bf16[640,256]{1,0:T(8,128)(2,1)S(1)} %add.22.ra), channel_id=1, source_target_pairs={{0,4},{4,0},{1,5},{5,1},{2,6},{6,2},{3,7},{7,3},{8,12},{12,8},{9,1... | collective-permute-start | bytes 983048 | tf_op jit(solution)/shard_map/ppermute | solution.py:34
  98.1 13.9 %all-to-all-done.1 = bf16[8,64,512]{2,1,0:T(8,128)(2,1)S(1)} async-done(((bf16[8,64,512]{2,1,0:T(8,128)(2,1)}), bf16[8,64,512]{2,1,0:T(8,128)(2,1)S(1)}, u32[]{:S(2)}, u32[]{:S(2)}) %all-to-all-start.1) | async-done | bytes 524320 | tf_op jit(solution)/shard_map/all_to_all | solution.py:240
  113.4 24.5 %all_to_all.20.parts = bf16[8,2,80,512]{3,2,1,0:T(8,128)(2,1)S(1)} all-to-all(bf16[8,2,80,512]{3,2,1,0:T(8,128)(2,1)S(1)} %seq.1), channel_id=1, replica_groups=mesh['xl'=2,'core'=2,'z'=8,'xh'=2,'y'=4] {'xh','y'}, dimensions={0} | all-to-all | bytes 2621440 | tf_op jit(solution)/shard_map/all_to_all | solution.py:243
  140.3 6.2 %collective-permute-done.18 = bf16[2,80,1024]{2,1,0:T(8,128)(2,1)S(1)} collective-permute-done((bf16[2,80,1024]{2,1,0:T(8,128)(2,1)S(1)}, bf16[2,80,1024]{2,1,0:T(8,128)(2,1)S(1)}, u32[]{:S(2)}, u32[]{:S(2)}) %collective-permute-start.18) | collective-permute-done | bytes 327712 | tf_op jit(solution)/shard_map/ppermute | solution.py:34
  151.0 20.2 %all_to_all.21 = f32[64,8,8]{2,1,0:T(8,128)S(1)} all-to-all(f32[64,8,8]{2,1,0:T(8,128)S(1)} %broadcast_in_dim.11), channel_id=1, replica_groups=mesh['xl'=2,'core'=2,'z'=8,'xh'=2,'y'=4] {'z','xh','y'}, dimensions={0} | all-to-all | bytes 32768 | tf_op jit(solution)/shard_map/all_to_all | solution.py:38
  (66 shorter events, 20.2 us)
Async XLA Ops:
  6.5 132.3 %copy-start = (bf16[8,80,1024]{2,1,0:T(8,128)(2,1)S(1)}, bf16[8,80,1024]{2,1,0:T(8,128)(2,1)}, u32[]{:S(2)}) copy-start(bf16[8,80,1024]{2,1,0:T(8,128)(2,1)} %param.13) | copy-start | bytes 3932164
  6.5 55.0 %all-gather.2.cloned.1.call-start = ((), (), s32[]{:S(2)}) async-start(), calls=%async_computation.4 | async-start | bytes 2949120 | tf_op jit(solution)/shard_map/all_gather | solution.py:213
  9.6 10.9 %collective-permute-start.1 = (bf16[216,512]{1,0:T(8,128)(2,1)}, bf16[216,512]{1,0:T(8,128)(2,1)S(1)}, u32[]{:S(2)}, u32[]{:S(2)}) collective-permute-start(bf16[216,512]{1,0:T(8,128)(2,1)} %pick_half.1.refs_9_), channel_id=1, source_target_pairs={{0,3},{1,0},{2,1},{3,2},{4,7},{5,4},{6,5},{7,6},{8,11},{9,8},{10,9... | collective-permute-start | bytes 663560 | tf_op jit(solution)/shard_map/ppermute | solution.py:34
  14.6 8.8 %collective-permute-start.6 = (bf16[216,512]{1,0:T(8,128)(2,1)}, bf16[216,512]{1,0:T(8,128)(2,1)S(1)}, u32[]{:S(2)}, u32[]{:S(2)}) collective-permute-start(bf16[216,512]{1,0:T(8,128)(2,1)} %get-tuple-element.19), channel_id=1, source_target_pairs={{0,1},{1,2},{2,3},{3,0},{4,5},{5,6},{6,7},{7,4},{8,9},{9,10},{10,1... | collective-permute-start | bytes 663560 | tf_op jit(solution)/shard_map/ppermute | solution.py:34
  17.2 10.3 %collective-permute-start.7 = (bf16[216,512]{1,0:T(8,128)(2,1)}, bf16[216,512]{1,0:T(8,128)(2,1)S(1)}, u32[]{:S(2)}, u32[]{:S(2)}) collective-permute-start(bf16[216,512]{1,0:T(8,128)(2,1)} %get-tuple-element.20), channel_id=1, source_target_pairs={{0,3},{1,0},{2,1},{3,2},{4,7},{5,4},{6,5},{7,6},{8,11},{9,8},{10,9... | collective-permute-start | bytes 663560 | tf_op jit(solution)/shard_map/ppermute | solution.py:34
  17.2 14.1 %collective-permute-start = (bf16[216,512]{1,0:T(8,128)(2,1)S(1)}, bf16[216,512]{1,0:T(8,128)(2,1)S(1)}, u32[]{:S(2)}, u32[]{:S(2)}) collective-permute-start(bf16[216,512]{1,0:T(8,128)(2,1)S(1)} %copy-done.10), channel_id=1, source_target_pairs={{0,1},{1,2},{2,3},{3,0},{4,5},{5,6},{6,7},{7,4},{8,9},{9,10},{10,1... | collective-permute-start | bytes 663560 | tf_op jit(solution)/shard_map/ppermute | solution.py:34
  20.4 14.3 %collective-permute-start.2 = (bf16[216,512]{1,0:T(8,128)(2,1)S(1)}, bf16[216,512]{1,0:T(8,128)(2,1)S(1)}, u32[]{:S(2)}, u32[]{:S(2)}) collective-permute-start(bf16[216,512]{1,0:T(8,128)(2,1)S(1)} %collective-permute-done.1.h2), channel_id=1, source_target_pairs={{0,3},{1,0},{2,1},{3,2},{4,7},{5,4},{6,5},{7,6},{8,11},{9,8},{10,9... | collective-permute-start | bytes 663560 | tf_op jit(solution)/shard_map/ppermute | solution.py:34
  20.5 14.2 %collective-permute-start.9 = (bf16[80,2560]{1,0:T(8,128)(2,1)S(1)}, bf16[80,2560]{1,0:T(8,128)(2,1)S(1)}, u32[]{:S(2)}, u32[]{:S(2)}) collective-permute-start(bf16[80,2560]{1,0:T(8,128)(2,1)S(1)} %halve.1.b_own), channel_id=1, source_target_pairs={{0,132},{4,128},{128,4},{132,0},{1,133},{5,129},{129,5},{133,1},{2... | collective-permute-start | bytes 1228808 | tf_op jit(solution)/shard_map/ppermute | solution.py:34
  23.4 11.3 %collective-permute-start.8 = (bf16[216,512]{1,0:T(8,128)(2,1)}, bf16[216,512]{1,0:T(8,128)(2,1)S(1)}, u32[]{:S(2)}, u32[]{:S(2)}) collective-permute-start(bf16[216,512]{1,0:T(8,128)(2,1)} %get-tuple-element.21), channel_id=1, source_target_pairs={{0,2},{1,3},{2,0},{3,1},{4,6},{5,7},{6,4},{7,5},{8,10},{9,11},{10,... | collective-permute-start | bytes 663560 | tf_op jit(solution)/shard_map/ppermute | solution.py:34
  27.5 7.2 %collective-permute-start.4 = (bf16[216,512]{1,0:T(8,128)(2,1)S(1)}, bf16[216,512]{1,0:T(8,128)(2,1)S(1)}, u32[]{:S(2)}, u32[]{:S(2)}) collective-permute-start(bf16[216,512]{1,0:T(8,128)(2,1)S(1)} %collective-permute-done.1.h2), channel_id=1, source_target_pairs={{0,64},{64,0},{1,65},{65,1},{2,66},{66,2},{3,67},{67,3},{4,68},{68... | collective-permute-start | bytes 663560 | tf_op jit(solution)/shard_map/ppermute | solution.py:34
  31.3 3.4 %collective-permute-start.3 = (bf16[216,512]{1,0:T(8,128)(2,1)S(1)}, bf16[216,512]{1,0:T(8,128)(2,1)S(1)}, u32[]{:S(2)}, u32[]{:S(2)}) collective-permute-start(bf16[216,512]{1,0:T(8,128)(2,1)S(1)} %collective-permute-done.h1), channel_id=1, source_target_pairs={{0,64},{64,0},{1,65},{65,1},{2,66},{66,2},{3,67},{67,3},{4,68},{68... | collective-permute-start | bytes 663560 | tf_op jit(solution)/shard_map/ppermute | solution.py:34
  34.7 1.5 collective-permute-start.5
  39.3 20.5 %collective-permute-start.10 = (bf16[160,2560]{1,0:T(8,128)(2,1)}, bf16[160,2560]{1,0:T(8,128)(2,1)S(1)}, u32[]{:S(2)}, u32[]{:S(2)}) collective-permute-start(bf16[160,2560]{1,0:T(8,128)(2,1)} %get-tuple-element.22.b0), channel_id=1, source_target_pairs={{0,1},{1,2},{2,3},{3,0},{4,5},{5,6},{6,7},{7,4},{8,9},{9,10},{10,1... | collective-permute-start | bytes 2457608 | tf_op jit(solution)/shard_map/ppermute | solution.py:34
  39.9 21.6 %collective-permute-start.11 = (bf16[160,2560]{1,0:T(8,128)(2,1)}, bf16[160,2560]{1,0:T(8,128)(2,1)}, u32[]{:S(2)}, u32[]{:S(2)}) collective-permute-start(bf16[160,2560]{1,0:T(8,128)(2,1)} %get-tuple-element.22.b0), channel_id=1, source_target_pairs={{0,3},{1,0},{2,1},{3,2},{4,7},{5,4},{6,5},{7,6},{8,11},{9,8},{10,9... | collective-permute-start | bytes 2457608 | tf_op jit(solution)/shard_map/ppermute | solution.py:34
  41.4 42.3 %all-to-all-start = ((bf16[16,64,512]{2,1,0:T(8,128)(2,1)}), bf16[16,64,512]{2,1,0:T(8,128)(2,1)S(1)}, u32[]{:S(2)}, u32[]{:S(2)}) async-start(bf16[16,64,512]{2,1,0:T(8,128)(2,1)} %bitcast.26), calls=%async_computation | async-start | bytes 2097152 | tf_op jit(solution)/shard_map/all_to_all | solution.py:231
  64.7 13.2 %collective-permute-start.12 = (bf16[256,2560]{1,0:T(8,128)(2,1)S(1)}, bf16[256,2560]{1,0:T(8,128)(2,1)S(1)}, u32[]{:S(2)}, u32[]{:S(2)}) collective-permute-start(bf16[256,2560]{1,0:T(8,128)(2,1)S(1)} %get-tuple-element.23), channel_id=1, source_target_pairs={{0,64},{64,0},{1,65},{65,1},{2,66},{66,2},{3,67},{67,3},{4,68},{68... | collective-permute-start | bytes 3932168 | tf_op jit(solution)/shard_map/ppermute | solution.py:34
  64.8 11.9 %collective-permute-start.13 = (bf16[160,1280]{1,0:T(8,128)(2,1)S(1)}, bf16[160,1280]{1,0:T(8,128)(2,1)S(1)}, u32[]{:S(2)}, u32[]{:S(2)}) collective-permute-start(bf16[160,1280]{1,0:T(8,128)(2,1)S(1)} %get-tuple-element.24), channel_id=1, source_target_pairs={{0,1},{1,2},{2,3},{3,0},{4,5},{5,6},{6,7},{7,4},{8,9},{9,10},{10,1... | collective-permute-start | bytes 1228808 | tf_op jit(solution)/shard_map/ppermute | solution.py:34
  65.3 12.6 %collective-permute-start.14 = (bf16[160,1280]{1,0:T(8,128)(2,1)S(1)}, bf16[160,1280]{1,0:T(8,128)(2,1)S(1)}, u32[]{:S(2)}, u32[]{:S(2)}) collective-permute-start(bf16[160,1280]{1,0:T(8,128)(2,1)S(1)} %get-tuple-element.25), channel_id=1, source_target_pairs={{0,3},{1,0},{2,1},{3,2},{4,7},{5,4},{6,5},{7,6},{8,11},{9,8},{10,9... | collective-permute-start | bytes 1228808 | tf_op jit(solution)/shard_map/ppermute | solution.py:34
  83.7 10.1 %collective-permute-start.15 = (f32[640,256]{1,0:T(8,128)}, f32[640,256]{1,0:T(8,128)}, u32[]{:S(2)}, u32[]{:S(2)}) collective-permute-start(f32[640,256]{1,0:T(8,128)} %get-tuple-element.27.refs_0_), channel_id=1, source_target_pairs={{0,64},{64,0},{1,65},{65,1},{2,66},{66,2},{3,67},{67,3},{4,68},{68... | collective-permute-start | bytes 1966088 | tf_op jit(solution)/shard_map/ppermute | solution.py:34
  85.2 26.8 %all-to-all-start.1 = ((bf16[8,64,512]{2,1,0:T(8,128)(2,1)}), bf16[8,64,512]{2,1,0:T(8,128)(2,1)S(1)}, u32[]{:S(2)}, u32[]{:S(2)}) async-start(bf16[8,64,512]{2,1,0:T(8,128)(2,1)} %live.1), calls=%async_computation.1 | async-start | bytes 1048576 | tf_op jit(solution)/shard_map/all_to_all | solution.py:240
  95.0 17.0 %collective-permute-start.16 = (bf16[640,256]{1,0:T(8,128)(2,1)S(1)}, bf16[640,256]{1,0:T(8,128)(2,1)S(1)}, u32[]{:S(2)}, u32[]{:S(2)}) collective-permute-start(bf16[640,256]{1,0:T(8,128)(2,1)S(1)} %add.22.ra), channel_id=1, source_target_pairs={{0,4},{4,0},{1,5},{5,1},{2,6},{6,2},{3,7},{7,3},{8,12},{12,8},{9,1... | collective-permute-start | bytes 983048 | tf_op jit(solution)/shard_map/ppermute | solution.py:34
  138.1 8.4 %collective-permute-start.18 = (bf16[2,80,1024]{2,1,0:T(8,128)(2,1)S(1)}, bf16[2,80,1024]{2,1,0:T(8,128)(2,1)S(1)}, u32[]{:S(2)}, u32[]{:S(2)}) collective-permute-start(bf16[2,80,1024]{2,1,0:T(8,128)(2,1)S(1)} %sums.1), channel_id=1, source_target_pairs={{0,128},{128,0},{1,129},{129,1},{2,130},{130,2},{3,131},{131,3},{4... | collective-permute-start | bytes 983048 | tf_op jit(solution)/shard_map/ppermute | solution.py:34
  138.9 9.1 %collective-permute-start.17 = (bf16[2,80,1024]{2,1,0:T(8,128)(2,1)S(1)}, bf16[2,80,1024]{2,1,0:T(8,128)(2,1)S(1)}, u32[]{:S(2)}, u32[]{:S(2)}) collective-permute-start(bf16[2,80,1024]{2,1,0:T(8,128)(2,1)S(1)} %sums.1), channel_id=1, source_target_pairs={{0,64},{64,0},{1,65},{65,1},{2,66},{66,2},{3,67},{67,3},{4,68},{68... | collective-permute-start | bytes 983048 | tf_op jit(solution)/shard_map/ppermute | solution.py:34
  146.5 2.9 %collective-permute-start.19 = (bf16[2,80,1024]{2,1,0:T(8,128)(2,1)S(1)}, bf16[2,80,1024]{2,1,0:T(8,128)(2,1)S(1)}, u32[]{:S(2)}, u32[]{:S(2)}) collective-permute-start(bf16[2,80,1024]{2,1,0:T(8,128)(2,1)S(1)} %collective-permute-done.18), channel_id=1, source_target_pairs={{0,64},{64,0},{1,65},{65,1},{2,66},{66,2},{3,67},{67,3},{4,68},{68... | collective-permute-start | bytes 983048 | tf_op jit(solution)/shard_map/ppermute | solution.py:34
  (10 other events, 105.5 us)
Sparse Core Ops, SparseCore 0:
  9.1 44.9 all-gather.1

commit v12 on v10

--- a/solution.py
+++ b/solution.py
@@ -134,7 +134,7 @@
         o_ref[n] = total
 
 
-def acts_kernel(core_ref, a_ref, sib, b0, b1, b2, b3a, b3b, keep, send):
+def acts_kernel(core_ref, a_ref, sib, b0, b1, b2, b3a, b3b, aside, keep, send):
     half = sib.shape[1]
     mine = a_ref[:, pl.ds(pl.multiple_of(core_ref[0] * half, 128), half)]
     for tokens, out in ((sib[...], send), (mine, keep)):
@@ -209,12 +209,12 @@
     b1, b2 = shift(b0, y=1), shift(b0, y=-1)
     b3a, b3b = shift(b1[:, : half // 2], y=1), shift(b2[:, half // 2 :], y=-1)
     parts = lax.all_to_all(partial.reshape(16, 64, 512), ("xh", "z"), split_axis=0, concat_axis=0, tiled=True)
+    copies = call(live_kernel, arr(8, 64, 512), "live", [parts], [y[None], seq_lens], [])
     wide = jax.ShapeDtypeStruct((640, 256), F32)
     sib = shift(call(cut_kernel, arr(256, half), "cut", [acts], [core[None]], [b1, b2]), core=1)
-    keep, send = call(acts_kernel, [wide, wide], "acts", [acts, sib, b0, b1, b2, b3a, b3b], [core[None]])
+    keep, send = call(acts_kernel, [wide, wide], "acts", [acts, sib, b0, b1, b2, b3a, b3b], [core[None]], [copies])
     ra = call(add_kernel, arr(640, 256), "add", [keep, shift(send, core=1)])
     rb = shift(ra, xh=1)
-    copies = call(live_kernel, arr(8, 64, 512), "live", [parts], [y[None], seq_lens], [send])
     rotated = lax.all_to_all(copies, "z", split_axis=0, concat_axis=0, tiled=True).reshape(512, 512)
 
     tiles = call(seq_kernel, arr(8, 2, 80, 512), "seq", [ra, rb, rotated], [xh[None], y[None]])

time: 178 us -> 180 us (1.011)
  starting transfers between devices: 37.2 us -> 33.4 us
  local copies, waits for them, and re-layouts: 3.69 us -> 6.93 us
    all_to_all x1, waiting for transfers between devices: 0.01 us -> 12.8 us  [per_device(): lax.all_to_all(partial.reshape(16, 64, 512), ('xh', 'z'), split_axis=0, c...]
    ppermute x20, waiting for transfers between devices: 40.8 us -> 29.7 us  [shift(): return lax.ppermute(x, axes, pairs)]
    all_to_all x1, starting transfers between devices: 8.47 us -> 5 us  [per_device(): lax.all_to_all(copies, 'z', split_axis=0, concat_axis=0, tiled=True)]
  transfers between devices with their start and end apart: 23 -> 23, of which waited for: 10 -> 9; matrix products, arithmetic and copies ran while one was open for 3% -> 3% of each run, Pallas kernels for 8% -> 6%
where the time goes in v12:
time: 180 us
  waiting for transfers between devices  58 us (32%)
  blocking collectives  44.7 us (25%)
  starting transfers between devices  33.4 us (19%)
  Pallas kernels  16.8 us (9%)
  between operations  13.5 us (8%)
  local copies, waits for them, and re-layouts  6.93 us (4%)
  matrix products  5.87 us (3%)
    ppermute x20, waiting for transfers between devices, shift(): return lax.ppermute(x, axes, pairs)  29.7 us
    all_to_all x1, blocking collectives, per_device(): lax.all_to_all(tiles, ('xh', 'y'), split_axis=0, concat_axis=0, tiled=True)  24.5 us
    all_to_all x1, blocking collectives, spread(): lax.all_to_all(jnp.broadcast_to(x[None], (count,) + x.shape), axes, split...  20.2 us
    ppermute x20, starting transfers between devices, shift(): return lax.ppermute(x, axes, pairs)  17.3 us
    all_to_all x1, waiting for transfers between devices, per_device(): lax.all_to_all(copies, 'z', split_axis=0, concat_axis=0, tiled=True)  14.8 us
    all_to_all x1, waiting for transfers between devices, per_device(): lax.all_to_all(partial.reshape(16, 64, 512), ('xh', 'z'), split_axis=0, c...  12.8 us
    pallas_call x7, Pallas kernels, call(): pl.pallas_call(kernel, out_shape=out, in_specs=specs, out_specs=jax.tree....  12.4 us
    all_to_all x1, starting transfers between devices, per_device(): lax.all_to_all(partial.reshape(16, 64, 512), ('xh', 'z'), split_axis=0, c...  11.1 us
  transfers between devices with their start and end apart: 23, of which 9 were waited for; matrix products, arithmetic and copies ran while one was open for 3% of the time, Pallas kernels for 6%

profile of v12, /device:TPU:24, one launch (start us, length us, event | category | flops | bytes accessed | tf_op | source)
XLA Modules:
  0.0 179.9 jit_solution(6125339206153395565)
XLA Ops:
  7.3 4.3 %pick.1 = (bf16[216,1024]{1,0:T(8,128)(2,1)}, bf16[216,512]{1,0:T(8,128)(2,1)}, bf16[216,512]{1,0:T(8,128)(2,1)}, bf16[216,512]{1,0:T(8,128)(2,1)}, bf16[216,512]{1,0:T(8,128)(2,1)}, /*index=5*/bf16[216,512]{1,0:T(8,128)(2,1)}) custom-call(s32[8]{0:T(128)} %ids.1, s32[1]{0:T(128)} %bitcast.1.y_ref, s32[1]{0:T(128)} %bitcast.2.core_ref.s_ref, ...), custom_call_target="tpu_custom_call" | custom-call | tf_op jit(solution)/shard_map/pick/pallas_call | solution.py:80
  12.4 2.5 %collective-permute-start = (bf16[216,512]{1,0:T(8,128)(2,1)}, bf16[216,512]{1,0:T(8,128)(2,1)S(1)}, u32[]{:S(2)}, u32[]{:S(2)}) collective-permute-start(bf16[216,512]{1,0:T(8,128)(2,1)} %get-tuple-element.16), channel_id=1, source_target_pairs={{0,1},{1,2},{2,3},{3,0},{4,5},{5,6},{6,7},{7,4},{8,9},{9,10},{10,1... | collective-permute-start | bytes 663560 | tf_op jit(solution)/shard_map/ppermute | solution.py:34
  16.9 4.5 %collective-permute-done.1.h2 = bf16[216,512]{1,0:T(8,128)(2,1)S(1)} collective-permute-done((bf16[216,512]{1,0:T(8,128)(2,1)}, bf16[216,512]{1,0:T(8,128)(2,1)S(1)}, u32[]{:S(2)}, u32[]{:S(2)}) %collective-permute-start.1) | collective-permute-done | bytes 221216 | tf_op jit(solution)/shard_map/ppermute | solution.py:34
  21.4 2.8 %collective-permute-start.9 = (bf16[80,2560]{1,0:T(8,128)(2,1)S(1)}, bf16[80,2560]{1,0:T(8,128)(2,1)S(1)}, u32[]{:S(2)}, u32[]{:S(2)}) collective-permute-start(bf16[80,2560]{1,0:T(8,128)(2,1)S(1)} %halve.1.b_own), channel_id=1, source_target_pairs={{0,132},{4,128},{128,4},{132,0},{1,133},{5,129},{129,5},{133,1},{2... | collective-permute-start | bytes 1228808 | tf_op jit(solution)/shard_map/ppermute | solution.py:34
  26.1 8.3 %collective-permute-done.2.h3 = bf16[216,512]{1,0:T(8,128)(2,1)S(1)} collective-permute-done((bf16[216,512]{1,0:T(8,128)(2,1)S(1)}, bf16[216,512]{1,0:T(8,128)(2,1)S(1)}, u32[]{:S(2)}, u32[]{:S(2)}) %collective-permute-start.2) | collective-permute-done | bytes 221216 | tf_op jit(solution)/shard_map/ppermute | solution.py:34
  35.9 2.3 %grads.1 = (bf16[1024,512]{1,0:T(8,128)(2,1)S(1)}, bf16[160,2560]{1,0:T(8,128)(2,1)}) custom-call(s32[1]{0:T(128)} %bitcast.2.core_ref.s_ref, bf16[216,1024]{1,0:T(8,128)(2,1)S(1)} %copy-done.7, bf16[216,512]{1,0:T(8,128)(2,1)S(1)} %collective-permute-done.h1, bf16[216,512]{1,0:T(8,128)(2,1)S(1)} %collective-permute-done.1.h2, ...), custom_call_target="tpu_custom_call" | custom-call | flops 1 | bytes 1 | tf_op jit(solution)/shard_map/grads/pallas_call | solution.py:176
  39.2 2.0 %collective-permute-start.11 = (bf16[160,2560]{1,0:T(8,128)(2,1)}, bf16[160,2560]{1,0:T(8,128)(2,1)S(1)}, u32[]{:S(2)}, u32[]{:S(2)}) collective-permute-start(bf16[160,2560]{1,0:T(8,128)(2,1)} %get-tuple-element.21.b0), channel_id=1, source_target_pairs={{0,3},{1,0},{2,1},{3,2},{4,7},{5,4},{6,5},{7,6},{8,11},{9,8},{10,9... | collective-permute-start | bytes 2457608 | tf_op jit(solution)/shard_map/ppermute | solution.py:34
  41.2 11.1 %all-to-all-start = ((bf16[16,64,512]{2,1,0:T(8,128)(2,1)}), bf16[16,64,512]{2,1,0:T(8,128)(2,1)}, u32[]{:S(2)}, u32[]{:S(2)}) async-start(bf16[16,64,512]{2,1,0:T(8,128)(2,1)} %bitcast.26), calls=%async_computation | async-start | bytes 2097152 | tf_op jit(solution)/shard_map/all_to_all | solution.py:211
  52.3 7.4 %collective-permute-done.10.refs_0_.b1 = bf16[160,2560]{1,0:T(8,128)(2,1)S(1)} collective-permute-done((bf16[160,2560]{1,0:T(8,128)(2,1)}, bf16[160,2560]{1,0:T(8,128)(2,1)S(1)}, u32[]{:S(2)}, u32[]{:S(2)}) %collective-permute-start.10) | collective-permute-done | bytes 819232 | tf_op jit(solution)/shard_map/ppermute | solution.py:34
  60.9 1.7 copy-done.1
  65.7 1.7 collective-permute-start.14
  67.4 12.8 %all-to-all-done.parts = bf16[16,64,512]{2,1,0:T(8,128)(2,1)} async-done(((bf16[16,64,512]{2,1,0:T(8,128)(2,1)}), bf16[16,64,512]{2,1,0:T(8,128)(2,1)}, u32[]{:S(2)}, u32[]{:S(2)}) %all-to-all-start) | async-done | bytes 1048608 | tf_op jit(solution)/shard_map/all_to_all | solution.py:211
  80.2 2.2 %live.1.aside = bf16[8,64,512]{2,1,0:T(8,128)(2,1)} custom-call(s32[1]{0:T(128)} %bitcast.1.y_ref, s32[2]{0:T(128)S(1)} %copy-done.9, bf16[16,64,512]{2,1,0:T(8,128)(2,1)} %all-to-all-done.parts), custom_call_target="tpu_custom_call" | custom-call | flops 1 | bytes 1 | tf_op jit(solution)/shard_map/live/pallas_call | solution.py:176
  82.4 1.7 copy-done.2
  84.2 5.2 %acts.1 = (f32[640,256]{1,0:T(8,128)S(1)}, f32[640,256]{1,0:T(8,128)}) custom-call(s32[1]{0:T(128)} %bitcast.2.core_ref.s_ref, bf16[256,5120]{1,0:T(8,128)(2,1)S(1)} %copy-done.2, bf16[256,2560]{1,0:T(8,128)(2,1)} %collective-permute-done.12.sib, bf16[160,2560]{1,0:T(8,128)(2,1)} %get-tuple-element.21.b0, ...), custom_call_target="tpu_custom_call" | custom-call | flops 1 | bytes 1 | tf_op jit(solution)/shard_map/acts/pallas_call | solution.py:176
  90.2 5.0 %all-to-all-start.1 = ((bf16[8,64,512]{2,1,0:T(8,128)(2,1)}), bf16[8,64,512]{2,1,0:T(8,128)(2,1)S(1)}, u32[]{:S(2)}, u32[]{:S(2)}) async-start(bf16[8,64,512]{2,1,0:T(8,128)(2,1)} %live.1.aside), calls=%async_computation.1 | async-start | bytes 1048576 | tf_op jit(solution)/shard_map/all_to_all | solution.py:218
  95.3 3.1 %collective-permute-start.16 = (bf16[640,256]{1,0:T(8,128)(2,1)S(1)}, bf16[640,256]{1,0:T(8,128)(2,1)S(1)}, u32[]{:S(2)}, u32[]{:S(2)}) collective-permute-start(bf16[640,256]{1,0:T(8,128)(2,1)S(1)} %add.22.ra), channel_id=1, source_target_pairs={{0,4},{4,0},{1,5},{5,1},{2,6},{6,2},{3,7},{7,3},{8,12},{12,8},{9,1... | collective-permute-start | bytes 983048 | tf_op jit(solution)/shard_map/ppermute | solution.py:34
  98.4 14.8 %all-to-all-done.1 = bf16[8,64,512]{2,1,0:T(8,128)(2,1)S(1)} async-done(((bf16[8,64,512]{2,1,0:T(8,128)(2,1)}), bf16[8,64,512]{2,1,0:T(8,128)(2,1)S(1)}, u32[]{:S(2)}, u32[]{:S(2)}) %all-to-all-start.1) | async-done | bytes 524320 | tf_op jit(solution)/shard_map/all_to_all | solution.py:218
  114.6 24.5 %all_to_all.20.parts = bf16[8,2,80,512]{3,2,1,0:T(8,128)(2,1)S(1)} all-to-all(bf16[8,2,80,512]{3,2,1,0:T(8,128)(2,1)S(1)} %seq.1), channel_id=1, replica_groups=mesh['xl'=2,'core'=2,'z'=8,'xh'=2,'y'=4] {'xh','y'}, dimensions={0} | all-to-all | bytes 2621440 | tf_op jit(solution)/shard_map/all_to_all | solution.py:221
  140.1 1.5 convolution_bitcast_fusion.3
  141.6 6.1 %collective-permute-done.18 = bf16[2,80,1024]{2,1,0:T(8,128)(2,1)S(1)} collective-permute-done((bf16[2,80,1024]{2,1,0:T(8,128)(2,1)S(1)}, bf16[2,80,1024]{2,1,0:T(8,128)(2,1)S(1)}, u32[]{:S(2)}, u32[]{:S(2)}) %collective-permute-start.18) | collective-permute-done | bytes 327712 | tf_op jit(solution)/shard_map/ppermute | solution.py:34
  149.1 1.5 convolution_bitcast_fusion.2
  150.6 1.5 convolution_bitcast_fusion
  152.2 20.2 %all_to_all.21 = f32[64,8,8]{2,1,0:T(8,128)S(1)} all-to-all(f32[64,8,8]{2,1,0:T(8,128)S(1)} %broadcast_in_dim.11), channel_id=1, replica_groups=mesh['xl'=2,'core'=2,'z'=8,'xh'=2,'y'=4] {'z','xh','y'}, dimensions={0} | all-to-all | bytes 32768 | tf_op jit(solution)/shard_map/all_to_all | solution.py:38
  (65 shorter events, 17.6 us)
Async XLA Ops:
  6.5 133.6 %copy-start = (bf16[8,80,1024]{2,1,0:T(8,128)(2,1)S(1)}, bf16[8,80,1024]{2,1,0:T(8,128)(2,1)}, u32[]{:S(2)}) copy-start(bf16[8,80,1024]{2,1,0:T(8,128)(2,1)} %param.13) | copy-start | bytes 3932164
  6.5 54.4 %all-gather.2.cloned.1.call-start = ((), (), s32[]{:S(2)}) async-start(), calls=%async_computation.4 | async-start | bytes 2949120 | tf_op jit(solution)/shard_map/all_gather | solution.py:193
  11.6 9.8 %collective-permute-start.1 = (bf16[216,512]{1,0:T(8,128)(2,1)}, bf16[216,512]{1,0:T(8,128)(2,1)S(1)}, u32[]{:S(2)}, u32[]{:S(2)}) collective-permute-start(bf16[216,512]{1,0:T(8,128)(2,1)} %get-tuple-element.16), channel_id=1, source_target_pairs={{0,3},{1,0},{2,1},{3,2},{4,7},{5,4},{6,5},{7,6},{8,11},{9,8},{10,9... | collective-permute-start | bytes 663560 | tf_op jit(solution)/shard_map/ppermute | solution.py:34
  12.4 11.9 %collective-permute-start = (bf16[216,512]{1,0:T(8,128)(2,1)}, bf16[216,512]{1,0:T(8,128)(2,1)S(1)}, u32[]{:S(2)}, u32[]{:S(2)}) collective-permute-start(bf16[216,512]{1,0:T(8,128)(2,1)} %get-tuple-element.16), channel_id=1, source_target_pairs={{0,1},{1,2},{2,3},{3,0},{4,5},{5,6},{6,7},{7,4},{8,9},{9,10},{10,1... | collective-permute-start | bytes 663560 | tf_op jit(solution)/shard_map/ppermute | solution.py:34
  14.9 10.5 %collective-permute-start.6 = (bf16[216,512]{1,0:T(8,128)(2,1)}, bf16[216,512]{1,0:T(8,128)(2,1)S(1)}, u32[]{:S(2)}, u32[]{:S(2)}) collective-permute-start(bf16[216,512]{1,0:T(8,128)(2,1)} %get-tuple-element.18), channel_id=1, source_target_pairs={{0,1},{1,2},{2,3},{3,0},{4,5},{5,6},{6,7},{7,4},{8,9},{9,10},{10,1... | collective-permute-start | bytes 663560 | tf_op jit(solution)/shard_map/ppermute | solution.py:34
  15.6 10.5 %collective-permute-start.7 = (bf16[216,512]{1,0:T(8,128)(2,1)}, bf16[216,512]{1,0:T(8,128)(2,1)S(1)}, u32[]{:S(2)}, u32[]{:S(2)}) collective-permute-start(bf16[216,512]{1,0:T(8,128)(2,1)} %get-tuple-element.19), channel_id=1, source_target_pairs={{0,3},{1,0},{2,1},{3,2},{4,7},{5,4},{6,5},{7,6},{8,11},{9,8},{10,9... | collective-permute-start | bytes 663560 | tf_op jit(solution)/shard_map/ppermute | solution.py:34
  21.4 13.1 %collective-permute-start.2 = (bf16[216,512]{1,0:T(8,128)(2,1)S(1)}, bf16[216,512]{1,0:T(8,128)(2,1)S(1)}, u32[]{:S(2)}, u32[]{:S(2)}) collective-permute-start(bf16[216,512]{1,0:T(8,128)(2,1)S(1)} %collective-permute-done.1.h2), channel_id=1, source_target_pairs={{0,3},{1,0},{2,1},{3,2},{4,7},{5,4},{6,5},{7,6},{8,11},{9,8},{10,9... | collective-permute-start | bytes 663560 | tf_op jit(solution)/shard_map/ppermute | solution.py:34
  21.4 13.0 %collective-permute-start.9 = (bf16[80,2560]{1,0:T(8,128)(2,1)S(1)}, bf16[80,2560]{1,0:T(8,128)(2,1)S(1)}, u32[]{:S(2)}, u32[]{:S(2)}) collective-permute-start(bf16[80,2560]{1,0:T(8,128)(2,1)S(1)} %halve.1.b_own), channel_id=1, source_target_pairs={{0,132},{4,128},{128,4},{132,0},{1,133},{5,129},{129,5},{133,1},{2... | collective-permute-start | bytes 1228808 | tf_op jit(solution)/shard_map/ppermute | solution.py:34
  24.3 10.2 %collective-permute-start.8 = (bf16[216,512]{1,0:T(8,128)(2,1)}, bf16[216,512]{1,0:T(8,128)(2,1)S(1)}, u32[]{:S(2)}, u32[]{:S(2)}) collective-permute-start(bf16[216,512]{1,0:T(8,128)(2,1)} %get-tuple-element.20), channel_id=1, source_target_pairs={{0,2},{1,3},{2,0},{3,1},{4,6},{5,7},{6,4},{7,5},{8,10},{9,11},{10,... | collective-permute-start | bytes 663560 | tf_op jit(solution)/shard_map/ppermute | solution.py:34
  25.4 9.1 %collective-permute-start.4 = (bf16[216,512]{1,0:T(8,128)(2,1)S(1)}, bf16[216,512]{1,0:T(8,128)(2,1)S(1)}, u32[]{:S(2)}, u32[]{:S(2)}) collective-permute-start(bf16[216,512]{1,0:T(8,128)(2,1)S(1)} %collective-permute-done.1.h2), channel_id=1, source_target_pairs={{0,64},{64,0},{1,65},{65,1},{2,66},{66,2},{3,67},{67,3},{4,68},{68... | collective-permute-start | bytes 663560 | tf_op jit(solution)/shard_map/ppermute | solution.py:34
  26.1 8.4 %collective-permute-start.3 = (bf16[216,512]{1,0:T(8,128)(2,1)S(1)}, bf16[216,512]{1,0:T(8,128)(2,1)S(1)}, u32[]{:S(2)}, u32[]{:S(2)}) collective-permute-start(bf16[216,512]{1,0:T(8,128)(2,1)S(1)} %collective-permute-done.h1), channel_id=1, source_target_pairs={{0,64},{64,0},{1,65},{65,1},{2,66},{66,2},{3,67},{67,3},{4,68},{68... | collective-permute-start | bytes 663560 | tf_op jit(solution)/shard_map/ppermute | solution.py:34
  34.5 1.5 collective-permute-start.5
  39.2 20.5 %collective-permute-start.10 = (bf16[160,2560]{1,0:T(8,128)(2,1)}, bf16[160,2560]{1,0:T(8,128)(2,1)S(1)}, u32[]{:S(2)}, u32[]{:S(2)}) collective-permute-start(bf16[160,2560]{1,0:T(8,128)(2,1)} %get-tuple-element.21.b0), channel_id=1, source_target_pairs={{0,1},{1,2},{2,3},{3,0},{4,5},{5,6},{6,7},{7,4},{8,9},{9,10},{10,1... | collective-permute-start | bytes 2457608 | tf_op jit(solution)/shard_map/ppermute | solution.py:34
  39.2 21.7 %collective-permute-start.11 = (bf16[160,2560]{1,0:T(8,128)(2,1)}, bf16[160,2560]{1,0:T(8,128)(2,1)S(1)}, u32[]{:S(2)}, u32[]{:S(2)}) collective-permute-start(bf16[160,2560]{1,0:T(8,128)(2,1)} %get-tuple-element.21.b0), channel_id=1, source_target_pairs={{0,3},{1,0},{2,1},{3,2},{4,7},{5,4},{6,5},{7,6},{8,11},{9,8},{10,9... | collective-permute-start | bytes 2457608 | tf_op jit(solution)/shard_map/ppermute | solution.py:34
  41.2 39.0 %all-to-all-start = ((bf16[16,64,512]{2,1,0:T(8,128)(2,1)}), bf16[16,64,512]{2,1,0:T(8,128)(2,1)}, u32[]{:S(2)}, u32[]{:S(2)}) async-start(bf16[16,64,512]{2,1,0:T(8,128)(2,1)} %bitcast.26), calls=%async_computation | async-start | bytes 2097152 | tf_op jit(solution)/shard_map/all_to_all | solution.py:211
  63.8 18.6 %collective-permute-start.12 = (bf16[256,2560]{1,0:T(8,128)(2,1)}, bf16[256,2560]{1,0:T(8,128)(2,1)}, u32[]{:S(2)}, u32[]{:S(2)}) collective-permute-start(bf16[256,2560]{1,0:T(8,128)(2,1)} %cut.1), channel_id=1, source_target_pairs={{0,64},{64,0},{1,65},{65,1},{2,66},{66,2},{3,67},{67,3},{4,68},{68... | collective-permute-start | bytes 3932168 | tf_op jit(solution)/shard_map/ppermute | solution.py:34
  64.6 17.8 %collective-permute-start.13 = (bf16[160,1280]{1,0:T(8,128)(2,1)}, bf16[160,1280]{1,0:T(8,128)(2,1)S(1)}, u32[]{:S(2)}, u32[]{:S(2)}) collective-permute-start(bf16[160,1280]{1,0:T(8,128)(2,1)} %slice.8), channel_id=1, source_target_pairs={{0,1},{1,2},{2,3},{3,0},{4,5},{5,6},{6,7},{7,4},{8,9},{9,10},{10,1... | collective-permute-start | bytes 1228808 | tf_op jit(solution)/shard_map/ppermute | solution.py:34
  65.7 16.7 %collective-permute-start.14 = (bf16[160,1280]{1,0:T(8,128)(2,1)}, bf16[160,1280]{1,0:T(8,128)(2,1)}, u32[]{:S(2)}, u32[]{:S(2)}) collective-permute-start(bf16[160,1280]{1,0:T(8,128)(2,1)} %slice.9), channel_id=1, source_target_pairs={{0,3},{1,0},{2,1},{3,2},{4,7},{5,4},{6,5},{7,6},{8,11},{9,8},{10,9... | collective-permute-start | bytes 1228808 | tf_op jit(solution)/shard_map/ppermute | solution.py:34
  90.2 5.0 %collective-permute-start.15 = (f32[640,256]{1,0:T(8,128)}, f32[640,256]{1,0:T(8,128)S(1)}, u32[]{:S(2)}, u32[]{:S(2)}) collective-permute-start(f32[640,256]{1,0:T(8,128)} %get-tuple-element.24), channel_id=1, source_target_pairs={{0,64},{64,0},{1,65},{65,1},{2,66},{66,2},{3,67},{67,3},{4,68},{68... | collective-permute-start | bytes 1966088 | tf_op jit(solution)/shard_map/ppermute | solution.py:34
  90.2 23.0 %all-to-all-start.1 = ((bf16[8,64,512]{2,1,0:T(8,128)(2,1)}), bf16[8,64,512]{2,1,0:T(8,128)(2,1)S(1)}, u32[]{:S(2)}, u32[]{:S(2)}) async-start(bf16[8,64,512]{2,1,0:T(8,128)(2,1)} %live.1.aside), calls=%async_computation.1 | async-start | bytes 1048576 | tf_op jit(solution)/shard_map/all_to_all | solution.py:218
  95.3 17.9 %collective-permute-start.16 = (bf16[640,256]{1,0:T(8,128)(2,1)S(1)}, bf16[640,256]{1,0:T(8,128)(2,1)S(1)}, u32[]{:S(2)}, u32[]{:S(2)}) collective-permute-start(bf16[640,256]{1,0:T(8,128)(2,1)S(1)} %add.22.ra), channel_id=1, source_target_pairs={{0,4},{4,0},{1,5},{5,1},{2,6},{6,2},{3,7},{7,3},{8,12},{12,8},{9,1... | collective-permute-start | bytes 983048 | tf_op jit(solution)/shard_map/ppermute | solution.py:34
  139.3 8.4 %collective-permute-start.18 = (bf16[2,80,1024]{2,1,0:T(8,128)(2,1)S(1)}, bf16[2,80,1024]{2,1,0:T(8,128)(2,1)S(1)}, u32[]{:S(2)}, u32[]{:S(2)}) collective-permute-start(bf16[2,80,1024]{2,1,0:T(8,128)(2,1)S(1)} %sums.1), channel_id=1, source_target_pairs={{0,128},{128,0},{1,129},{129,1},{2,130},{130,2},{3,131},{131,3},{4... | collective-permute-start | bytes 983048 | tf_op jit(solution)/shard_map/ppermute | solution.py:34
  140.1 9.0 %collective-permute-start.17 = (bf16[2,80,1024]{2,1,0:T(8,128)(2,1)S(1)}, bf16[2,80,1024]{2,1,0:T(8,128)(2,1)S(1)}, u32[]{:S(2)}, u32[]{:S(2)}) collective-permute-start(bf16[2,80,1024]{2,1,0:T(8,128)(2,1)S(1)} %sums.1), channel_id=1, source_target_pairs={{0,64},{64,0},{1,65},{65,1},{2,66},{66,2},{3,67},{67,3},{4,68},{68... | collective-permute-start | bytes 983048 | tf_op jit(solution)/shard_map/ppermute | solution.py:34
  147.7 2.9 %collective-permute-start.19 = (bf16[2,80,1024]{2,1,0:T(8,128)(2,1)S(1)}, bf16[2,80,1024]{2,1,0:T(8,128)(2,1)S(1)}, u32[]{:S(2)}, u32[]{:S(2)}) collective-permute-start(bf16[2,80,1024]{2,1,0:T(8,128)(2,1)S(1)} %collective-permute-done.18), channel_id=1, source_target_pairs={{0,64},{64,0},{1,65},{65,1},{2,66},{66,2},{3,67},{67,3},{4,68},{68... | collective-permute-start | bytes 983048 | tf_op jit(solution)/shard_map/ppermute | solution.py:34
  (9 other events, 89.6 us)
Sparse Core Ops, SparseCore 0:
  9.1 44.9 all-gather.1

commit v13 on v10

--- a/solution.py
+++ b/solution.py
@@ -233,7 +233,7 @@
     scores = jnp.concatenate(
         [lax.dynamic_index_in_dim(scored, here ^ d, 0, keepdims=False) for d in range(4)], axis=0
     )
-    return jnp.sum(spread(scores, ("z", "xh", "y"), 64), axis=0)
+    return jnp.sum(spread(scores.reshape(1, 64), ("z", "xh", "y"), 64), axis=0).reshape(8, 8)
 
 
 def solution(mesh):

time: 178 us -> 176 us (0.989)
  blocking collectives: 44.7 us -> 40.9 us
    all_to_all x1, blocking collectives: 20.2 us -> 16.4 us  [spread(): lax.all_to_all(jnp.broadcast_to(x[None], (count,) + x.shape), axes, split...]
where the time goes in v13:
time: 176 us; the launch traced here: 174 us
  waiting for transfers between devices  56.5 us (32%)
  blocking collectives  40.9 us (23%)
  starting transfers between devices  37.2 us (21%)
  Pallas kernels  15.2 us (9%)
  between operations  13.6 us (8%)
  matrix products  5.87 us (3%)
  local copies, waits for them, and re-layouts  4.45 us (3%)
    ppermute x20, waiting for transfers between devices, shift(): return lax.ppermute(x, axes, pairs)  40.8 us
    all_to_all x1, blocking collectives, per_device(): lax.all_to_all(tiles, ('xh', 'y'), split_axis=0, concat_axis=0, tiled=True)  24.5 us
    ppermute x20, starting transfers between devices, shift(): return lax.ppermute(x, axes, pairs)  17.7 us
    all_to_all x1, blocking collectives, spread(): lax.all_to_all(jnp.broadcast_to(x[None], (count,) + x.shape), axes, split...  16.4 us
    all_to_all x1, waiting for transfers between devices, per_device(): lax.all_to_all(copies, 'z', split_axis=0, concat_axis=0, tiled=True)  15 us
    all_to_all x1, starting transfers between devices, per_device(): lax.all_to_all(partial.reshape(16, 64, 512), ('xh', 'z'), split_axis=0, c...  11.1 us
    pallas_call x7, Pallas kernels, call(): pl.pallas_call(kernel, out_shape=out, in_specs=specs, out_specs=jax.tree....  10.9 us
    all_to_all x1, starting transfers between devices, per_device(): lax.all_to_all(copies, 'z', split_axis=0, concat_axis=0, tiled=True)  8.47 us
  transfers between devices with their start and end apart: 23, of which 10 were waited for; matrix products, arithmetic and copies ran while one was open for 3% of the time, Pallas kernels for 8%

profile of v13, /device:TPU:24, one launch (start us, length us, event | category | flops | bytes accessed | tf_op | source)
XLA Modules:
  0.0 173.7 jit_solution(9870840341510934847)
XLA Ops:
  7.3 4.3 %pick.1 = (bf16[216,1024]{1,0:T(8,128)(2,1)}, bf16[216,512]{1,0:T(8,128)(2,1)}, bf16[216,512]{1,0:T(8,128)(2,1)}, bf16[216,512]{1,0:T(8,128)(2,1)}, bf16[216,512]{1,0:T(8,128)(2,1)}, /*index=5*/bf16[216,512]{1,0:T(8,128)(2,1)}) custom-call(s32[8]{0:T(128)} %ids.1, s32[1]{0:T(128)} %bitcast.1.y_ref, s32[1]{0:T(128)} %bitcast.2.core_ref.s_ref, ...), custom_call_target="tpu_custom_call" | custom-call | tf_op jit(solution)/shard_map/pick/pallas_call | solution.py:80
  12.4 2.5 %collective-permute-start = (bf16[216,512]{1,0:T(8,128)(2,1)}, bf16[216,512]{1,0:T(8,128)(2,1)S(1)}, u32[]{:S(2)}, u32[]{:S(2)}) collective-permute-start(bf16[216,512]{1,0:T(8,128)(2,1)} %get-tuple-element.16), channel_id=1, source_target_pairs={{0,1},{1,2},{2,3},{3,0},{4,5},{5,6},{6,7},{7,4},{8,9},{9,10},{10,1... | collective-permute-start | bytes 663560 | tf_op jit(solution)/shard_map/ppermute | solution.py:34
  16.9 4.5 %collective-permute-done.1.h2 = bf16[216,512]{1,0:T(8,128)(2,1)S(1)} collective-permute-done((bf16[216,512]{1,0:T(8,128)(2,1)}, bf16[216,512]{1,0:T(8,128)(2,1)S(1)}, u32[]{:S(2)}, u32[]{:S(2)}) %collective-permute-start.1) | collective-permute-done | bytes 221216 | tf_op jit(solution)/shard_map/ppermute | solution.py:34
  21.4 2.8 %collective-permute-start.9 = (bf16[80,2560]{1,0:T(8,128)(2,1)S(1)}, bf16[80,2560]{1,0:T(8,128)(2,1)S(1)}, u32[]{:S(2)}, u32[]{:S(2)}) collective-permute-start(bf16[80,2560]{1,0:T(8,128)(2,1)S(1)} %halve.1.b_own), channel_id=1, source_target_pairs={{0,132},{4,128},{128,4},{132,0},{1,133},{5,129},{129,5},{133,1},{2... | collective-permute-start | bytes 1228808 | tf_op jit(solution)/shard_map/ppermute | solution.py:34
  26.1 8.3 %collective-permute-done.2.h3 = bf16[216,512]{1,0:T(8,128)(2,1)S(1)} collective-permute-done((bf16[216,512]{1,0:T(8,128)(2,1)S(1)}, bf16[216,512]{1,0:T(8,128)(2,1)S(1)}, u32[]{:S(2)}, u32[]{:S(2)}) %collective-permute-start.2) | collective-permute-done | bytes 221216 | tf_op jit(solution)/shard_map/ppermute | solution.py:34
  35.9 2.2 %grads.1 = (bf16[1024,512]{1,0:T(8,128)(2,1)S(1)}, bf16[160,2560]{1,0:T(8,128)(2,1)}) custom-call(s32[1]{0:T(128)} %bitcast.2.core_ref.s_ref, bf16[216,1024]{1,0:T(8,128)(2,1)S(1)} %copy-done.7, bf16[216,512]{1,0:T(8,128)(2,1)S(1)} %collective-permute-done.h1, bf16[216,512]{1,0:T(8,128)(2,1)S(1)} %collective-permute-done.1.h2, ...), custom_call_target="tpu_custom_call" | custom-call | flops 1 | bytes 1 | tf_op jit(solution)/shard_map/grads/pallas_call | solution.py:176
  39.1 2.0 %collective-permute-start.11 = (bf16[160,2560]{1,0:T(8,128)(2,1)}, bf16[160,2560]{1,0:T(8,128)(2,1)S(1)}, u32[]{:S(2)}, u32[]{:S(2)}) collective-permute-start(bf16[160,2560]{1,0:T(8,128)(2,1)} %get-tuple-element.21.b0), channel_id=1, source_target_pairs={{0,3},{1,0},{2,1},{3,2},{4,7},{5,4},{6,5},{7,6},{8,11},{9,8},{10,9... | collective-permute-start | bytes 2457608 | tf_op jit(solution)/shard_map/ppermute | solution.py:34
  41.2 11.1 %all-to-all-start = ((bf16[16,64,512]{2,1,0:T(8,128)(2,1)}), bf16[16,64,512]{2,1,0:T(8,128)(2,1)}, u32[]{:S(2)}, u32[]{:S(2)}) async-start(bf16[16,64,512]{2,1,0:T(8,128)(2,1)} %bitcast.27), calls=%async_computation | async-start | bytes 2097152 | tf_op jit(solution)/shard_map/all_to_all | solution.py:211
  52.3 7.4 %collective-permute-done.10.refs_0_.b1 = bf16[160,2560]{1,0:T(8,128)(2,1)S(1)} collective-permute-done((bf16[160,2560]{1,0:T(8,128)(2,1)}, bf16[160,2560]{1,0:T(8,128)(2,1)S(1)}, u32[]{:S(2)}, u32[]{:S(2)}) %collective-permute-start.10) | collective-permute-done | bytes 819232 | tf_op jit(solution)/shard_map/ppermute | solution.py:34
  60.9 1.7 %copy-done.1 = bf16[256,5120]{1,0:T(8,128)(2,1)S(1)} copy-done((bf16[256,5120]{1,0:T(8,128)(2,1)S(1)}, bf16[256,5120]{1,0:T(8,128)(2,1)}, u32[]{:S(2)}) %copy-start.1) | copy-done | bytes 2621464
  63.4 1.8 %collective-permute-start.14 = (bf16[160,1280]{1,0:T(8,128)(2,1)S(1)}, bf16[160,1280]{1,0:T(8,128)(2,1)S(1)}, u32[]{:S(2)}, u32[]{:S(2)}) collective-permute-start(bf16[160,1280]{1,0:T(8,128)(2,1)S(1)} %slice.9), channel_id=1, source_target_pairs={{0,3},{1,0},{2,1},{3,2},{4,7},{5,4},{6,5},{7,6},{8,11},{9,8},{10,9... | collective-permute-start | bytes 1228808 | tf_op jit(solution)/shard_map/ppermute | solution.py:34
  65.2 9.7 %collective-permute-done.13.b3a = bf16[160,1280]{1,0:T(8,128)(2,1)S(1)} collective-permute-done((bf16[160,1280]{1,0:T(8,128)(2,1)S(1)}, bf16[160,1280]{1,0:T(8,128)(2,1)S(1)}, u32[]{:S(2)}, u32[]{:S(2)}) %collective-permute-start.13) | collective-permute-done | bytes 409632 | tf_op jit(solution)/shard_map/ppermute | solution.py:34
  76.3 4.7 %acts.1 = (f32[640,256]{1,0:T(8,128)S(1)}, f32[640,256]{1,0:T(8,128)}) custom-call(s32[1]{0:T(128)} %bitcast.2.core_ref.s_ref, bf16[256,5120]{1,0:T(8,128)(2,1)S(1)} %copy-done.2, bf16[256,2560]{1,0:T(8,128)(2,1)S(1)} %collective-permute-done.12.sib, bf16[160,2560]{1,0:T(8,128)(2,1)} %get-tuple-element.21.b0, ...), custom_call_target="tpu_custom_call" | custom-call | flops 1 | bytes 1 | tf_op jit(solution)/shard_map/acts/pallas_call | solution.py:176
  81.9 2.3 %live.1 = bf16[8,64,512]{2,1,0:T(8,128)(2,1)} custom-call(s32[1]{0:T(128)} %bitcast.1.y_ref, s32[2]{0:T(128)S(1)} %copy-done.9, bf16[16,64,512]{2,1,0:T(8,128)(2,1)} %all-to-all-done.parts, f32[640,256]{1,0:T(8,128)} %get-tuple-element.23.refs_0_), custom_call_target="tpu_custom_call" | custom-call | flops 1 | bytes 1 | tf_op jit(solution)/shard_map/live/pallas_call | solution.py:176
  84.2 8.5 %all-to-all-start.1 = ((bf16[8,64,512]{2,1,0:T(8,128)(2,1)}), bf16[8,64,512]{2,1,0:T(8,128)(2,1)S(1)}, u32[]{:S(2)}, u32[]{:S(2)}) async-start(bf16[8,64,512]{2,1,0:T(8,128)(2,1)} %live.1), calls=%async_computation.1 | async-start | bytes 1048576 | tf_op jit(solution)/shard_map/all_to_all | solution.py:218
  92.7 3.1 %collective-permute-start.16 = (bf16[640,256]{1,0:T(8,128)(2,1)S(1)}, bf16[640,256]{1,0:T(8,128)(2,1)S(1)}, u32[]{:S(2)}, u32[]{:S(2)}) collective-permute-start(bf16[640,256]{1,0:T(8,128)(2,1)S(1)} %add.22.ra), channel_id=1, source_target_pairs={{0,4},{4,0},{1,5},{5,1},{2,6},{6,2},{3,7},{7,3},{8,12},{12,8},{9,1... | collective-permute-start | bytes 983048 | tf_op jit(solution)/shard_map/ppermute | solution.py:34
  95.8 15.0 %all-to-all-done.1 = bf16[8,64,512]{2,1,0:T(8,128)(2,1)S(1)} async-done(((bf16[8,64,512]{2,1,0:T(8,128)(2,1)}), bf16[8,64,512]{2,1,0:T(8,128)(2,1)S(1)}, u32[]{:S(2)}, u32[]{:S(2)}) %all-to-all-start.1) | async-done | bytes 524320 | tf_op jit(solution)/shard_map/all_to_all | solution.py:218
  112.2 24.5 %all_to_all.20.parts = bf16[8,2,80,512]{3,2,1,0:T(8,128)(2,1)S(1)} all-to-all(bf16[8,2,80,512]{3,2,1,0:T(8,128)(2,1)S(1)} %seq.1), channel_id=1, replica_groups=mesh['xl'=2,'core'=2,'z'=8,'xh'=2,'y'=4] {'xh','y'}, dimensions={0} | all-to-all | bytes 2621440 | tf_op jit(solution)/shard_map/all_to_all | solution.py:221
  137.6 1.5 convolution_bitcast_fusion.3
  139.1 6.1 %collective-permute-done.18 = bf16[2,80,1024]{2,1,0:T(8,128)(2,1)S(1)} collective-permute-done((bf16[2,80,1024]{2,1,0:T(8,128)(2,1)S(1)}, bf16[2,80,1024]{2,1,0:T(8,128)(2,1)S(1)}, u32[]{:S(2)}, u32[]{:S(2)}) %collective-permute-start.18) | collective-permute-done | bytes 327712 | tf_op jit(solution)/shard_map/ppermute | solution.py:34
  145.2 1.5 convolution_bitcast_fusion.1
  146.7 1.5 convolution_bitcast_fusion.2
  148.2 1.5 convolution_bitcast_fusion
  149.8 16.4 %all_to_all.21 = f32[64,1,64]{2,1,0:T(1,128)S(1)} all-to-all(f32[64,1,64]{2,1,0:T(1,128)S(1)} %broadcast_in_dim.26), channel_id=1, replica_groups=mesh['xl'=2,'core'=2,'z'=8,'xh'=2,'y'=4] {'z','xh','y'}, dimensions={0} | all-to-all | bytes 32768 | tf_op jit(solution)/shard_map/all_to_all | solution.py:38
  (67 shorter events, 15.4 us)
Async XLA Ops:
  6.5 131.1 %copy-start = (bf16[8,80,1024]{2,1,0:T(8,128)(2,1)S(1)}, bf16[8,80,1024]{2,1,0:T(8,128)(2,1)}, u32[]{:S(2)}) copy-start(bf16[8,80,1024]{2,1,0:T(8,128)(2,1)} %param.13) | copy-start | bytes 3932164
  6.5 54.3 %all-gather.2.cloned.1.call-start = ((), (), s32[]{:S(2)}) async-start(), calls=%async_computation.4 | async-start | bytes 2949120 | tf_op jit(solution)/shard_map/all_gather | solution.py:193
  11.6 9.8 %collective-permute-start.1 = (bf16[216,512]{1,0:T(8,128)(2,1)}, bf16[216,512]{1,0:T(8,128)(2,1)S(1)}, u32[]{:S(2)}, u32[]{:S(2)}) collective-permute-start(bf16[216,512]{1,0:T(8,128)(2,1)} %get-tuple-element.16), channel_id=1, source_target_pairs={{0,3},{1,0},{2,1},{3,2},{4,7},{5,4},{6,5},{7,6},{8,11},{9,8},{10,9... | collective-permute-start | bytes 663560 | tf_op jit(solution)/shard_map/ppermute | solution.py:34
  12.4 11.9 %collective-permute-start = (bf16[216,512]{1,0:T(8,128)(2,1)}, bf16[216,512]{1,0:T(8,128)(2,1)S(1)}, u32[]{:S(2)}, u32[]{:S(2)}) collective-permute-start(bf16[216,512]{1,0:T(8,128)(2,1)} %get-tuple-element.16), channel_id=1, source_target_pairs={{0,1},{1,2},{2,3},{3,0},{4,5},{5,6},{6,7},{7,4},{8,9},{9,10},{10,1... | collective-permute-start | bytes 663560 | tf_op jit(solution)/shard_map/ppermute | solution.py:34
  14.9 10.5 %collective-permute-start.6 = (bf16[216,512]{1,0:T(8,128)(2,1)}, bf16[216,512]{1,0:T(8,128)(2,1)S(1)}, u32[]{:S(2)}, u32[]{:S(2)}) collective-permute-start(bf16[216,512]{1,0:T(8,128)(2,1)} %get-tuple-element.18), channel_id=1, source_target_pairs={{0,1},{1,2},{2,3},{3,0},{4,5},{5,6},{6,7},{7,4},{8,9},{9,10},{10,1... | collective-permute-start | bytes 663560 | tf_op jit(solution)/shard_map/ppermute | solution.py:34
  15.6 10.5 %collective-permute-start.7 = (bf16[216,512]{1,0:T(8,128)(2,1)}, bf16[216,512]{1,0:T(8,128)(2,1)S(1)}, u32[]{:S(2)}, u32[]{:S(2)}) collective-permute-start(bf16[216,512]{1,0:T(8,128)(2,1)} %get-tuple-element.19), channel_id=1, source_target_pairs={{0,3},{1,0},{2,1},{3,2},{4,7},{5,4},{6,5},{7,6},{8,11},{9,8},{10,9... | collective-permute-start | bytes 663560 | tf_op jit(solution)/shard_map/ppermute | solution.py:34
  21.4 13.1 %collective-permute-start.2 = (bf16[216,512]{1,0:T(8,128)(2,1)S(1)}, bf16[216,512]{1,0:T(8,128)(2,1)S(1)}, u32[]{:S(2)}, u32[]{:S(2)}) collective-permute-start(bf16[216,512]{1,0:T(8,128)(2,1)S(1)} %collective-permute-done.1.h2), channel_id=1, source_target_pairs={{0,3},{1,0},{2,1},{3,2},{4,7},{5,4},{6,5},{7,6},{8,11},{9,8},{10,9... | collective-permute-start | bytes 663560 | tf_op jit(solution)/shard_map/ppermute | solution.py:34
  21.4 13.0 %collective-permute-start.9 = (bf16[80,2560]{1,0:T(8,128)(2,1)S(1)}, bf16[80,2560]{1,0:T(8,128)(2,1)S(1)}, u32[]{:S(2)}, u32[]{:S(2)}) collective-permute-start(bf16[80,2560]{1,0:T(8,128)(2,1)S(1)} %halve.1.b_own), channel_id=1, source_target_pairs={{0,132},{4,128},{128,4},{132,0},{1,133},{5,129},{129,5},{133,1},{2... | collective-permute-start | bytes 1228808 | tf_op jit(solution)/shard_map/ppermute | solution.py:34
  24.3 10.2 %collective-permute-start.8 = (bf16[216,512]{1,0:T(8,128)(2,1)}, bf16[216,512]{1,0:T(8,128)(2,1)S(1)}, u32[]{:S(2)}, u32[]{:S(2)}) collective-permute-start(bf16[216,512]{1,0:T(8,128)(2,1)} %get-tuple-element.20), channel_id=1, source_target_pairs={{0,2},{1,3},{2,0},{3,1},{4,6},{5,7},{6,4},{7,5},{8,10},{9,11},{10,... | collective-permute-start | bytes 663560 | tf_op jit(solution)/shard_map/ppermute | solution.py:34
  25.4 9.1 %collective-permute-start.4 = (bf16[216,512]{1,0:T(8,128)(2,1)S(1)}, bf16[216,512]{1,0:T(8,128)(2,1)S(1)}, u32[]{:S(2)}, u32[]{:S(2)}) collective-permute-start(bf16[216,512]{1,0:T(8,128)(2,1)S(1)} %collective-permute-done.1.h2), channel_id=1, source_target_pairs={{0,64},{64,0},{1,65},{65,1},{2,66},{66,2},{3,67},{67,3},{4,68},{68... | collective-permute-start | bytes 663560 | tf_op jit(solution)/shard_map/ppermute | solution.py:34
  26.1 8.4 %collective-permute-start.3 = (bf16[216,512]{1,0:T(8,128)(2,1)S(1)}, bf16[216,512]{1,0:T(8,128)(2,1)S(1)}, u32[]{:S(2)}, u32[]{:S(2)}) collective-permute-start(bf16[216,512]{1,0:T(8,128)(2,1)S(1)} %collective-permute-done.h1), channel_id=1, source_target_pairs={{0,64},{64,0},{1,65},{65,1},{2,66},{66,2},{3,67},{67,3},{4,68},{68... | collective-permute-start | bytes 663560 | tf_op jit(solution)/shard_map/ppermute | solution.py:34
  34.5 1.5 collective-permute-start.5
  39.1 20.5 %collective-permute-start.10 = (bf16[160,2560]{1,0:T(8,128)(2,1)}, bf16[160,2560]{1,0:T(8,128)(2,1)S(1)}, u32[]{:S(2)}, u32[]{:S(2)}) collective-permute-start(bf16[160,2560]{1,0:T(8,128)(2,1)} %get-tuple-element.21.b0), channel_id=1, source_target_pairs={{0,1},{1,2},{2,3},{3,0},{4,5},{5,6},{6,7},{7,4},{8,9},{9,10},{10,1... | collective-permute-start | bytes 2457608 | tf_op jit(solution)/shard_map/ppermute | solution.py:34
  39.1 21.7 %collective-permute-start.11 = (bf16[160,2560]{1,0:T(8,128)(2,1)}, bf16[160,2560]{1,0:T(8,128)(2,1)S(1)}, u32[]{:S(2)}, u32[]{:S(2)}) collective-permute-start(bf16[160,2560]{1,0:T(8,128)(2,1)} %get-tuple-element.21.b0), channel_id=1, source_target_pairs={{0,3},{1,0},{2,1},{3,2},{4,7},{5,4},{6,5},{7,6},{8,11},{9,8},{10,9... | collective-permute-start | bytes 2457608 | tf_op jit(solution)/shard_map/ppermute | solution.py:34
  41.2 40.7 %all-to-all-start = ((bf16[16,64,512]{2,1,0:T(8,128)(2,1)}), bf16[16,64,512]{2,1,0:T(8,128)(2,1)}, u32[]{:S(2)}, u32[]{:S(2)}) async-start(bf16[16,64,512]{2,1,0:T(8,128)(2,1)} %bitcast.27), calls=%async_computation | async-start | bytes 2097152 | tf_op jit(solution)/shard_map/all_to_all | solution.py:211
  62.7 13.6 %collective-permute-start.12 = (bf16[256,2560]{1,0:T(8,128)(2,1)S(1)}, bf16[256,2560]{1,0:T(8,128)(2,1)S(1)}, u32[]{:S(2)}, u32[]{:S(2)}) collective-permute-start(bf16[256,2560]{1,0:T(8,128)(2,1)S(1)} %cut.1), channel_id=1, source_target_pairs={{0,64},{64,0},{1,65},{65,1},{2,66},{66,2},{3,67},{67,3},{4,68},{68... | collective-permute-start | bytes 3932168 | tf_op jit(solution)/shard_map/ppermute | solution.py:34
  62.8 12.1 %collective-permute-start.13 = (bf16[160,1280]{1,0:T(8,128)(2,1)S(1)}, bf16[160,1280]{1,0:T(8,128)(2,1)S(1)}, u32[]{:S(2)}, u32[]{:S(2)}) collective-permute-start(bf16[160,1280]{1,0:T(8,128)(2,1)S(1)} %slice.8), channel_id=1, source_target_pairs={{0,1},{1,2},{2,3},{3,0},{4,5},{5,6},{6,7},{7,4},{8,9},{9,10},{10,1... | collective-permute-start | bytes 1228808 | tf_op jit(solution)/shard_map/ppermute | solution.py:34
  63.4 12.9 %collective-permute-start.14 = (bf16[160,1280]{1,0:T(8,128)(2,1)S(1)}, bf16[160,1280]{1,0:T(8,128)(2,1)S(1)}, u32[]{:S(2)}, u32[]{:S(2)}) collective-permute-start(bf16[160,1280]{1,0:T(8,128)(2,1)S(1)} %slice.9), channel_id=1, source_target_pairs={{0,3},{1,0},{2,1},{3,2},{4,7},{5,4},{6,5},{7,6},{8,11},{9,8},{10,9... | collective-permute-start | bytes 1228808 | tf_op jit(solution)/shard_map/ppermute | solution.py:34
  81.9 10.8 %collective-permute-start.15 = (f32[640,256]{1,0:T(8,128)}, f32[640,256]{1,0:T(8,128)S(1)}, u32[]{:S(2)}, u32[]{:S(2)}) collective-permute-start(f32[640,256]{1,0:T(8,128)} %get-tuple-element.23.refs_0_), channel_id=1, source_target_pairs={{0,64},{64,0},{1,65},{65,1},{2,66},{66,2},{3,67},{67,3},{4,68},{68... | collective-permute-start | bytes 1966088 | tf_op jit(solution)/shard_map/ppermute | solution.py:34
  84.2 26.6 %all-to-all-start.1 = ((bf16[8,64,512]{2,1,0:T(8,128)(2,1)}), bf16[8,64,512]{2,1,0:T(8,128)(2,1)S(1)}, u32[]{:S(2)}, u32[]{:S(2)}) async-start(bf16[8,64,512]{2,1,0:T(8,128)(2,1)} %live.1), calls=%async_computation.1 | async-start | bytes 1048576 | tf_op jit(solution)/shard_map/all_to_all | solution.py:218
  92.7 18.1 %collective-permute-start.16 = (bf16[640,256]{1,0:T(8,128)(2,1)S(1)}, bf16[640,256]{1,0:T(8,128)(2,1)S(1)}, u32[]{:S(2)}, u32[]{:S(2)}) collective-permute-start(bf16[640,256]{1,0:T(8,128)(2,1)S(1)} %add.22.ra), channel_id=1, source_target_pairs={{0,4},{4,0},{1,5},{5,1},{2,6},{6,2},{3,7},{7,3},{8,12},{12,8},{9,1... | collective-permute-start | bytes 983048 | tf_op jit(solution)/shard_map/ppermute | solution.py:34
  136.8 8.4 %collective-permute-start.18 = (bf16[2,80,1024]{2,1,0:T(8,128)(2,1)S(1)}, bf16[2,80,1024]{2,1,0:T(8,128)(2,1)S(1)}, u32[]{:S(2)}, u32[]{:S(2)}) collective-permute-start(bf16[2,80,1024]{2,1,0:T(8,128)(2,1)S(1)} %sums.1), channel_id=1, source_target_pairs={{0,128},{128,0},{1,129},{129,1},{2,130},{130,2},{3,131},{131,3},{4... | collective-permute-start | bytes 983048 | tf_op jit(solution)/shard_map/ppermute | solution.py:34
  137.6 9.1 %collective-permute-start.17 = (bf16[2,80,1024]{2,1,0:T(8,128)(2,1)S(1)}, bf16[2,80,1024]{2,1,0:T(8,128)(2,1)S(1)}, u32[]{:S(2)}, u32[]{:S(2)}) collective-permute-start(bf16[2,80,1024]{2,1,0:T(8,128)(2,1)S(1)} %sums.1), channel_id=1, source_target_pairs={{0,64},{64,0},{1,65},{65,1},{2,66},{66,2},{3,67},{67,3},{4,68},{68... | collective-permute-start | bytes 983048 | tf_op jit(solution)/shard_map/ppermute | solution.py:34
  145.2 2.9 %collective-permute-start.19 = (bf16[2,80,1024]{2,1,0:T(8,128)(2,1)S(1)}, bf16[2,80,1024]{2,1,0:T(8,128)(2,1)S(1)}, u32[]{:S(2)}, u32[]{:S(2)}) collective-permute-start(bf16[2,80,1024]{2,1,0:T(8,128)(2,1)S(1)} %collective-permute-done.18), channel_id=1, source_target_pairs={{0,64},{64,0},{1,65},{65,1},{2,66},{66,2},{3,67},{67,3},{4,68},{68... | collective-permute-start | bytes 983048 | tf_op jit(solution)/shard_map/ppermute | solution.py:34
  (9 other events, 109.4 us)
Sparse Core Ops, SparseCore 0:
  9.1 44.9 all-gather.1

commit v14 on v13

--- a/solution.py
+++ b/solution.py
@@ -86,27 +86,27 @@
     )(block_ids, y[None], core[None], *[basis_out] * 8, out_grads)
 
 
-def halve_kernel(s_ref, b_ref, o_ref):
-    o_ref[...] = b_ref[...]
-
-
-def halve(core, basis_in):
-    rows, half = basis_in.shape[0], basis_in.shape[1] // 2
+def halve_kernel(s_ref, b_ref, *refs):
+    refs[-1][...] = b_ref[...]
+
+
+def halve(which, x, aside=(), params=ROOM):
+    rows, half = x.shape[0], x.shape[1] // 2
     spec = pltpu.PrefetchScalarGridSpec(
         num_scalar_prefetch=1,
         grid=(1,),
-        in_specs=[pl.BlockSpec((rows, half), lambda g, s: (0, s[0]))],
+        in_specs=[pl.BlockSpec((rows, half), lambda g, s: (0, s[0]))]
+        + [pl.BlockSpec(memory_space=pl.ANY)] * len(aside),
         out_specs=pl.BlockSpec((rows, half), lambda g, s: (0, 0)),
     )
     return pl.pallas_call(
-        halve_kernel, grid_spec=spec, out_shape=arr(rows, half), compiler_params=ROOM, name="halve"
-    )(core[None], basis_in)
-
-
-def cut_kernel(core_ref, a_ref, *refs):
-    o_ref = refs[-1]
-    half = o_ref.shape[1]
-    o_ref[...] = a_ref[:, pl.ds(pl.multiple_of((1 - core_ref[0]) * half, 128), half)]
+        halve_kernel,
+        grid_spec=spec,
+        out_shape=arr(rows, half),
+        compiler_params=params,
+        cost_estimate=TINY,
+        name="halve",
+    )(which[None], x, *aside)
 
 
 def grads_kernel(core_ref, c0, h1, h2, h3, o1, o2, o3, g0, g1, g2, g3, b_own, b_far, o_ref, b0):
@@ -210,7 +210,7 @@
     b3a, b3b = shift(b1[:, : half // 2], y=1), shift(b2[:, half // 2 :], y=-1)
     parts = lax.all_to_all(partial.reshape(16, 64, 512), ("xh", "z"), split_axis=0, concat_axis=0, tiled=True)
     wide = jax.ShapeDtypeStruct((640, 256), F32)
-    sib = shift(call(cut_kernel, arr(256, half), "cut", [acts], [core[None]], [b1, b2]), core=1)
+    sib = shift(halve(1 - core, acts, [b1, b2], pltpu.CompilerParams(vmem_limit_bytes=50 * 1024 * 1024)), core=1)
     keep, send = call(acts_kernel, [wide, wide], "acts", [acts, sib, b0, b1, b2, b3a, b3b], [core[None]])
     ra = call(add_kernel, arr(640, 256), "add", [keep, shift(send, core=1)])
     rb = shift(ra, xh=1)

time: 176 us -> 176 us (level)
    unnamed x20 -> x18, local copies, waits for them, and re-layouts: 3.6 us -> 1.87 us
    pallas_call x7 -> x6, Pallas kernels: 10.9 us -> 10.8 us  [call(): pl.pallas_call(kernel, out_shape=out, in_specs=specs, out_specs=jax.tree....]
  transfers between devices with their start and end apart: 23 -> 23, of which waited for: 10 -> 10; matrix products, arithmetic and copies ran while one was open for 3% -> 3% of each run, Pallas kernels for 8% -> 9%
where the time goes in v14:
time: 176 us; the launch traced here: 173 us
  waiting for transfers between devices  56.5 us (32%)
  blocking collectives  40.9 us (23%)
  starting transfers between devices  37.2 us (21%)
  Pallas kernels  16.6 us (9%)
  between operations  13.6 us (8%)
  matrix products  5.87 us (3%)
  local copies, waits for them, and re-layouts  2.72 us (2%)
    ppermute x20, waiting for transfers between devices, shift(): return lax.ppermute(x, axes, pairs)  40.8 us
    all_to_all x1, blocking collectives, per_device(): lax.all_to_all(tiles, ('xh', 'y'), split_axis=0, concat_axis=0, tiled=True)  24.5 us
    ppermute x20, starting transfers between devices, shift(): return lax.ppermute(x, axes, pairs)  17.7 us
    all_to_all x1, blocking collectives, spread(): lax.all_to_all(jnp.broadcast_to(x[None], (count,) + x.shape), axes, split...  16.4 us
    all_to_all x1, waiting for transfers between devices, per_device(): lax.all_to_all(copies, 'z', split_axis=0, concat_axis=0, tiled=True)  15 us
    all_to_all x1, starting transfers between devices, per_device(): lax.all_to_all(partial.reshape(16, 64, 512), ('xh', 'z'), split_axis=0, c...  11.1 us
    pallas_call x6, Pallas kernels, call(): pl.pallas_call(kernel, out_shape=out, in_specs=specs, out_specs=jax.tree....  10.8 us
    all_to_all x1, starting transfers between devices, per_device(): lax.all_to_all(copies, 'z', split_axis=0, concat_axis=0, tiled=True)  8.46 us
  transfers between devices with their start and end apart: 23, of which 10 were waited for; matrix products, arithmetic and copies ran while one was open for 3% of the time, Pallas kernels for 9%

profile of v14, /device:TPU:24, one launch (start us, length us, event | category | flops | bytes accessed | tf_op | source)
XLA Modules:
  0.0 173.4 jit_solution(12948393111212185248)
XLA Ops:
  7.3 4.3 %pick.1 = (bf16[216,1024]{1,0:T(8,128)(2,1)}, bf16[216,512]{1,0:T(8,128)(2,1)}, bf16[216,512]{1,0:T(8,128)(2,1)}, bf16[216,512]{1,0:T(8,128)(2,1)}, bf16[216,512]{1,0:T(8,128)(2,1)}, /*index=5*/bf16[216,512]{1,0:T(8,128)(2,1)}) custom-call(s32[8]{0:T(128)} %ids.1, s32[1]{0:T(128)} %bitcast.1.y_ref, s32[1]{0:T(128)} %bitcast.2.core_ref.s_ref, ...), custom_call_target="tpu_custom_call" | custom-call | tf_op jit(solution)/shard_map/pick/pallas_call | solution.py:80
  12.4 2.5 %collective-permute-start = (bf16[216,512]{1,0:T(8,128)(2,1)}, bf16[216,512]{1,0:T(8,128)(2,1)S(1)}, u32[]{:S(2)}, u32[]{:S(2)}) collective-permute-start(bf16[216,512]{1,0:T(8,128)(2,1)} %get-tuple-element.16), channel_id=1, source_target_pairs={{0,1},{1,2},{2,3},{3,0},{4,5},{5,6},{6,7},{7,4},{8,9},{9,10},{10,1... | collective-permute-start | bytes 663560 | tf_op jit(solution)/shard_map/ppermute | solution.py:34
  16.9 4.5 %collective-permute-done.1.h2 = bf16[216,512]{1,0:T(8,128)(2,1)S(1)} collective-permute-done((bf16[216,512]{1,0:T(8,128)(2,1)}, bf16[216,512]{1,0:T(8,128)(2,1)S(1)}, u32[]{:S(2)}, u32[]{:S(2)}) %collective-permute-start.1) | collective-permute-done | bytes 221216 | tf_op jit(solution)/shard_map/ppermute | solution.py:34
  21.4 2.8 %collective-permute-start.9 = (bf16[80,2560]{1,0:T(8,128)(2,1)S(1)}, bf16[80,2560]{1,0:T(8,128)(2,1)S(1)}, u32[]{:S(2)}, u32[]{:S(2)}) collective-permute-start(bf16[80,2560]{1,0:T(8,128)(2,1)S(1)} %halve.2.b_own), channel_id=1, source_target_pairs={{0,132},{4,128},{128,4},{132,0},{1,133},{5,129},{129,5},{133,1},{2... | collective-permute-start | bytes 1228808 | tf_op jit(solution)/shard_map/ppermute | solution.py:34
  26.1 8.3 %collective-permute-done.2.h3 = bf16[216,512]{1,0:T(8,128)(2,1)S(1)} collective-permute-done((bf16[216,512]{1,0:T(8,128)(2,1)S(1)}, bf16[216,512]{1,0:T(8,128)(2,1)S(1)}, u32[]{:S(2)}, u32[]{:S(2)}) %collective-permute-start.2) | collective-permute-done | bytes 221216 | tf_op jit(solution)/shard_map/ppermute | solution.py:34
  35.9 2.2 %grads.1 = (bf16[1024,512]{1,0:T(8,128)(2,1)S(1)}, bf16[160,2560]{1,0:T(8,128)(2,1)}) custom-call(s32[1]{0:T(128)} %bitcast.2.core_ref.s_ref, bf16[216,1024]{1,0:T(8,128)(2,1)S(1)} %copy-done.6, bf16[216,512]{1,0:T(8,128)(2,1)S(1)} %collective-permute-done.h1, bf16[216,512]{1,0:T(8,128)(2,1)S(1)} %collective-permute-done.1.h2, ...), custom_call_target="tpu_custom_call" | custom-call | flops 1 | bytes 1 | tf_op jit(solution)/shard_map/grads/pallas_call | solution.py:176
  39.1 2.0 %collective-permute-start.11 = (bf16[160,2560]{1,0:T(8,128)(2,1)}, bf16[160,2560]{1,0:T(8,128)(2,1)S(1)}, u32[]{:S(2)}, u32[]{:S(2)}) collective-permute-start(bf16[160,2560]{1,0:T(8,128)(2,1)} %get-tuple-element.21.b0), channel_id=1, source_target_pairs={{0,3},{1,0},{2,1},{3,2},{4,7},{5,4},{6,5},{7,6},{8,11},{9,8},{10,9... | collective-permute-start | bytes 2457608 | tf_op jit(solution)/shard_map/ppermute | solution.py:34
  41.2 11.1 %all-to-all-start = ((bf16[16,64,512]{2,1,0:T(8,128)(2,1)}), bf16[16,64,512]{2,1,0:T(8,128)(2,1)}, u32[]{:S(2)}, u32[]{:S(2)}) async-start(bf16[16,64,512]{2,1,0:T(8,128)(2,1)} %bitcast.28), calls=%async_computation | async-start | bytes 2097152 | tf_op jit(solution)/shard_map/all_to_all | solution.py:211
  52.3 7.4 %collective-permute-done.10.refs_0_.b1 = bf16[160,2560]{1,0:T(8,128)(2,1)S(1)} collective-permute-done((bf16[160,2560]{1,0:T(8,128)(2,1)}, bf16[160,2560]{1,0:T(8,128)(2,1)S(1)}, u32[]{:S(2)}, u32[]{:S(2)}) %collective-permute-start.10) | collective-permute-done | bytes 819232 | tf_op jit(solution)/shard_map/ppermute | solution.py:34
  60.9 1.6 halve.3
  63.1 1.8 %collective-permute-start.14 = (bf16[160,1280]{1,0:T(8,128)(2,1)S(1)}, bf16[160,1280]{1,0:T(8,128)(2,1)S(1)}, u32[]{:S(2)}, u32[]{:S(2)}) collective-permute-start(bf16[160,1280]{1,0:T(8,128)(2,1)S(1)} %slice.9), channel_id=1, source_target_pairs={{0,3},{1,0},{2,1},{3,2},{4,7},{5,4},{6,5},{7,6},{8,11},{9,8},{10,9... | collective-permute-start | bytes 1228808 | tf_op jit(solution)/shard_map/ppermute | solution.py:34
  64.9 9.7 %collective-permute-done.13.b3a = bf16[160,1280]{1,0:T(8,128)(2,1)S(1)} collective-permute-done((bf16[160,1280]{1,0:T(8,128)(2,1)S(1)}, bf16[160,1280]{1,0:T(8,128)(2,1)S(1)}, u32[]{:S(2)}, u32[]{:S(2)}) %collective-permute-start.13) | collective-permute-done | bytes 409632 | tf_op jit(solution)/shard_map/ppermute | solution.py:34
  76.0 4.7 %acts.1 = (f32[640,256]{1,0:T(8,128)S(1)}, f32[640,256]{1,0:T(8,128)}) custom-call(s32[1]{0:T(128)} %bitcast.2.core_ref.s_ref, bf16[256,5120]{1,0:T(8,128)(2,1)S(1)} %copy-done.1, bf16[256,2560]{1,0:T(8,128)(2,1)S(1)} %collective-permute-done.12.sib, bf16[160,2560]{1,0:T(8,128)(2,1)} %get-tuple-element.21.b0, ...), custom_call_target="tpu_custom_call" | custom-call | flops 1 | bytes 1 | tf_op jit(solution)/shard_map/acts/pallas_call | solution.py:176
  81.6 2.3 %live.1 = bf16[8,64,512]{2,1,0:T(8,128)(2,1)} custom-call(s32[1]{0:T(128)} %bitcast.1.y_ref, s32[2]{0:T(128)S(1)} %copy-done.8, bf16[16,64,512]{2,1,0:T(8,128)(2,1)} %all-to-all-done.parts, f32[640,256]{1,0:T(8,128)} %get-tuple-element.23.refs_0_), custom_call_target="tpu_custom_call" | custom-call | flops 1 | bytes 1 | tf_op jit(solution)/shard_map/live/pallas_call | solution.py:176
  83.9 8.5 %all-to-all-start.1 = ((bf16[8,64,512]{2,1,0:T(8,128)(2,1)}), bf16[8,64,512]{2,1,0:T(8,128)(2,1)S(1)}, u32[]{:S(2)}, u32[]{:S(2)}) async-start(bf16[8,64,512]{2,1,0:T(8,128)(2,1)} %live.1), calls=%async_computation.1 | async-start | bytes 1048576 | tf_op jit(solution)/shard_map/all_to_all | solution.py:218
  92.4 3.1 %collective-permute-start.16 = (bf16[640,256]{1,0:T(8,128)(2,1)S(1)}, bf16[640,256]{1,0:T(8,128)(2,1)S(1)}, u32[]{:S(2)}, u32[]{:S(2)}) collective-permute-start(bf16[640,256]{1,0:T(8,128)(2,1)S(1)} %add.22.ra), channel_id=1, source_target_pairs={{0,4},{4,0},{1,5},{5,1},{2,6},{6,2},{3,7},{7,3},{8,12},{12,8},{9,1... | collective-permute-start | bytes 983048 | tf_op jit(solution)/shard_map/ppermute | solution.py:34
  95.5 15.0 %all-to-all-done.1 = bf16[8,64,512]{2,1,0:T(8,128)(2,1)S(1)} async-done(((bf16[8,64,512]{2,1,0:T(8,128)(2,1)}), bf16[8,64,512]{2,1,0:T(8,128)(2,1)S(1)}, u32[]{:S(2)}, u32[]{:S(2)}) %all-to-all-start.1) | async-done | bytes 524320 | tf_op jit(solution)/shard_map/all_to_all | solution.py:218
  111.9 24.5 %all_to_all.20.parts = bf16[8,2,80,512]{3,2,1,0:T(8,128)(2,1)S(1)} all-to-all(bf16[8,2,80,512]{3,2,1,0:T(8,128)(2,1)S(1)} %seq.1), channel_id=1, replica_groups=mesh['xl'=2,'core'=2,'z'=8,'xh'=2,'y'=4] {'xh','y'}, dimensions={0} | all-to-all | bytes 2621440 | tf_op jit(solution)/shard_map/all_to_all | solution.py:221
  137.3 1.5 convolution_bitcast_fusion.3
  138.8 6.1 %collective-permute-done.18 = bf16[2,80,1024]{2,1,0:T(8,128)(2,1)S(1)} collective-permute-done((bf16[2,80,1024]{2,1,0:T(8,128)(2,1)S(1)}, bf16[2,80,1024]{2,1,0:T(8,128)(2,1)S(1)}, u32[]{:S(2)}, u32[]{:S(2)}) %collective-permute-start.18) | collective-permute-done | bytes 327712 | tf_op jit(solution)/shard_map/ppermute | solution.py:34
  144.9 1.5 convolution_bitcast_fusion.1
  146.4 1.5 convolution_bitcast_fusion.2
  147.9 1.5 convolution_bitcast_fusion
  149.5 16.4 %all_to_all.21 = f32[64,1,64]{2,1,0:T(1,128)S(1)} all-to-all(f32[64,1,64]{2,1,0:T(1,128)S(1)} %broadcast_in_dim.29), channel_id=1, replica_groups=mesh['xl'=2,'core'=2,'z'=8,'xh'=2,'y'=4] {'z','xh','y'}, dimensions={0} | all-to-all | bytes 32768 | tf_op jit(solution)/shard_map/all_to_all | solution.py:38
  (65 shorter events, 15.3 us)
Async XLA Ops:
  6.5 130.8 %copy-start = (bf16[8,80,1024]{2,1,0:T(8,128)(2,1)S(1)}, bf16[8,80,1024]{2,1,0:T(8,128)(2,1)}, u32[]{:S(2)}) copy-start(bf16[8,80,1024]{2,1,0:T(8,128)(2,1)} %param.13) | copy-start | bytes 3932164
  6.5 54.3 %all-gather.2.cloned.1.call-start = ((), (), s32[]{:S(2)}) async-start(), calls=%async_computation.4 | async-start | bytes 2949120 | tf_op jit(solution)/shard_map/all_gather | solution.py:193
  11.6 9.8 %collective-permute-start.1 = (bf16[216,512]{1,0:T(8,128)(2,1)}, bf16[216,512]{1,0:T(8,128)(2,1)S(1)}, u32[]{:S(2)}, u32[]{:S(2)}) collective-permute-start(bf16[216,512]{1,0:T(8,128)(2,1)} %get-tuple-element.16), channel_id=1, source_target_pairs={{0,3},{1,0},{2,1},{3,2},{4,7},{5,4},{6,5},{7,6},{8,11},{9,8},{10,9... | collective-permute-start | bytes 663560 | tf_op jit(solution)/shard_map/ppermute | solution.py:34
  12.4 11.9 %collective-permute-start = (bf16[216,512]{1,0:T(8,128)(2,1)}, bf16[216,512]{1,0:T(8,128)(2,1)S(1)}, u32[]{:S(2)}, u32[]{:S(2)}) collective-permute-start(bf16[216,512]{1,0:T(8,128)(2,1)} %get-tuple-element.16), channel_id=1, source_target_pairs={{0,1},{1,2},{2,3},{3,0},{4,5},{5,6},{6,7},{7,4},{8,9},{9,10},{10,1... | collective-permute-start | bytes 663560 | tf_op jit(solution)/shard_map/ppermute | solution.py:34
  14.9 10.5 %collective-permute-start.6 = (bf16[216,512]{1,0:T(8,128)(2,1)}, bf16[216,512]{1,0:T(8,128)(2,1)S(1)}, u32[]{:S(2)}, u32[]{:S(2)}) collective-permute-start(bf16[216,512]{1,0:T(8,128)(2,1)} %get-tuple-element.18), channel_id=1, source_target_pairs={{0,1},{1,2},{2,3},{3,0},{4,5},{5,6},{6,7},{7,4},{8,9},{9,10},{10,1... | collective-permute-start | bytes 663560 | tf_op jit(solution)/shard_map/ppermute | solution.py:34
  15.6 10.5 %collective-permute-start.7 = (bf16[216,512]{1,0:T(8,128)(2,1)}, bf16[216,512]{1,0:T(8,128)(2,1)S(1)}, u32[]{:S(2)}, u32[]{:S(2)}) collective-permute-start(bf16[216,512]{1,0:T(8,128)(2,1)} %get-tuple-element.19), channel_id=1, source_target_pairs={{0,3},{1,0},{2,1},{3,2},{4,7},{5,4},{6,5},{7,6},{8,11},{9,8},{10,9... | collective-permute-start | bytes 663560 | tf_op jit(solution)/shard_map/ppermute | solution.py:34
  21.4 13.1 %collective-permute-start.2 = (bf16[216,512]{1,0:T(8,128)(2,1)S(1)}, bf16[216,512]{1,0:T(8,128)(2,1)S(1)}, u32[]{:S(2)}, u32[]{:S(2)}) collective-permute-start(bf16[216,512]{1,0:T(8,128)(2,1)S(1)} %collective-permute-done.1.h2), channel_id=1, source_target_pairs={{0,3},{1,0},{2,1},{3,2},{4,7},{5,4},{6,5},{7,6},{8,11},{9,8},{10,9... | collective-permute-start | bytes 663560 | tf_op jit(solution)/shard_map/ppermute | solution.py:34
  21.4 13.0 %collective-permute-start.9 = (bf16[80,2560]{1,0:T(8,128)(2,1)S(1)}, bf16[80,2560]{1,0:T(8,128)(2,1)S(1)}, u32[]{:S(2)}, u32[]{:S(2)}) collective-permute-start(bf16[80,2560]{1,0:T(8,128)(2,1)S(1)} %halve.2.b_own), channel_id=1, source_target_pairs={{0,132},{4,128},{128,4},{132,0},{1,133},{5,129},{129,5},{133,1},{2... | collective-permute-start | bytes 1228808 | tf_op jit(solution)/shard_map/ppermute | solution.py:34
  24.3 10.2 %collective-permute-start.8 = (bf16[216,512]{1,0:T(8,128)(2,1)}, bf16[216,512]{1,0:T(8,128)(2,1)S(1)}, u32[]{:S(2)}, u32[]{:S(2)}) collective-permute-start(bf16[216,512]{1,0:T(8,128)(2,1)} %get-tuple-element.20), channel_id=1, source_target_pairs={{0,2},{1,3},{2,0},{3,1},{4,6},{5,7},{6,4},{7,5},{8,10},{9,11},{10,... | collective-permute-start | bytes 663560 | tf_op jit(solution)/shard_map/ppermute | solution.py:34
  25.4 9.1 %collective-permute-start.4 = (bf16[216,512]{1,0:T(8,128)(2,1)S(1)}, bf16[216,512]{1,0:T(8,128)(2,1)S(1)}, u32[]{:S(2)}, u32[]{:S(2)}) collective-permute-start(bf16[216,512]{1,0:T(8,128)(2,1)S(1)} %collective-permute-done.1.h2), channel_id=1, source_target_pairs={{0,64},{64,0},{1,65},{65,1},{2,66},{66,2},{3,67},{67,3},{4,68},{68... | collective-permute-start | bytes 663560 | tf_op jit(solution)/shard_map/ppermute | solution.py:34
  26.1 8.4 %collective-permute-start.3 = (bf16[216,512]{1,0:T(8,128)(2,1)S(1)}, bf16[216,512]{1,0:T(8,128)(2,1)S(1)}, u32[]{:S(2)}, u32[]{:S(2)}) collective-permute-start(bf16[216,512]{1,0:T(8,128)(2,1)S(1)} %collective-permute-done.h1), channel_id=1, source_target_pairs={{0,64},{64,0},{1,65},{65,1},{2,66},{66,2},{3,67},{67,3},{4,68},{68... | collective-permute-start | bytes 663560 | tf_op jit(solution)/shard_map/ppermute | solution.py:34
  34.5 1.5 collective-permute-start.5
  39.1 20.5 %collective-permute-start.10 = (bf16[160,2560]{1,0:T(8,128)(2,1)}, bf16[160,2560]{1,0:T(8,128)(2,1)S(1)}, u32[]{:S(2)}, u32[]{:S(2)}) collective-permute-start(bf16[160,2560]{1,0:T(8,128)(2,1)} %get-tuple-element.21.b0), channel_id=1, source_target_pairs={{0,1},{1,2},{2,3},{3,0},{4,5},{5,6},{6,7},{7,4},{8,9},{9,10},{10,1... | collective-permute-start | bytes 2457608 | tf_op jit(solution)/shard_map/ppermute | solution.py:34
  39.1 21.7 %collective-permute-start.11 = (bf16[160,2560]{1,0:T(8,128)(2,1)}, bf16[160,2560]{1,0:T(8,128)(2,1)S(1)}, u32[]{:S(2)}, u32[]{:S(2)}) collective-permute-start(bf16[160,2560]{1,0:T(8,128)(2,1)} %get-tuple-element.21.b0), channel_id=1, source_target_pairs={{0,3},{1,0},{2,1},{3,2},{4,7},{5,4},{6,5},{7,6},{8,11},{9,8},{10,9... | collective-permute-start | bytes 2457608 | tf_op jit(solution)/shard_map/ppermute | solution.py:34
  41.2 40.4 %all-to-all-start = ((bf16[16,64,512]{2,1,0:T(8,128)(2,1)}), bf16[16,64,512]{2,1,0:T(8,128)(2,1)}, u32[]{:S(2)}, u32[]{:S(2)}) async-start(bf16[16,64,512]{2,1,0:T(8,128)(2,1)} %bitcast.28), calls=%async_computation | async-start | bytes 2097152 | tf_op jit(solution)/shard_map/all_to_all | solution.py:211
  62.4 13.6 %collective-permute-start.12 = (bf16[256,2560]{1,0:T(8,128)(2,1)S(1)}, bf16[256,2560]{1,0:T(8,128)(2,1)S(1)}, u32[]{:S(2)}, u32[]{:S(2)}) collective-permute-start(bf16[256,2560]{1,0:T(8,128)(2,1)S(1)} %halve.3), channel_id=1, source_target_pairs={{0,64},{64,0},{1,65},{65,1},{2,66},{66,2},{3,67},{67,3},{4,68},{68... | collective-permute-start | bytes 3932168 | tf_op jit(solution)/shard_map/ppermute | solution.py:34
  62.5 12.1 %collective-permute-start.13 = (bf16[160,1280]{1,0:T(8,128)(2,1)S(1)}, bf16[160,1280]{1,0:T(8,128)(2,1)S(1)}, u32[]{:S(2)}, u32[]{:S(2)}) collective-permute-start(bf16[160,1280]{1,0:T(8,128)(2,1)S(1)} %slice.8), channel_id=1, source_target_pairs={{0,1},{1,2},{2,3},{3,0},{4,5},{5,6},{6,7},{7,4},{8,9},{9,10},{10,1... | collective-permute-start | bytes 1228808 | tf_op jit(solution)/shard_map/ppermute | solution.py:34
  63.1 12.9 %collective-permute-start.14 = (bf16[160,1280]{1,0:T(8,128)(2,1)S(1)}, bf16[160,1280]{1,0:T(8,128)(2,1)S(1)}, u32[]{:S(2)}, u32[]{:S(2)}) collective-permute-start(bf16[160,1280]{1,0:T(8,128)(2,1)S(1)} %slice.9), channel_id=1, source_target_pairs={{0,3},{1,0},{2,1},{3,2},{4,7},{5,4},{6,5},{7,6},{8,11},{9,8},{10,9... | collective-permute-start | bytes 1228808 | tf_op jit(solution)/shard_map/ppermute | solution.py:34
  81.6 10.8 %collective-permute-start.15 = (f32[640,256]{1,0:T(8,128)}, f32[640,256]{1,0:T(8,128)S(1)}, u32[]{:S(2)}, u32[]{:S(2)}) collective-permute-start(f32[640,256]{1,0:T(8,128)} %get-tuple-element.23.refs_0_), channel_id=1, source_target_pairs={{0,64},{64,0},{1,65},{65,1},{2,66},{66,2},{3,67},{67,3},{4,68},{68... | collective-permute-start | bytes 1966088 | tf_op jit(solution)/shard_map/ppermute | solution.py:34
  83.9 26.6 %all-to-all-start.1 = ((bf16[8,64,512]{2,1,0:T(8,128)(2,1)}), bf16[8,64,512]{2,1,0:T(8,128)(2,1)S(1)}, u32[]{:S(2)}, u32[]{:S(2)}) async-start(bf16[8,64,512]{2,1,0:T(8,128)(2,1)} %live.1), calls=%async_computation.1 | async-start | bytes 1048576 | tf_op jit(solution)/shard_map/all_to_all | solution.py:218
  92.4 18.1 %collective-permute-start.16 = (bf16[640,256]{1,0:T(8,128)(2,1)S(1)}, bf16[640,256]{1,0:T(8,128)(2,1)S(1)}, u32[]{:S(2)}, u32[]{:S(2)}) collective-permute-start(bf16[640,256]{1,0:T(8,128)(2,1)S(1)} %add.22.ra), channel_id=1, source_target_pairs={{0,4},{4,0},{1,5},{5,1},{2,6},{6,2},{3,7},{7,3},{8,12},{12,8},{9,1... | collective-permute-start | bytes 983048 | tf_op jit(solution)/shard_map/ppermute | solution.py:34
  136.5 8.4 %collective-permute-start.18 = (bf16[2,80,1024]{2,1,0:T(8,128)(2,1)S(1)}, bf16[2,80,1024]{2,1,0:T(8,128)(2,1)S(1)}, u32[]{:S(2)}, u32[]{:S(2)}) collective-permute-start(bf16[2,80,1024]{2,1,0:T(8,128)(2,1)S(1)} %sums.1), channel_id=1, source_target_pairs={{0,128},{128,0},{1,129},{129,1},{2,130},{130,2},{3,131},{131,3},{4... | collective-permute-start | bytes 983048 | tf_op jit(solution)/shard_map/ppermute | solution.py:34
  137.3 9.1 %collective-permute-start.17 = (bf16[2,80,1024]{2,1,0:T(8,128)(2,1)S(1)}, bf16[2,80,1024]{2,1,0:T(8,128)(2,1)S(1)}, u32[]{:S(2)}, u32[]{:S(2)}) collective-permute-start(bf16[2,80,1024]{2,1,0:T(8,128)(2,1)S(1)} %sums.1), channel_id=1, source_target_pairs={{0,64},{64,0},{1,65},{65,1},{2,66},{66,2},{3,67},{67,3},{4,68},{68... | collective-permute-start | bytes 983048 | tf_op jit(solution)/shard_map/ppermute | solution.py:34
  144.9 2.9 %collective-permute-start.19 = (bf16[2,80,1024]{2,1,0:T(8,128)(2,1)S(1)}, bf16[2,80,1024]{2,1,0:T(8,128)(2,1)S(1)}, u32[]{:S(2)}, u32[]{:S(2)}) collective-permute-start(bf16[2,80,1024]{2,1,0:T(8,128)(2,1)S(1)} %collective-permute-done.18), channel_id=1, source_target_pairs={{0,64},{64,0},{1,65},{65,1},{2,66},{66,2},{3,67},{67,3},{4,68},{68... | collective-permute-start | bytes 983048 | tf_op jit(solution)/shard_map/ppermute | solution.py:34
  (8 other events, 109.1 us)
Sparse Core Ops, SparseCore 0:
  9.1 44.9 all-gather.1
